TPU v7x, 256 devices: a whole 4x4x8 slice. The times are simulated.
256 devices in a mesh: patch: 16 (over y, x), span: 8 (over z), wall: 2 (over core).
Axes of the slice: x: 4, y: 4, z: 8, core: 2. Of those that a mesh axis runs over, the one named last changes fastest.
Arguments:
- rhs: float32 [32, 16, 5, 16384], P('span', 'wall', None, 'patch'), may hold values from -24 to 24
- jac: float32 [32, 16, 5, 5, 16384], P('span', 'wall', None, None, 'patch'), may hold values from -2 to 24
- jac_inv: float32 [32, 16, 5, 5, 16384], P('span', 'wall', None, None, 'patch'), may hold values from -0.04 to 0.13
- wall_coupling: float32 [5, 5], replicated, may hold values from -1.2 to 1.2
- span_coupling: float32 [5, 5], replicated, may hold values from -1.2 to 1.2
- block_owner: int32 [32, 16, 128], P('span', 'wall', 'patch'), may hold values from 0 to 15, as said below
- block_slot: int32 [32, 16, 128], P('span', 'wall', 'patch'), may hold values from 0 to 3
- coarse_inv: float32 [8, 2, 5, 10, 64], P('span', 'wall', None, None, 'patch'), may hold values from -0.045 to 0.045
Outputs:
- solution: float32 [32, 16, 5, 16384], P('span', 'wall', None, 'patch')
Inputs may be any that keep to these rules, and one draw needn't show every extreme that they name: `block_owner`: A device's blocks are those of its 4 spanwise cells, 8 wall-normal cells and 1024 lines. Of one device's 256 blocks at most 32 name one owner; in every span and wall group one owner receives exactly 32 blocks from each of the 16 devices along the patch axis.
All inputs are finite; a program needn't handle non-finite values.
Results may differ from a plain program's by a relative error of at most 0.000094.
Values sent between devices are 32-bit elements; how exact they have to be, the bound alone decides.
No kernel may reach another device: no remote copies, remote signals or barrier semaphores. Data moves between devices by JAX's collectives and lax.ppermute only.
A program may use at most 64 MiB of HBM per device.

v0:
```python
import jax
import jax.numpy as jnp
from jax import lax
from jax.sharding import PartitionSpec as P


def extended(array, sides, width):
    for axis, dim in sides:
        size, length = (lax.axis_size(axis), array.shape[dim])
        up = [(i, (i + 1) % size) for i in range(size - 1)]
        down = [(j, i) for i, j in up]
        last = lax.slice_in_dim(array, length - width, length, axis=dim)
        initial = lax.slice_in_dim(array, 0, width, axis=dim)
        before = lax.ppermute(last, axis, up)
        after = lax.ppermute(initial, axis, down)
        array = jnp.concatenate([before, array, after], axis=dim)
    return array


def apply_adjoint(field, jac, wall_coupling, span_coupling):
    highest = lax.Precision.HIGHEST
    padded = extended(field, (("span", 0), ("wall", 1)), 1)
    interior = padded[1:-1, 1:-1]
    own_term = jnp.sum(jac * interior[:, :, :, None, :], axis=2)
    near_wall = padded[1:-1, 2:] + padded[1:-1, :-2]
    near_span = padded[2:, 1:-1] + padded[:-2, 1:-1]
    wall_term = jnp.einsum("ki,swkl->swil", wall_coupling, near_wall, precision=highest)
    span_term = jnp.einsum("ki,swkl->swil", span_coupling, near_span, precision=highest)
    return own_term - wall_term - span_term


def precondition(defect, jac_inv):
    return jnp.sum(jac_inv * defect[:, :, None, :, :], axis=3)


def coarse_line(coarse_res, line_inv, groups, aggregates, equations):
    highest = lax.Precision.HIGHEST
    gathered = lax.all_gather(coarse_res[None], "wall", axis=0, tiled=True)
    gathered = gathered.reshape(groups, aggregates, equations, 128)
    coarse_fix = jnp.einsum("iBkg,Bgkj->gij", line_inv, gathered, precision=highest)
    return coarse_fix.reshape(aggregates, equations * 128)


def local(rhs, jac, jac_inv, wall_coupling, span_coupling, block_owner, block_slot, coarse_inv):
    highest = lax.Precision.HIGHEST
    first_pass = precondition(rhs, jac_inv)
    second = first_pass + precondition(
        rhs - apply_adjoint(first_pass, jac, wall_coupling, span_coupling), jac_inv
    )
    defect = rhs - apply_adjoint(second, jac, wall_coupling, span_coupling)
    span_count, wall_count, equations, line_count = defect.shape
    per_line = line_count // 128
    blocks = defect.reshape(span_count, wall_count, equations, per_line, 128)
    blocks = blocks.transpose(0, 1, 3, 2, 4).reshape(
        span_count * wall_count * per_line, equations * 128
    )
    block_total = blocks.shape[0]
    owners = lax.axis_size("patch")
    groups = lax.axis_size("wall")
    aggregates = coarse_inv.shape[-1]
    line_inv = coarse_inv.reshape(equations, groups, equations, aggregates)
    owners_of = block_owner.reshape(block_total)
    slots_of = block_slot.reshape(block_total)
    capacity = max(2, 2 * block_total // owners)
    to_owner = (owners_of[:, None] == jnp.arange(owners, dtype=jnp.int32)[None, :]).astype(
        jnp.int32
    )
    rank_in = jnp.sum(to_owner * (jnp.cumsum(to_owner, axis=0) - 1), axis=1)
    placement = owners_of * capacity + rank_in
    picker_int = (
        placement[:, None] == jnp.arange(owners * capacity, dtype=jnp.int32)[None, :]
    ).astype(jnp.int32)
    picker = picker_int.astype(jnp.float32)
    outgoing = jnp.dot(picker.T, blocks, precision=highest).reshape(
        owners, capacity, equations * 128
    )
    slot_ids = (jnp.sum(picker_int * (slots_of + 1)[:, None], axis=0) - 1).reshape(owners, capacity)
    received, got_slots = (
        lax.all_to_all(outgoing, "patch", split_axis=0, concat_axis=0, tiled=True),
        lax.all_to_all(slot_ids, "patch", split_axis=0, concat_axis=0, tiled=True),
    )
    member = (
        got_slots.reshape(owners * capacity)[:, None]
        == jnp.arange(aggregates, dtype=jnp.int32)[None, :]
    ).astype(jnp.float32)
    coarse_res = jnp.dot(
        member.T, received.reshape(owners * capacity, equations * 128), precision=highest
    )
    coarse_fix = coarse_line(coarse_res, line_inv, groups, aggregates, equations)
    reply = jnp.dot(member, coarse_fix, precision=highest).reshape(
        owners, capacity, equations * 128
    )
    returned = lax.all_to_all(reply, "patch", split_axis=0, concat_axis=0, tiled=True)
    correction = jnp.dot(
        picker, returned.reshape(owners * capacity, equations * 128), precision=highest
    )
    correction = correction.reshape(span_count, wall_count, per_line, equations, 128)
    correction = correction.transpose(0, 1, 3, 2, 4).reshape(
        span_count, wall_count, equations, line_count
    )
    third_pass = second + correction
    return third_pass + precondition(
        rhs - apply_adjoint(third_pass, jac, wall_coupling, span_coupling), jac_inv
    )


def solution(mesh):
    return jax.shard_map(
        local,
        mesh=mesh,
        in_specs=(
            P("span", "wall", None, "patch"),
            P("span", "wall", None, None, "patch"),
            P("span", "wall", None, None, "patch"),
            P(),
            P(),
            P("span", "wall", "patch"),
            P("span", "wall", "patch"),
            P("span", "wall", None, None, "patch"),
        ),
        out_specs=P("span", "wall", None, "patch"),
        check_vma=False,
    )
```

profile of v0, /device:TPU:1, one launch (start us, length us, event | category | flops | bytes accessed | tf_op | source)
XLA Modules:
  0.0 157.1 jit_solution(11848900065748180655)
XLA Ops:
  0.0 2.8 %multiply_reduce_fusion.5 = f32[4,8,5,1024]{3,1,2,0:T(8,128)S(1)} fusion(f32[4,8,5,5,1024]{4,1,3,2,0:T(8,128)} %param.10, f32[4,8,5,1024]{3,1,2,0:T(8,128)} %param.8), kind=kLoop, calls=%fused_computation.5 | loop fusion | flops 1474560 | bytes 4587520 | tf_op jit(solution)/shard_map/reduce_sum | solution.py:33
  4.4 4.4 %collective-permute-start = (f32[1,8,5,1024]{3,1,2,0:T(8,128)}, f32[1,8,5,1024]{3,1,2,0:T(8,128)S(1)}, u32[]{:S(2)}, u32[]{:S(2)}) collective-permute-start(f32[1,8,5,1024]{3,1,2,0:T(8,128)} %get-tuple-element.22), channel_id=1, source_target_pairs={{0,2},{2,4},{4,6},{6,8},{8,10},{10,12},{12,14},{1,3},{3,5},{5,7},{... | collective-permute-start | bytes 491528 | tf_op jit(solution)/shard_map/ppermute | solution.py:14
  10.3 2.5 %multiply_reduce_fusion.4 = f32[4,8,5,1024]{3,1,2,0:T(8,128)} fusion(f32[4,8,5,5,1024]{4,1,3,2,0:T(8,128)S(1)} %copy-done.1, f32[4,8,5,1024]{3,1,2,0:T(8,128)} %copy-done.4), kind=kLoop, calls=%fused_computation.4 | loop fusion | flops 1474560 | bytes 4587520 | tf_op jit(solution)/shard_map/reduce_sum | solution.py:24
  13.7 2.4 %collective-permute-done.1 = f32[1,8,5,1024]{3,1,2,0:T(8,128)} collective-permute-done((f32[1,8,5,1024]{3,1,2,0:T(8,128)}, f32[1,8,5,1024]{3,1,2,0:T(8,128)}, u32[]{:S(2)}, u32[]{:S(2)}) %collective-permute-start.1) | collective-permute-done | bytes 163872 | tf_op jit(solution)/shard_map/ppermute | solution.py:15
  17.7 3.6 %collective-permute-start.2 = (f32[6,1,5,1024]{3,1,2,0:T(1,128)S(1)}, f32[6,1,5,1024]{3,1,2,0:T(1,128)S(1)}, u32[]{:S(2)}, u32[]{:S(2)}) collective-permute-start(f32[6,1,5,1024]{3,1,2,0:T(1,128)S(1)} %get-tuple-element.15), channel_id=1, source_target_pairs={{1,0},{3,2},{5,4},{7,6},{9,8},{11,10},{13,12},{15,14},{17,16},{19,... | collective-permute-start | bytes 368648 | tf_op jit(solution)/shard_map/ppermute | solution.py:15
  22.8 1.8 %collective-permute-done.3 = f32[6,1,5,1024]{3,1,2,0:T(1,128)S(1)} collective-permute-done((f32[6,1,5,1024]{3,1,2,0:T(1,128)S(1)}, f32[6,1,5,1024]{3,1,2,0:T(1,128)S(1)}, u32[]{:S(2)}, u32[]{:S(2)}) %collective-permute-start.3) | collective-permute-done | bytes 122912 | tf_op jit(solution)/shard_map/ppermute | solution.py:14
  24.6 2.2 %fusion.17 = (f32[4,8,5,1024]{3,1,2,0:T(8,128)S(1)}, f32[4,8,5,1024]{3,1,2,0:T(8,128)S(1)}) fusion(f32[6,1,5,1024]{3,1,2,0:T(1,128)S(1)} %collective-permute-done.3, f32[1,8,5,1024]{3,1,2,0:T(8,128)} %collective-permute-done.1, f32[4,8,5,1024]{3,1,2,0:T(8,128)} %copy-done.4, f32[1,8,5,1024]{3,1,2,0:T(8,128)S(1)} %collective-permute-done, ...), kind=kLoop, calls=%fused_computation.45 | loop fusion | flops 1638400 | bytes 2539520 | tf_op jit(solution)/shard_map/add | solution.py:25
  33.3 3.5 %collective-permute-start.4 = (f32[1,8,5,1024]{3,1,2,0:T(8,128)}, f32[1,8,5,1024]{3,1,2,0:T(8,128)S(1)}, u32[]{:S(2)}, u32[]{:S(2)}) collective-permute-start(f32[1,8,5,1024]{3,1,2,0:T(8,128)} %get-tuple-element.20), channel_id=1, source_target_pairs={{0,2},{2,4},{4,6},{6,8},{8,10},{10,12},{12,14},{1,3},{3,5},{5,7},{... | collective-permute-start | bytes 491528 | tf_op jit(solution)/shard_map/ppermute | solution.py:14
  38.9 6.8 %all-to-all-start = ((s32[16,1,32]{2,1,0:T(1,128)}), s32[16,1,32]{2,1,0:T(1,128)S(1)}, u32[]{:S(2)}, u32[]{:S(2)}) async-start(s32[16,1,32]{2,1,0:T(1,128)} %sub.48), calls=%async_computation | async-start | bytes 16384 | tf_op jit(solution)/shard_map/all_to_all | solution.py:80
  47.8 2.9 %collective-permute-start.6 = (f32[6,1,5,1024]{3,1,2,0:T(1,128)S(1)}, f32[6,1,5,1024]{3,1,2,0:T(1,128)S(1)}, u32[]{:S(2)}, u32[]{:S(2)}) collective-permute-start(f32[6,1,5,1024]{3,1,2,0:T(1,128)S(1)} %get-tuple-element.11), channel_id=1, source_target_pairs={{1,0},{3,2},{5,4},{7,6},{9,8},{11,10},{13,12},{15,14},{17,16},{19,... | collective-permute-start | bytes 368648 | tf_op jit(solution)/shard_map/ppermute | solution.py:15
  59.0 2.5 %fusion.22 = f32[16,32,640]{2,1,0:T(8,128)} fusion(f32[256,640,1]{1,0,2:T(8,128)S(1)} %bitcast.115, s32[16,32]{1,0:T(8,128)S(1)} %multiply_add_fusion.1, s32[256]{0:T(256)S(1)} %multiply_add_fusion.2), kind=kOutput, calls=%fused_computation.61 | convolution fusion | flops 1007026176 | bytes 1969152 | tf_op jit(solution)/shard_map/dot_general | solution.py:74
  61.6 6.8 %all-to-all-start.1 = ((f32[16,32,640]{2,1,0:T(8,128)}), f32[16,32,640]{2,1,0:T(8,128)}, u32[]{:S(2)}, u32[]{:S(2)}) async-start(f32[16,32,640]{2,1,0:T(8,128)} %fusion.22), calls=%async_computation.1 | async-start | bytes 2621440 | tf_op jit(solution)/shard_map/all_to_all | solution.py:79
  69.8 17.0 %all-to-all-done.1 = f32[16,32,640]{2,1,0:T(8,128)} async-done(((f32[16,32,640]{2,1,0:T(8,128)}), f32[16,32,640]{2,1,0:T(8,128)}, u32[]{:S(2)}, u32[]{:S(2)}) %all-to-all-start.1) | async-done | bytes 1310752 | tf_op jit(solution)/shard_map/all_to_all | solution.py:79
  86.9 1.9 %convolution_bitcast_fusion.2 = f32[1,4,640]{2,1,0:T(4,128)S(1)} fusion(f32[512,640]{1,0:T(8,128)} %bitcast.17, s32[512]{0:T(512)S(1)} %eq.138), kind=kOutput, calls=%fused_computation.8 | convolution fusion | flops 15730688 | bytes 1323008 | tf_op jit(solution)/shard_map/dot_general | solution.py:86
  88.8 4.8 %all-gather.1 = f32[2,4,640]{2,1,0:T(4,128)S(1)} all-gather(f32[1,4,640]{2,1,0:T(4,128)S(1)} %convolution_bitcast_fusion.2), channel_id=2, replica_groups=mesh['patch'=16,'span'=8,'wall'=2] {'wall'}, dimensions={0}, use_global_device_ids=true | all-gather | bytes 30720 | tf_op jit(solution)/shard_map/all_gather | solution.py:38
  93.8 1.9 %fusion.34 = f32[16,32,640]{2,1,0:T(8,128)} fusion(f32[4,640,1]{1,0,2:T(4,128)S(1)} %reshape.192, s32[16,32]{1,0:T(8,128)S(1)} %bitcast.116), kind=kOutput, calls=%fused_computation.87 | convolution fusion | flops 15730688 | bytes 1323008 | tf_op jit(solution)/shard_map/dot_general | solution.py:90
  95.7 4.4 %all-to-all-start.2 = ((f32[16,32,640]{2,1,0:T(8,128)}), f32[16,32,640]{2,1,0:T(8,128)}, u32[]{:S(2)}, u32[]{:S(2)}) async-start(f32[16,32,640]{2,1,0:T(8,128)} %fusion.34), calls=%async_computation.2 | async-start | bytes 2621440 | tf_op jit(solution)/shard_map/all_to_all | solution.py:93
  100.2 21.4 %all-to-all-done.2 = f32[16,32,640]{2,1,0:T(8,128)} async-done(((f32[16,32,640]{2,1,0:T(8,128)}), f32[16,32,640]{2,1,0:T(8,128)}, u32[]{:S(2)}, u32[]{:S(2)}) %all-to-all-start.2) | async-done | bytes 1310752 | tf_op jit(solution)/shard_map/all_to_all | solution.py:93
  121.7 2.8 %copy.143 = f32[640,512]{1,0:T(8,128)} copy(f32[640,512]{0,1:T(8,128)} %bitcast.22) | data formatting | bytes 2621440 | tf_op jit(solution)/shard_map/dot_general | solution.py:94
  124.5 2.9 %convolution_bitcast_fusion = f32[4,8,5,8,128]{4,3,2,1,0:T(8,128)S(1)} fusion(f32[5,128,512,1,1]{2,1,0,4,3:T(8,128)} %bitcast.114, s32[4,8,8]{2,1,0:T(8,128)S(1)} %multiply_add_fusion), kind=kOutput, calls=%fused_computation.6 | convolution fusion | flops 1007026176 | bytes 1967104 | tf_op jit(solution)/shard_map/dot_general | solution.py:94
  128.3 2.0 %reshape.180 = f32[4,8,5,1024]{3,1,2,0:T(8,128)} reshape(f32[4,8,5,8,128]{4,3,1,2,0:T(8,128)} %copy.144) | data formatting | bytes 1310720 | tf_op jit(solution)/shard_map/reshape | solution.py:98
  131.7 4.9 %collective-permute-start.8 = (f32[1,8,5,1024]{3,1,2,0:T(8,128)S(1)}, f32[1,8,5,1024]{3,1,2,0:T(8,128)S(1)}, u32[]{:S(2)}, u32[]{:S(2)}) collective-permute-start(f32[1,8,5,1024]{3,1,2,0:T(8,128)S(1)} %get-tuple-element.18), channel_id=1, source_target_pairs={{0,2},{2,4},{4,6},{6,8},{8,10},{10,12},{12,14},{1,3},{3,5},{5,7},{... | collective-permute-start | bytes 491528 | tf_op jit(solution)/shard_map/ppermute | solution.py:14
  138.8 5.4 %collective-permute-done.9 = f32[1,8,5,1024]{3,1,2,0:T(8,128)S(1)} collective-permute-done((f32[1,8,5,1024]{3,1,2,0:T(8,128)S(1)}, f32[1,8,5,1024]{3,1,2,0:T(8,128)S(1)}, u32[]{:S(2)}, u32[]{:S(2)}) %collective-permute-start.9) | collective-permute-done | bytes 163872 | tf_op jit(solution)/shard_map/ppermute | solution.py:15
  144.4 4.0 %collective-permute-start.10 = (f32[6,1,5,1024]{3,1,2,0:T(1,128)S(1)}, f32[6,1,5,1024]{3,1,2,0:T(1,128)S(1)}, u32[]{:S(2)}, u32[]{:S(2)}) collective-permute-start(f32[6,1,5,1024]{3,1,2,0:T(1,128)S(1)} %get-tuple-element.7), channel_id=1, source_target_pairs={{1,0},{3,2},{5,4},{7,6},{9,8},{11,10},{13,12},{15,14},{17,16},{19,... | collective-permute-start | bytes 368648 | tf_op jit(solution)/shard_map/ppermute | solution.py:15
  (98 shorter events, 41.1 us)
Async XLA Ops:
  0.0 28.2 %copy-start = (f32[5,5]{1,0:T(8,128)S(1)}, f32[5,5]{1,0:T(8,128)}, u32[]{:S(2)}) copy-start(f32[5,5]{1,0:T(8,128)} %param.12) | copy-start | bytes 304
  0.0 10.1 %copy-start.12 = (s32[4,8,8]{2,1,0:T(8,128)S(1)}, s32[4,8,8]{2,1,0:T(8,128)}, u32[]{:S(2)}) copy-start(s32[4,8,8]{2,1,0:T(8,128)} %param.13) | copy-start | bytes 3076
  0.0 10.2 %copy-start.1 = (f32[4,8,5,5,1024]{4,1,3,2,0:T(8,128)S(1)}, f32[4,8,5,5,1024]{4,1,3,2,0:T(8,128)}, u32[]{:S(2)}) copy-start(f32[4,8,5,5,1024]{4,1,3,2,0:T(8,128)} %param.9) | copy-start | bytes 9830404
  3.6 9.9 %copy-start.14 = (s32[4,8,8]{2,1,0:T(8,128)S(1)}, s32[4,8,8]{2,1,0:T(8,128)}, u32[]{:S(2)}) copy-start(s32[4,8,8]{2,1,0:T(8,128)} %param.14) | copy-start | bytes 3076
  4.4 9.3 %collective-permute-start = (f32[1,8,5,1024]{3,1,2,0:T(8,128)}, f32[1,8,5,1024]{3,1,2,0:T(8,128)S(1)}, u32[]{:S(2)}, u32[]{:S(2)}) collective-permute-start(f32[1,8,5,1024]{3,1,2,0:T(8,128)} %get-tuple-element.22), channel_id=1, source_target_pairs={{0,2},{2,4},{4,6},{6,8},{8,10},{10,12},{12,14},{1,3},{3,5},{5,7},{... | collective-permute-start | bytes 491528 | tf_op jit(solution)/shard_map/ppermute | solution.py:14
  8.8 7.3 %collective-permute-start.1 = (f32[1,8,5,1024]{3,1,2,0:T(8,128)}, f32[1,8,5,1024]{3,1,2,0:T(8,128)}, u32[]{:S(2)}, u32[]{:S(2)}) collective-permute-start(f32[1,8,5,1024]{3,1,2,0:T(8,128)} %get-tuple-element.21), channel_id=1, source_target_pairs={{2,0},{4,2},{6,4},{8,6},{10,8},{12,10},{14,12},{3,1},{5,3},{7,5},{... | collective-permute-start | bytes 491528 | tf_op jit(solution)/shard_map/ppermute | solution.py:15
  10.3 16.5 %copy-start.13 = (f32[5,5]{1,0:T(8,128)S(1)}, f32[5,5]{1,0:T(8,128)}, u32[]{:S(2)}) copy-start(f32[5,5]{1,0:T(8,128)} %param.11) | copy-start | bytes 304
  17.7 5.1 %collective-permute-start.2 = (f32[6,1,5,1024]{3,1,2,0:T(1,128)S(1)}, f32[6,1,5,1024]{3,1,2,0:T(1,128)S(1)}, u32[]{:S(2)}, u32[]{:S(2)}) collective-permute-start(f32[6,1,5,1024]{3,1,2,0:T(1,128)S(1)} %get-tuple-element.15), channel_id=1, source_target_pairs={{1,0},{3,2},{5,4},{7,6},{9,8},{11,10},{13,12},{15,14},{17,16},{19,... | collective-permute-start | bytes 368648 | tf_op jit(solution)/shard_map/ppermute | solution.py:15
  21.3 3.2 %collective-permute-start.3 = (f32[6,1,5,1024]{3,1,2,0:T(1,128)S(1)}, f32[6,1,5,1024]{3,1,2,0:T(1,128)S(1)}, u32[]{:S(2)}, u32[]{:S(2)}) collective-permute-start(f32[6,1,5,1024]{3,1,2,0:T(1,128)S(1)} %get-tuple-element.16), channel_id=1, source_target_pairs={{0,1},{2,3},{4,5},{6,7},{8,9},{10,11},{12,13},{14,15},{16,17},{18,... | collective-permute-start | bytes 368648 | tf_op jit(solution)/shard_map/ppermute | solution.py:14
  22.8 6.8 %copy-start.8 = (f32[4,8,5,1024]{3,1,2,0:T(8,128)S(1)}, f32[4,8,5,1024]{3,1,2,0:T(8,128)}, u32[]{:S(2)}) copy-start(f32[4,8,5,1024]{3,1,2,0:T(8,128)} %param.8) | copy-start | bytes 1966084
  22.8 6.8 %copy-start.11 = (f32[4,8,5,1024]{3,1,2,0:T(8,128)S(1)}, f32[4,8,5,1024]{3,1,2,0:T(8,128)}, u32[]{:S(2)}) copy-start(f32[4,8,5,1024]{3,1,2,0:T(8,128)} %multiply_reduce_fusion.4) | copy-start | bytes 1966084
  33.3 12.3 %collective-permute-start.4 = (f32[1,8,5,1024]{3,1,2,0:T(8,128)}, f32[1,8,5,1024]{3,1,2,0:T(8,128)S(1)}, u32[]{:S(2)}, u32[]{:S(2)}) collective-permute-start(f32[1,8,5,1024]{3,1,2,0:T(8,128)} %get-tuple-element.20), channel_id=1, source_target_pairs={{0,2},{2,4},{4,6},{6,8},{8,10},{10,12},{12,14},{1,3},{3,5},{5,7},{... | collective-permute-start | bytes 491528 | tf_op jit(solution)/shard_map/ppermute | solution.py:14
  36.9 9.3 %collective-permute-start.5 = (f32[1,8,5,1024]{3,1,2,0:T(8,128)}, f32[1,8,5,1024]{3,1,2,0:T(8,128)}, u32[]{:S(2)}, u32[]{:S(2)}) collective-permute-start(f32[1,8,5,1024]{3,1,2,0:T(8,128)} %get-tuple-element.19), channel_id=1, source_target_pairs={{2,0},{4,2},{6,4},{8,6},{10,8},{12,10},{14,12},{3,1},{5,3},{7,5},{... | collective-permute-start | bytes 491528 | tf_op jit(solution)/shard_map/ppermute | solution.py:15
  38.9 22.7 %all-to-all-start = ((s32[16,1,32]{2,1,0:T(1,128)}), s32[16,1,32]{2,1,0:T(1,128)S(1)}, u32[]{:S(2)}, u32[]{:S(2)}) async-start(s32[16,1,32]{2,1,0:T(1,128)} %sub.48), calls=%async_computation | async-start | bytes 16384 | tf_op jit(solution)/shard_map/all_to_all | solution.py:80
  45.6 8.3 %copy-start.7 = (f32[4,8,5,1024]{3,1,2,0:T(8,128)S(1)}, f32[4,8,5,1024]{3,1,2,0:T(8,128)}, u32[]{:S(2)}) copy-start(f32[4,8,5,1024]{3,1,2,0:T(8,128)} %copy-done.6) | copy-start | bytes 1966084
  47.8 6.0 %collective-permute-start.6 = (f32[6,1,5,1024]{3,1,2,0:T(1,128)S(1)}, f32[6,1,5,1024]{3,1,2,0:T(1,128)S(1)}, u32[]{:S(2)}, u32[]{:S(2)}) collective-permute-start(f32[6,1,5,1024]{3,1,2,0:T(1,128)S(1)} %get-tuple-element.11), channel_id=1, source_target_pairs={{1,0},{3,2},{5,4},{7,6},{9,8},{11,10},{13,12},{15,14},{17,16},{19,... | collective-permute-start | bytes 368648 | tf_op jit(solution)/shard_map/ppermute | solution.py:15
  50.7 3.2 %collective-permute-start.7 = (f32[6,1,5,1024]{3,1,2,0:T(1,128)S(1)}, f32[6,1,5,1024]{3,1,2,0:T(1,128)S(1)}, u32[]{:S(2)}, u32[]{:S(2)}) collective-permute-start(f32[6,1,5,1024]{3,1,2,0:T(1,128)S(1)} %get-tuple-element.12), channel_id=1, source_target_pairs={{0,1},{2,3},{4,5},{6,7},{8,9},{10,11},{12,13},{14,15},{16,17},{18,... | collective-permute-start | bytes 368648 | tf_op jit(solution)/shard_map/ppermute | solution.py:14
  58.9 9.5 %copy-start.15 = (f32[1,1,5,10,4]{3,4,2,1,0:T(4,128)S(1)}, f32[1,1,5,10,4]{3,4,2,1,0:T(4,128)}, u32[]{:S(2)}) copy-start(f32[1,1,5,10,4]{3,4,2,1,0:T(4,128)} %param.15) | copy-start | bytes 2404
  61.6 25.3 %all-to-all-start.1 = ((f32[16,32,640]{2,1,0:T(8,128)}), f32[16,32,640]{2,1,0:T(8,128)}, u32[]{:S(2)}, u32[]{:S(2)}) async-start(f32[16,32,640]{2,1,0:T(8,128)} %fusion.22), calls=%async_computation.1 | async-start | bytes 2621440 | tf_op jit(solution)/shard_map/all_to_all | solution.py:79
  95.7 25.9 %all-to-all-start.2 = ((f32[16,32,640]{2,1,0:T(8,128)}), f32[16,32,640]{2,1,0:T(8,128)}, u32[]{:S(2)}, u32[]{:S(2)}) async-start(f32[16,32,640]{2,1,0:T(8,128)} %fusion.34), calls=%async_computation.2 | async-start | bytes 2621440 | tf_op jit(solution)/shard_map/all_to_all | solution.py:93
  131.7 7.2 %collective-permute-start.8 = (f32[1,8,5,1024]{3,1,2,0:T(8,128)S(1)}, f32[1,8,5,1024]{3,1,2,0:T(8,128)S(1)}, u32[]{:S(2)}, u32[]{:S(2)}) collective-permute-start(f32[1,8,5,1024]{3,1,2,0:T(8,128)S(1)} %get-tuple-element.18), channel_id=1, source_target_pairs={{0,2},{2,4},{4,6},{6,8},{8,10},{10,12},{12,14},{1,3},{3,5},{5,7},{... | collective-permute-start | bytes 491528 | tf_op jit(solution)/shard_map/ppermute | solution.py:14
  136.6 7.6 %collective-permute-start.9 = (f32[1,8,5,1024]{3,1,2,0:T(8,128)S(1)}, f32[1,8,5,1024]{3,1,2,0:T(8,128)S(1)}, u32[]{:S(2)}, u32[]{:S(2)}) collective-permute-start(f32[1,8,5,1024]{3,1,2,0:T(8,128)S(1)} %get-tuple-element.17), channel_id=1, source_target_pairs={{2,0},{4,2},{6,4},{8,6},{10,8},{12,10},{14,12},{3,1},{5,3},{7,5},{... | collective-permute-start | bytes 491528 | tf_op jit(solution)/shard_map/ppermute | solution.py:15
  144.4 6.0 %collective-permute-start.10 = (f32[6,1,5,1024]{3,1,2,0:T(1,128)S(1)}, f32[6,1,5,1024]{3,1,2,0:T(1,128)S(1)}, u32[]{:S(2)}, u32[]{:S(2)}) collective-permute-start(f32[6,1,5,1024]{3,1,2,0:T(1,128)S(1)} %get-tuple-element.7), channel_id=1, source_target_pairs={{1,0},{3,2},{5,4},{7,6},{9,8},{11,10},{13,12},{15,14},{17,16},{19,... | collective-permute-start | bytes 368648 | tf_op jit(solution)/shard_map/ppermute | solution.py:15
  148.4 3.2 %collective-permute-start.11 = (f32[6,1,5,1024]{3,1,2,0:T(1,128)S(1)}, f32[6,1,5,1024]{3,1,2,0:T(1,128)S(1)}, u32[]{:S(2)}, u32[]{:S(2)}) collective-permute-start(f32[6,1,5,1024]{3,1,2,0:T(1,128)S(1)} %get-tuple-element.8), channel_id=1, source_target_pairs={{0,1},{2,3},{4,5},{6,7},{8,9},{10,11},{12,13},{14,15},{16,17},{18,... | collective-permute-start | bytes 368648 | tf_op jit(solution)/shard_map/ppermute | solution.py:14
  (7 other events, 16.0 us)
where the time goes:
time: 158 us; the launch traced here: 157 us
  waiting for transfers between devices  50.7 us (32%)
  starting transfers between devices  49.4 us (31%)
  other arithmetic  22.1 us (14%)
  matrix products  17.9 us (11%)
  local copies, waits for them, and re-layouts  11.7 us (7%)
  blocking collectives  4.81 us (3%)
    all_to_all x1, waiting for transfers between devices, local(): lax.all_to_all(reply, 'patch', split_axis=0, concat_axis=0, tiled=True)  21.4 us
    ppermute x6, starting transfers between devices, extended(): before = lax.ppermute(last, axis, up)  17.1 us
    all_to_all x1, waiting for transfers between devices, local(): lax.all_to_all(outgoing, 'patch', split_axis=0, concat_axis=0, tiled=True)  17 us
    ppermute x6, starting transfers between devices, extended(): after = lax.ppermute(initial, axis, down)  14.3 us
    ppermute x6, waiting for transfers between devices, extended(): after = lax.ppermute(initial, axis, down)  8.24 us
    all_to_all x1, starting transfers between devices, local(): lax.all_to_all(outgoing, 'patch', split_axis=0, concat_axis=0, tiled=True)  6.8 us
    all_to_all x1, starting transfers between devices, local(): lax.all_to_all(slot_ids, 'patch', split_axis=0, concat_axis=0, tiled=True)  6.75 us
    all_gather x1, blocking collectives, coarse_line(): gathered = lax.all_gather(coarse_res[None], 'wall', axis=0, tiled=True)  4.81 us
  transfers between devices with their start and end apart: 15, of which 9 were waited for; matrix products, arithmetic and copies ran while one was open for 11% of the time, Pallas kernels for 0%

commit v1 on v0

v1 whole, which is shorter than its diff:
```python
import functools

import jax
import jax.numpy as jnp
from jax import lax
from jax.experimental import pallas as pl
from jax.experimental.pallas import tpu as pltpu
from jax.sharding import PartitionSpec as P

LANES = 128
VMEM = pl.BlockSpec(memory_space=pltpu.VMEM)
SMEM = pl.BlockSpec(memory_space=pltpu.SMEM)
HIGHEST = lax.Precision.HIGHEST


def call(kernel, outs, n_smem, *args):
    size = 4 * sum(a.size for a in (*args, *outs))
    return pl.pallas_call(
        kernel,
        out_shape=outs,
        in_specs=[SMEM] * n_smem + [VMEM] * (len(args) - n_smem),
        out_specs=[VMEM] * len(outs),
        cost_estimate=pl.CostEstimate(flops=size, bytes_accessed=size, transcendentals=0),
        compiler_params=pltpu.CompilerParams(vmem_limit_bytes=20 * 2**20),
    )(*args)


def mix(coupling, values):
    n = len(values)
    return [
        functools.reduce(lambda a, b: a + b, [coupling[k, i] * values[k] for k in range(n)])
        for i in range(n)
    ]


def sweep(jinv, s, lanes, values):
    n = len(values)
    return [
        functools.reduce(lambda a, b: a + b, [jinv[s, i, k, :, lanes] * values[k] for k in range(n)])
        for i in range(n)
    ]


def wall_edges(flags, planes, out):
    row = jnp.where(flags[1] == 0, 7, 0)
    for s, plane in enumerate(planes):
        for k in range(5):
            out[s * 5 + k, :] = plane(k, row)


def for_lanes(body, length):
    @pl.loop(0, length // LANES)
    def _(q):
        body(pl.ds(pl.multiple_of(q * LANES, LANES), LANES), q)


def first_kernel(flags, rhs, jinv, first, edge_a, edge_b, edge_w):
    even = flags[0] == 1

    def body(lanes, q):
        ends = {}
        for s in range(4):
            ends[s] = sweep(jinv, s, lanes, [rhs[s, k, :, lanes] for k in range(5)])
            for k in range(5):
                first[s, k, :, lanes] = ends[s][k]
        for k in range(5):
            edge_a[k, :, lanes] = jnp.where(even, ends[3][k], ends[0][k])
            edge_b[k, :, lanes] = jnp.where(even, ends[0][k], ends[3][k])

    for_lanes(body, rhs.shape[-1])
    wall_edges(flags, [functools.partial(lambda s, k, r: first[s, k, r, :], s) for s in range(4)], edge_w)


def local_apply(flags, wall, span, planes, halo_w, jac, lanes, s):
    own = planes[s]
    rows = lax.broadcasted_iota(jnp.int32, own[0].shape, 0)
    other_side = rows == jnp.where(flags[1] == 0, 7, 0)
    near_wall, near_span = [], []
    for k in range(5):
        up = jnp.where(rows == 7, 0.0, pltpu.roll(own[k], 7, 0))
        down = jnp.where(rows == 0, 0.0, pltpu.roll(own[k], 1, 0))
        beyond = jnp.where(other_side, halo_w[s * 5 + k, lanes][None, :], 0.0)
        near_wall.append(up + down + beyond)
        around = [planes[n][k] for n in (s - 1, s + 1) if 0 <= n < 4]
        near_span.append(functools.reduce(lambda a, b: a + b, around))
    from_wall, from_span = mix(wall, near_wall), mix(span, near_span)
    return [
        functools.reduce(lambda a, b: a + b, [jac[s, k, i, :, lanes] * own[k] for k in range(5)])
        - from_wall[i] - from_span[i]
        for i in range(5)
    ]


def second_local_kernel(flags, wall, span, first, halo_w, rhs, jac, jinv, out):
    def body(lanes, q):
        planes = [[first[s, k, :, lanes] for k in range(5)] for s in range(4)]
        for s in range(4):
            applied = local_apply(flags, wall, span, planes, halo_w, jac, lanes, s)
            swept = sweep(jinv, s, lanes, [rhs[s, k, :, lanes] - applied[k] for k in range(5)])
            for k in range(5):
                out[s, k, :, lanes] = planes[s][k] + swept[k]

    for_lanes(body, rhs.shape[-1])


def second_edge_kernel(flags, span, inner, halo_a, halo_b, jinv, edge_a, edge_b, edge_w):
    even = flags[0] == 1
    plane_a = jnp.where(even, 3, 0)
    plane_b = 3 - plane_a

    def body(lanes, q):
        for plane, halo, edge in ((plane_a, halo_a, edge_a), (plane_b, halo_b, edge_b)):
            beyond = mix(span, [halo[k, :, lanes] for k in range(5)])
            swept = sweep(jinv, plane, lanes, beyond)
            for k in range(5):
                edge[k, :, lanes] = inner[plane, k, :, lanes] + swept[k]

    for_lanes(body, inner.shape[-1])
    row = jnp.where(flags[1] == 0, 7, 0)
    for k in range(5):
        for s in (1, 2):
            edge_w[s * 5 + k, :] = inner[s, k, row, :]
        a, b = edge_a[k, row, :], edge_b[k, row, :]
        edge_w[k, :] = jnp.where(even, b, a)
        edge_w[15 + k, :] = jnp.where(even, a, b)


def planes_of(flags, inner, edge_a, edge_b, lanes):
    even = flags[0] == 1
    a = [edge_a[k, :, lanes] for k in range(5)]
    b = [edge_b[k, :, lanes] for k in range(5)]
    return [
        [jnp.where(even, b[k], a[k]) for k in range(5)],
        [inner[1, k, :, lanes] for k in range(5)],
        [inner[2, k, :, lanes] for k in range(5)],
        [jnp.where(even, a[k], b[k]) for k in range(5)],
    ]


def defect_local_kernel(flags, wall, span, inner, edge_a, edge_b, halo_w, rhs, jac, second, defect):
    def body(lanes, q):
        planes = planes_of(flags, inner, edge_a, edge_b, lanes)
        for s in range(4):
            applied = local_apply(flags, wall, span, planes, halo_w, jac, lanes, s)
            for k in range(5):
                second[s, k, :, lanes] = planes[s][k]
                defect[s, k, :, lanes] = rhs[s, k, :, lanes] - applied[k]

    for_lanes(body, rhs.shape[-1])


def restrict_kernel(flags, span, defect_in, halo_a, halo_b, onehot_t, defect, partial):
    even = flags[0] == 1
    plane_a = jnp.where(even, 3, 0)
    plane_b = 3 - plane_a

    def body(lanes, q):
        for s in (1, 2):
            for k in range(5):
                defect[s, k, :, lanes] = defect_in[s, k, :, lanes]
        for plane, halo in ((plane_a, halo_a), (plane_b, halo_b)):
            beyond = mix(span, [halo[k, :, lanes] for k in range(5)])
            for k in range(5):
                defect[plane, k, :, lanes] = defect_in[plane, k, :, lanes] + beyond[k]

    for_lanes(body, defect.shape[-1])
    tiles = defect.shape[-1] // LANES
    for k in range(5):
        rows = jnp.concatenate(
            [defect[s, k, :, q * LANES : (q + 1) * LANES] for s in range(4) for q in range(tiles)], axis=0
        )
        partial[:, k * LANES : (k + 1) * LANES] = jnp.dot(
            onehot_t[...], rows, precision=HIGHEST, preferred_element_type=jnp.float32
        )


def smooth_kernel(second, defect, jinv, base):
    def body(lanes, q):
        for s in range(4):
            swept = sweep(jinv, s, lanes, [defect[s, k, :, lanes] for k in range(5)])
            for k in range(5):
                base[s, k, :, lanes] = second[s, k, :, lanes] + swept[k]

    for_lanes(body, base.shape[-1])


def sum_kernel(received, total):
    sums = functools.reduce(lambda a, b: a + b, [received[8 * i : 8 * i + 8, :] for i in range(received.shape[0] // 8)])
    total[...] = sums[:4] + sums[4:]


def coarse_kernel(own_inv, other_inv, own, other, out):
    columns = own.shape[1]
    for i in range(5):
        terms = []
        for k in range(5):
            lanes = slice(k * LANES, (k + 1) * LANES)
            terms.append(own_inv[i * 5 + k] * own[:, lanes])
            terms.append(other_inv[i * 5 + k] * other[:, lanes])
        fix = functools.reduce(lambda a, b: a + b, terms)
        for p in range(out.shape[0]):
            out[p, :, i * LANES : (i + 1) * LANES] = fix
    del columns


def prolong_kernel(flags, onehot, fix, out, edge_a, edge_b, edge_w):
    even = flags[0] == 1
    tiles = out.shape[-1] // LANES
    for k in range(5):
        rows = jnp.dot(
            onehot[...], fix[:, k * LANES : (k + 1) * LANES], precision=HIGHEST, preferred_element_type=jnp.float32
        )
        for q in range(tiles):
            lanes = slice(q * LANES, (q + 1) * LANES)
            tile = [rows[(s * tiles + q) * 8 : (s * tiles + q) * 8 + 8] for s in range(4)]
            for s in range(4):
                out[s, k, :, lanes] = tile[s]
            edge_a[k, :, lanes] = jnp.where(even, tile[3], tile[0])
            edge_b[k, :, lanes] = jnp.where(even, tile[0], tile[3])
    wall_edges(flags, [functools.partial(lambda s, k, r: out[s, k, r, :], s) for s in range(4)], edge_w)


def final_local_kernel(flags, wall, span, base, fix, halo_w, jac, jinv, out):
    def body(lanes, q):
        planes = [[fix[s, k, :, lanes] for k in range(5)] for s in range(4)]
        for s in range(4):
            applied = local_apply(flags, wall, span, planes, halo_w, jac, lanes, s)
            swept = sweep(jinv, s, lanes, applied)
            for k in range(5):
                out[s, k, :, lanes] = base[s, k, :, lanes] + (planes[s][k] - swept[k])

    for_lanes(body, base.shape[-1])


def final_edge_kernel(flags, span, inner, halo_a, halo_b, jinv, out):
    plane_a = jnp.where(flags[0] == 1, 3, 0)
    plane_b = 3 - plane_a

    def body(lanes, q):
        for s in (1, 2):
            for k in range(5):
                out[s, k, :, lanes] = inner[s, k, :, lanes]
        for plane, halo in ((plane_a, halo_a), (plane_b, halo_b)):
            beyond = mix(span, [halo[k, :, lanes] for k in range(5)])
            swept = sweep(jinv, plane, lanes, beyond)
            for k in range(5):
                out[plane, k, :, lanes] = inner[plane, k, :, lanes] + swept[k]

    for_lanes(body, inner.shape[-1])


def exchange(edge_a, edge_b, edge_w):
    size = lax.axis_size("span")
    pairs = [(i, i + 1) for i in range(size - 1)]
    even = [p for i, j in pairs[0::2] for p in ((i, j), (j, i))]
    odd = [p for i, j in pairs[1::2] for p in ((i, j), (j, i))]
    return (
        lax.ppermute(edge_a, "span", even),
        lax.ppermute(edge_b, "span", odd),
        lax.ppermute(edge_w, "wall", [(0, 1), (1, 0)]),
    )


def local(rhs, jac, jac_inv, wall_coupling, span_coupling, block_owner, block_slot, coarse_inv):
    f32 = jnp.float32
    rhs = rhs.transpose(0, 2, 1, 3)
    jac = jac.transpose(0, 2, 3, 1, 4)
    jinv = jac_inv.transpose(0, 2, 3, 1, 4)
    field = jax.ShapeDtypeStruct(rhs.shape, f32)
    plane = jax.ShapeDtypeStruct(rhs.shape[1:], f32)
    edge = jax.ShapeDtypeStruct((20, rhs.shape[-1]), f32)
    span_at, wall_at = lax.axis_index("span"), lax.axis_index("wall")
    flags = jnp.stack([1 - span_at % 2, wall_at]).astype(jnp.int32)
    owners, slots = lax.axis_size("patch"), coarse_inv.shape[-1]
    aggregates = owners * slots
    named = (block_owner * slots + block_slot).transpose(0, 2, 1).reshape(-1)
    ids = jnp.arange(aggregates, dtype=jnp.int32)
    onehot = (named[:, None] == ids[None, :]).astype(f32)
    onehot_t = (named[None, :] == ids[:, None]).astype(f32)
    inv = coarse_inv.reshape(5, 2, 5, slots)
    own_inv = lax.dynamic_index_in_dim(inv, wall_at, 1, keepdims=False).reshape(25, slots, 1)
    other_inv = lax.dynamic_index_in_dim(inv, 1 - wall_at, 1, keepdims=False).reshape(25, slots, 1)
    own_inv = jnp.broadcast_to(own_inv, (25, slots, LANES))
    other_inv = jnp.broadcast_to(other_inv, (25, slots, LANES))

    first, a, b, w = call(first_kernel, [field, plane, plane, edge], 1, flags, rhs, jinv)
    halo_a, halo_b, halo_w = exchange(a, b, w)
    [inner] = call(second_local_kernel, [field], 3, flags, wall_coupling, span_coupling, first, halo_w, rhs, jac, jinv)
    a, b, w = call(second_edge_kernel, [plane, plane, edge], 2, flags, span_coupling, inner, halo_a, halo_b, jinv)
    halo_a, halo_b, halo_w = exchange(a, b, w)
    second, defect = call(
        defect_local_kernel, [field, field], 3, flags, wall_coupling, span_coupling, inner, a, b, halo_w, rhs, jac
    )
    part = jax.ShapeDtypeStruct((aggregates, 5 * LANES), f32)
    defect, partial = call(
        restrict_kernel, [field, part], 2, flags, span_coupling, defect, halo_a, halo_b, onehot_t
    )
    received = lax.all_to_all(partial, "patch", split_axis=0, concat_axis=0, tiled=True)
    [base] = call(smooth_kernel, [field], 0, second, defect, jinv)
    [mine] = call(sum_kernel, [jax.ShapeDtypeStruct((slots, 5 * LANES), f32)], 0, received)
    theirs = lax.ppermute(mine, "wall", [(0, 1), (1, 0)])
    [reply] = call(
        coarse_kernel, [jax.ShapeDtypeStruct((owners, slots, 5 * LANES), f32)], 0, own_inv, other_inv, mine, theirs
    )
    fixes = lax.all_to_all(reply, "patch", split_axis=0, concat_axis=0, tiled=True)
    fixes = fixes.reshape(aggregates, 5 * LANES)
    fix, a, b, w = call(prolong_kernel, [field, plane, plane, edge], 1, flags, onehot, fixes)
    halo_a, halo_b, halo_w = exchange(a, b, w)
    [inner] = call(
        final_local_kernel, [field], 3, flags, wall_coupling, span_coupling, base, fix, halo_w, jac, jinv
    )
    [out] = call(final_edge_kernel, [field], 2, flags, span_coupling, inner, halo_a, halo_b, jinv)
    return out.transpose(0, 2, 1, 3)


def solution(mesh):
    return jax.shard_map(
        local,
        mesh=mesh,
        in_specs=(
            P("span", "wall", None, "patch"),
            P("span", "wall", None, None, "patch"),
            P("span", "wall", None, None, "patch"),
            P(),
            P(),
            P("span", "wall", "patch"),
            P("span", "wall", "patch"),
            P("span", "wall", None, None, "patch"),
        ),
        out_specs=P("span", "wall", None, "patch"),
        check_vma=False,
    )
```

time: 158 us -> 83.5 us (0.53)
  the two profiles are of different devices: /device:TPU:1 before, /device:TPU:33 now
where the time goes in v1:
time: 83.5 us; the launch traced here: 82.8 us
  starting transfers between devices  31.8 us (38%)
  local copies, waits for them, and re-layouts  18.1 us (22%)
  waiting for transfers between devices  15.8 us (19%)
  Pallas kernels  15.3 us (18%)
  other arithmetic  1.45 us (2%)
    pallas_call x11, Pallas kernels, call(): pl.pallas_call(kernel, out_shape=outs, in_specs=[SMEM] * n_smem + [VMEM]...  15.3 us
    ppermute x3, starting transfers between devices, exchange(): lax.ppermute(edge_b, 'span', odd)  13.6 us
    unnamed x38, local copies, waits for them, and re-layouts  12.7 us
    all_to_all x1, waiting for transfers between devices, local(): lax.all_to_all(partial, 'patch', split_axis=0, concat_axis=0, tiled=True)  7.02 us
    all_to_all x1, starting transfers between devices, local(): lax.all_to_all(partial, 'patch', split_axis=0, concat_axis=0, tiled=True)  6.8 us
    all_to_all x1, waiting for transfers between devices, local(): lax.all_to_all(reply, 'patch', split_axis=0, concat_axis=0, tiled=True)  6.67 us
    all_to_all x1, starting transfers between devices, local(): lax.all_to_all(reply, 'patch', split_axis=0, concat_axis=0, tiled=True)  4.16 us
    ppermute x3, starting transfers between devices, exchange(): lax.ppermute(edge_w, 'wall', [(0, 1), (1, 0)])  3.14 us
  transfers between devices with their start and end apart: 12, of which 4 were waited for; matrix products, arithmetic and copies ran while one was open for 5% of the time, Pallas kernels for 8%

profile of v1, /device:TPU:33, one launch (start us, length us, event | category | flops | bytes accessed | tf_op | source)
XLA Modules:
  0.0 82.8 jit_solution(4803405707402996202)
XLA Ops:
  0.1 1.9 %copy-done = f32[4,8,5,5,1024]{4,1,3,2,0:T(8,128)S(1)} copy-done((f32[4,8,5,5,1024]{4,1,3,2,0:T(8,128)S(1)}, f32[4,8,5,5,1024]{4,1,3,2,0:T(8,128)}, u32[]{:S(2)}) %copy-start) | copy-done | bytes 3276824
  3.1 1.9 %shard_map.82 = (f32[4,5,8,1024]{3,2,1,0:T(8,128)S(1)}, f32[5,8,1024]{2,1,0:T(8,128)}, f32[5,8,1024]{2,1,0:T(8,128)}, f32[20,1024]{1,0:T(8,128)}) custom-call(s32[2]{0:T(128)S(1)} %pad_add_fusion.flags, f32[4,5,8,1024]{3,2,1,0:T(8,128)S(1)} %bitcast.23, f32[4,5,5,8,1024]{4,3,2,1,0:T(8,128)S(1)} %bitcast.14), custom_call_target="tpu_custom_call" | custom-call | flops 4997128 | bytes 4997128 | tf_op jit(solution)/shard_map/pallas_call | solution.py:18
  6.5 1.6 %collective-permute-start.1 = (f32[5,8,1024]{2,1,0:T(8,128)}, f32[5,8,1024]{2,1,0:T(8,128)S(1)}, u32[]{:S(2)}, u32[]{:S(2)}) collective-permute-start(f32[5,8,1024]{2,1,0:T(8,128)} %get-tuple-element.22), channel_id=1, source_target_pairs={{0,2},{2,0},{4,6},{6,4},{8,10},{10,8},{12,14},{14,12},{1,3},{3,1},... | collective-permute-start | bytes 491528 | tf_op jit(solution)/shard_map/ppermute | solution.py:258
  8.1 3.6 %collective-permute-start.2 = (f32[5,8,1024]{2,1,0:T(8,128)}, f32[5,8,1024]{2,1,0:T(8,128)}, u32[]{:S(2)}, u32[]{:S(2)}) collective-permute-start(f32[5,8,1024]{2,1,0:T(8,128)} %get-tuple-element.23), channel_id=1, source_target_pairs={{2,4},{4,2},{6,8},{8,6},{10,12},{12,10},{3,5},{5,3},{7,9},{9,7},{1... | collective-permute-start | bytes 491528 | tf_op jit(solution)/shard_map/ppermute | solution.py:259
  12.3 1.4 %copy.13 = s32[4,8,8]{2,1,0:T(8,128)} copy(s32[4,8,8]{1,2,0:T(8,128)} %add_bitcast_fusion) | data formatting | bytes 2048 | tf_op jit(solution)/shard_map/transpose | solution.py:276
  14.6 1.9 %copy-done.2 = f32[4,8,5,5,1024]{4,1,3,2,0:T(8,128)S(1)} copy-done((f32[4,8,5,5,1024]{4,1,3,2,0:T(8,128)S(1)}, f32[4,8,5,5,1024]{4,1,3,2,0:T(8,128)}, u32[]{:S(2)}) %copy-start.2) | copy-done | bytes 3276824
  17.6 1.1 %copy-done.8 = f32[4,5,8,1024]{3,2,1,0:T(8,128)S(1)} copy-done((f32[4,5,8,1024]{3,2,1,0:T(8,128)S(1)}, f32[4,5,8,1024]{3,2,1,0:T(8,128)}, u32[]{:S(2)}) %copy-start.8) | copy-done | bytes 655384
  18.7 2.2 %shard_map.83.inner = f32[4,5,8,1024]{3,2,1,0:T(8,128)S(1)} custom-call(s32[2]{0:T(128)S(1)} %pad_add_fusion.flags, f32[5,5]{1,0:T(8,128)S(1)} %copy-done.15, f32[5,5]{1,0:T(8,128)S(1)} %copy-done.14, f32[4,5,8,1024]{3,2,1,0:T(8,128)S(1)} %copy-done.8, f32[20,1024]{1,0:T(8,128)S(1)} %collective-permute-done.halo_w, f32[4,5,8,1024]{3,2,1,0:T(8,128)S(1)} %bitcast.24, ...), custom_call_target="tpu_custom_call" | custom-call | flops 8601808 | bytes 8601808 | tf_op jit(solution)/shard_map/pallas_call | solution.py:18
  20.9 1.5 %shard_map.84 = (f32[5,8,1024]{2,1,0:T(8,128)S(1)}, f32[5,8,1024]{2,1,0:T(8,128)S(1)}, f32[20,1024]{1,0:T(8,128)S(1)}) custom-call(s32[2]{0:T(128)S(1)} %pad_add_fusion.flags, f32[5,5]{1,0:T(8,128)S(1)} %copy-done.14, f32[4,5,8,1024]{3,2,1,0:T(8,128)S(1)} %shard_map.83.inner, f32[5,8,1024]{2,1,0:T(8,128)S(1)} %collective-permute-done.1.halo_a, ...), custom_call_target="tpu_custom_call" | custom-call | flops 4669548 | bytes 4669548 | tf_op jit(solution)/shard_map/pallas_call | solution.py:18
  23.1 5.5 %collective-permute-start.5 = (f32[5,8,1024]{2,1,0:T(8,128)S(1)}, f32[5,8,1024]{2,1,0:T(8,128)S(1)}, u32[]{:S(2)}, u32[]{:S(2)}) collective-permute-start(f32[5,8,1024]{2,1,0:T(8,128)S(1)} %get-tuple-element.25.edge_b), channel_id=1, source_target_pairs={{2,4},{4,2},{6,8},{8,6},{10,12},{12,10},{3,5},{5,3},{7,9},{9,7},{1... | collective-permute-start | bytes 491528 | tf_op jit(solution)/shard_map/ppermute | solution.py:259
  28.6 1.8 %shard_map.85 = (f32[4,5,8,1024]{3,2,1,0:T(8,128)S(1)}, f32[4,5,8,1024]{3,2,1,0:T(8,128)S(1)}) custom-call(s32[2]{0:T(128)S(1)} %pad_add_fusion.flags, f32[5,5]{1,0:T(8,128)S(1)} %copy-done.15, f32[5,5]{1,0:T(8,128)S(1)} %copy-done.14, f32[4,5,8,1024]{3,2,1,0:T(8,128)S(1)} %shard_map.83.inner, f32[5,8,1024]{2,1,0:T(8,128)S(1)} %get-tuple-element.24.edge_a, ...), custom_call_target="tpu_custom_call" | custom-call | flops 6308048 | bytes 6308048 | tf_op jit(solution)/shard_map/pallas_call | solution.py:18
  31.3 1.6 %collective-permute-done.5.halo_b = f32[5,8,1024]{2,1,0:T(8,128)S(1)} collective-permute-done((f32[5,8,1024]{2,1,0:T(8,128)S(1)}, f32[5,8,1024]{2,1,0:T(8,128)S(1)}, u32[]{:S(2)}, u32[]{:S(2)}) %collective-permute-start.5) | collective-permute-done | bytes 163872 | tf_op jit(solution)/shard_map/ppermute | solution.py:259
  32.9 1.3 %shard_map.86 = (f32[4,5,8,1024]{3,2,1,0:T(8,128)S(1)}, f32[64,640]{1,0:T(8,128)S(1)}) custom-call(s32[2]{0:T(128)S(1)} %pad_add_fusion.flags, f32[5,5]{1,0:T(8,128)S(1)} %copy-done.14, f32[4,5,8,1024]{3,2,1,0:T(8,128)S(1)} %get-tuple-element.28.defect_in, f32[5,8,1024]{2,1,0:T(8,128)S(1)} %collective-permute-done.4.halo_a, ...), custom_call_target="tpu_custom_call" | custom-call | flops 1867884 | bytes 1867884 | tf_op jit(solution)/shard_map/pallas_call | solution.py:18
  35.7 6.8 %all-to-all-start = ((f32[16,4,640]{2,1,0:T(4,128)}), f32[16,4,640]{2,1,0:T(4,128)}, u32[]{:S(2)}, u32[]{:S(2)}) async-start(f32[16,4,640]{2,1,0:T(4,128)} %all_to_all.10), calls=%async_computation | async-start | bytes 327680 | tf_op jit(solution)/shard_map/all_to_all | solution.py:298
  42.6 7.0 %all-to-all-done = f32[16,4,640]{2,1,0:T(4,128)} async-done(((f32[16,4,640]{2,1,0:T(4,128)}), f32[16,4,640]{2,1,0:T(4,128)}, u32[]{:S(2)}, u32[]{:S(2)}) %all-to-all-start) | async-done | bytes 163872 | tf_op jit(solution)/shard_map/all_to_all | solution.py:298
  50.7 2.4 %collective-permute-start.6 = (f32[4,640]{1,0:T(4,128)S(1)}, f32[4,640]{1,0:T(4,128)S(1)}, u32[]{:S(2)}, u32[]{:S(2)}) collective-permute-start(f32[4,640]{1,0:T(4,128)S(1)} %shard_map.88.own), channel_id=1, source_target_pairs={{0,1},{1,0},{2,3},{3,2},{4,5},{5,4},{6,7},{7,6},{8,9},{9,8},{10,11... | collective-permute-start | bytes 30728 | tf_op jit(solution)/shard_map/ppermute | solution.py:301
  54.7 4.2 %all-to-all-start.1 = ((f32[16,4,640]{2,1,0:T(4,128)}), f32[16,4,640]{2,1,0:T(4,128)}, u32[]{:S(2)}, u32[]{:S(2)}) async-start(f32[16,4,640]{2,1,0:T(4,128)} %shard_map.89), calls=%async_computation.1 | async-start | bytes 327680 | tf_op jit(solution)/shard_map/all_to_all | solution.py:305
  59.6 6.7 %all-to-all-done.1 = f32[16,4,640]{2,1,0:T(4,128)} async-done(((f32[16,4,640]{2,1,0:T(4,128)}), f32[16,4,640]{2,1,0:T(4,128)}, u32[]{:S(2)}, u32[]{:S(2)}) %all-to-all-start.1) | async-done | bytes 163872 | tf_op jit(solution)/shard_map/all_to_all | solution.py:305
  68.2 1.2 %shard_map.90 = (f32[4,5,8,1024]{3,2,1,0:T(8,128)S(1)}, f32[5,8,1024]{2,1,0:T(8,128)S(1)}, f32[5,8,1024]{2,1,0:T(8,128)S(1)}, f32[20,1024]{1,0:T(8,128)S(1)}) custom-call(s32[2]{0:T(128)S(1)} %pad_add_fusion.flags, f32[256,64]{1,0:T(8,128)S(1)} %copy-done.13, f32[64,640]{1,0:T(8,128)S(1)} %reshape.17.fix), custom_call_target="tpu_custom_call" | custom-call | flops 1294344 | bytes 1294344 | tf_op jit(solution)/shard_map/pallas_call | solution.py:18
  69.5 4.5 %collective-permute-start.9 = (f32[5,8,1024]{2,1,0:T(8,128)S(1)}, f32[5,8,1024]{2,1,0:T(8,128)S(1)}, u32[]{:S(2)}, u32[]{:S(2)}) collective-permute-start(f32[5,8,1024]{2,1,0:T(8,128)S(1)} %get-tuple-element.34), channel_id=1, source_target_pairs={{2,4},{4,2},{6,8},{8,6},{10,12},{12,10},{3,5},{5,3},{7,9},{9,7},{1... | collective-permute-start | bytes 491528 | tf_op jit(solution)/shard_map/ppermute | solution.py:259
  74.1 1.8 %collective-permute-start.7 = (f32[20,1024]{1,0:T(8,128)S(1)}, f32[20,1024]{1,0:T(8,128)S(1)}, u32[]{:S(2)}, u32[]{:S(2)}) collective-permute-start(f32[20,1024]{1,0:T(8,128)S(1)} %get-tuple-element.32), channel_id=1, source_target_pairs={{0,1},{1,0},{2,3},{3,2},{4,5},{5,4},{6,7},{7,6},{8,9},{9,8},{10,11... | collective-permute-start | bytes 245768 | tf_op jit(solution)/shard_map/ppermute | solution.py:260
  77.0 1.1 %copy-done.12 = f32[4,5,8,1024]{3,2,1,0:T(8,128)S(1)} copy-done((f32[4,5,8,1024]{3,2,1,0:T(8,128)S(1)}, f32[4,5,8,1024]{3,2,1,0:T(8,128)}, u32[]{:S(2)}) %copy-start.12) | copy-done | bytes 655384
  78.7 2.1 %shard_map.91.inner = f32[4,5,8,1024]{3,2,1,0:T(8,128)S(1)} custom-call(s32[2]{0:T(128)S(1)} %pad_add_fusion.flags, f32[5,5]{1,0:T(8,128)S(1)} %copy-done.15, f32[5,5]{1,0:T(8,128)S(1)} %copy-done.14, f32[4,5,8,1024]{3,2,1,0:T(8,128)S(1)} %shard_map.87.base, f32[4,5,8,1024]{3,2,1,0:T(8,128)S(1)} %get-tuple-element.31.fix, ...), custom_call_target="tpu_custom_call" | custom-call | flops 8601808 | bytes 8601808 | tf_op jit(solution)/shard_map/pallas_call | solution.py:18
  80.9 1.9 %shard_map.92 = f32[4,5,8,1024]{3,2,1,0:T(8,128)} custom-call(s32[2]{0:T(128)S(1)} %pad_add_fusion.flags, f32[5,5]{1,0:T(8,128)S(1)} %copy-done.14, f32[4,5,8,1024]{3,2,1,0:T(8,128)S(1)} %shard_map.91.inner, f32[5,8,1024]{2,1,0:T(8,128)S(1)} %collective-permute-done.8.halo_a, f32[5,8,1024]{2,1,0:T(8,128)S(1)} %collective-permute-done.9.halo_b, ...), custom_call_target="tpu_custom_call" | custom-call | flops 4915308 | bytes 4915308 | tf_op jit(solution)/shard_map/pallas_call | solution.py:18
  (66 shorter events, 15.5 us)
Async XLA Ops:
  0.0 14.5 %copy-start.14 = (f32[5,5]{1,0:T(8,128)S(1)}, f32[5,5]{1,0:T(8,128)}, u32[]{:S(2)}) copy-start(f32[5,5]{1,0:T(8,128)} %span.11) | copy-start | bytes 304
  0.0 14.6 %copy-start.15 = (f32[5,5]{1,0:T(8,128)S(1)}, f32[5,5]{1,0:T(8,128)}, u32[]{:S(2)}) copy-start(f32[5,5]{1,0:T(8,128)} %wall.5) | copy-start | bytes 304
  0.1 1.9 %copy-start = (f32[4,8,5,5,1024]{4,1,3,2,0:T(8,128)S(1)}, f32[4,8,5,5,1024]{4,1,3,2,0:T(8,128)}, u32[]{:S(2)}) copy-start(f32[4,8,5,5,1024]{4,1,3,2,0:T(8,128)} %param.10) | copy-start | bytes 9830404
  2.0 1.1 %copy-start.5 = (f32[4,8,5,1024]{3,1,2,0:T(8,128)S(1)}, f32[4,8,5,1024]{3,1,2,0:T(8,128)}, u32[]{:S(2)}) copy-start(f32[4,8,5,1024]{3,1,2,0:T(8,128)} %param.8) | copy-start | bytes 1966084
  3.1 8.6 %copy-start.16 = (s32[4,8,8]{2,1,0:T(8,128)S(1)}, s32[4,8,8]{2,1,0:T(8,128)}, u32[]{:S(2)}) copy-start(s32[4,8,8]{2,1,0:T(8,128)} %param.14) | copy-start | bytes 3076
  3.1 8.6 %copy-start.17 = (s32[4,8,8]{2,1,0:T(8,128)S(1)}, s32[4,8,8]{2,1,0:T(8,128)}, u32[]{:S(2)}) copy-start(s32[4,8,8]{2,1,0:T(8,128)} %param.13) | copy-start | bytes 3076
  3.1 11.5 %copy-start.1 = (f32[4,8,5,5,1024]{4,1,3,2,0:T(8,128)S(1)}, f32[4,8,5,5,1024]{4,1,3,2,0:T(8,128)}, u32[]{:S(2)}) copy-start(f32[4,8,5,5,1024]{4,1,3,2,0:T(8,128)} %param.10) | copy-start | bytes 9830404
  5.9 8.7 %collective-permute-start = (f32[20,1024]{1,0:T(8,128)}, f32[20,1024]{1,0:T(8,128)S(1)}, u32[]{:S(2)}, u32[]{:S(2)}) collective-permute-start(f32[20,1024]{1,0:T(8,128)} %get-tuple-element.21), channel_id=1, source_target_pairs={{0,1},{1,0},{2,3},{3,2},{4,5},{5,4},{6,7},{7,6},{8,9},{9,8},{10,11... | collective-permute-start | bytes 245768 | tf_op jit(solution)/shard_map/ppermute | solution.py:260
  6.5 14.4 %collective-permute-start.1 = (f32[5,8,1024]{2,1,0:T(8,128)}, f32[5,8,1024]{2,1,0:T(8,128)S(1)}, u32[]{:S(2)}, u32[]{:S(2)}) collective-permute-start(f32[5,8,1024]{2,1,0:T(8,128)} %get-tuple-element.22), channel_id=1, source_target_pairs={{0,2},{2,0},{4,6},{6,4},{8,10},{10,8},{12,14},{14,12},{1,3},{3,1},... | collective-permute-start | bytes 491528 | tf_op jit(solution)/shard_map/ppermute | solution.py:258
  8.1 12.8 %collective-permute-start.2 = (f32[5,8,1024]{2,1,0:T(8,128)}, f32[5,8,1024]{2,1,0:T(8,128)}, u32[]{:S(2)}, u32[]{:S(2)}) collective-permute-start(f32[5,8,1024]{2,1,0:T(8,128)} %get-tuple-element.23), channel_id=1, source_target_pairs={{2,4},{4,2},{6,8},{8,6},{10,12},{12,10},{3,5},{5,3},{7,9},{9,7},{1... | collective-permute-start | bytes 491528 | tf_op jit(solution)/shard_map/ppermute | solution.py:259
  14.6 1.9 %copy-start.2 = (f32[4,8,5,5,1024]{4,1,3,2,0:T(8,128)S(1)}, f32[4,8,5,5,1024]{4,1,3,2,0:T(8,128)}, u32[]{:S(2)}) copy-start(f32[4,8,5,5,1024]{4,1,3,2,0:T(8,128)} %param.9) | copy-start | bytes 9830404
  16.5 1.1 %copy-start.6 = (f32[4,8,5,1024]{3,1,2,0:T(8,128)S(1)}, f32[4,8,5,1024]{3,1,2,0:T(8,128)}, u32[]{:S(2)}) copy-start(f32[4,8,5,1024]{3,1,2,0:T(8,128)} %param.8) | copy-start | bytes 1966084
  20.9 7.7 %copy-start.3 = (f32[4,8,5,5,1024]{4,1,3,2,0:T(8,128)S(1)}, f32[4,8,5,5,1024]{4,1,3,2,0:T(8,128)}, u32[]{:S(2)}) copy-start(f32[4,8,5,5,1024]{4,1,3,2,0:T(8,128)} %param.9) | copy-start | bytes 9830404
  22.4 6.2 %collective-permute-start.3 = (f32[20,1024]{1,0:T(8,128)S(1)}, f32[20,1024]{1,0:T(8,128)S(1)}, u32[]{:S(2)}, u32[]{:S(2)}) collective-permute-start(f32[20,1024]{1,0:T(8,128)S(1)} %get-tuple-element.26), channel_id=1, source_target_pairs={{0,1},{1,0},{2,3},{3,2},{4,5},{5,4},{6,7},{7,6},{8,9},{9,8},{10,11... | collective-permute-start | bytes 245768 | tf_op jit(solution)/shard_map/ppermute | solution.py:260
  23.1 8.2 %collective-permute-start.4 = (f32[5,8,1024]{2,1,0:T(8,128)S(1)}, f32[5,8,1024]{2,1,0:T(8,128)S(1)}, u32[]{:S(2)}, u32[]{:S(2)}) collective-permute-start(f32[5,8,1024]{2,1,0:T(8,128)S(1)} %get-tuple-element.24.edge_a), channel_id=1, source_target_pairs={{0,2},{2,0},{4,6},{6,4},{8,10},{10,8},{12,14},{14,12},{1,3},{3,1},... | collective-permute-start | bytes 491528 | tf_op jit(solution)/shard_map/ppermute | solution.py:258
  23.1 9.8 %collective-permute-start.5 = (f32[5,8,1024]{2,1,0:T(8,128)S(1)}, f32[5,8,1024]{2,1,0:T(8,128)S(1)}, u32[]{:S(2)}, u32[]{:S(2)}) collective-permute-start(f32[5,8,1024]{2,1,0:T(8,128)S(1)} %get-tuple-element.25.edge_b), channel_id=1, source_target_pairs={{2,4},{4,2},{6,8},{8,6},{10,12},{12,10},{3,5},{5,3},{7,9},{9,7},{1... | collective-permute-start | bytes 491528 | tf_op jit(solution)/shard_map/ppermute | solution.py:259
  28.6 13.9 %copy-start.18 = (f32[1,1,5,10,4]{3,4,2,1,0:T(4,128)S(1)}, f32[1,1,5,10,4]{3,4,2,1,0:T(4,128)}, u32[]{:S(2)}) copy-start(f32[1,1,5,10,4]{3,4,2,1,0:T(4,128)} %param.15) | copy-start | bytes 2404
  35.7 13.9 %all-to-all-start = ((f32[16,4,640]{2,1,0:T(4,128)}), f32[16,4,640]{2,1,0:T(4,128)}, u32[]{:S(2)}, u32[]{:S(2)}) async-start(f32[16,4,640]{2,1,0:T(4,128)} %all_to_all.10), calls=%async_computation | async-start | bytes 327680 | tf_op jit(solution)/shard_map/all_to_all | solution.py:298
  50.7 3.2 %collective-permute-start.6 = (f32[4,640]{1,0:T(4,128)S(1)}, f32[4,640]{1,0:T(4,128)S(1)}, u32[]{:S(2)}, u32[]{:S(2)}) collective-permute-start(f32[4,640]{1,0:T(4,128)S(1)} %shard_map.88.own), channel_id=1, source_target_pairs={{0,1},{1,0},{2,3},{3,2},{4,5},{5,4},{6,7},{7,6},{8,9},{9,8},{10,11... | collective-permute-start | bytes 30728 | tf_op jit(solution)/shard_map/ppermute | solution.py:301
  54.7 11.6 %all-to-all-start.1 = ((f32[16,4,640]{2,1,0:T(4,128)}), f32[16,4,640]{2,1,0:T(4,128)}, u32[]{:S(2)}, u32[]{:S(2)}) async-start(f32[16,4,640]{2,1,0:T(4,128)} %shard_map.89), calls=%async_computation.1 | async-start | bytes 327680 | tf_op jit(solution)/shard_map/all_to_all | solution.py:305
  68.2 10.5 %copy-start.4 = (f32[4,8,5,5,1024]{4,1,3,2,0:T(8,128)S(1)}, f32[4,8,5,5,1024]{4,1,3,2,0:T(8,128)}, u32[]{:S(2)}) copy-start(f32[4,8,5,5,1024]{4,1,3,2,0:T(8,128)} %param.9) | copy-start | bytes 9830404
  69.4 11.4 %collective-permute-start.8 = (f32[5,8,1024]{2,1,0:T(8,128)S(1)}, f32[5,8,1024]{2,1,0:T(8,128)S(1)}, u32[]{:S(2)}, u32[]{:S(2)}) collective-permute-start(f32[5,8,1024]{2,1,0:T(8,128)S(1)} %get-tuple-element.33), channel_id=1, source_target_pairs={{0,2},{2,0},{4,6},{6,4},{8,10},{10,8},{12,14},{14,12},{1,3},{3,1},... | collective-permute-start | bytes 491528 | tf_op jit(solution)/shard_map/ppermute | solution.py:258
  69.5 11.4 %collective-permute-start.9 = (f32[5,8,1024]{2,1,0:T(8,128)S(1)}, f32[5,8,1024]{2,1,0:T(8,128)S(1)}, u32[]{:S(2)}, u32[]{:S(2)}) collective-permute-start(f32[5,8,1024]{2,1,0:T(8,128)S(1)} %get-tuple-element.34), channel_id=1, source_target_pairs={{2,4},{4,2},{6,8},{8,6},{10,12},{12,10},{3,5},{5,3},{7,9},{9,7},{1... | collective-permute-start | bytes 491528 | tf_op jit(solution)/shard_map/ppermute | solution.py:259
  74.1 4.6 %collective-permute-start.7 = (f32[20,1024]{1,0:T(8,128)S(1)}, f32[20,1024]{1,0:T(8,128)S(1)}, u32[]{:S(2)}, u32[]{:S(2)}) collective-permute-start(f32[20,1024]{1,0:T(8,128)S(1)} %get-tuple-element.32), channel_id=1, source_target_pairs={{0,1},{1,0},{2,3},{3,2},{4,5},{5,4},{6,7},{7,6},{8,9},{9,8},{10,11... | collective-permute-start | bytes 245768 | tf_op jit(solution)/shard_map/ppermute | solution.py:260
  (7 other events, 6.7 us)

commit v2 on v0

v2 whole, which is shorter than its diff:
```python
import functools
import math

import jax
import jax.numpy as jnp
from jax import lax
from jax.experimental import pallas as pl
from jax.experimental.pallas import tpu as pltpu
from jax.sharding import PartitionSpec as P

LANES = 128
VMEM = pl.BlockSpec(memory_space=pltpu.VMEM)
SMEM = pl.BlockSpec(memory_space=pltpu.SMEM)
HBM = pl.BlockSpec(memory_space=pltpu.HBM)
HIGHEST = lax.Precision.HIGHEST
F32 = jnp.float32


def shaped(*shape):
    return jax.ShapeDtypeStruct(shape, F32)


def in_hbm(array):
    return pltpu.with_memory_space_constraint(array, pltpu.HBM)


def call(kernel, outs, args, places=None, out_places=None, scratch=(), aliases=None):
    size = 2 * sum(math.prod(a.shape) for a in (*args, *outs))
    return pl.pallas_call(
        kernel,
        out_shape=outs,
        in_specs=places or [VMEM] * len(args),
        out_specs=out_places or [VMEM] * len(outs),
        scratch_shapes=scratch,
        input_output_aliases=aliases or {},
        cost_estimate=pl.CostEstimate(flops=size, bytes_accessed=size, transcendentals=0),
        compiler_params=pltpu.CompilerParams(vmem_limit_bytes=8 * 2**20),
    )(*args)


def total(terms):
    return functools.reduce(lambda a, b: a + b, terms)


def position():
    span_at, wall_at = lax.axis_index("span"), lax.axis_index("wall")
    odd = lax.rem(span_at, 2)
    plane_a = 3 - 3 * odd
    return odd == 0, plane_a, 3 - plane_a, 7 - 7 * wall_at


def inside():
    at, size = lax.axis_index("span"), lax.axis_size("span")
    return jnp.logical_and(at > 0, at < size - 1)


def mix(splat, which, values):
    return [total([splat[which, k, i] * values[k] for k in range(5)]) for i in range(5)]


def sweep(jinv, s, lanes, values):
    return [total([jinv[s, i, k, :, lanes] * values[k] for k in range(5)]) for i in range(5)]


def beyond_span(splat, halo, lanes, real=None):
    values = [halo[k, :, lanes] for k in range(5)]
    if real is not None:
        values = [jnp.where(real, v, 0.0) for v in values]
    return mix(splat, 1, values)


def for_lanes(body, length):
    @pl.loop(0, length // LANES)
    def _(q):
        body(pl.ds(pl.multiple_of(q * LANES, LANES), LANES))


def first_kernel(wall, span, rhs_in, jinv_in, rhs, jinv, splat, first, edge_a, edge_b, edge_w, sems):
    copies = [pltpu.make_async_copy(rhs_in, rhs, sems.at[4])]
    copies += [pltpu.make_async_copy(jinv_in.at[s], jinv.at[s], sems.at[s]) for s in range(4)]
    for copy in copies:
        copy.start()
    for which, coupling in enumerate((wall, span)):
        for k in range(5):
            for i in range(5):
                splat[which, k, i] = jnp.full((8, LANES), coupling[k, i], F32)
    even, plane_a, plane_b, row = position()
    copies[0].wait()
    for s in range(4):
        copies[1 + s].wait()

        def body(lanes, s=s):
            swept = sweep(jinv, s, lanes, [rhs[s, k, :, lanes] for k in range(5)])
            for k in range(5):
                first[s, k, :, lanes] = swept[k]

        for_lanes(body, rhs.shape[-1])
        for k in range(5):
            edge_w[s * 5 + k, :] = first[s, k, row, :]
    for k in range(5):
        edge_a[k] = first[plane_a, k]
        edge_b[k] = first[plane_b, k]


def local_apply(splat, row, planes, halo_w, jac, lanes, s):
    own = planes[s]
    rows = lax.broadcasted_iota(jnp.int32, own[0].shape, 0)
    other_side = rows == row
    near_wall, near_span = [], []
    for k in range(5):
        up = jnp.where(rows == 7, 0.0, pltpu.roll(own[k], 7, 0))
        down = jnp.where(rows == 0, 0.0, pltpu.roll(own[k], 1, 0))
        beyond = jnp.where(other_side, halo_w[s * 5 + k, lanes][None, :], 0.0)
        near_wall.append(up + down + beyond)
        near_span.append(total([planes[n][k] for n in (s - 1, s + 1) if 0 <= n < 4]))
    from_wall, from_span = mix(splat, 0, near_wall), mix(splat, 1, near_span)
    return [
        total([jac[s, k, i, :, lanes] * own[k] for k in range(5)]) - (from_wall[i] + from_span[i])
        for i in range(5)
    ]


def hot_rows(owner, slot, tiles):
    ids = lax.broadcasted_iota(jnp.int32, (8, LANES), 1)
    hot = []
    for s in range(4):
        named = owner[s] * 4 + slot[s]
        hot += [jnp.where(named[:, q : q + 1] == ids, 1.0, 0.0) for q in range(tiles)]
    return jnp.concatenate(hot, axis=0)


def second_local_kernel(splat, first, halo_w, rhs, jinv, owner, slot, jac_in, inner, jac, onehot_t, sems):
    copies = [pltpu.make_async_copy(jac_in.at[s], jac.at[s], sems.at[s]) for s in range(4)]
    for copy in copies:
        copy.start()
    row = position()[3]
    onehot_t[...] = hot_rows(owner, slot, rhs.shape[-1] // LANES).T[: onehot_t.shape[0]]
    for s in range(4):
        copies[s].wait()

        def body(lanes, s=s):
            planes = [[first[n, k, :, lanes] for k in range(5)] if abs(n - s) < 2 else None for n in range(4)]
            applied = local_apply(splat, row, planes, halo_w, jac, lanes, s)
            swept = sweep(jinv, s, lanes, [rhs[s, k, :, lanes] - applied[k] for k in range(5)])
            for k in range(5):
                inner[s, k, :, lanes] = planes[s][k] + swept[k]

        for_lanes(body, rhs.shape[-1])


def second_edge_kernel(splat, inner, halo_a, halo_b, jinv, edge_a, edge_b, edge_w):
    even, plane_a, plane_b, row = position()
    real = inside()

    def body(lanes):
        for plane, halo, edge, there in ((plane_a, halo_a, edge_a, None), (plane_b, halo_b, edge_b, real)):
            swept = sweep(jinv, plane, lanes, beyond_span(splat, halo, lanes, there))
            for k in range(5):
                edge[k, :, lanes] = inner[plane, k, :, lanes] + swept[k]

    for_lanes(body, inner.shape[-1])
    for k in range(5):
        for s in (1, 2):
            edge_w[s * 5 + k, :] = inner[s, k, row, :]
        a, b = edge_a[k, row, :], edge_b[k, row, :]
        edge_w[k, :] = jnp.where(even, b, a)
        edge_w[15 + k, :] = jnp.where(even, a, b)


def planes_of(even, inner, edge_a, edge_b, lanes):
    a = [edge_a[k, :, lanes] for k in range(5)]
    b = [edge_b[k, :, lanes] for k in range(5)]
    return [
        [jnp.where(even, b[k], a[k]) for k in range(5)],
        [inner[1, k, :, lanes] for k in range(5)],
        [inner[2, k, :, lanes] for k in range(5)],
        [jnp.where(even, a[k], b[k]) for k in range(5)],
    ]


def defect_local_kernel(splat, inner, edge_a, edge_b, halo_w, rhs, jac, jinv, onehot_t, base, partial, defect):
    even, _, _, row = position()

    def body(lanes):
        planes = planes_of(even, inner, edge_a, edge_b, lanes)
        for s in range(4):
            applied = local_apply(splat, row, planes, halo_w, jac, lanes, s)
            rest = [rhs[s, k, :, lanes] - applied[k] for k in range(5)]
            swept = sweep(jinv, s, lanes, rest)
            for k in range(5):
                base[s, k, :, lanes] = planes[s][k] + swept[k]
                defect[s, k, :, lanes] = rest[k]

    for_lanes(body, rhs.shape[-1])
    tiles = defect.shape[-1] // LANES
    for k in range(5):
        rows = jnp.concatenate(
            [defect[s, k, :, q * LANES : (q + 1) * LANES] for s in range(4) for q in range(tiles)], axis=0
        )
        partial[:, k * LANES : (k + 1) * LANES] = jnp.dot(
            onehot_t[...], rows, precision=HIGHEST, preferred_element_type=F32
        )


def restrict_kernel(splat, inner, base, halo_a, halo_b, onehot_t, jinv, partial, base_out, edges, sems):
    even, plane_a, plane_b, _ = position()
    real = inside()
    copies = [pltpu.make_async_copy(base.at[pl.ds(1, 2)], base_out.at[pl.ds(1, 2)], sems.at[2])]
    copies[0].start()
    tiles = halo_a.shape[-1] // LANES
    parts = []
    for n, (plane, halo, there) in enumerate(((plane_a, halo_a, None), (plane_b, halo_b, real))):
        for q in range(tiles):
            lanes = slice(q * LANES, (q + 1) * LANES)
            beyond = beyond_span(splat, halo, lanes, there)
            parts.append(beyond)
            swept = sweep(jinv, plane, lanes, beyond)
            for k in range(5):
                edges[n, k, :, lanes] = base[plane, k, :, lanes] + swept[k]
        copies.append(pltpu.make_async_copy(edges.at[n], base_out.at[plane], sems.at[n]))
        copies[-1].start()
    width = 8 * tiles
    low, high = onehot_t[:, :width], onehot_t[:, 3 * width :]
    hot = jnp.concatenate([jnp.where(even, high, low), jnp.where(even, low, high)], axis=1)
    slots = partial.shape[1]
    for k in range(5):
        rows = jnp.concatenate([part[k] for part in parts], axis=0)
        sums = inner[:, k * LANES : (k + 1) * LANES] + jnp.dot(
            hot, rows, precision=HIGHEST, preferred_element_type=F32
        )
        for p in range(partial.shape[0]):
            partial[p, :, k * LANES : (k + 1) * LANES] = sums[p * slots : (p + 1) * slots]
    for copy in copies:
        copy.wait()


def sum_kernel(received, sums):
    sums[...] = total([received[p] for p in range(received.shape[0])])


def coarse_kernel(inv, own, other, out):
    first_group = lax.axis_index("wall") == 0
    groups = [
        [jnp.where(first_group, x[:, k * LANES : (k + 1) * LANES], y[:, k * LANES : (k + 1) * LANES]) for k in range(5)]
        for x, y in ((own, other), (other, own))
    ]
    for i in range(5):
        rows = inv[i]
        fix = total([rows[:, c * 5 + k : c * 5 + k + 1] * groups[c][k] for c in range(2) for k in range(5)])
        for p in range(out.shape[0]):
            out[p, :, i * LANES : (i + 1) * LANES] = fix


def prolong_kernel(owner, slot, fixes, out, edge_a, edge_b, edge_w, fix):
    _, plane_a, plane_b, row = position()
    tiles = out.shape[-1] // LANES
    owners, slots, _ = fixes.shape
    for p in range(owners):
        fix[p * slots : (p + 1) * slots, :] = fixes[p]
    hot = hot_rows(owner, slot, tiles)[:, : owners * slots]
    for k in range(5):
        rows = jnp.dot(hot, fix[:, k * LANES : (k + 1) * LANES], precision=HIGHEST, preferred_element_type=F32)
        for s in range(4):
            for q in range(tiles):
                at = (s * tiles + q) * 8
                out[s, k, :, q * LANES : (q + 1) * LANES] = rows[at : at + 8]
    for k in range(5):
        edge_a[k] = out[plane_a, k]
        edge_b[k] = out[plane_b, k]
        for s in range(4):
            edge_w[s * 5 + k, :] = out[s, k, row, :]


def final_local_kernel(splat, fix, halo_w, base_in, jac_in, jinv_in, out, inner, jinv, base, jac, sems):
    row = position()[3]
    loads = []
    for s in range(4):
        loads += [
            pltpu.make_async_copy(source.at[s], here.at[s], sems.at[n, s])
            for n, (source, here) in enumerate(((jac_in, jac), (jinv_in, jinv), (base_in, base)))
        ]
    for load in loads:
        load.start()
    stores = []
    for s in range(4):
        for load in loads[3 * s : 3 * s + 3]:
            load.wait()

        def body(lanes, s=s):
            planes = [[fix[n, k, :, lanes] for k in range(5)] if abs(n - s) < 2 else None for n in range(4)]
            applied = local_apply(splat, row, planes, halo_w, jac, lanes, s)
            swept = sweep(jinv, s, lanes, applied)
            for k in range(5):
                inner[s, k, :, lanes] = base[s, k, :, lanes] + (planes[s][k] - swept[k])

        for_lanes(body, fix.shape[-1])
        if s in (1, 2):
            stores.append(pltpu.make_async_copy(inner.at[s], out.at[s], sems.at[3, s]))
            stores[-1].start()
    for store in stores:
        store.wait()


def final_edge_kernel(splat, inner, halo_a, halo_b, jinv, out_in, out, edges, sems):
    del out_in
    _, plane_a, plane_b, _ = position()
    real = inside()
    stores = []
    for n, (plane, halo, there) in enumerate(((plane_a, halo_a, None), (plane_b, halo_b, real))):

        def body(lanes, n=n, plane=plane, halo=halo, there=there):
            swept = sweep(jinv, plane, lanes, beyond_span(splat, halo, lanes, there))
            for k in range(5):
                edges[n, k, :, lanes] = inner[plane, k, :, lanes] + swept[k]

        for_lanes(body, inner.shape[-1])
        stores.append(pltpu.make_async_copy(edges.at[n], out.at[plane], sems.at[n]))
        stores[-1].start()
    for store in stores:
        store.wait()


def exchange(edge_a, edge_b, edge_w):
    size = lax.axis_size("span")
    even = [p for i in range(0, size, 2) for p in ((i, i + 1), (i + 1, i))]
    odd = [((i + 1) % size, (j + 1) % size) for i, j in even]
    return (
        lax.ppermute(edge_a, "span", even),
        lax.ppermute(edge_b, "span", odd),
        lax.ppermute(edge_w, "wall", [(0, 1), (1, 0)]),
    )


def local(rhs, jac, jac_inv, wall_coupling, span_coupling, block_owner, block_slot, coarse_inv):
    rhs = in_hbm(rhs.transpose(0, 2, 1, 3))
    jac_in = in_hbm(jac.transpose(0, 2, 3, 1, 4))
    jinv_in = in_hbm(jac_inv.transpose(0, 2, 3, 1, 4))
    inv = coarse_inv[0, 0].transpose(0, 2, 1)
    field, plane, edge = shaped(*rhs.shape), shaped(*rhs.shape[1:]), shaped(20, rhs.shape[-1])
    field_out = pltpu.HBM(rhs.shape, F32)
    matrices = shaped(*jac_in.shape)
    outer = pltpu.VMEM((2, *rhs.shape[1:]), F32)
    owners, slots = lax.axis_size("patch"), coarse_inv.shape[-1]
    aggregates, columns = owners * slots, 5 * LANES
    chunks = shaped(owners, slots, columns)

    rhs, jinv, splat, first, a, b, w = call(
        first_kernel,
        [field, matrices, shaped(2, 5, 5, 8, LANES), field, plane, plane, edge],
        [wall_coupling, span_coupling, rhs, jinv_in],
        places=[SMEM, SMEM, HBM, HBM],
        scratch=[pltpu.SemaphoreType.DMA((5,))],
    )
    halo_a, halo_b, halo_w = exchange(a, b, w)
    inner, jac, onehot_t = call(
        second_local_kernel,
        [field, matrices, shaped(aggregates, block_owner.size)],
        [splat, first, halo_w, rhs, jinv, block_owner, block_slot, jac_in],
        places=[VMEM] * 7 + [HBM],
        scratch=[pltpu.SemaphoreType.DMA((4,))],
    )
    a, b, w = call(second_edge_kernel, [plane, plane, edge], [splat, inner, halo_a, halo_b, jinv])
    halo_a, halo_b, halo_w = exchange(a, b, w)
    base, partial = call(
        defect_local_kernel,
        [field, shaped(aggregates, columns)],
        [splat, inner, a, b, halo_w, rhs, jac, jinv, onehot_t],
        scratch=[pltpu.VMEM(rhs.shape, F32)],
    )
    partial, base = call(
        restrict_kernel,
        [chunks, field_out],
        [splat, partial, base, halo_a, halo_b, onehot_t, jinv],
        out_places=[VMEM, HBM],
        scratch=[outer, pltpu.SemaphoreType.DMA((3,))],
    )
    received = lax.all_to_all(partial, "patch", split_axis=0, concat_axis=0, tiled=True)
    [mine] = call(sum_kernel, [shaped(slots, columns)], [received])
    theirs = lax.ppermute(mine, "wall", [(0, 1), (1, 0)])
    [reply] = call(coarse_kernel, [chunks], [inv, mine, theirs])
    fixes = lax.all_to_all(reply, "patch", split_axis=0, concat_axis=0, tiled=True)
    fix, a, b, w = call(
        prolong_kernel,
        [field, plane, plane, edge],
        [block_owner, block_slot, fixes],
        scratch=[pltpu.VMEM((aggregates, columns), F32)],
    )
    halo_a, halo_b, halo_w = exchange(a, b, w)
    out, inner, jinv = call(
        final_local_kernel,
        [field_out, field, matrices],
        [splat, fix, halo_w, in_hbm(base), jac_in, jinv_in],
        places=[VMEM] * 3 + [HBM] * 3,
        out_places=[HBM, VMEM, VMEM],
        scratch=[pltpu.VMEM(rhs.shape, F32), pltpu.VMEM(jac_in.shape, F32), pltpu.SemaphoreType.DMA((4, 4))],
    )
    [out] = call(
        final_edge_kernel,
        [field_out],
        [splat, inner, halo_a, halo_b, jinv, in_hbm(out)],
        places=[VMEM] * 5 + [HBM],
        out_places=[HBM],
        scratch=[outer, pltpu.SemaphoreType.DMA((2,))],
        aliases={5: 0},
    )
    return out.transpose(0, 2, 1, 3)


def solution(mesh):
    return jax.shard_map(
        local,
        mesh=mesh,
        in_specs=(
            P("span", "wall", None, "patch"),
            P("span", "wall", None, None, "patch"),
            P("span", "wall", None, None, "patch"),
            P(),
            P(),
            P("span", "wall", "patch"),
            P("span", "wall", "patch"),
            P("span", "wall", None, None, "patch"),
        ),
        out_specs=P("span", "wall", None, "patch"),
        check_vma=False,
    )
```

time: 158 us -> 63.4 us (0.40)
  waiting for transfers between devices: 50.7 us -> 4.34 us
  starting transfers between devices: 49.4 us -> 18.7 us
  other arithmetic: 22.1 us -> 0 us
  blocking collectives: 4.81 us -> 23.4 us
  matrix products: 17.9 us -> 0 us
  Pallas kernels: 0 us -> 15.2 us
  local copies, waits for them, and re-layouts: 11.7 us -> 1.4 us
    all_to_all x3 -> x0, waiting for transfers between devices: 38.4 us -> none  [the longest x1 21.4 us: local(): lax.all_to_all(reply, 'patch', split_axis=0, concat_axis=0, tiled=True)]
    all_to_all x0 -> x2, blocking collectives: none -> 23.4 us  [the longest x1 13.7 us: local(): lax.all_to_all(partial, 'patch', split_axis=0, concat_axis=0, tiled=True)]
    all_to_all x3 -> x0, starting transfers between devices: 17.9 us -> none  [the longest x1 6.8 us: local(): lax.all_to_all(outgoing, 'patch', split_axis=0, concat_axis=0, tiled=True)]
    dot_general x11 -> x0, matrix products: 17.9 us -> none  [the longest x3 4.23 us: apply_adjoint(): jnp.einsum('ki,swkl->swil', wall_coupling, near_wall, precision=highest)]
    pallas_call x0 -> x10, Pallas kernels: none -> 15.2 us  [call(): pl.pallas_call(kernel, out_shape=outs, in_specs=places or [VMEM] * len(ar...]
    ppermute x12 -> x10, starting transfers between devices: 31.4 us -> 18.7 us  [the longest x3 7.88 us: exchange(): lax.ppermute(edge_b, 'span', odd)]
    reduce_sum x8 -> x0, other arithmetic: 8.54 us -> none  [the longest x3 4.57 us: apply_adjoint(): own_term = jnp.sum(jac * interior[:, :, :, None, :], axis=2)]
    ppermute x12 -> x10, waiting for transfers between devices: 12.2 us -> 4.34 us  [the longest x3 2.83 us: exchange(): lax.ppermute(edge_w, 'wall', [(0, 1), (1, 0)])]
  transfers between devices with their start and end apart: 15 -> 10, of which waited for: 9 -> 5; matrix products, arithmetic and copies ran while one was open for 11% -> 0% of each run, Pallas kernels for 0% -> 13%
where the time goes in v2:
time: 63.4 us; the launch traced here: 63.1 us
  blocking collectives  23.4 us (37%)
  starting transfers between devices  18.7 us (29%)
  Pallas kernels  15.2 us (24%)
  waiting for transfers between devices  4.34 us (7%)
  local copies, waits for them, and re-layouts  1.4 us (2%)
    pallas_call x10, Pallas kernels, call(): pl.pallas_call(kernel, out_shape=outs, in_specs=places or [VMEM] * len(ar...  15.2 us
    all_to_all x1, blocking collectives, local(): lax.all_to_all(partial, 'patch', split_axis=0, concat_axis=0, tiled=True)  13.7 us
    all_to_all x1, blocking collectives, local(): lax.all_to_all(reply, 'patch', split_axis=0, concat_axis=0, tiled=True)  9.77 us
    ppermute x3, starting transfers between devices, exchange(): lax.ppermute(edge_b, 'span', odd)  7.88 us
    ppermute x3, starting transfers between devices, exchange(): lax.ppermute(edge_w, 'wall', [(0, 1), (1, 0)])  5.28 us
    ppermute x3, starting transfers between devices, exchange(): lax.ppermute(edge_a, 'span', even)  2.88 us
    ppermute x3, waiting for transfers between devices, exchange(): lax.ppermute(edge_w, 'wall', [(0, 1), (1, 0)])  2.83 us
    ppermute x1, starting transfers between devices, local(): theirs = lax.ppermute(mine, 'wall', [(0, 1), (1, 0)])  2.61 us
  transfers between devices with their start and end apart: 10, of which 5 were waited for; matrix products, arithmetic and copies ran while one was open for 0% of the time, Pallas kernels for 13%

profile of v2, /device:TPU:1, one launch (start us, length us, event | category | flops | bytes accessed | tf_op | source)
XLA Modules:
  0.0 63.1 jit_solution(9953919375557688918)
XLA Ops:
  0.0 0.7 %copy-done.3 = f32[5,5]{1,0:T(8,128)S(1)} copy-done((f32[5,5]{1,0:T(8,128)S(1)}, f32[5,5]{1,0:T(8,128)}, u32[]{:S(2)}) %copy-start.3) | copy-done | bytes 124
  0.7 0.7 %copy-done.4 = f32[5,5]{1,0:T(8,128)S(1)} copy-done((f32[5,5]{1,0:T(8,128)S(1)}, f32[5,5]{1,0:T(8,128)}, u32[]{:S(2)}) %copy-start.4) | copy-done | bytes 124
  1.4 3.0 %shard_map.82 = (f32[4,5,8,1024]{3,2,1,0:T(8,128)S(1)}, f32[4,5,5,8,1024]{4,3,2,1,0:T(8,128)S(1)}, f32[2,5,5,8,128]{4,3,2,1,0:T(8,128)S(1)}, f32[4,5,8,1024]{3,2...) custom-call(f32[5,5]{1,0:T(8,128)S(1)} %copy-done.3, ...), custom_call_target="tpu_custom_call" | custom-call | flops 4567140 | bytes 4567140 | tf_op jit(solution)/shard_map/pallas_call | solution.py:29
  4.4 2.6 %collective-permute-start.1 = (f32[5,8,1024]{2,1,0:T(8,128)S(1)}, f32[5,8,1024]{2,1,0:T(8,128)S(1)}, u32[]{:S(2)}, u32[]{:S(2)}) collective-permute-start(f32[5,8,1024]{2,1,0:T(8,128)S(1)} %get-tuple-element.35), channel_id=1, source_target_pairs={{0,2},{2,0},{4,6},{6,4},{8,10},{10,8},{12,14},{14,12},{1,3},{3,1},... | collective-permute-start | bytes 491528 | tf_op jit(solution)/shard_map/ppermute | solution.py:328
  6.9 4.7 %collective-permute-start.2 = (f32[5,8,1024]{2,1,0:T(8,128)S(1)}, f32[5,8,1024]{2,1,0:T(8,128)S(1)}, u32[]{:S(2)}, u32[]{:S(2)}) collective-permute-start(f32[5,8,1024]{2,1,0:T(8,128)S(1)} %get-tuple-element.36), channel_id=1, source_target_pairs={{2,4},{4,2},{6,8},{8,6},{10,12},{12,10},{14,0},{0,14},{3,5},{5,3},... | collective-permute-start | bytes 491528 | tf_op jit(solution)/shard_map/ppermute | solution.py:329
  11.6 1.2 %collective-permute-start = (f32[20,1024]{1,0:T(8,128)S(1)}, f32[20,1024]{1,0:T(8,128)S(1)}, u32[]{:S(2)}, u32[]{:S(2)}) collective-permute-start(f32[20,1024]{1,0:T(8,128)S(1)} %get-tuple-element.31), channel_id=1, source_target_pairs={{0,1},{1,0},{2,3},{3,2},{4,5},{5,4},{6,7},{7,6},{8,9},{9,8},{10,11... | collective-permute-start | bytes 245768 | tf_op jit(solution)/shard_map/ppermute | solution.py:330
  12.8 0.9 %collective-permute-done.halo_w = f32[20,1024]{1,0:T(8,128)S(1)} collective-permute-done((f32[20,1024]{1,0:T(8,128)S(1)}, f32[20,1024]{1,0:T(8,128)S(1)}, u32[]{:S(2)}, u32[]{:S(2)}) %collective-permute-start) | collective-permute-done | bytes 81952 | tf_op jit(solution)/shard_map/ppermute | solution.py:330
  13.8 2.8 %shard_map.83 = (f32[4,5,8,1024]{3,2,1,0:T(8,128)S(1)}, f32[4,5,5,8,1024]{4,3,2,1,0:T(8,128)S(1)}, f32[64,256]{1,0:T(8,128)S(1)}) custom-call(f32[2,5,5,8,128]{4,3,2,1,0:T(8,128)S(1)} %get-tuple-element.29.splat, f32[4,5,8,1024]{3,2,1,0:T(8,128)S(1)} %get-tuple-element.30.first, f32[20,1024]{1,0:T(8,128)S(1)} %collective-permute-done.halo_w, ...), custom_call_target="tpu_custom_call" | custom-call | flops 6075392 | bytes 6075392 | tf_op jit(solution)/shard_map/pallas_call | solution.py:29
  17.1 1.4 %collective-permute-start.5 = (f32[5,8,1024]{2,1,0:T(8,128)S(1)}, f32[5,8,1024]{2,1,0:T(8,128)S(1)}, u32[]{:S(2)}, u32[]{:S(2)}) collective-permute-start(f32[5,8,1024]{2,1,0:T(8,128)S(1)} %get-tuple-element.38.edge_b), channel_id=1, source_target_pairs={{2,4},{4,2},{6,8},{8,6},{10,12},{12,10},{14,0},{0,14},{3,5},{5,3},... | collective-permute-start | bytes 491528 | tf_op jit(solution)/shard_map/ppermute | solution.py:329
  18.6 1.7 %collective-permute-start.3 = (f32[20,1024]{1,0:T(8,128)S(1)}, f32[20,1024]{1,0:T(8,128)S(1)}, u32[]{:S(2)}, u32[]{:S(2)}) collective-permute-start(f32[20,1024]{1,0:T(8,128)S(1)} %get-tuple-element.39), channel_id=1, source_target_pairs={{0,1},{1,0},{2,3},{3,2},{4,5},{5,4},{6,7},{7,6},{8,9},{9,8},{10,11... | collective-permute-start | bytes 245768 | tf_op jit(solution)/shard_map/ppermute | solution.py:330
  20.3 0.9 %collective-permute-done.3.halo_w = f32[20,1024]{1,0:T(8,128)S(1)} collective-permute-done((f32[20,1024]{1,0:T(8,128)S(1)}, f32[20,1024]{1,0:T(8,128)S(1)}, u32[]{:S(2)}, u32[]{:S(2)}) %collective-permute-start.3) | collective-permute-done | bytes 81952 | tf_op jit(solution)/shard_map/ppermute | solution.py:330
  21.2 1.9 %shard_map.85 = (f32[4,5,8,1024]{3,2,1,0:T(8,128)S(1)}, f32[64,640]{1,0:T(8,128)S(1)}) custom-call(f32[2,5,5,8,128]{4,3,2,1,0:T(8,128)S(1)} %get-tuple-element.29.splat, f32[4,5,8,1024]{3,2,1,0:T(8,128)S(1)} %get-tuple-element.34.inner, f32[5,8,1024]{2,1,0:T(8,128)S(1)} %get-tuple-element.37.edge_a, f32[5,8,1024]{2,1,0:T(8,128)S(1)} %get-tuple-element.38.edge_b, ...), custom_call_target="tpu_custom_call" | custom-call | flops 4681728 | bytes 4681728 | tf_op jit(solution)/shard_map/pallas_call | solution.py:29
  23.2 0.7 %collective-permute-done.5.halo_b = f32[5,8,1024]{2,1,0:T(8,128)S(1)} collective-permute-done((f32[5,8,1024]{2,1,0:T(8,128)S(1)}, f32[5,8,1024]{2,1,0:T(8,128)S(1)}, u32[]{:S(2)}, u32[]{:S(2)}) %collective-permute-start.5) | collective-permute-done | bytes 163872 | tf_op jit(solution)/shard_map/ppermute | solution.py:329
  23.9 1.3 %shard_map.86 = (f32[16,4,640]{2,1,0:T(4,128)S(1)}, f32[4,5,8,1024]{3,2,1,0:T(8,128)}) custom-call(f32[2,5,5,8,128]{4,3,2,1,0:T(8,128)S(1)} %get-tuple-element.29.splat, f32[64,640]{1,0:T(8,128)S(1)} %get-tuple-element.42.inner, f32[4,5,8,1024]{3,2,1,0:T(8,128)S(1)} %get-tuple-element.43.base, f32[5,8,1024]{2,1,0:T(8,128)S(1)} %collective-permute-done.4.halo_a, ...), custom_call_target="tpu_custom_call" | custom-call | flops 2756608 | bytes 2756608 | tf_op jit(solution)/shard_map/pallas_call | solution.py:29
  25.1 13.7 %all_to_all.10.received = f32[16,4,640]{2,1,0:T(4,128)S(1)} all-to-all(f32[16,4,640]{2,1,0:T(4,128)S(1)} %get-tuple-element.44), channel_id=1, replica_groups=mesh['patch'=16,'span'=8,'wall'=2] {'patch'}, dimensions={0} | all-to-all | bytes 327680 | tf_op jit(solution)/shard_map/all_to_all | solution.py:377
  38.8 2.6 %collective-permute-start.6 = (f32[4,640]{1,0:T(4,128)S(1)}, f32[4,640]{1,0:T(4,128)S(1)}, u32[]{:S(2)}, u32[]{:S(2)}) collective-permute-start(f32[4,640]{1,0:T(4,128)S(1)} %shard_map.87.own), channel_id=1, source_target_pairs={{0,1},{1,0},{2,3},{3,2},{4,5},{5,4},{6,7},{7,6},{8,9},{9,8},{10,11... | collective-permute-start | bytes 30728 | tf_op jit(solution)/shard_map/ppermute | solution.py:379
  41.4 0.8 %collective-permute-done.6.other = f32[4,640]{1,0:T(4,128)S(1)} collective-permute-done((f32[4,640]{1,0:T(4,128)S(1)}, f32[4,640]{1,0:T(4,128)S(1)}, u32[]{:S(2)}, u32[]{:S(2)}) %collective-permute-start.6) | collective-permute-done | bytes 10272 | tf_op jit(solution)/shard_map/ppermute | solution.py:379
  42.4 9.8 %all_to_all.11.fixes = f32[16,4,640]{2,1,0:T(4,128)S(1)} all-to-all(f32[16,4,640]{2,1,0:T(4,128)S(1)} %shard_map.88), channel_id=1, replica_groups=mesh['patch'=16,'span'=8,'wall'=2] {'patch'}, dimensions={0} | all-to-all | bytes 327680 | tf_op jit(solution)/shard_map/all_to_all | solution.py:381
  52.2 0.8 %shard_map.89 = (f32[4,5,8,1024]{3,2,1,0:T(8,128)S(1)}, f32[5,8,1024]{2,1,0:T(8,128)S(1)}, f32[5,8,1024]{2,1,0:T(8,128)S(1)}, f32[20,1024]{1,0:T(8,128)S(1)}) custom-call(s32[4,8,8]{2,1,0:T(8,128)S(1)} %copy-done, s32[4,8,8]{2,1,0:T(8,128)S(1)} %copy-done.1, f32[16,4,640]{2,1,0:T(4,128)S(1)} %all_to_all.11.fixes), custom_call_target="tpu_custom_call" | custom-call | flops 615424 | bytes 615424 | tf_op jit(solution)/shard_map/pallas_call | solution.py:29
  53.2 1.8 %collective-permute-start.9 = (f32[5,8,1024]{2,1,0:T(8,128)S(1)}, f32[5,8,1024]{2,1,0:T(8,128)S(1)}, u32[]{:S(2)}, u32[]{:S(2)}) collective-permute-start(f32[5,8,1024]{2,1,0:T(8,128)S(1)} %get-tuple-element.50), channel_id=1, source_target_pairs={{2,4},{4,2},{6,8},{8,6},{10,12},{12,10},{14,0},{0,14},{3,5},{5,3},... | collective-permute-start | bytes 491528 | tf_op jit(solution)/shard_map/ppermute | solution.py:329
  55.0 2.3 %collective-permute-start.7 = (f32[20,1024]{1,0:T(8,128)S(1)}, f32[20,1024]{1,0:T(8,128)S(1)}, u32[]{:S(2)}, u32[]{:S(2)}) collective-permute-start(f32[20,1024]{1,0:T(8,128)S(1)} %get-tuple-element.46), channel_id=1, source_target_pairs={{0,1},{1,0},{2,3},{3,2},{4,5},{5,4},{6,7},{7,6},{8,9},{9,8},{10,11... | collective-permute-start | bytes 245768 | tf_op jit(solution)/shard_map/ppermute | solution.py:330
  57.3 0.9 %collective-permute-done.7.halo_w = f32[20,1024]{1,0:T(8,128)S(1)} collective-permute-done((f32[20,1024]{1,0:T(8,128)S(1)}, f32[20,1024]{1,0:T(8,128)S(1)}, u32[]{:S(2)}, u32[]{:S(2)}) %collective-permute-start.7) | collective-permute-done | bytes 81952 | tf_op jit(solution)/shard_map/ppermute | solution.py:330
  58.3 3.7 %shard_map.90 = (f32[4,5,8,1024]{3,2,1,0:T(8,128)}, f32[4,5,8,1024]{3,2,1,0:T(8,128)S(1)}, f32[4,5,5,8,1024]{4,3,2,1,0:T(8,128)S(1)}) custom-call(f32[2,5,5,8,128]{4,3,2,1,0:T(8,128)S(1)} %get-tuple-element.29.splat, f32[4,5,8,1024]{3,2,1,0:T(8,128)S(1)} %get-tuple-element.45.fix, f32[20,1024]{1,0:T(8,128)S(1)} %collective-permute-done.7.halo_w, ...), custom_call_target="tpu_custom_call" | custom-call | flops 6369280 | bytes 6369280 | tf_op jit(solution)/shard_map/pallas_call | solution.py:29
  62.0 1.1 %shard_map.91 = f32[4,5,8,1024]{3,2,1,0:T(8,128)} custom-call(f32[2,5,5,8,128]{4,3,2,1,0:T(8,128)S(1)} %get-tuple-element.29.splat, f32[4,5,8,1024]{3,2,1,0:T(8,128)S(1)} %get-tuple-element.48.inner, f32[5,8,1024]{2,1,0:T(8,128)S(1)} %collective-permute-done.8.halo_a, ...), custom_call_target="tpu_custom_call", output_to_operand_aliasing={{}: (5, {})} | custom-call | flops 2887680 | bytes 2887680 | tf_op jit(solution)/shard_map/pallas_call | solution.py:29
  (18 shorter events, 0.9 us)
Async XLA Ops:
  0.0 13.8 %copy-start.1 = (s32[4,8,8]{2,1,0:T(8,128)S(1)}, s32[4,8,8]{2,1,0:T(8,128)}, u32[]{:S(2)}) copy-start(s32[4,8,8]{2,1,0:T(8,128)} %slot.3) | copy-start | bytes 3076
  0.0 13.8 %copy-start = (s32[4,8,8]{2,1,0:T(8,128)S(1)}, s32[4,8,8]{2,1,0:T(8,128)}, u32[]{:S(2)}) copy-start(s32[4,8,8]{2,1,0:T(8,128)} %owner.3) | copy-start | bytes 3076
  0.0 0.7 %copy-start.3 = (f32[5,5]{1,0:T(8,128)S(1)}, f32[5,5]{1,0:T(8,128)}, u32[]{:S(2)}) copy-start(f32[5,5]{1,0:T(8,128)} %wall.1) | copy-start | bytes 304
  0.7 0.7 %copy-start.4 = (f32[5,5]{1,0:T(8,128)S(1)}, f32[5,5]{1,0:T(8,128)}, u32[]{:S(2)}) copy-start(f32[5,5]{1,0:T(8,128)} %span.1) | copy-start | bytes 304
  4.4 12.2 %collective-permute-start.1 = (f32[5,8,1024]{2,1,0:T(8,128)S(1)}, f32[5,8,1024]{2,1,0:T(8,128)S(1)}, u32[]{:S(2)}, u32[]{:S(2)}) collective-permute-start(f32[5,8,1024]{2,1,0:T(8,128)S(1)} %get-tuple-element.35), channel_id=1, source_target_pairs={{0,2},{2,0},{4,6},{6,4},{8,10},{10,8},{12,14},{14,12},{1,3},{3,1},... | collective-permute-start | bytes 491528 | tf_op jit(solution)/shard_map/ppermute | solution.py:328
  6.9 9.7 %collective-permute-start.2 = (f32[5,8,1024]{2,1,0:T(8,128)S(1)}, f32[5,8,1024]{2,1,0:T(8,128)S(1)}, u32[]{:S(2)}, u32[]{:S(2)}) collective-permute-start(f32[5,8,1024]{2,1,0:T(8,128)S(1)} %get-tuple-element.36), channel_id=1, source_target_pairs={{2,4},{4,2},{6,8},{8,6},{10,12},{12,10},{14,0},{0,14},{3,5},{5,3},... | collective-permute-start | bytes 491528 | tf_op jit(solution)/shard_map/ppermute | solution.py:329
  11.6 2.2 %collective-permute-start = (f32[20,1024]{1,0:T(8,128)S(1)}, f32[20,1024]{1,0:T(8,128)S(1)}, u32[]{:S(2)}, u32[]{:S(2)}) collective-permute-start(f32[20,1024]{1,0:T(8,128)S(1)} %get-tuple-element.31), channel_id=1, source_target_pairs={{0,1},{1,0},{2,3},{3,2},{4,5},{5,4},{6,7},{7,6},{8,9},{9,8},{10,11... | collective-permute-start | bytes 245768 | tf_op jit(solution)/shard_map/ppermute | solution.py:330
  17.0 6.2 %collective-permute-start.4 = (f32[5,8,1024]{2,1,0:T(8,128)S(1)}, f32[5,8,1024]{2,1,0:T(8,128)S(1)}, u32[]{:S(2)}, u32[]{:S(2)}) collective-permute-start(f32[5,8,1024]{2,1,0:T(8,128)S(1)} %get-tuple-element.37.edge_a), channel_id=1, source_target_pairs={{0,2},{2,0},{4,6},{6,4},{8,10},{10,8},{12,14},{14,12},{1,3},{3,1},... | collective-permute-start | bytes 491528 | tf_op jit(solution)/shard_map/ppermute | solution.py:328
  17.1 6.7 %collective-permute-start.5 = (f32[5,8,1024]{2,1,0:T(8,128)S(1)}, f32[5,8,1024]{2,1,0:T(8,128)S(1)}, u32[]{:S(2)}, u32[]{:S(2)}) collective-permute-start(f32[5,8,1024]{2,1,0:T(8,128)S(1)} %get-tuple-element.38.edge_b), channel_id=1, source_target_pairs={{2,4},{4,2},{6,8},{8,6},{10,12},{12,10},{14,0},{0,14},{3,5},{5,3},... | collective-permute-start | bytes 491528 | tf_op jit(solution)/shard_map/ppermute | solution.py:329
  18.6 2.7 %collective-permute-start.3 = (f32[20,1024]{1,0:T(8,128)S(1)}, f32[20,1024]{1,0:T(8,128)S(1)}, u32[]{:S(2)}, u32[]{:S(2)}) collective-permute-start(f32[20,1024]{1,0:T(8,128)S(1)} %get-tuple-element.39), channel_id=1, source_target_pairs={{0,1},{1,0},{2,3},{3,2},{4,5},{5,4},{6,7},{7,6},{8,9},{9,8},{10,11... | collective-permute-start | bytes 245768 | tf_op jit(solution)/shard_map/ppermute | solution.py:330
  23.2 19.1 %copy-start.2 = (f32[1,1,5,10,4]{3,4,2,1,0:T(4,128)S(1)}, f32[1,1,5,10,4]{3,4,2,1,0:T(4,128)}, u32[]{:S(2)}) copy-start(f32[1,1,5,10,4]{3,4,2,1,0:T(4,128)} %param.15) | copy-start | bytes 2404
  38.8 3.4 %collective-permute-start.6 = (f32[4,640]{1,0:T(4,128)S(1)}, f32[4,640]{1,0:T(4,128)S(1)}, u32[]{:S(2)}, u32[]{:S(2)}) collective-permute-start(f32[4,640]{1,0:T(4,128)S(1)} %shard_map.87.own), channel_id=1, source_target_pairs={{0,1},{1,0},{2,3},{3,2},{4,5},{5,4},{6,7},{7,6},{8,9},{9,8},{10,11... | collective-permute-start | bytes 30728 | tf_op jit(solution)/shard_map/ppermute | solution.py:379
  53.0 9.0 %collective-permute-start.8 = (f32[5,8,1024]{2,1,0:T(8,128)S(1)}, f32[5,8,1024]{2,1,0:T(8,128)S(1)}, u32[]{:S(2)}, u32[]{:S(2)}) collective-permute-start(f32[5,8,1024]{2,1,0:T(8,128)S(1)} %get-tuple-element.49), channel_id=1, source_target_pairs={{0,2},{2,0},{4,6},{6,4},{8,10},{10,8},{12,14},{14,12},{1,3},{3,1},... | collective-permute-start | bytes 491528 | tf_op jit(solution)/shard_map/ppermute | solution.py:328
  53.2 8.8 %collective-permute-start.9 = (f32[5,8,1024]{2,1,0:T(8,128)S(1)}, f32[5,8,1024]{2,1,0:T(8,128)S(1)}, u32[]{:S(2)}, u32[]{:S(2)}) collective-permute-start(f32[5,8,1024]{2,1,0:T(8,128)S(1)} %get-tuple-element.50), channel_id=1, source_target_pairs={{2,4},{4,2},{6,8},{8,6},{10,12},{12,10},{14,0},{0,14},{3,5},{5,3},... | collective-permute-start | bytes 491528 | tf_op jit(solution)/shard_map/ppermute | solution.py:329
  55.0 3.3 %collective-permute-start.7 = (f32[20,1024]{1,0:T(8,128)S(1)}, f32[20,1024]{1,0:T(8,128)S(1)}, u32[]{:S(2)}, u32[]{:S(2)}) collective-permute-start(f32[20,1024]{1,0:T(8,128)S(1)} %get-tuple-element.46), channel_id=1, source_target_pairs={{0,1},{1,0},{2,3},{3,2},{4,5},{5,4},{6,7},{7,6},{8,9},{9,8},{10,11... | collective-permute-start | bytes 245768 | tf_op jit(solution)/shard_map/ppermute | solution.py:330

commit v3 on v2

--- a/solution.py
+++ b/solution.py
@@ -12,7 +12,6 @@
 VMEM = pl.BlockSpec(memory_space=pltpu.VMEM)
 SMEM = pl.BlockSpec(memory_space=pltpu.SMEM)
 HBM = pl.BlockSpec(memory_space=pltpu.HBM)
-HIGHEST = lax.Precision.HIGHEST
 F32 = jnp.float32
 
 
@@ -75,19 +74,52 @@
         body(pl.ds(pl.multiple_of(q * LANES, LANES), LANES))
 
 
-def first_kernel(wall, span, rhs_in, jinv_in, rhs, jinv, splat, first, edge_a, edge_b, edge_w, sems):
-    copies = [pltpu.make_async_copy(rhs_in, rhs, sems.at[4])]
-    copies += [pltpu.make_async_copy(jinv_in.at[s], jinv.at[s], sems.at[s]) for s in range(4)]
-    for copy in copies:
+def picked_sums(hot, rows):
+    hot = hot.astype(jnp.bfloat16)
+    high = rows.astype(jnp.bfloat16)
+    rest = rows - high.astype(F32)
+    middle = rest.astype(jnp.bfloat16)
+    low = (rest - middle.astype(F32)).astype(jnp.bfloat16)
+    return total([jnp.dot(hot, part, preferred_element_type=F32) for part in (low, middle, high)])
+
+
+def hot_rows(owner, slot, tiles):
+    ids = lax.broadcasted_iota(jnp.int32, (8, LANES), 1)
+    hot = []
+    for s in range(4):
+        named = owner[s] * 4 + slot[s]
+        hot += [jnp.where(named[:, q : q + 1] == ids, 1.0, 0.0) for q in range(tiles)]
+    return jnp.concatenate(hot, axis=0)
+
+
+def first_kernel(
+    wall_in, span_in, owner_in, slot_in, rhs_in, jinv_in, jac_in,
+    rhs, jinv, jac, splat, onehot_t, first, edge_a, edge_b, edge_w,
+    wall, span, owner, slot, small_sems, sems,
+):
+    small = [
+        pltpu.make_async_copy(source, here, small_sems.at[n])
+        for n, (source, here) in enumerate(
+            ((wall_in, wall), (span_in, span), (owner_in, owner), (slot_in, slot), (rhs_in, rhs))
+        )
+    ]
+    slabs = [pltpu.make_async_copy(jinv_in.at[s], jinv.at[s], sems.at[0, s]) for s in range(4)]
+    later = [pltpu.make_async_copy(jac_in.at[s], jac.at[s], sems.at[1, s]) for s in range(4)]
+    for copy in small + slabs + later:
         copy.start()
+    small[0].wait()
+    small[1].wait()
     for which, coupling in enumerate((wall, span)):
         for k in range(5):
             for i in range(5):
                 splat[which, k, i] = jnp.full((8, LANES), coupling[k, i], F32)
-    even, plane_a, plane_b, row = position()
-    copies[0].wait()
+    small[2].wait()
+    small[3].wait()
+    onehot_t[...] = hot_rows(owner, slot, rhs.shape[-1] // LANES).T[: onehot_t.shape[0]]
+    _, plane_a, plane_b, row = position()
+    small[4].wait()
     for s in range(4):
-        copies[1 + s].wait()
+        slabs[s].wait()
 
         def body(lanes, s=s):
             swept = sweep(jinv, s, lanes, [rhs[s, k, :, lanes] for k in range(5)])
@@ -100,6 +132,8 @@
     for k in range(5):
         edge_a[k] = first[plane_a, k]
         edge_b[k] = first[plane_b, k]
+    for copy in later:
+        copy.wait()
 
 
 def local_apply(splat, row, planes, halo_w, jac, lanes, s):
@@ -120,32 +154,18 @@
     ]
 
 
-def hot_rows(owner, slot, tiles):
-    ids = lax.broadcasted_iota(jnp.int32, (8, LANES), 1)
-    hot = []
-    for s in range(4):
-        named = owner[s] * 4 + slot[s]
-        hot += [jnp.where(named[:, q : q + 1] == ids, 1.0, 0.0) for q in range(tiles)]
-    return jnp.concatenate(hot, axis=0)
-
-
-def second_local_kernel(splat, first, halo_w, rhs, jinv, owner, slot, jac_in, inner, jac, onehot_t, sems):
-    copies = [pltpu.make_async_copy(jac_in.at[s], jac.at[s], sems.at[s]) for s in range(4)]
-    for copy in copies:
-        copy.start()
+def second_local_kernel(splat, first, halo_w, rhs, jac, jinv, inner):
     row = position()[3]
-    onehot_t[...] = hot_rows(owner, slot, rhs.shape[-1] // LANES).T[: onehot_t.shape[0]]
-    for s in range(4):
-        copies[s].wait()
-
-        def body(lanes, s=s):
-            planes = [[first[n, k, :, lanes] for k in range(5)] if abs(n - s) < 2 else None for n in range(4)]
+
+    def body(lanes):
+        planes = [[first[n, k, :, lanes] for k in range(5)] for n in range(4)]
+        for s in range(4):
             applied = local_apply(splat, row, planes, halo_w, jac, lanes, s)
             swept = sweep(jinv, s, lanes, [rhs[s, k, :, lanes] - applied[k] for k in range(5)])
             for k in range(5):
                 inner[s, k, :, lanes] = planes[s][k] + swept[k]
 
-        for_lanes(body, rhs.shape[-1])
+    for_lanes(body, rhs.shape[-1])
 
 
 def second_edge_kernel(splat, inner, halo_a, halo_b, jinv, edge_a, edge_b, edge_w):
@@ -197,9 +217,7 @@
         rows = jnp.concatenate(
             [defect[s, k, :, q * LANES : (q + 1) * LANES] for s in range(4) for q in range(tiles)], axis=0
         )
-        partial[:, k * LANES : (k + 1) * LANES] = jnp.dot(
-            onehot_t[...], rows, precision=HIGHEST, preferred_element_type=F32
-        )
+        partial[:, k * LANES : (k + 1) * LANES] = picked_sums(onehot_t[...], rows)
 
 
 def restrict_kernel(splat, inner, base, halo_a, halo_b, onehot_t, jinv, partial, base_out, edges, sems):
@@ -223,13 +241,10 @@
     low, high = onehot_t[:, :width], onehot_t[:, 3 * width :]
     hot = jnp.concatenate([jnp.where(even, high, low), jnp.where(even, low, high)], axis=1)
     slots = partial.shape[1]
-    for k in range(5):
-        rows = jnp.concatenate([part[k] for part in parts], axis=0)
-        sums = inner[:, k * LANES : (k + 1) * LANES] + jnp.dot(
-            hot, rows, precision=HIGHEST, preferred_element_type=F32
-        )
-        for p in range(partial.shape[0]):
-            partial[p, :, k * LANES : (k + 1) * LANES] = sums[p * slots : (p + 1) * slots]
+    rows = jnp.concatenate([jnp.concatenate(part, axis=1) for part in parts], axis=0)
+    sums = inner[...] + picked_sums(hot, rows)
+    for p in range(partial.shape[0]):
+        partial[p] = sums[p * slots : (p + 1) * slots]
     for copy in copies:
         copy.wait()
 
@@ -259,7 +274,7 @@
         fix[p * slots : (p + 1) * slots, :] = fixes[p]
     hot = hot_rows(owner, slot, tiles)[:, : owners * slots]
     for k in range(5):
-        rows = jnp.dot(hot, fix[:, k * LANES : (k + 1) * LANES], precision=HIGHEST, preferred_element_type=F32)
+        rows = picked_sums(hot, fix[:, k * LANES : (k + 1) * LANES])
         for s in range(4):
             for q in range(tiles):
                 at = (s * tiles + q) * 8
@@ -271,20 +286,12 @@
             edge_w[s * 5 + k, :] = out[s, k, row, :]
 
 
-def final_local_kernel(splat, fix, halo_w, base_in, jac_in, jinv_in, out, inner, jinv, base, jac, sems):
+def final_local_kernel(splat, fix, halo_w, jac, jinv, base_in, out, inner, base, sems):
     row = position()[3]
-    loads = []
-    for s in range(4):
-        loads += [
-            pltpu.make_async_copy(source.at[s], here.at[s], sems.at[n, s])
-            for n, (source, here) in enumerate(((jac_in, jac), (jinv_in, jinv), (base_in, base)))
-        ]
-    for load in loads:
-        load.start()
+    load = pltpu.make_async_copy(base_in, base, sems.at[4])
+    load.start()
     stores = []
     for s in range(4):
-        for load in loads[3 * s : 3 * s + 3]:
-            load.wait()
 
         def body(lanes, s=s):
             planes = [[fix[n, k, :, lanes] for k in range(5)] if abs(n - s) < 2 else None for n in range(4)]
@@ -293,9 +300,11 @@
             for k in range(5):
                 inner[s, k, :, lanes] = base[s, k, :, lanes] + (planes[s][k] - swept[k])
 
+        if s == 0:
+            load.wait()
         for_lanes(body, fix.shape[-1])
         if s in (1, 2):
-            stores.append(pltpu.make_async_copy(inner.at[s], out.at[s], sems.at[3, s]))
+            stores.append(pltpu.make_async_copy(inner.at[s], out.at[s], sems.at[s]))
             stores[-1].start()
     for store in stores:
         store.wait()
@@ -333,8 +342,8 @@
 
 def local(rhs, jac, jac_inv, wall_coupling, span_coupling, block_owner, block_slot, coarse_inv):
     rhs = in_hbm(rhs.transpose(0, 2, 1, 3))
-    jac_in = in_hbm(jac.transpose(0, 2, 3, 1, 4))
-    jinv_in = in_hbm(jac_inv.transpose(0, 2, 3, 1, 4))
+    jac_in = jac.transpose(0, 2, 3, 1, 4)
+    jinv_in = jac_inv.transpose(0, 2, 3, 1, 4)
     inv = coarse_inv[0, 0].transpose(0, 2, 1)
     field, plane, edge = shaped(*rhs.shape), shaped(*rhs.shape[1:]), shaped(20, rhs.shape[-1])
     field_out = pltpu.HBM(rhs.shape, F32)
@@ -344,21 +353,25 @@
     aggregates, columns = owners * slots, 5 * LANES
     chunks = shaped(owners, slots, columns)
 
-    rhs, jinv, splat, first, a, b, w = call(
+    rhs, jinv, jac, splat, onehot_t, first, a, b, w = call(
         first_kernel,
-        [field, matrices, shaped(2, 5, 5, 8, LANES), field, plane, plane, edge],
-        [wall_coupling, span_coupling, rhs, jinv_in],
-        places=[SMEM, SMEM, HBM, HBM],
-        scratch=[pltpu.SemaphoreType.DMA((5,))],
+        [
+            field, matrices, matrices, shaped(2, 5, 5, 8, LANES), shaped(aggregates, block_owner.size),
+            field, plane, plane, edge,
+        ],
+        [in_hbm(x) for x in (wall_coupling, span_coupling, block_owner, block_slot, rhs, jinv_in, jac_in)],
+        places=[HBM] * 7,
+        scratch=[
+            pltpu.SMEM(wall_coupling.shape, F32),
+            pltpu.SMEM(span_coupling.shape, F32),
+            pltpu.VMEM(block_owner.shape, jnp.int32),
+            pltpu.VMEM(block_owner.shape, jnp.int32),
+            pltpu.SemaphoreType.DMA((5,)),
+            pltpu.SemaphoreType.DMA((2, 4)),
+        ],
     )
     halo_a, halo_b, halo_w = exchange(a, b, w)
-    inner, jac, onehot_t = call(
-        second_local_kernel,
-        [field, matrices, shaped(aggregates, block_owner.size)],
-        [splat, first, halo_w, rhs, jinv, block_owner, block_slot, jac_in],
-        places=[VMEM] * 7 + [HBM],
-        scratch=[pltpu.SemaphoreType.DMA((4,))],
-    )
+    [inner] = call(second_local_kernel, [field], [splat, first, halo_w, rhs, jac, jinv])
     a, b, w = call(second_edge_kernel, [plane, plane, edge], [splat, inner, halo_a, halo_b, jinv])
     halo_a, halo_b, halo_w = exchange(a, b, w)
     base, partial = call(
@@ -386,18 +399,18 @@
         scratch=[pltpu.VMEM((aggregates, columns), F32)],
     )
     halo_a, halo_b, halo_w = exchange(a, b, w)
-    out, inner, jinv = call(
+    out, inner = call(
         final_local_kernel,
-        [field_out, field, matrices],
-        [splat, fix, halo_w, in_hbm(base), jac_in, jinv_in],
-        places=[VMEM] * 3 + [HBM] * 3,
-        out_places=[HBM, VMEM, VMEM],
-        scratch=[pltpu.VMEM(rhs.shape, F32), pltpu.VMEM(jac_in.shape, F32), pltpu.SemaphoreType.DMA((4, 4))],
+        [field_out, field],
+        [splat, fix, halo_w, jac_in, jinv_in, in_hbm(base)],
+        places=[VMEM] * 5 + [HBM],
+        out_places=[HBM, VMEM],
+        scratch=[pltpu.VMEM(rhs.shape, F32), pltpu.SemaphoreType.DMA((5,))],
     )
     [out] = call(
         final_edge_kernel,
         [field_out],
-        [splat, inner, halo_a, halo_b, jinv, in_hbm(out)],
+        [splat, inner, halo_a, halo_b, jinv_in, in_hbm(out)],
         places=[VMEM] * 5 + [HBM],
         out_places=[HBM],
         scratch=[outer, pltpu.SemaphoreType.DMA((2,))],

time: 63.4 us -> 61.5 us (0.970)
  starting transfers between devices: 18.7 us -> 20.7 us
  Pallas kernels: 15.2 us -> 13.3 us
  local copies, waits for them, and re-layouts: 1.4 us -> 0.03 us
  waiting for transfers between devices: 4.34 us -> 3.68 us
    pallas_call x10, Pallas kernels: 15.2 us -> 13.3 us  [call(): pl.pallas_call(kernel, out_shape=outs, in_specs=places or [VMEM] * len(ar...]
    ppermute x3, starting transfers between devices: 7.88 us -> 9.67 us  [exchange(): lax.ppermute(edge_b, 'span', odd)]
    unnamed x10, local copies, waits for them, and re-layouts: 1.4 us -> 0.03 us
    ppermute x3, waiting for transfers between devices: 0.67 us -> 0.01 us  [exchange(): lax.ppermute(edge_b, 'span', odd)]
  transfers between devices with their start and end apart: 10 -> 10, of which waited for: 5 -> 4; matrix products, arithmetic and copies ran while one was open for 0% -> 0% of each run, Pallas kernels for 13% -> 10%
where the time goes in v3:
time: 61.5 us; the launch traced here: 61.3 us
  blocking collectives  23.5 us (38%)
  starting transfers between devices  20.7 us (34%)
  Pallas kernels  13.3 us (22%)
  waiting for transfers between devices  3.68 us (6%)
    all_to_all x1, blocking collectives, local(): lax.all_to_all(partial, 'patch', split_axis=0, concat_axis=0, tiled=True)  13.7 us
    pallas_call x10, Pallas kernels, call(): pl.pallas_call(kernel, out_shape=outs, in_specs=places or [VMEM] * len(ar...  13.3 us
    all_to_all x1, blocking collectives, local(): lax.all_to_all(reply, 'patch', split_axis=0, concat_axis=0, tiled=True)  9.77 us
    ppermute x3, starting transfers between devices, exchange(): lax.ppermute(edge_b, 'span', odd)  9.67 us
    ppermute x3, starting transfers between devices, exchange(): lax.ppermute(edge_w, 'wall', [(0, 1), (1, 0)])  5.71 us
    ppermute x3, starting transfers between devices, exchange(): lax.ppermute(edge_a, 'span', even)  3.17 us
    ppermute x3, waiting for transfers between devices, exchange(): lax.ppermute(edge_w, 'wall', [(0, 1), (1, 0)])  2.83 us
    ppermute x1, starting transfers between devices, local(): theirs = lax.ppermute(mine, 'wall', [(0, 1), (1, 0)])  2.15 us
  transfers between devices with their start and end apart: 10, of which 4 were waited for; matrix products, arithmetic and copies ran while one was open for 0% of the time, Pallas kernels for 10%

profile of v3, /device:TPU:1, one launch (start us, length us, event | category | flops | bytes accessed | tf_op | source)
XLA Modules:
  0.0 61.3 jit_solution(18086352118843964181)
XLA Ops:
  0.0 3.7 %shard_map.82 = (f32[4,5,8,1024]{3,2,1,0:T(8,128)S(1)}, f32[4,5,5,8,1024]{4,3,2,1,0:T(8,128)S(1)}, f32[4,5,5,8,1024]{4,3,2,1,0:T(8,128)S(1)}, f32[2,5,5,8,128]{4...) custom-call(f32[5,5]{1,0:T(8,128)} %wall_in.1, ...), custom_call_target="tpu_custom_call" | custom-call | flops 7877732 | bytes 7877732 | tf_op jit(solution)/shard_map/pallas_call | solution.py:28
  3.7 2.6 %collective-permute-start.1 = (f32[5,8,1024]{2,1,0:T(8,128)S(1)}, f32[5,8,1024]{2,1,0:T(8,128)S(1)}, u32[]{:S(2)}, u32[]{:S(2)}) collective-permute-start(f32[5,8,1024]{2,1,0:T(8,128)S(1)} %get-tuple-element.33), channel_id=1, source_target_pairs={{0,2},{2,0},{4,6},{6,4},{8,10},{10,8},{12,14},{14,12},{1,3},{3,1},... | collective-permute-start | bytes 491528 | tf_op jit(solution)/shard_map/ppermute | solution.py:337
  6.3 4.7 %collective-permute-start.2 = (f32[5,8,1024]{2,1,0:T(8,128)S(1)}, f32[5,8,1024]{2,1,0:T(8,128)S(1)}, u32[]{:S(2)}, u32[]{:S(2)}) collective-permute-start(f32[5,8,1024]{2,1,0:T(8,128)S(1)} %get-tuple-element.34), channel_id=1, source_target_pairs={{2,4},{4,2},{6,8},{8,6},{10,12},{12,10},{14,0},{0,14},{3,5},{5,3},... | collective-permute-start | bytes 491528 | tf_op jit(solution)/shard_map/ppermute | solution.py:338
  10.9 1.2 %collective-permute-start = (f32[20,1024]{1,0:T(8,128)S(1)}, f32[20,1024]{1,0:T(8,128)S(1)}, u32[]{:S(2)}, u32[]{:S(2)}) collective-permute-start(f32[20,1024]{1,0:T(8,128)S(1)} %get-tuple-element.29), channel_id=1, source_target_pairs={{0,1},{1,0},{2,3},{3,2},{4,5},{5,4},{6,7},{7,6},{8,9},{9,8},{10,11... | collective-permute-start | bytes 245768 | tf_op jit(solution)/shard_map/ppermute | solution.py:339
  12.2 0.9 %collective-permute-done.halo_w = f32[20,1024]{1,0:T(8,128)S(1)} collective-permute-done((f32[20,1024]{1,0:T(8,128)S(1)}, f32[20,1024]{1,0:T(8,128)S(1)}, u32[]{:S(2)}, u32[]{:S(2)}) %collective-permute-start) | collective-permute-done | bytes 81952 | tf_op jit(solution)/shard_map/ppermute | solution.py:339
  13.1 1.5 %shard_map.83.inner = f32[4,5,8,1024]{3,2,1,0:T(8,128)S(1)} custom-call(f32[2,5,5,8,128]{4,3,2,1,0:T(8,128)S(1)} %get-tuple-element.27.splat, f32[4,5,8,1024]{3,2,1,0:T(8,128)S(1)} %get-tuple-element.28.first, f32[20,1024]{1,0:T(8,128)S(1)} %collective-permute-done.halo_w, f32[4,5,8,1024]{3,2,1,0:T(8,128)S(1)} %get-tuple-element.30.rhs, ...), custom_call_target="tpu_custom_call" | custom-call | flops 4403200 | bytes 4403200 | tf_op jit(solution)/shard_map/pallas_call | solution.py:28
  14.6 0.4 shard_map.84
  15.1 2.3 %collective-permute-start.5 = (f32[5,8,1024]{2,1,0:T(8,128)S(1)}, f32[5,8,1024]{2,1,0:T(8,128)S(1)}, u32[]{:S(2)}, u32[]{:S(2)}) collective-permute-start(f32[5,8,1024]{2,1,0:T(8,128)S(1)} %get-tuple-element.36.edge_b), channel_id=1, source_target_pairs={{2,4},{4,2},{6,8},{8,6},{10,12},{12,10},{14,0},{0,14},{3,5},{5,3},... | collective-permute-start | bytes 491528 | tf_op jit(solution)/shard_map/ppermute | solution.py:338
  17.5 2.1 %collective-permute-start.3 = (f32[20,1024]{1,0:T(8,128)S(1)}, f32[20,1024]{1,0:T(8,128)S(1)}, u32[]{:S(2)}, u32[]{:S(2)}) collective-permute-start(f32[20,1024]{1,0:T(8,128)S(1)} %get-tuple-element.37), channel_id=1, source_target_pairs={{0,1},{1,0},{2,3},{3,2},{4,5},{5,4},{6,7},{7,6},{8,9},{9,8},{10,11... | collective-permute-start | bytes 245768 | tf_op jit(solution)/shard_map/ppermute | solution.py:339
  19.6 0.9 %collective-permute-done.3.halo_w = f32[20,1024]{1,0:T(8,128)S(1)} collective-permute-done((f32[20,1024]{1,0:T(8,128)S(1)}, f32[20,1024]{1,0:T(8,128)S(1)}, u32[]{:S(2)}, u32[]{:S(2)}) %collective-permute-start.3) | collective-permute-done | bytes 81952 | tf_op jit(solution)/shard_map/ppermute | solution.py:339
  20.6 1.8 %shard_map.85 = (f32[4,5,8,1024]{3,2,1,0:T(8,128)S(1)}, f32[64,640]{1,0:T(8,128)S(1)}) custom-call(f32[2,5,5,8,128]{4,3,2,1,0:T(8,128)S(1)} %get-tuple-element.27.splat, f32[4,5,8,1024]{3,2,1,0:T(8,128)S(1)} %shard_map.83.inner, f32[5,8,1024]{2,1,0:T(8,128)S(1)} %get-tuple-element.35.edge_a, f32[5,8,1024]{2,1,0:T(8,128)S(1)} %get-tuple-element.36.edge_b, ...), custom_call_target="tpu_custom_call" | custom-call | flops 4681728 | bytes 4681728 | tf_op jit(solution)/shard_map/pallas_call | solution.py:28
  22.4 1.1 %shard_map.86 = (f32[16,4,640]{2,1,0:T(4,128)S(1)}, f32[4,5,8,1024]{3,2,1,0:T(8,128)}) custom-call(f32[2,5,5,8,128]{4,3,2,1,0:T(8,128)S(1)} %get-tuple-element.27.splat, f32[64,640]{1,0:T(8,128)S(1)} %get-tuple-element.39.inner, f32[4,5,8,1024]{3,2,1,0:T(8,128)S(1)} %get-tuple-element.40.base, f32[5,8,1024]{2,1,0:T(8,128)S(1)} %collective-permute-done.4.halo_a, ...), custom_call_target="tpu_custom_call" | custom-call | flops 2756608 | bytes 2756608 | tf_op jit(solution)/shard_map/pallas_call | solution.py:28
  23.5 13.7 %all_to_all.10.received = f32[16,4,640]{2,1,0:T(4,128)S(1)} all-to-all(f32[16,4,640]{2,1,0:T(4,128)S(1)} %get-tuple-element.41), channel_id=1, replica_groups=mesh['patch'=16,'span'=8,'wall'=2] {'patch'}, dimensions={0} | all-to-all | bytes 327680 | tf_op jit(solution)/shard_map/all_to_all | solution.py:390
  37.3 2.1 %collective-permute-start.6 = (f32[4,640]{1,0:T(4,128)S(1)}, f32[4,640]{1,0:T(4,128)S(1)}, u32[]{:S(2)}, u32[]{:S(2)}) collective-permute-start(f32[4,640]{1,0:T(4,128)S(1)} %shard_map.87.own), channel_id=1, source_target_pairs={{0,1},{1,0},{2,3},{3,2},{4,5},{5,4},{6,7},{7,6},{8,9},{9,8},{10,11... | collective-permute-start | bytes 30728 | tf_op jit(solution)/shard_map/ppermute | solution.py:392
  39.4 0.8 %collective-permute-done.6.other = f32[4,640]{1,0:T(4,128)S(1)} collective-permute-done((f32[4,640]{1,0:T(4,128)S(1)}, f32[4,640]{1,0:T(4,128)S(1)}, u32[]{:S(2)}, u32[]{:S(2)}) %collective-permute-start.6) | collective-permute-done | bytes 10272 | tf_op jit(solution)/shard_map/ppermute | solution.py:392
  40.2 0.2 shard_map.88
  40.4 9.8 %all_to_all.11.fixes = f32[16,4,640]{2,1,0:T(4,128)S(1)} all-to-all(f32[16,4,640]{2,1,0:T(4,128)S(1)} %shard_map.88), channel_id=1, replica_groups=mesh['patch'=16,'span'=8,'wall'=2] {'patch'}, dimensions={0} | all-to-all | bytes 327680 | tf_op jit(solution)/shard_map/all_to_all | solution.py:394
  50.2 0.5 shard_map.89
  50.7 0.5 collective-permute-start.8
  51.2 2.7 %collective-permute-start.9 = (f32[5,8,1024]{2,1,0:T(8,128)S(1)}, f32[5,8,1024]{2,1,0:T(8,128)S(1)}, u32[]{:S(2)}, u32[]{:S(2)}) collective-permute-start(f32[5,8,1024]{2,1,0:T(8,128)S(1)} %get-tuple-element.47), channel_id=1, source_target_pairs={{2,4},{4,2},{6,8},{8,6},{10,12},{12,10},{14,0},{0,14},{3,5},{5,3},... | collective-permute-start | bytes 491528 | tf_op jit(solution)/shard_map/ppermute | solution.py:338
  53.9 2.3 %collective-permute-start.7 = (f32[20,1024]{1,0:T(8,128)S(1)}, f32[20,1024]{1,0:T(8,128)S(1)}, u32[]{:S(2)}, u32[]{:S(2)}) collective-permute-start(f32[20,1024]{1,0:T(8,128)S(1)} %get-tuple-element.43), channel_id=1, source_target_pairs={{0,1},{1,0},{2,3},{3,2},{4,5},{5,4},{6,7},{7,6},{8,9},{9,8},{10,11... | collective-permute-start | bytes 245768 | tf_op jit(solution)/shard_map/ppermute | solution.py:339
  56.2 0.9 %collective-permute-done.7.halo_w = f32[20,1024]{1,0:T(8,128)S(1)} collective-permute-done((f32[20,1024]{1,0:T(8,128)S(1)}, f32[20,1024]{1,0:T(8,128)S(1)}, u32[]{:S(2)}, u32[]{:S(2)}) %collective-permute-start.7) | collective-permute-done | bytes 81952 | tf_op jit(solution)/shard_map/ppermute | solution.py:339
  57.2 3.0 %shard_map.90 = (f32[4,5,8,1024]{3,2,1,0:T(8,128)}, f32[4,5,8,1024]{3,2,1,0:T(8,128)S(1)}) custom-call(f32[2,5,5,8,128]{4,3,2,1,0:T(8,128)S(1)} %get-tuple-element.27.splat, f32[4,5,8,1024]{3,2,1,0:T(8,128)S(1)} %get-tuple-element.42.fix, f32[20,1024]{1,0:T(8,128)S(1)} %collective-permute-done.7.halo_w, f32[4,5,5,8,1024]{4,3,2,1,0:T(8,128)S(1)} %bitcast.11, ...), custom_call_target="tpu_custom_call" | custom-call | flops 4730880 | bytes 4730880 | tf_op jit(solution)/shard_map/pallas_call | solution.py:28
  60.2 1.1 %shard_map.91 = f32[4,5,8,1024]{3,2,1,0:T(8,128)} custom-call(f32[2,5,5,8,128]{4,3,2,1,0:T(8,128)S(1)} %get-tuple-element.27.splat, f32[4,5,8,1024]{3,2,1,0:T(8,128)S(1)} %get-tuple-element.45.inner, f32[5,8,1024]{2,1,0:T(8,128)S(1)} %collective-permute-done.8.halo_a, ...), custom_call_target="tpu_custom_call", output_to_operand_aliasing={{}: (5, {})} | custom-call | flops 2887680 | bytes 2887680 | tf_op jit(solution)/shard_map/pallas_call | solution.py:28
  (18 shorter events, 0.2 us)
Async XLA Ops:
  3.7 10.9 %collective-permute-start.1 = (f32[5,8,1024]{2,1,0:T(8,128)S(1)}, f32[5,8,1024]{2,1,0:T(8,128)S(1)}, u32[]{:S(2)}, u32[]{:S(2)}) collective-permute-start(f32[5,8,1024]{2,1,0:T(8,128)S(1)} %get-tuple-element.33), channel_id=1, source_target_pairs={{0,2},{2,0},{4,6},{6,4},{8,10},{10,8},{12,14},{14,12},{1,3},{3,1},... | collective-permute-start | bytes 491528 | tf_op jit(solution)/shard_map/ppermute | solution.py:337
  6.3 8.4 %collective-permute-start.2 = (f32[5,8,1024]{2,1,0:T(8,128)S(1)}, f32[5,8,1024]{2,1,0:T(8,128)S(1)}, u32[]{:S(2)}, u32[]{:S(2)}) collective-permute-start(f32[5,8,1024]{2,1,0:T(8,128)S(1)} %get-tuple-element.34), channel_id=1, source_target_pairs={{2,4},{4,2},{6,8},{8,6},{10,12},{12,10},{14,0},{0,14},{3,5},{5,3},... | collective-permute-start | bytes 491528 | tf_op jit(solution)/shard_map/ppermute | solution.py:338
  10.9 2.2 %collective-permute-start = (f32[20,1024]{1,0:T(8,128)S(1)}, f32[20,1024]{1,0:T(8,128)S(1)}, u32[]{:S(2)}, u32[]{:S(2)}) collective-permute-start(f32[20,1024]{1,0:T(8,128)S(1)} %get-tuple-element.29), channel_id=1, source_target_pairs={{0,1},{1,0},{2,3},{3,2},{4,5},{5,4},{6,7},{7,6},{8,9},{9,8},{10,11... | collective-permute-start | bytes 245768 | tf_op jit(solution)/shard_map/ppermute | solution.py:339
  15.0 7.4 %collective-permute-start.4 = (f32[5,8,1024]{2,1,0:T(8,128)S(1)}, f32[5,8,1024]{2,1,0:T(8,128)S(1)}, u32[]{:S(2)}, u32[]{:S(2)}) collective-permute-start(f32[5,8,1024]{2,1,0:T(8,128)S(1)} %get-tuple-element.35.edge_a), channel_id=1, source_target_pairs={{0,2},{2,0},{4,6},{6,4},{8,10},{10,8},{12,14},{14,12},{1,3},{3,1},... | collective-permute-start | bytes 491528 | tf_op jit(solution)/shard_map/ppermute | solution.py:337
  15.1 7.3 %collective-permute-start.5 = (f32[5,8,1024]{2,1,0:T(8,128)S(1)}, f32[5,8,1024]{2,1,0:T(8,128)S(1)}, u32[]{:S(2)}, u32[]{:S(2)}) collective-permute-start(f32[5,8,1024]{2,1,0:T(8,128)S(1)} %get-tuple-element.36.edge_b), channel_id=1, source_target_pairs={{2,4},{4,2},{6,8},{8,6},{10,12},{12,10},{14,0},{0,14},{3,5},{5,3},... | collective-permute-start | bytes 491528 | tf_op jit(solution)/shard_map/ppermute | solution.py:338
  17.5 3.1 %collective-permute-start.3 = (f32[20,1024]{1,0:T(8,128)S(1)}, f32[20,1024]{1,0:T(8,128)S(1)}, u32[]{:S(2)}, u32[]{:S(2)}) collective-permute-start(f32[20,1024]{1,0:T(8,128)S(1)} %get-tuple-element.37), channel_id=1, source_target_pairs={{0,1},{1,0},{2,3},{3,2},{4,5},{5,4},{6,7},{7,6},{8,9},{9,8},{10,11... | collective-permute-start | bytes 245768 | tf_op jit(solution)/shard_map/ppermute | solution.py:339
  20.6 36.6 %copy-start.1 = (f32[4,8,5,5,1024]{4,1,3,2,0:T(8,128)S(1)}, f32[4,8,5,5,1024]{4,1,3,2,0:T(8,128)}, u32[]{:S(2)}) copy-start(f32[4,8,5,5,1024]{4,1,3,2,0:T(8,128)} %param.9) | copy-start | bytes 9830404
  22.4 17.9 %copy-start.4 = (f32[1,1,5,10,4]{3,4,2,1,0:T(4,128)S(1)}, f32[1,1,5,10,4]{3,4,2,1,0:T(4,128)}, u32[]{:S(2)}) copy-start(f32[1,1,5,10,4]{3,4,2,1,0:T(4,128)} %param.15) | copy-start | bytes 2404
  22.4 27.8 %copy-start.2 = (s32[4,8,8]{2,1,0:T(8,128)S(1)}, s32[4,8,8]{2,1,0:T(8,128)}, u32[]{:S(2)}) copy-start(s32[4,8,8]{2,1,0:T(8,128)} %owner.1) | copy-start | bytes 3076
  22.4 27.8 %copy-start.3 = (s32[4,8,8]{2,1,0:T(8,128)S(1)}, s32[4,8,8]{2,1,0:T(8,128)}, u32[]{:S(2)}) copy-start(s32[4,8,8]{2,1,0:T(8,128)} %slot.1) | copy-start | bytes 3076
  22.4 34.8 %copy-start = (f32[4,8,5,5,1024]{4,1,3,2,0:T(8,128)S(1)}, f32[4,8,5,5,1024]{4,1,3,2,0:T(8,128)}, u32[]{:S(2)}) copy-start(f32[4,8,5,5,1024]{4,1,3,2,0:T(8,128)} %param.10) | copy-start | bytes 9830404
  37.3 3.0 %collective-permute-start.6 = (f32[4,640]{1,0:T(4,128)S(1)}, f32[4,640]{1,0:T(4,128)S(1)}, u32[]{:S(2)}, u32[]{:S(2)}) collective-permute-start(f32[4,640]{1,0:T(4,128)S(1)} %shard_map.87.own), channel_id=1, source_target_pairs={{0,1},{1,0},{2,3},{3,2},{4,5},{5,4},{6,7},{7,6},{8,9},{9,8},{10,11... | collective-permute-start | bytes 30728 | tf_op jit(solution)/shard_map/ppermute | solution.py:392
  50.7 9.5 %collective-permute-start.8 = (f32[5,8,1024]{2,1,0:T(8,128)S(1)}, f32[5,8,1024]{2,1,0:T(8,128)S(1)}, u32[]{:S(2)}, u32[]{:S(2)}) collective-permute-start(f32[5,8,1024]{2,1,0:T(8,128)S(1)} %get-tuple-element.46), channel_id=1, source_target_pairs={{0,2},{2,0},{4,6},{6,4},{8,10},{10,8},{12,14},{14,12},{1,3},{3,1},... | collective-permute-start | bytes 491528 | tf_op jit(solution)/shard_map/ppermute | solution.py:337
  51.2 9.0 %collective-permute-start.9 = (f32[5,8,1024]{2,1,0:T(8,128)S(1)}, f32[5,8,1024]{2,1,0:T(8,128)S(1)}, u32[]{:S(2)}, u32[]{:S(2)}) collective-permute-start(f32[5,8,1024]{2,1,0:T(8,128)S(1)} %get-tuple-element.47), channel_id=1, source_target_pairs={{2,4},{4,2},{6,8},{8,6},{10,12},{12,10},{14,0},{0,14},{3,5},{5,3},... | collective-permute-start | bytes 491528 | tf_op jit(solution)/shard_map/ppermute | solution.py:338
  53.9 3.3 %collective-permute-start.7 = (f32[20,1024]{1,0:T(8,128)S(1)}, f32[20,1024]{1,0:T(8,128)S(1)}, u32[]{:S(2)}, u32[]{:S(2)}) collective-permute-start(f32[20,1024]{1,0:T(8,128)S(1)} %get-tuple-element.43), channel_id=1, source_target_pairs={{0,1},{1,0},{2,3},{3,2},{4,5},{5,4},{6,7},{7,6},{8,9},{9,8},{10,11... | collective-permute-start | bytes 245768 | tf_op jit(solution)/shard_map/ppermute | solution.py:339

commit v4 on v3

--- a/solution.py
+++ b/solution.py
@@ -93,8 +93,8 @@
 
 
 def first_kernel(
-    wall_in, span_in, owner_in, slot_in, rhs_in, jinv_in, jac_in,
-    rhs, jinv, jac, splat, onehot_t, first, edge_a, edge_b, edge_w,
+    wall_in, span_in, owner_in, slot_in, rhs_in, jinv_in,
+    rhs, jinv, splat, onehot_t, first, edge_a, edge_b, edge_w,
     wall, span, owner, slot, small_sems, sems,
 ):
     small = [
@@ -103,9 +103,8 @@
             ((wall_in, wall), (span_in, span), (owner_in, owner), (slot_in, slot), (rhs_in, rhs))
         )
     ]
-    slabs = [pltpu.make_async_copy(jinv_in.at[s], jinv.at[s], sems.at[0, s]) for s in range(4)]
-    later = [pltpu.make_async_copy(jac_in.at[s], jac.at[s], sems.at[1, s]) for s in range(4)]
-    for copy in small + slabs + later:
+    slabs = [pltpu.make_async_copy(jinv_in.at[s], jinv.at[s], sems.at[s]) for s in range(4)]
+    for copy in small + slabs:
         copy.start()
     small[0].wait()
     small[1].wait()
@@ -132,8 +131,6 @@
     for k in range(5):
         edge_a[k] = first[plane_a, k]
         edge_b[k] = first[plane_b, k]
-    for copy in later:
-        copy.wait()
 
 
 def local_apply(splat, row, planes, halo_w, jac, lanes, s):
@@ -168,7 +165,7 @@
     for_lanes(body, rhs.shape[-1])
 
 
-def second_edge_kernel(splat, inner, halo_a, halo_b, jinv, edge_a, edge_b, edge_w):
+def second_edge_kernel(splat, inner, halo_b, halo_a, jinv, edge_a, edge_b, edge_w):
     even, plane_a, plane_b, row = position()
     real = inside()
 
@@ -198,7 +195,7 @@
     ]
 
 
-def defect_local_kernel(splat, inner, edge_a, edge_b, halo_w, rhs, jac, jinv, onehot_t, base, partial, defect):
+def defect_local_kernel(splat, inner, edge_b, edge_a, halo_w, rhs, jac, jinv, onehot_t, base, partial, defect):
     even, _, _, row = position()
 
     def body(lanes):
@@ -220,7 +217,7 @@
         partial[:, k * LANES : (k + 1) * LANES] = picked_sums(onehot_t[...], rows)
 
 
-def restrict_kernel(splat, inner, base, halo_a, halo_b, onehot_t, jinv, partial, base_out, edges, sems):
+def restrict_kernel(splat, inner, base, halo_b, halo_a, onehot_t, jinv, partial, base_out, edges, sems):
     even, plane_a, plane_b, _ = position()
     real = inside()
     copies = [pltpu.make_async_copy(base.at[pl.ds(1, 2)], base_out.at[pl.ds(1, 2)], sems.at[2])]
@@ -288,21 +285,24 @@
 
 def final_local_kernel(splat, fix, halo_w, jac, jinv, base_in, out, inner, base, sems):
     row = position()[3]
-    load = pltpu.make_async_copy(base_in, base, sems.at[4])
+    load = pltpu.make_async_copy(base_in, base, sems.at[0])
     load.start()
     stores = []
-    for s in range(4):
+    for s in (1, 2, 0, 3):
 
         def body(lanes, s=s):
             planes = [[fix[n, k, :, lanes] for k in range(5)] if abs(n - s) < 2 else None for n in range(4)]
             applied = local_apply(splat, row, planes, halo_w, jac, lanes, s)
             swept = sweep(jinv, s, lanes, applied)
             for k in range(5):
-                inner[s, k, :, lanes] = base[s, k, :, lanes] + (planes[s][k] - swept[k])
-
-        if s == 0:
+                change = planes[s][k] - swept[k]
+                inner[s, k, :, lanes] = change if s == 1 else base[s, k, :, lanes] + change
+
+        for_lanes(body, fix.shape[-1])
+        if s == 1:
             load.wait()
-        for_lanes(body, fix.shape[-1])
+            for k in range(5):
+                inner[1, k] += base[1, k]
         if s in (1, 2):
             stores.append(pltpu.make_async_copy(inner.at[s], out.at[s], sems.at[s]))
             stores[-1].start()
@@ -310,7 +310,7 @@
         store.wait()
 
 
-def final_edge_kernel(splat, inner, halo_a, halo_b, jinv, out_in, out, edges, sems):
+def final_edge_kernel(splat, inner, halo_b, halo_a, jinv, out_in, out, edges, sems):
     del out_in
     _, plane_a, plane_b, _ = position()
     real = inside()
@@ -333,11 +333,10 @@
     size = lax.axis_size("span")
     even = [p for i in range(0, size, 2) for p in ((i, i + 1), (i + 1, i))]
     odd = [((i + 1) % size, (j + 1) % size) for i, j in even]
-    return (
-        lax.ppermute(edge_a, "span", even),
-        lax.ppermute(edge_b, "span", odd),
-        lax.ppermute(edge_w, "wall", [(0, 1), (1, 0)]),
-    )
+    halo_b = lax.ppermute(edge_b, "span", odd)
+    halo_w = lax.ppermute(edge_w, "wall", [(0, 1), (1, 0)])
+    halo_a = lax.ppermute(edge_a, "span", even)
+    return halo_a, halo_b, halo_w
 
 
 def local(rhs, jac, jac_inv, wall_coupling, span_coupling, block_owner, block_slot, coarse_inv):
@@ -353,37 +352,37 @@
     aggregates, columns = owners * slots, 5 * LANES
     chunks = shaped(owners, slots, columns)
 
-    rhs, jinv, jac, splat, onehot_t, first, a, b, w = call(
+    rhs, jinv, splat, onehot_t, first, a, b, w = call(
         first_kernel,
         [
-            field, matrices, matrices, shaped(2, 5, 5, 8, LANES), shaped(aggregates, block_owner.size),
+            field, matrices, shaped(2, 5, 5, 8, LANES), shaped(aggregates, block_owner.size),
             field, plane, plane, edge,
         ],
-        [in_hbm(x) for x in (wall_coupling, span_coupling, block_owner, block_slot, rhs, jinv_in, jac_in)],
-        places=[HBM] * 7,
+        [in_hbm(x) for x in (wall_coupling, span_coupling, block_owner, block_slot, rhs, jinv_in)],
+        places=[HBM] * 6,
         scratch=[
             pltpu.SMEM(wall_coupling.shape, F32),
             pltpu.SMEM(span_coupling.shape, F32),
             pltpu.VMEM(block_owner.shape, jnp.int32),
             pltpu.VMEM(block_owner.shape, jnp.int32),
             pltpu.SemaphoreType.DMA((5,)),
-            pltpu.SemaphoreType.DMA((2, 4)),
+            pltpu.SemaphoreType.DMA((4,)),
         ],
     )
     halo_a, halo_b, halo_w = exchange(a, b, w)
-    [inner] = call(second_local_kernel, [field], [splat, first, halo_w, rhs, jac, jinv])
-    a, b, w = call(second_edge_kernel, [plane, plane, edge], [splat, inner, halo_a, halo_b, jinv])
+    [inner] = call(second_local_kernel, [field], [splat, first, halo_w, rhs, jac_in, jinv])
+    a, b, w = call(second_edge_kernel, [plane, plane, edge], [splat, inner, halo_b, halo_a, jinv])
     halo_a, halo_b, halo_w = exchange(a, b, w)
     base, partial = call(
         defect_local_kernel,
         [field, shaped(aggregates, columns)],
-        [splat, inner, a, b, halo_w, rhs, jac, jinv, onehot_t],
+        [splat, inner, b, a, halo_w, rhs, jac_in, jinv, onehot_t],
         scratch=[pltpu.VMEM(rhs.shape, F32)],
     )
     partial, base = call(
         restrict_kernel,
         [chunks, field_out],
-        [splat, partial, base, halo_a, halo_b, onehot_t, jinv],
+        [splat, partial, base, halo_b, halo_a, onehot_t, jinv],
         out_places=[VMEM, HBM],
         scratch=[outer, pltpu.SemaphoreType.DMA((3,))],
     )
@@ -405,12 +404,12 @@
         [splat, fix, halo_w, jac_in, jinv_in, in_hbm(base)],
         places=[VMEM] * 5 + [HBM],
         out_places=[HBM, VMEM],
-        scratch=[pltpu.VMEM(rhs.shape, F32), pltpu.SemaphoreType.DMA((5,))],
+        scratch=[pltpu.VMEM(rhs.shape, F32), pltpu.SemaphoreType.DMA((3,))],
     )
     [out] = call(
         final_edge_kernel,
         [field_out],
-        [splat, inner, halo_a, halo_b, jinv_in, in_hbm(out)],
+        [splat, inner, halo_b, halo_a, jinv_in, in_hbm(out)],
         places=[VMEM] * 5 + [HBM],
         out_places=[HBM],
         scratch=[outer, pltpu.SemaphoreType.DMA((2,))],

time: 61.5 us -> 59 us (0.959)
  starting transfers between devices: 20.7 us -> 18.3 us
  Pallas kernels: 13.3 us -> 11.7 us
  waiting for transfers between devices: 3.68 us -> 5.02 us
    ppermute x9, starting transfers between devices: 18.6 us -> 14.5 us  [the longest x3 9.66 us: exchange(): halo_b = lax.ppermute(edge_b, 'span', odd)]
    ppermute x1, starting transfers between devices: 2.15 us -> 3.84 us  [local(): theirs = lax.ppermute(mine, 'wall', [(0, 1), (1, 0)])]
    pallas_call x10, Pallas kernels: 13.3 us -> 11.7 us  [call(): pl.pallas_call(kernel, out_shape=outs, in_specs=places or [VMEM] * len(ar...]
    ppermute x9, waiting for transfers between devices: 2.85 us -> 4.19 us  [the longest x3 2.83 us: exchange(): halo_w = lax.ppermute(edge_w, 'wall', [(0, 1), (1, 0)])]
  transfers between devices with their start and end apart: 10 -> 10, of which waited for: 4 -> 6; matrix products, arithmetic and copies ran while one was open for 0% -> 0% of each run, Pallas kernels for 10% -> 10%
where the time goes in v4:
time: 59 us; the launch traced here: 58.8 us
  blocking collectives  23.5 us (40%)
  starting transfers between devices  18.3 us (31%)
  Pallas kernels  11.7 us (20%)
  waiting for transfers between devices  5.02 us (9%)
    all_to_all x1, blocking collectives, local(): lax.all_to_all(partial, 'patch', split_axis=0, concat_axis=0, tiled=True)  13.8 us
    pallas_call x10, Pallas kernels, call(): pl.pallas_call(kernel, out_shape=outs, in_specs=places or [VMEM] * len(ar...  11.7 us
    all_to_all x1, blocking collectives, local(): lax.all_to_all(reply, 'patch', split_axis=0, concat_axis=0, tiled=True)  9.77 us
    ppermute x3, starting transfers between devices, exchange(): halo_b = lax.ppermute(edge_b, 'span', odd)  9.66 us
    ppermute x3, starting transfers between devices, exchange(): halo_w = lax.ppermute(edge_w, 'wall', [(0, 1), (1, 0)])  4.84 us
    ppermute x1, starting transfers between devices, local(): theirs = lax.ppermute(mine, 'wall', [(0, 1), (1, 0)])  3.84 us
    ppermute x3, waiting for transfers between devices, exchange(): halo_w = lax.ppermute(edge_w, 'wall', [(0, 1), (1, 0)])  2.83 us
  transfers between devices with their start and end apart: 10, of which 6 were waited for; matrix products, arithmetic and copies ran while one was open for 0% of the time, Pallas kernels for 10%

profile of v4, /device:TPU:1, one launch (start us, length us, event | category | flops | bytes accessed | tf_op | source)
XLA Modules:
  0.0 58.8 jit_solution(8914501809056499307)
XLA Ops:
  0.0 2.9 %shard_map.82 = (f32[4,5,8,1024]{3,2,1,0:T(8,128)S(1)}, f32[4,5,5,8,1024]{4,3,2,1,0:T(8,128)S(1)}, f32[2,5,5,8,128]{4,3,2,1,0:T(8,128)S(1)}, f32[64,256]{1,0:T(8...) custom-call(f32[5,5]{1,0:T(8,128)} %wall_in.1, ...), custom_call_target="tpu_custom_call" | custom-call | flops 4600932 | bytes 4600932 | tf_op jit(solution)/shard_map/pallas_call | solution.py:28
  2.9 6.5 %collective-permute-start.1 = (f32[5,8,1024]{2,1,0:T(8,128)S(1)}, f32[5,8,1024]{2,1,0:T(8,128)S(1)}, u32[]{:S(2)}, u32[]{:S(2)}) collective-permute-start(f32[5,8,1024]{2,1,0:T(8,128)S(1)} %get-tuple-element.31), channel_id=1, source_target_pairs={{2,4},{4,2},{6,8},{8,6},{10,12},{12,10},{14,0},{0,14},{3,5},{5,3},... | collective-permute-start | bytes 491528 | tf_op jit(solution)/shard_map/ppermute | solution.py:336
  9.4 1.0 %collective-permute-start = (f32[20,1024]{1,0:T(8,128)S(1)}, f32[20,1024]{1,0:T(8,128)S(1)}, u32[]{:S(2)}, u32[]{:S(2)}) collective-permute-start(f32[20,1024]{1,0:T(8,128)S(1)} %get-tuple-element.28), channel_id=1, source_target_pairs={{0,1},{1,0},{2,3},{3,2},{4,5},{5,4},{6,7},{7,6},{8,9},{9,8},{10,11... | collective-permute-start | bytes 245768 | tf_op jit(solution)/shard_map/ppermute | solution.py:337
  10.3 0.9 %collective-permute-done.halo_w = f32[20,1024]{1,0:T(8,128)S(1)} collective-permute-done((f32[20,1024]{1,0:T(8,128)S(1)}, f32[20,1024]{1,0:T(8,128)S(1)}, u32[]{:S(2)}, u32[]{:S(2)}) %collective-permute-start) | collective-permute-done | bytes 81952 | tf_op jit(solution)/shard_map/ppermute | solution.py:337
  11.3 1.5 %shard_map.83.inner = f32[4,5,8,1024]{3,2,1,0:T(8,128)S(1)} custom-call(f32[2,5,5,8,128]{4,3,2,1,0:T(8,128)S(1)} %get-tuple-element.26.splat, f32[4,5,8,1024]{3,2,1,0:T(8,128)S(1)} %get-tuple-element.27.first, f32[20,1024]{1,0:T(8,128)S(1)} %collective-permute-done.halo_w, f32[4,5,8,1024]{3,2,1,0:T(8,128)S(1)} %get-tuple-element.29.rhs, ...), custom_call_target="tpu_custom_call" | custom-call | flops 4403200 | bytes 4403200 | tf_op jit(solution)/shard_map/pallas_call | solution.py:28
  12.8 0.5 collective-permute-done.1.halo_b
  13.3 0.8 %collective-permute-done.2.halo_a = f32[5,8,1024]{2,1,0:T(8,128)S(1)} collective-permute-done((f32[5,8,1024]{2,1,0:T(8,128)S(1)}, f32[5,8,1024]{2,1,0:T(8,128)S(1)}, u32[]{:S(2)}, u32[]{:S(2)}) %collective-permute-start.2) | collective-permute-done | bytes 163872 | tf_op jit(solution)/shard_map/ppermute | solution.py:338
  14.1 0.4 shard_map.84
  14.5 1.6 %collective-permute-start.4 = (f32[5,8,1024]{2,1,0:T(8,128)S(1)}, f32[5,8,1024]{2,1,0:T(8,128)S(1)}, u32[]{:S(2)}, u32[]{:S(2)}) collective-permute-start(f32[5,8,1024]{2,1,0:T(8,128)S(1)} %get-tuple-element.33.edge_b), channel_id=1, source_target_pairs={{2,4},{4,2},{6,8},{8,6},{10,12},{12,10},{14,0},{0,14},{3,5},{5,3},... | collective-permute-start | bytes 491528 | tf_op jit(solution)/shard_map/ppermute | solution.py:336
  16.1 1.8 %collective-permute-start.3 = (f32[20,1024]{1,0:T(8,128)S(1)}, f32[20,1024]{1,0:T(8,128)S(1)}, u32[]{:S(2)}, u32[]{:S(2)}) collective-permute-start(f32[20,1024]{1,0:T(8,128)S(1)} %get-tuple-element.35), channel_id=1, source_target_pairs={{0,1},{1,0},{2,3},{3,2},{4,5},{5,4},{6,7},{7,6},{8,9},{9,8},{10,11... | collective-permute-start | bytes 245768 | tf_op jit(solution)/shard_map/ppermute | solution.py:337
  17.9 0.9 %collective-permute-done.3.halo_w = f32[20,1024]{1,0:T(8,128)S(1)} collective-permute-done((f32[20,1024]{1,0:T(8,128)S(1)}, f32[20,1024]{1,0:T(8,128)S(1)}, u32[]{:S(2)}, u32[]{:S(2)}) %collective-permute-start.3) | collective-permute-done | bytes 81952 | tf_op jit(solution)/shard_map/ppermute | solution.py:337
  18.9 1.8 %shard_map.85 = (f32[4,5,8,1024]{3,2,1,0:T(8,128)S(1)}, f32[64,640]{1,0:T(8,128)S(1)}) custom-call(f32[2,5,5,8,128]{4,3,2,1,0:T(8,128)S(1)} %get-tuple-element.26.splat, f32[4,5,8,1024]{3,2,1,0:T(8,128)S(1)} %shard_map.83.inner, f32[5,8,1024]{2,1,0:T(8,128)S(1)} %get-tuple-element.33.edge_b, f32[5,8,1024]{2,1,0:T(8,128)S(1)} %get-tuple-element.34.edge_a, ...), custom_call_target="tpu_custom_call" | custom-call | flops 4681728 | bytes 4681728 | tf_op jit(solution)/shard_map/pallas_call | solution.py:28
  20.7 1.1 %shard_map.86 = (f32[16,4,640]{2,1,0:T(4,128)S(1)}, f32[4,5,8,1024]{3,2,1,0:T(8,128)}) custom-call(f32[2,5,5,8,128]{4,3,2,1,0:T(8,128)S(1)} %get-tuple-element.26.splat, f32[64,640]{1,0:T(8,128)S(1)} %get-tuple-element.37.inner, f32[4,5,8,1024]{3,2,1,0:T(8,128)S(1)} %get-tuple-element.38.base, f32[5,8,1024]{2,1,0:T(8,128)S(1)} %collective-permute-done.4.halo_b, ...), custom_call_target="tpu_custom_call" | custom-call | flops 2756608 | bytes 2756608 | tf_op jit(solution)/shard_map/pallas_call | solution.py:28
  21.8 13.8 %all_to_all.10.received = f32[16,4,640]{2,1,0:T(4,128)S(1)} all-to-all(f32[16,4,640]{2,1,0:T(4,128)S(1)} %get-tuple-element.39), channel_id=1, replica_groups=mesh['patch'=16,'span'=8,'wall'=2] {'patch'}, dimensions={0} | all-to-all | bytes 327680 | tf_op jit(solution)/shard_map/all_to_all | solution.py:389
  35.6 3.8 %collective-permute-start.6 = (f32[4,640]{1,0:T(4,128)S(1)}, f32[4,640]{1,0:T(4,128)S(1)}, u32[]{:S(2)}, u32[]{:S(2)}) collective-permute-start(f32[4,640]{1,0:T(4,128)S(1)} %shard_map.87.own), channel_id=1, source_target_pairs={{0,1},{1,0},{2,3},{3,2},{4,5},{5,4},{6,7},{7,6},{8,9},{9,8},{10,11... | collective-permute-start | bytes 30728 | tf_op jit(solution)/shard_map/ppermute | solution.py:391
  39.4 0.8 %collective-permute-done.6.other = f32[4,640]{1,0:T(4,128)S(1)} collective-permute-done((f32[4,640]{1,0:T(4,128)S(1)}, f32[4,640]{1,0:T(4,128)S(1)}, u32[]{:S(2)}, u32[]{:S(2)}) %collective-permute-start.6) | collective-permute-done | bytes 10272 | tf_op jit(solution)/shard_map/ppermute | solution.py:391
  40.3 0.2 shard_map.88
  40.4 9.8 %all_to_all.11.fixes = f32[16,4,640]{2,1,0:T(4,128)S(1)} all-to-all(f32[16,4,640]{2,1,0:T(4,128)S(1)} %shard_map.88), channel_id=1, replica_groups=mesh['patch'=16,'span'=8,'wall'=2] {'patch'}, dimensions={0} | all-to-all | bytes 327680 | tf_op jit(solution)/shard_map/all_to_all | solution.py:393
  50.2 0.5 shard_map.89
  50.8 1.6 %collective-permute-start.8 = (f32[5,8,1024]{2,1,0:T(8,128)S(1)}, f32[5,8,1024]{2,1,0:T(8,128)S(1)}, u32[]{:S(2)}, u32[]{:S(2)}) collective-permute-start(f32[5,8,1024]{2,1,0:T(8,128)S(1)} %get-tuple-element.44), channel_id=1, source_target_pairs={{2,4},{4,2},{6,8},{8,6},{10,12},{12,10},{14,0},{0,14},{3,5},{5,3},... | collective-permute-start | bytes 491528 | tf_op jit(solution)/shard_map/ppermute | solution.py:336
  52.3 2.1 %collective-permute-start.7 = (f32[20,1024]{1,0:T(8,128)S(1)}, f32[20,1024]{1,0:T(8,128)S(1)}, u32[]{:S(2)}, u32[]{:S(2)}) collective-permute-start(f32[20,1024]{1,0:T(8,128)S(1)} %get-tuple-element.41), channel_id=1, source_target_pairs={{0,1},{1,0},{2,3},{3,2},{4,5},{5,4},{6,7},{7,6},{8,9},{9,8},{10,11... | collective-permute-start | bytes 245768 | tf_op jit(solution)/shard_map/ppermute | solution.py:337
  54.4 0.9 %collective-permute-done.7.halo_w = f32[20,1024]{1,0:T(8,128)S(1)} collective-permute-done((f32[20,1024]{1,0:T(8,128)S(1)}, f32[20,1024]{1,0:T(8,128)S(1)}, u32[]{:S(2)}, u32[]{:S(2)}) %collective-permute-start.7) | collective-permute-done | bytes 81952 | tf_op jit(solution)/shard_map/ppermute | solution.py:337
  55.3 2.3 %shard_map.90 = (f32[4,5,8,1024]{3,2,1,0:T(8,128)}, f32[4,5,8,1024]{3,2,1,0:T(8,128)S(1)}) custom-call(f32[2,5,5,8,128]{4,3,2,1,0:T(8,128)S(1)} %get-tuple-element.26.splat, f32[4,5,8,1024]{3,2,1,0:T(8,128)S(1)} %get-tuple-element.40.fix, f32[20,1024]{1,0:T(8,128)S(1)} %collective-permute-done.7.halo_w, f32[4,5,5,8,1024]{4,3,2,1,0:T(8,128)S(1)} %bitcast.9, ...), custom_call_target="tpu_custom_call" | custom-call | flops 4730880 | bytes 4730880 | tf_op jit(solution)/shard_map/pallas_call | solution.py:28
  57.7 1.1 %shard_map.91 = f32[4,5,8,1024]{3,2,1,0:T(8,128)} custom-call(f32[2,5,5,8,128]{4,3,2,1,0:T(8,128)S(1)} %get-tuple-element.26.splat, f32[4,5,8,1024]{3,2,1,0:T(8,128)S(1)} %get-tuple-element.43.inner, f32[5,8,1024]{2,1,0:T(8,128)S(1)} %collective-permute-done.8.halo_b, ...), custom_call_target="tpu_custom_call", output_to_operand_aliasing={{}: (5, {})} | custom-call | flops 2887680 | bytes 2887680 | tf_op jit(solution)/shard_map/pallas_call | solution.py:28
  (18 shorter events, 0.1 us)
Async XLA Ops:
  0.0 11.3 %copy-start = (f32[4,8,5,5,1024]{4,1,3,2,0:T(8,128)S(1)}, f32[4,8,5,5,1024]{4,1,3,2,0:T(8,128)}, u32[]{:S(2)}) copy-start(f32[4,8,5,5,1024]{4,1,3,2,0:T(8,128)} %param.9) | copy-start | bytes 9830404
  2.9 10.4 %collective-permute-start.1 = (f32[5,8,1024]{2,1,0:T(8,128)S(1)}, f32[5,8,1024]{2,1,0:T(8,128)S(1)}, u32[]{:S(2)}, u32[]{:S(2)}) collective-permute-start(f32[5,8,1024]{2,1,0:T(8,128)S(1)} %get-tuple-element.31), channel_id=1, source_target_pairs={{2,4},{4,2},{6,8},{8,6},{10,12},{12,10},{14,0},{0,14},{3,5},{5,3},... | collective-permute-start | bytes 491528 | tf_op jit(solution)/shard_map/ppermute | solution.py:336
  9.4 4.7 %collective-permute-start.2 = (f32[5,8,1024]{2,1,0:T(8,128)S(1)}, f32[5,8,1024]{2,1,0:T(8,128)S(1)}, u32[]{:S(2)}, u32[]{:S(2)}) collective-permute-start(f32[5,8,1024]{2,1,0:T(8,128)S(1)} %get-tuple-element.32), channel_id=1, source_target_pairs={{0,2},{2,0},{4,6},{6,4},{8,10},{10,8},{12,14},{14,12},{1,3},{3,1},... | collective-permute-start | bytes 491528 | tf_op jit(solution)/shard_map/ppermute | solution.py:338
  9.4 1.9 %collective-permute-start = (f32[20,1024]{1,0:T(8,128)S(1)}, f32[20,1024]{1,0:T(8,128)S(1)}, u32[]{:S(2)}, u32[]{:S(2)}) collective-permute-start(f32[20,1024]{1,0:T(8,128)S(1)} %get-tuple-element.28), channel_id=1, source_target_pairs={{0,1},{1,0},{2,3},{3,2},{4,5},{5,4},{6,7},{7,6},{8,9},{9,8},{10,11... | collective-permute-start | bytes 245768 | tf_op jit(solution)/shard_map/ppermute | solution.py:337
  14.5 6.2 %collective-permute-start.4 = (f32[5,8,1024]{2,1,0:T(8,128)S(1)}, f32[5,8,1024]{2,1,0:T(8,128)S(1)}, u32[]{:S(2)}, u32[]{:S(2)}) collective-permute-start(f32[5,8,1024]{2,1,0:T(8,128)S(1)} %get-tuple-element.33.edge_b), channel_id=1, source_target_pairs={{2,4},{4,2},{6,8},{8,6},{10,12},{12,10},{14,0},{0,14},{3,5},{5,3},... | collective-permute-start | bytes 491528 | tf_op jit(solution)/shard_map/ppermute | solution.py:336
  16.1 4.6 %collective-permute-start.5 = (f32[5,8,1024]{2,1,0:T(8,128)S(1)}, f32[5,8,1024]{2,1,0:T(8,128)S(1)}, u32[]{:S(2)}, u32[]{:S(2)}) collective-permute-start(f32[5,8,1024]{2,1,0:T(8,128)S(1)} %get-tuple-element.34.edge_a), channel_id=1, source_target_pairs={{0,2},{2,0},{4,6},{6,4},{8,10},{10,8},{12,14},{14,12},{1,3},{3,1},... | collective-permute-start | bytes 491528 | tf_op jit(solution)/shard_map/ppermute | solution.py:338
  16.1 2.8 %collective-permute-start.3 = (f32[20,1024]{1,0:T(8,128)S(1)}, f32[20,1024]{1,0:T(8,128)S(1)}, u32[]{:S(2)}, u32[]{:S(2)}) collective-permute-start(f32[20,1024]{1,0:T(8,128)S(1)} %get-tuple-element.35), channel_id=1, source_target_pairs={{0,1},{1,0},{2,3},{3,2},{4,5},{5,4},{6,7},{7,6},{8,9},{9,8},{10,11... | collective-permute-start | bytes 245768 | tf_op jit(solution)/shard_map/ppermute | solution.py:337
  20.7 19.6 %copy-start.4 = (f32[1,1,5,10,4]{3,4,2,1,0:T(4,128)S(1)}, f32[1,1,5,10,4]{3,4,2,1,0:T(4,128)}, u32[]{:S(2)}) copy-start(f32[1,1,5,10,4]{3,4,2,1,0:T(4,128)} %param.15) | copy-start | bytes 2404
  20.7 29.5 %copy-start.2 = (s32[4,8,8]{2,1,0:T(8,128)S(1)}, s32[4,8,8]{2,1,0:T(8,128)}, u32[]{:S(2)}) copy-start(s32[4,8,8]{2,1,0:T(8,128)} %owner.1) | copy-start | bytes 3076
  20.7 29.5 %copy-start.3 = (s32[4,8,8]{2,1,0:T(8,128)S(1)}, s32[4,8,8]{2,1,0:T(8,128)}, u32[]{:S(2)}) copy-start(s32[4,8,8]{2,1,0:T(8,128)} %slot.1) | copy-start | bytes 3076
  20.7 34.6 %copy-start.1 = (f32[4,8,5,5,1024]{4,1,3,2,0:T(8,128)S(1)}, f32[4,8,5,5,1024]{4,1,3,2,0:T(8,128)}, u32[]{:S(2)}) copy-start(f32[4,8,5,5,1024]{4,1,3,2,0:T(8,128)} %param.10) | copy-start | bytes 9830404
  35.6 4.7 %collective-permute-start.6 = (f32[4,640]{1,0:T(4,128)S(1)}, f32[4,640]{1,0:T(4,128)S(1)}, u32[]{:S(2)}, u32[]{:S(2)}) collective-permute-start(f32[4,640]{1,0:T(4,128)S(1)} %shard_map.87.own), channel_id=1, source_target_pairs={{0,1},{1,0},{2,3},{3,2},{4,5},{5,4},{6,7},{7,6},{8,9},{9,8},{10,11... | collective-permute-start | bytes 30728 | tf_op jit(solution)/shard_map/ppermute | solution.py:391
  50.8 6.9 %collective-permute-start.8 = (f32[5,8,1024]{2,1,0:T(8,128)S(1)}, f32[5,8,1024]{2,1,0:T(8,128)S(1)}, u32[]{:S(2)}, u32[]{:S(2)}) collective-permute-start(f32[5,8,1024]{2,1,0:T(8,128)S(1)} %get-tuple-element.44), channel_id=1, source_target_pairs={{2,4},{4,2},{6,8},{8,6},{10,12},{12,10},{14,0},{0,14},{3,5},{5,3},... | collective-permute-start | bytes 491528 | tf_op jit(solution)/shard_map/ppermute | solution.py:336
  52.3 5.3 %collective-permute-start.9 = (f32[5,8,1024]{2,1,0:T(8,128)S(1)}, f32[5,8,1024]{2,1,0:T(8,128)S(1)}, u32[]{:S(2)}, u32[]{:S(2)}) collective-permute-start(f32[5,8,1024]{2,1,0:T(8,128)S(1)} %get-tuple-element.45), channel_id=1, source_target_pairs={{0,2},{2,0},{4,6},{6,4},{8,10},{10,8},{12,14},{14,12},{1,3},{3,1},... | collective-permute-start | bytes 491528 | tf_op jit(solution)/shard_map/ppermute | solution.py:338
  52.3 3.0 %collective-permute-start.7 = (f32[20,1024]{1,0:T(8,128)S(1)}, f32[20,1024]{1,0:T(8,128)S(1)}, u32[]{:S(2)}, u32[]{:S(2)}) collective-permute-start(f32[20,1024]{1,0:T(8,128)S(1)} %get-tuple-element.41), channel_id=1, source_target_pairs={{0,1},{1,0},{2,3},{3,2},{4,5},{5,4},{6,7},{7,6},{8,9},{9,8},{10,11... | collective-permute-start | bytes 245768 | tf_op jit(solution)/shard_map/ppermute | solution.py:337

commit v5 on v4

--- a/solution.py
+++ b/solution.py
@@ -68,6 +68,14 @@
     return mix(splat, 1, values)
 
 
+def wall_rows(splat, raw, out):
+    for q in range(out.shape[-1] // LANES):
+        lanes = slice(q * LANES, (q + 1) * LANES)
+        mixed = mix(splat, 0, [raw[k, :, lanes] for k in range(5)])
+        for i in range(5):
+            out[4 * i : 4 * i + 4, lanes] = mixed[i][:4]
+
+
 def for_lanes(body, length):
     @pl.loop(0, length // LANES)
     def _(q):
@@ -95,7 +103,7 @@
 def first_kernel(
     wall_in, span_in, owner_in, slot_in, rhs_in, jinv_in,
     rhs, jinv, splat, onehot_t, first, edge_a, edge_b, edge_w,
-    wall, span, owner, slot, small_sems, sems,
+    wall, span, owner, slot, raw, small_sems, sems,
 ):
     small = [
         pltpu.make_async_copy(source, here, small_sems.at[n])
@@ -127,22 +135,21 @@
 
         for_lanes(body, rhs.shape[-1])
         for k in range(5):
-            edge_w[s * 5 + k, :] = first[s, k, row, :]
+            raw[k, s, :] = first[s, k, row, :]
     for k in range(5):
         edge_a[k] = first[plane_a, k]
         edge_b[k] = first[plane_b, k]
-
-
-def local_apply(splat, row, planes, halo_w, jac, lanes, s):
+    wall_rows(splat, raw, edge_w)
+
+
+def local_apply(splat, planes, jac, lanes, s):
     own = planes[s]
     rows = lax.broadcasted_iota(jnp.int32, own[0].shape, 0)
-    other_side = rows == row
     near_wall, near_span = [], []
     for k in range(5):
         up = jnp.where(rows == 7, 0.0, pltpu.roll(own[k], 7, 0))
         down = jnp.where(rows == 0, 0.0, pltpu.roll(own[k], 1, 0))
-        beyond = jnp.where(other_side, halo_w[s * 5 + k, lanes][None, :], 0.0)
-        near_wall.append(up + down + beyond)
+        near_wall.append(up + down)
         near_span.append(total([planes[n][k] for n in (s - 1, s + 1) if 0 <= n < 4]))
     from_wall, from_span = mix(splat, 0, near_wall), mix(splat, 1, near_span)
     return [
@@ -151,21 +158,37 @@
     ]
 
 
-def second_local_kernel(splat, first, halo_w, rhs, jac, jinv, inner):
-    row = position()[3]
-
+def with_wall(rest, halo_w, s, lanes, row):
+    rows = lax.broadcasted_iota(jnp.int32, (8, LANES), 0)
+    return [
+        rest[s, i, :, lanes] + jnp.where(rows == row, halo_w[4 * i + s, lanes][None, :], 0.0) for i in range(5)
+    ]
+
+
+def first_residual_kernel(splat, first, rhs, jac, rest):
     def body(lanes):
         planes = [[first[n, k, :, lanes] for k in range(5)] for n in range(4)]
         for s in range(4):
-            applied = local_apply(splat, row, planes, halo_w, jac, lanes, s)
-            swept = sweep(jinv, s, lanes, [rhs[s, k, :, lanes] - applied[k] for k in range(5)])
-            for k in range(5):
-                inner[s, k, :, lanes] = planes[s][k] + swept[k]
+            applied = local_apply(splat, planes, jac, lanes, s)
+            for k in range(5):
+                rest[s, k, :, lanes] = rhs[s, k, :, lanes] - applied[k]
 
     for_lanes(body, rhs.shape[-1])
 
 
-def second_edge_kernel(splat, inner, halo_b, halo_a, jinv, edge_a, edge_b, edge_w):
+def second_local_kernel(first, rest, halo_w, jinv, inner):
+    row = position()[3]
+
+    def body(lanes):
+        for s in range(4):
+            swept = sweep(jinv, s, lanes, with_wall(rest, halo_w, s, lanes, row))
+            for k in range(5):
+                inner[s, k, :, lanes] = first[s, k, :, lanes] + swept[k]
+
+    for_lanes(body, rest.shape[-1])
+
+
+def second_edge_kernel(splat, inner, halo_b, halo_a, jinv, edge_a, edge_b, edge_w, raw):
     even, plane_a, plane_b, row = position()
     real = inside()
 
@@ -178,10 +201,11 @@
     for_lanes(body, inner.shape[-1])
     for k in range(5):
         for s in (1, 2):
-            edge_w[s * 5 + k, :] = inner[s, k, row, :]
+            raw[k, s, :] = inner[s, k, row, :]
         a, b = edge_a[k, row, :], edge_b[k, row, :]
-        edge_w[k, :] = jnp.where(even, b, a)
-        edge_w[15 + k, :] = jnp.where(even, a, b)
+        raw[k, 0, :] = jnp.where(even, b, a)
+        raw[k, 3, :] = jnp.where(even, a, b)
+    wall_rows(splat, raw, edge_w)
 
 
 def planes_of(even, inner, edge_a, edge_b, lanes):
@@ -195,55 +219,68 @@
     ]
 
 
-def defect_local_kernel(splat, inner, edge_b, edge_a, halo_w, rhs, jac, jinv, onehot_t, base, partial, defect):
-    even, _, _, row = position()
+def second_residual_kernel(splat, inner, edge_b, edge_a, rhs, jac, rest):
+    even = position()[0]
 
     def body(lanes):
         planes = planes_of(even, inner, edge_a, edge_b, lanes)
         for s in range(4):
-            applied = local_apply(splat, row, planes, halo_w, jac, lanes, s)
-            rest = [rhs[s, k, :, lanes] - applied[k] for k in range(5)]
-            swept = sweep(jinv, s, lanes, rest)
+            applied = local_apply(splat, planes, jac, lanes, s)
+            for k in range(5):
+                rest[s, k, :, lanes] = rhs[s, k, :, lanes] - applied[k]
+
+    for_lanes(body, rhs.shape[-1])
+
+
+def defect_local_kernel(inner, edge_b, edge_a, rest, halo_w, jinv, onehot_t, partial, base_out, base, defect, sems):
+    even, _, _, row = position()
+
+    def body(lanes):
+        planes = planes_of(even, inner, edge_a, edge_b, lanes)
+        for s in range(4):
+            known = with_wall(rest, halo_w, s, lanes, row)
+            swept = sweep(jinv, s, lanes, known)
             for k in range(5):
                 base[s, k, :, lanes] = planes[s][k] + swept[k]
-                defect[s, k, :, lanes] = rest[k]
-
-    for_lanes(body, rhs.shape[-1])
+                defect[s, k, :, lanes] = known[k]
+
+    for_lanes(body, rest.shape[-1])
+    store = pltpu.make_async_copy(base, base_out, sems.at[0])
+    store.start()
     tiles = defect.shape[-1] // LANES
     for k in range(5):
         rows = jnp.concatenate(
             [defect[s, k, :, q * LANES : (q + 1) * LANES] for s in range(4) for q in range(tiles)], axis=0
         )
         partial[:, k * LANES : (k + 1) * LANES] = picked_sums(onehot_t[...], rows)
-
-
-def restrict_kernel(splat, inner, base, halo_b, halo_a, onehot_t, jinv, partial, base_out, edges, sems):
-    even, plane_a, plane_b, _ = position()
+    store.wait()
+
+
+def restrict_kernel(splat, inner, halo_b, halo_a, onehot_t, partial, late_out, late, sems):
     real = inside()
-    copies = [pltpu.make_async_copy(base.at[pl.ds(1, 2)], base_out.at[pl.ds(1, 2)], sems.at[2])]
-    copies[0].start()
+    at_a = 1 - lax.rem(lax.axis_index("span"), 2)
     tiles = halo_a.shape[-1] // LANES
-    parts = []
-    for n, (plane, halo, there) in enumerate(((plane_a, halo_a, None), (plane_b, halo_b, real))):
+    stores, parts = [], []
+    for n, (halo, there, at) in enumerate(((halo_b, real, 1 - at_a), (halo_a, None, at_a))):
         for q in range(tiles):
             lanes = slice(q * LANES, (q + 1) * LANES)
             beyond = beyond_span(splat, halo, lanes, there)
             parts.append(beyond)
-            swept = sweep(jinv, plane, lanes, beyond)
-            for k in range(5):
-                edges[n, k, :, lanes] = base[plane, k, :, lanes] + swept[k]
-        copies.append(pltpu.make_async_copy(edges.at[n], base_out.at[plane], sems.at[n]))
-        copies[-1].start()
+            for k in range(5):
+                late[n, k, :, lanes] = beyond[k]
+        stores.append(pltpu.make_async_copy(late.at[n], late_out.at[at], sems.at[n]))
+        stores[-1].start()
     width = 8 * tiles
+    even = at_a == 1
     low, high = onehot_t[:, :width], onehot_t[:, 3 * width :]
-    hot = jnp.concatenate([jnp.where(even, high, low), jnp.where(even, low, high)], axis=1)
+    hot = jnp.concatenate([jnp.where(even, low, high), jnp.where(even, high, low)], axis=1)
     slots = partial.shape[1]
     rows = jnp.concatenate([jnp.concatenate(part, axis=1) for part in parts], axis=0)
     sums = inner[...] + picked_sums(hot, rows)
     for p in range(partial.shape[0]):
         partial[p] = sums[p * slots : (p + 1) * slots]
-    for copy in copies:
-        copy.wait()
+    for store in stores:
+        store.wait()
 
 
 def sum_kernel(received, sums):
@@ -263,7 +300,7 @@
             out[p, :, i * LANES : (i + 1) * LANES] = fix
 
 
-def prolong_kernel(owner, slot, fixes, out, edge_a, edge_b, edge_w, fix):
+def prolong_kernel(splat, owner, slot, fixes, out, edge_a, edge_b, edge_w, fix, raw):
     _, plane_a, plane_b, row = position()
     tiles = out.shape[-1] // LANES
     owners, slots, _ = fixes.shape
@@ -280,31 +317,50 @@
         edge_a[k] = out[plane_a, k]
         edge_b[k] = out[plane_b, k]
         for s in range(4):
-            edge_w[s * 5 + k, :] = out[s, k, row, :]
-
-
-def final_local_kernel(splat, fix, halo_w, jac, jinv, base_in, out, inner, base, sems):
+            raw[k, s, :] = out[s, k, row, :]
+    wall_rows(splat, raw, edge_w)
+
+
+def final_residual_kernel(splat, fix, jac, rest):
+    def body(lanes):
+        planes = [[fix[n, k, :, lanes] for k in range(5)] for n in range(4)]
+        for s in range(4):
+            applied = local_apply(splat, planes, jac, lanes, s)
+            for k in range(5):
+                rest[s, k, :, lanes] = -applied[k]
+
+    for_lanes(body, fix.shape[-1])
+
+
+def final_local_kernel(fix, rest, halo_w, jinv, base_in, late_in, out, inner, base, late, sems):
     row = position()[3]
-    load = pltpu.make_async_copy(base_in, base, sems.at[0])
-    load.start()
+    loads = [
+        pltpu.make_async_copy(base_in.at[pl.ds(1, 2)], base.at[pl.ds(1, 2)], sems.at[0]),
+        pltpu.make_async_copy(late_in, late, sems.at[1]),
+        pltpu.make_async_copy(base_in.at[0], base.at[0], sems.at[2]),
+        pltpu.make_async_copy(base_in.at[3], base.at[3], sems.at[3]),
+    ]
+    for load in loads:
+        load.start()
     stores = []
     for s in (1, 2, 0, 3):
 
         def body(lanes, s=s):
-            planes = [[fix[n, k, :, lanes] for k in range(5)] if abs(n - s) < 2 else None for n in range(4)]
-            applied = local_apply(splat, row, planes, halo_w, jac, lanes, s)
-            swept = sweep(jinv, s, lanes, applied)
-            for k in range(5):
-                change = planes[s][k] - swept[k]
-                inner[s, k, :, lanes] = change if s == 1 else base[s, k, :, lanes] + change
-
+            known = with_wall(rest, halo_w, s, lanes, row)
+            if s in (0, 3):
+                known = [known[k] + late[s // 3, k, :, lanes] for k in range(5)]
+            swept = sweep(jinv, s, lanes, known)
+            for k in range(5):
+                inner[s, k, :, lanes] = (base[s, k, :, lanes] + fix[s, k, :, lanes]) + swept[k]
+
+        if s == 1:
+            loads[0].wait()
+        if s == 0:
+            for load in loads[1:]:
+                load.wait()
         for_lanes(body, fix.shape[-1])
-        if s == 1:
-            load.wait()
-            for k in range(5):
-                inner[1, k] += base[1, k]
         if s in (1, 2):
-            stores.append(pltpu.make_async_copy(inner.at[s], out.at[s], sems.at[s]))
+            stores.append(pltpu.make_async_copy(inner.at[s], out.at[s], sems.at[3 + s]))
             stores[-1].start()
     for store in stores:
         store.wait()
@@ -348,6 +404,7 @@
     field_out = pltpu.HBM(rhs.shape, F32)
     matrices = shaped(*jac_in.shape)
     outer = pltpu.VMEM((2, *rhs.shape[1:]), F32)
+    raw = pltpu.VMEM(rhs.shape[1:], F32)
     owners, slots = lax.axis_size("patch"), coarse_inv.shape[-1]
     aggregates, columns = owners * slots, 5 * LANES
     chunks = shaped(owners, slots, columns)
@@ -365,26 +422,33 @@
             pltpu.SMEM(span_coupling.shape, F32),
             pltpu.VMEM(block_owner.shape, jnp.int32),
             pltpu.VMEM(block_owner.shape, jnp.int32),
+            raw,
             pltpu.SemaphoreType.DMA((5,)),
             pltpu.SemaphoreType.DMA((4,)),
         ],
     )
+    jac, b = lax.optimization_barrier((jac_in, b))
     halo_a, halo_b, halo_w = exchange(a, b, w)
-    [inner] = call(second_local_kernel, [field], [splat, first, halo_w, rhs, jac_in, jinv])
-    a, b, w = call(second_edge_kernel, [plane, plane, edge], [splat, inner, halo_b, halo_a, jinv])
+    [rest] = call(first_residual_kernel, [field], [splat, first, rhs, jac])
+    [inner] = call(second_local_kernel, [field], [first, rest, halo_w, jinv])
+    a, b, w = call(
+        second_edge_kernel, [plane, plane, edge], [splat, inner, halo_b, halo_a, jinv], scratch=[raw]
+    )
     halo_a, halo_b, halo_w = exchange(a, b, w)
-    base, partial = call(
+    [rest] = call(second_residual_kernel, [field], [splat, inner, b, a, rhs, jac])
+    partial, base = call(
         defect_local_kernel,
-        [field, shaped(aggregates, columns)],
-        [splat, inner, b, a, halo_w, rhs, jac_in, jinv, onehot_t],
-        scratch=[pltpu.VMEM(rhs.shape, F32)],
-    )
-    partial, base = call(
+        [shaped(aggregates, columns), field_out],
+        [inner, b, a, rest, halo_w, jinv, onehot_t],
+        out_places=[VMEM, HBM],
+        scratch=[pltpu.VMEM(rhs.shape, F32), pltpu.VMEM(rhs.shape, F32), pltpu.SemaphoreType.DMA((1,))],
+    )
+    partial, late = call(
         restrict_kernel,
-        [chunks, field_out],
-        [splat, partial, base, halo_b, halo_a, onehot_t, jinv],
+        [chunks, pltpu.HBM((2, *plane.shape), F32)],
+        [splat, partial, halo_b, halo_a, onehot_t],
         out_places=[VMEM, HBM],
-        scratch=[outer, pltpu.SemaphoreType.DMA((3,))],
+        scratch=[outer, pltpu.SemaphoreType.DMA((2,))],
     )
     received = lax.all_to_all(partial, "patch", split_axis=0, concat_axis=0, tiled=True)
     [mine] = call(sum_kernel, [shaped(slots, columns)], [received])
@@ -394,17 +458,18 @@
     fix, a, b, w = call(
         prolong_kernel,
         [field, plane, plane, edge],
-        [block_owner, block_slot, fixes],
-        scratch=[pltpu.VMEM((aggregates, columns), F32)],
+        [splat, block_owner, block_slot, fixes],
+        scratch=[pltpu.VMEM((aggregates, columns), F32), raw],
     )
     halo_a, halo_b, halo_w = exchange(a, b, w)
+    [rest] = call(final_residual_kernel, [field], [splat, fix, jac])
     out, inner = call(
         final_local_kernel,
         [field_out, field],
-        [splat, fix, halo_w, jac_in, jinv_in, in_hbm(base)],
-        places=[VMEM] * 5 + [HBM],
+        [fix, rest, halo_w, jinv_in, in_hbm(base), in_hbm(late)],
+        places=[VMEM] * 4 + [HBM] * 2,
         out_places=[HBM, VMEM],
-        scratch=[pltpu.VMEM(rhs.shape, F32), pltpu.SemaphoreType.DMA((3,))],
+        scratch=[pltpu.VMEM(rhs.shape, F32), outer, pltpu.SemaphoreType.DMA((6,))],
     )
     [out] = call(
         final_edge_kernel,

time: 59 us -> 59 us (level)
  waiting for transfers between devices: 5.02 us -> 3.07 us
  Pallas kernels: 11.7 us -> 13.3 us
    ppermute x3, waiting for transfers between devices: 2.83 us -> 0.07 us  [exchange(): halo_w = lax.ppermute(edge_w, 'wall', [(0, 1), (1, 0)])]
    pallas_call x10 -> x13, Pallas kernels: 11.7 us -> 13.3 us  [call(): pl.pallas_call(kernel, out_shape=outs, in_specs=places or [VMEM] * len(ar...]
    ppermute x3, waiting for transfers between devices: 0.53 us -> 1.34 us  [exchange(): halo_b = lax.ppermute(edge_b, 'span', odd)]
  transfers between devices with their start and end apart: 10 -> 10, of which waited for: 6 -> 3; matrix products, arithmetic and copies ran while one was open for 0% -> 0% of each run, Pallas kernels for 10% -> 12%
where the time goes in v5:
time: 59 us; the launch traced here: 58.9 us
  blocking collectives  23.6 us (40%)
  starting transfers between devices  18.8 us (32%)
  Pallas kernels  13.3 us (23%)
  waiting for transfers between devices  3.07 us (5%)
    all_to_all x1, blocking collectives, local(): lax.all_to_all(partial, 'patch', split_axis=0, concat_axis=0, tiled=True)  13.8 us
    pallas_call x13, Pallas kernels, call(): pl.pallas_call(kernel, out_shape=outs, in_specs=places or [VMEM] * len(ar...  13.3 us
    all_to_all x1, blocking collectives, local(): lax.all_to_all(reply, 'patch', split_axis=0, concat_axis=0, tiled=True)  9.77 us
    ppermute x3, starting transfers between devices, exchange(): halo_b = lax.ppermute(edge_b, 'span', odd)  9.67 us
    ppermute x3, starting transfers between devices, exchange(): halo_w = lax.ppermute(edge_w, 'wall', [(0, 1), (1, 0)])  4.83 us
    ppermute x1, starting transfers between devices, local(): theirs = lax.ppermute(mine, 'wall', [(0, 1), (1, 0)])  4.25 us
    ppermute x3, waiting for transfers between devices, exchange(): halo_b = lax.ppermute(edge_b, 'span', odd)  1.34 us
  transfers between devices with their start and end apart: 10, of which 3 were waited for; matrix products, arithmetic and copies ran while one was open for 0% of the time, Pallas kernels for 12%

profile of v5, /device:TPU:1, one launch (start us, length us, event | category | flops | bytes accessed | tf_op | source)
XLA Modules:
  0.0 58.9 jit_solution(3279736629850292175)
XLA Ops:
  0.0 2.9 %shard_map.82 = (f32[4,5,8,1024]{3,2,1,0:T(8,128)S(1)}, f32[4,5,5,8,1024]{4,3,2,1,0:T(8,128)S(1)}, f32[2,5,5,8,128]{4,3,2,1,0:T(8,128)S(1)}, f32[64,256]{1,0:T(8...) custom-call(f32[5,5]{1,0:T(8,128)} %wall_in.1, ...), custom_call_target="tpu_custom_call" | custom-call | flops 4600932 | bytes 4600932 | tf_op jit(solution)/shard_map/pallas_call | solution.py:28
  2.9 6.5 %collective-permute-start.1 = (f32[5,8,1024]{2,1,0:T(8,128)S(1)}, f32[5,8,1024]{2,1,0:T(8,128)S(1)}, u32[]{:S(2)}, u32[]{:S(2)}) collective-permute-start(f32[5,8,1024]{2,1,0:T(8,128)S(1)} %get-tuple-element.35), channel_id=1, source_target_pairs={{2,4},{4,2},{6,8},{8,6},{10,12},{12,10},{14,0},{0,14},{3,5},{5,3},... | collective-permute-start | bytes 491528 | tf_op jit(solution)/shard_map/ppermute | solution.py:392
  9.4 1.0 %collective-permute-start = (f32[20,1024]{1,0:T(8,128)S(1)}, f32[20,1024]{1,0:T(8,128)S(1)}, u32[]{:S(2)}, u32[]{:S(2)}) collective-permute-start(f32[20,1024]{1,0:T(8,128)S(1)} %get-tuple-element.33), channel_id=1, source_target_pairs={{0,1},{1,0},{2,3},{3,2},{4,5},{5,4},{6,7},{7,6},{8,9},{9,8},{10,11... | collective-permute-start | bytes 245768 | tf_op jit(solution)/shard_map/ppermute | solution.py:393
  10.4 0.9 %shard_map.83.rest = f32[4,5,8,1024]{3,2,1,0:T(8,128)S(1)} custom-call(f32[2,5,5,8,128]{4,3,2,1,0:T(8,128)S(1)} %get-tuple-element.28.splat, f32[4,5,8,1024]{3,2,1,0:T(8,128)S(1)} %get-tuple-element.29.first, f32[4,5,8,1024]{3,2,1,0:T(8,128)S(1)} %get-tuple-element.30.rhs, f32[4,5,5,8,1024]{4,3,2,1,0:T(8,128)S(1)} %bitcast.7), custom_call_target="tpu_custom_call" | custom-call | flops 2723840 | bytes 2723840 | tf_op jit(solution)/shard_map/pallas_call | solution.py:28
  11.3 0.7 %shard_map.84.inner = f32[4,5,8,1024]{3,2,1,0:T(8,128)S(1)} custom-call(f32[4,5,8,1024]{3,2,1,0:T(8,128)S(1)} %get-tuple-element.29.first, f32[4,5,8,1024]{3,2,1,0:T(8,128)S(1)} %shard_map.83.rest, f32[20,1024]{1,0:T(8,128)S(1)} %collective-permute-done.halo_w, f32[4,5,5,8,1024]{4,3,2,1,0:T(8,128)S(1)} %get-tuple-element.34.jinv), custom_call_target="tpu_custom_call" | custom-call | flops 2662400 | bytes 2662400 | tf_op jit(solution)/shard_map/pallas_call | solution.py:28
  12.0 1.3 %collective-permute-done.1.halo_b = f32[5,8,1024]{2,1,0:T(8,128)S(1)} collective-permute-done((f32[5,8,1024]{2,1,0:T(8,128)S(1)}, f32[5,8,1024]{2,1,0:T(8,128)S(1)}, u32[]{:S(2)}, u32[]{:S(2)}) %collective-permute-start.1) | collective-permute-done | bytes 163872 | tf_op jit(solution)/shard_map/ppermute | solution.py:392
  13.3 0.8 %collective-permute-done.2.halo_a = f32[5,8,1024]{2,1,0:T(8,128)S(1)} collective-permute-done((f32[5,8,1024]{2,1,0:T(8,128)S(1)}, f32[5,8,1024]{2,1,0:T(8,128)S(1)}, u32[]{:S(2)}, u32[]{:S(2)}) %collective-permute-start.2) | collective-permute-done | bytes 163872 | tf_op jit(solution)/shard_map/ppermute | solution.py:394
  14.2 0.4 shard_map.85
  14.6 1.6 %collective-permute-start.4 = (f32[5,8,1024]{2,1,0:T(8,128)S(1)}, f32[5,8,1024]{2,1,0:T(8,128)S(1)}, u32[]{:S(2)}, u32[]{:S(2)}) collective-permute-start(f32[5,8,1024]{2,1,0:T(8,128)S(1)} %get-tuple-element.37.edge_b), channel_id=1, source_target_pairs={{2,4},{4,2},{6,8},{8,6},{10,12},{12,10},{14,0},{0,14},{3,5},{5,3},... | collective-permute-start | bytes 491528 | tf_op jit(solution)/shard_map/ppermute | solution.py:392
  16.2 1.8 %collective-permute-start.3 = (f32[20,1024]{1,0:T(8,128)S(1)}, f32[20,1024]{1,0:T(8,128)S(1)}, u32[]{:S(2)}, u32[]{:S(2)}) collective-permute-start(f32[20,1024]{1,0:T(8,128)S(1)} %get-tuple-element.39), channel_id=1, source_target_pairs={{0,1},{1,0},{2,3},{3,2},{4,5},{5,4},{6,7},{7,6},{8,9},{9,8},{10,11... | collective-permute-start | bytes 245768 | tf_op jit(solution)/shard_map/ppermute | solution.py:393
  18.1 0.9 %shard_map.86.rest = f32[4,5,8,1024]{3,2,1,0:T(8,128)S(1)} custom-call(f32[2,5,5,8,128]{4,3,2,1,0:T(8,128)S(1)} %get-tuple-element.28.splat, f32[4,5,8,1024]{3,2,1,0:T(8,128)S(1)} %shard_map.84.inner, f32[5,8,1024]{2,1,0:T(8,128)S(1)} %get-tuple-element.37.edge_b, f32[5,8,1024]{2,1,0:T(8,128)S(1)} %get-tuple-element.38.edge_a, ...), custom_call_target="tpu_custom_call" | custom-call | flops 2887680 | bytes 2887680 | tf_op jit(solution)/shard_map/pallas_call | solution.py:28
  19.0 1.6 %shard_map.87 = (f32[64,640]{1,0:T(8,128)S(1)}, f32[4,5,8,1024]{3,2,1,0:T(8,128)}) custom-call(f32[4,5,8,1024]{3,2,1,0:T(8,128)S(1)} %shard_map.84.inner, f32[5,8,1024]{2,1,0:T(8,128)S(1)} %get-tuple-element.37.edge_b, f32[5,8,1024]{2,1,0:T(8,128)S(1)} %get-tuple-element.38.edge_a, f32[4,5,8,1024]{3,2,1,0:T(8,128)S(1)} %shard_map.86.rest, ...), custom_call_target="tpu_custom_call" | custom-call | flops 2940928 | bytes 2940928 | tf_op jit(solution)/shard_map/pallas_call | solution.py:28
  20.6 0.9 %shard_map.88 = (f32[16,4,640]{2,1,0:T(4,128)S(1)}, f32[2,5,8,1024]{3,2,1,0:T(8,128)}) custom-call(f32[2,5,5,8,128]{4,3,2,1,0:T(8,128)S(1)} %get-tuple-element.28.splat, f32[64,640]{1,0:T(8,128)S(1)} %get-tuple-element.41.inner, f32[5,8,1024]{2,1,0:T(8,128)S(1)} %collective-permute-done.4.halo_b, f32[5,8,1024]{2,1,0:T(8,128)S(1)} %collective-permute-done.5.halo_a, ...), custom_call_target="tpu_custom_call" | custom-call | flops 626688 | bytes 626688 | tf_op jit(solution)/shard_map/pallas_call | solution.py:28
  21.6 13.8 %all_to_all.10.received = f32[16,4,640]{2,1,0:T(4,128)S(1)} all-to-all(f32[16,4,640]{2,1,0:T(4,128)S(1)} %get-tuple-element.42), channel_id=1, replica_groups=mesh['patch'=16,'span'=8,'wall'=2] {'patch'}, dimensions={0} | all-to-all | bytes 327680 | tf_op jit(solution)/shard_map/all_to_all | solution.py:453
  35.4 4.2 %collective-permute-start.6 = (f32[4,640]{1,0:T(4,128)S(1)}, f32[4,640]{1,0:T(4,128)S(1)}, u32[]{:S(2)}, u32[]{:S(2)}) collective-permute-start(f32[4,640]{1,0:T(4,128)S(1)} %shard_map.89.own), channel_id=1, source_target_pairs={{0,1},{1,0},{2,3},{3,2},{4,5},{5,4},{6,7},{7,6},{8,9},{9,8},{10,11... | collective-permute-start | bytes 30728 | tf_op jit(solution)/shard_map/ppermute | solution.py:455
  39.7 0.8 %collective-permute-done.6.other = f32[4,640]{1,0:T(4,128)S(1)} collective-permute-done((f32[4,640]{1,0:T(4,128)S(1)}, f32[4,640]{1,0:T(4,128)S(1)}, u32[]{:S(2)}, u32[]{:S(2)}) %collective-permute-start.6) | collective-permute-done | bytes 10272 | tf_op jit(solution)/shard_map/ppermute | solution.py:455
  40.5 0.2 shard_map.90
  40.7 9.8 %all_to_all.11.fixes = f32[16,4,640]{2,1,0:T(4,128)S(1)} all-to-all(f32[16,4,640]{2,1,0:T(4,128)S(1)} %shard_map.90), channel_id=1, replica_groups=mesh['patch'=16,'span'=8,'wall'=2] {'patch'}, dimensions={0} | all-to-all | bytes 327680 | tf_op jit(solution)/shard_map/all_to_all | solution.py:457
  50.4 0.6 shard_map.91
  51.0 1.6 %collective-permute-start.8 = (f32[5,8,1024]{2,1,0:T(8,128)S(1)}, f32[5,8,1024]{2,1,0:T(8,128)S(1)}, u32[]{:S(2)}, u32[]{:S(2)}) collective-permute-start(f32[5,8,1024]{2,1,0:T(8,128)S(1)} %get-tuple-element.48), channel_id=1, source_target_pairs={{2,4},{4,2},{6,8},{8,6},{10,12},{12,10},{14,0},{0,14},{3,5},{5,3},... | collective-permute-start | bytes 491528 | tf_op jit(solution)/shard_map/ppermute | solution.py:392
  52.6 2.1 %collective-permute-start.7 = (f32[20,1024]{1,0:T(8,128)S(1)}, f32[20,1024]{1,0:T(8,128)S(1)}, u32[]{:S(2)}, u32[]{:S(2)}) collective-permute-start(f32[20,1024]{1,0:T(8,128)S(1)} %get-tuple-element.44), channel_id=1, source_target_pairs={{0,1},{1,0},{2,3},{3,2},{4,5},{5,4},{6,7},{7,6},{8,9},{9,8},{10,11... | collective-permute-start | bytes 245768 | tf_op jit(solution)/shard_map/ppermute | solution.py:393
  54.6 0.9 %shard_map.92.rest = f32[4,5,8,1024]{3,2,1,0:T(8,128)S(1)} custom-call(f32[2,5,5,8,128]{4,3,2,1,0:T(8,128)S(1)} %get-tuple-element.28.splat, f32[4,5,8,1024]{3,2,1,0:T(8,128)S(1)} %get-tuple-element.43.fix, f32[4,5,5,8,1024]{4,3,2,1,0:T(8,128)S(1)} %bitcast.9), custom_call_target="tpu_custom_call" | custom-call | flops 2396160 | bytes 2396160 | tf_op jit(solution)/shard_map/pallas_call | solution.py:28
  55.6 2.1 %shard_map.93 = (f32[4,5,8,1024]{3,2,1,0:T(8,128)}, f32[4,5,8,1024]{3,2,1,0:T(8,128)S(1)}) custom-call(f32[4,5,8,1024]{3,2,1,0:T(8,128)S(1)} %get-tuple-element.43.fix, f32[4,5,8,1024]{3,2,1,0:T(8,128)S(1)} %shard_map.92.rest, f32[20,1024]{1,0:T(8,128)S(1)} %collective-permute-done.7.halo_w, f32[4,5,5,8,1024]{4,3,2,1,0:T(8,128)S(1)} %bitcast.11, ...), custom_call_target="tpu_custom_call" | custom-call | flops 3481600 | bytes 3481600 | tf_op jit(solution)/shard_map/pallas_call | solution.py:28
  57.7 1.1 %shard_map.94 = f32[4,5,8,1024]{3,2,1,0:T(8,128)} custom-call(f32[2,5,5,8,128]{4,3,2,1,0:T(8,128)S(1)} %get-tuple-element.28.splat, f32[4,5,8,1024]{3,2,1,0:T(8,128)S(1)} %get-tuple-element.47.inner, f32[5,8,1024]{2,1,0:T(8,128)S(1)} %collective-permute-done.8.halo_b, ...), custom_call_target="tpu_custom_call", output_to_operand_aliasing={{}: (5, {})} | custom-call | flops 2887680 | bytes 2887680 | tf_op jit(solution)/shard_map/pallas_call | solution.py:28
  (21 shorter events, 0.1 us)
Async XLA Ops:
  0.0 10.4 %copy-start = (f32[4,8,5,5,1024]{4,1,3,2,0:T(8,128)S(1)}, f32[4,8,5,5,1024]{4,1,3,2,0:T(8,128)}, u32[]{:S(2)}) copy-start(f32[4,8,5,5,1024]{4,1,3,2,0:T(8,128)} %param.9) | copy-start | bytes 9830404
  2.9 10.4 %collective-permute-start.1 = (f32[5,8,1024]{2,1,0:T(8,128)S(1)}, f32[5,8,1024]{2,1,0:T(8,128)S(1)}, u32[]{:S(2)}, u32[]{:S(2)}) collective-permute-start(f32[5,8,1024]{2,1,0:T(8,128)S(1)} %get-tuple-element.35), channel_id=1, source_target_pairs={{2,4},{4,2},{6,8},{8,6},{10,12},{12,10},{14,0},{0,14},{3,5},{5,3},... | collective-permute-start | bytes 491528 | tf_op jit(solution)/shard_map/ppermute | solution.py:392
  9.4 4.7 %collective-permute-start.2 = (f32[5,8,1024]{2,1,0:T(8,128)S(1)}, f32[5,8,1024]{2,1,0:T(8,128)S(1)}, u32[]{:S(2)}, u32[]{:S(2)}) collective-permute-start(f32[5,8,1024]{2,1,0:T(8,128)S(1)} %get-tuple-element.36), channel_id=1, source_target_pairs={{0,2},{2,0},{4,6},{6,4},{8,10},{10,8},{12,14},{14,12},{1,3},{3,1},... | collective-permute-start | bytes 491528 | tf_op jit(solution)/shard_map/ppermute | solution.py:394
  9.4 1.9 %collective-permute-start = (f32[20,1024]{1,0:T(8,128)S(1)}, f32[20,1024]{1,0:T(8,128)S(1)}, u32[]{:S(2)}, u32[]{:S(2)}) collective-permute-start(f32[20,1024]{1,0:T(8,128)S(1)} %get-tuple-element.33), channel_id=1, source_target_pairs={{0,1},{1,0},{2,3},{3,2},{4,5},{5,4},{6,7},{7,6},{8,9},{9,8},{10,11... | collective-permute-start | bytes 245768 | tf_op jit(solution)/shard_map/ppermute | solution.py:393
  14.6 6.0 %collective-permute-start.4 = (f32[5,8,1024]{2,1,0:T(8,128)S(1)}, f32[5,8,1024]{2,1,0:T(8,128)S(1)}, u32[]{:S(2)}, u32[]{:S(2)}) collective-permute-start(f32[5,8,1024]{2,1,0:T(8,128)S(1)} %get-tuple-element.37.edge_b), channel_id=1, source_target_pairs={{2,4},{4,2},{6,8},{8,6},{10,12},{12,10},{14,0},{0,14},{3,5},{5,3},... | collective-permute-start | bytes 491528 | tf_op jit(solution)/shard_map/ppermute | solution.py:392
  16.2 4.4 %collective-permute-start.5 = (f32[5,8,1024]{2,1,0:T(8,128)S(1)}, f32[5,8,1024]{2,1,0:T(8,128)S(1)}, u32[]{:S(2)}, u32[]{:S(2)}) collective-permute-start(f32[5,8,1024]{2,1,0:T(8,128)S(1)} %get-tuple-element.38.edge_a), channel_id=1, source_target_pairs={{0,2},{2,0},{4,6},{6,4},{8,10},{10,8},{12,14},{14,12},{1,3},{3,1},... | collective-permute-start | bytes 491528 | tf_op jit(solution)/shard_map/ppermute | solution.py:394
  16.2 2.8 %collective-permute-start.3 = (f32[20,1024]{1,0:T(8,128)S(1)}, f32[20,1024]{1,0:T(8,128)S(1)}, u32[]{:S(2)}, u32[]{:S(2)}) collective-permute-start(f32[20,1024]{1,0:T(8,128)S(1)} %get-tuple-element.39), channel_id=1, source_target_pairs={{0,1},{1,0},{2,3},{3,2},{4,5},{5,4},{6,7},{7,6},{8,9},{9,8},{10,11... | collective-permute-start | bytes 245768 | tf_op jit(solution)/shard_map/ppermute | solution.py:393
  19.0 21.5 %copy-start.4 = (f32[1,1,5,10,4]{3,4,2,1,0:T(4,128)S(1)}, f32[1,1,5,10,4]{3,4,2,1,0:T(4,128)}, u32[]{:S(2)}) copy-start(f32[1,1,5,10,4]{3,4,2,1,0:T(4,128)} %param.15) | copy-start | bytes 2404
  19.0 31.4 %copy-start.2 = (s32[4,8,8]{2,1,0:T(8,128)S(1)}, s32[4,8,8]{2,1,0:T(8,128)}, u32[]{:S(2)}) copy-start(s32[4,8,8]{2,1,0:T(8,128)} %owner.1) | copy-start | bytes 3076
  19.0 31.4 %copy-start.3 = (s32[4,8,8]{2,1,0:T(8,128)S(1)}, s32[4,8,8]{2,1,0:T(8,128)}, u32[]{:S(2)}) copy-start(s32[4,8,8]{2,1,0:T(8,128)} %slot.1) | copy-start | bytes 3076
  21.5 34.0 %copy-start.1 = (f32[4,8,5,5,1024]{4,1,3,2,0:T(8,128)S(1)}, f32[4,8,5,5,1024]{4,1,3,2,0:T(8,128)}, u32[]{:S(2)}) copy-start(f32[4,8,5,5,1024]{4,1,3,2,0:T(8,128)} %param.10) | copy-start | bytes 9830404
  35.4 5.1 %collective-permute-start.6 = (f32[4,640]{1,0:T(4,128)S(1)}, f32[4,640]{1,0:T(4,128)S(1)}, u32[]{:S(2)}, u32[]{:S(2)}) collective-permute-start(f32[4,640]{1,0:T(4,128)S(1)} %shard_map.89.own), channel_id=1, source_target_pairs={{0,1},{1,0},{2,3},{3,2},{4,5},{5,4},{6,7},{7,6},{8,9},{9,8},{10,11... | collective-permute-start | bytes 30728 | tf_op jit(solution)/shard_map/ppermute | solution.py:455
  51.0 6.7 %collective-permute-start.8 = (f32[5,8,1024]{2,1,0:T(8,128)S(1)}, f32[5,8,1024]{2,1,0:T(8,128)S(1)}, u32[]{:S(2)}, u32[]{:S(2)}) collective-permute-start(f32[5,8,1024]{2,1,0:T(8,128)S(1)} %get-tuple-element.48), channel_id=1, source_target_pairs={{2,4},{4,2},{6,8},{8,6},{10,12},{12,10},{14,0},{0,14},{3,5},{5,3},... | collective-permute-start | bytes 491528 | tf_op jit(solution)/shard_map/ppermute | solution.py:392
  52.6 5.2 %collective-permute-start.9 = (f32[5,8,1024]{2,1,0:T(8,128)S(1)}, f32[5,8,1024]{2,1,0:T(8,128)S(1)}, u32[]{:S(2)}, u32[]{:S(2)}) collective-permute-start(f32[5,8,1024]{2,1,0:T(8,128)S(1)} %get-tuple-element.49), channel_id=1, source_target_pairs={{0,2},{2,0},{4,6},{6,4},{8,10},{10,8},{12,14},{14,12},{1,3},{3,1},... | collective-permute-start | bytes 491528 | tf_op jit(solution)/shard_map/ppermute | solution.py:394
  52.6 3.0 %collective-permute-start.7 = (f32[20,1024]{1,0:T(8,128)S(1)}, f32[20,1024]{1,0:T(8,128)S(1)}, u32[]{:S(2)}, u32[]{:S(2)}) collective-permute-start(f32[20,1024]{1,0:T(8,128)S(1)} %get-tuple-element.44), channel_id=1, source_target_pairs={{0,1},{1,0},{2,3},{3,2},{4,5},{5,4},{6,7},{7,6},{8,9},{9,8},{10,11... | collective-permute-start | bytes 245768 | tf_op jit(solution)/shard_map/ppermute | solution.py:393

commit v6 on v5

--- a/solution.py
+++ b/solution.py
@@ -23,7 +23,7 @@
     return pltpu.with_memory_space_constraint(array, pltpu.HBM)
 
 
-def call(kernel, outs, args, places=None, out_places=None, scratch=(), aliases=None):
+def call(kernel, outs, args, places=None, out_places=None, scratch=()):
     size = 2 * sum(math.prod(a.shape) for a in (*args, *outs))
     return pl.pallas_call(
         kernel,
@@ -31,7 +31,6 @@
         in_specs=places or [VMEM] * len(args),
         out_specs=out_places or [VMEM] * len(outs),
         scratch_shapes=scratch,
-        input_output_aliases=aliases or {},
         cost_estimate=pl.CostEstimate(flops=size, bytes_accessed=size, transcendentals=0),
         compiler_params=pltpu.CompilerParams(vmem_limit_bytes=8 * 2**20),
     )(*args)
@@ -100,20 +99,45 @@
     return jnp.concatenate(hot, axis=0)
 
 
-def first_kernel(
-    wall_in, span_in, owner_in, slot_in, rhs_in, jinv_in,
-    rhs, jinv, splat, onehot_t, first, edge_a, edge_b, edge_w,
+def first_edge_kernel(rhs_in, jinv_in, edge_a, edge_b, rhs, jinv, sems):
+    _, plane_a, plane_b, _ = position()
+    outer = ((plane_b, edge_b), (plane_a, edge_a))
+    copies = [
+        pltpu.make_async_copy(source.at[plane], here.at[m], sems.at[n, m])
+        for m, (plane, _) in enumerate(outer)
+        for n, (source, here) in enumerate(((rhs_in, rhs), (jinv_in, jinv)))
+    ]
+    for copy in copies:
+        copy.start()
+    for m, (_, edge) in enumerate(outer):
+        copies[2 * m].wait()
+        copies[2 * m + 1].wait()
+
+        def body(lanes, m=m, edge=edge):
+            swept = sweep(jinv, m, lanes, [rhs[m, k, :, lanes] for k in range(5)])
+            for k in range(5):
+                edge[k, :, lanes] = swept[k]
+
+        for_lanes(body, rhs.shape[-1])
+
+
+def first_inner_kernel(
+    wall_in, span_in, owner_in, slot_in, rhs_in, jinv_in, edge_b, edge_a,
+    rhs, jinv, first, splat, onehot_t, edge_w,
     wall, span, owner, slot, raw, small_sems, sems,
 ):
     small = [
         pltpu.make_async_copy(source, here, small_sems.at[n])
-        for n, (source, here) in enumerate(
-            ((wall_in, wall), (span_in, span), (owner_in, owner), (slot_in, slot), (rhs_in, rhs))
-        )
+        for n, (source, here) in enumerate(((wall_in, wall), (span_in, span), (owner_in, owner), (slot_in, slot)))
     ]
-    slabs = [pltpu.make_async_copy(jinv_in.at[s], jinv.at[s], sems.at[s]) for s in range(4)]
-    for copy in small + slabs:
+    small.append(pltpu.make_async_copy(rhs_in, rhs, small_sems.at[4]))
+    slabs = {s: pltpu.make_async_copy(jinv_in.at[s], jinv.at[s], sems.at[s]) for s in (1, 2, 0, 3)}
+    for copy in (*small, *slabs.values()):
         copy.start()
+    even, _, _, row = position()
+    for k in range(5):
+        first[0, k] = jnp.where(even, edge_b[k], edge_a[k])
+        first[3, k] = jnp.where(even, edge_a[k], edge_b[k])
     small[0].wait()
     small[1].wait()
     for which, coupling in enumerate((wall, span)):
@@ -123,9 +147,8 @@
     small[2].wait()
     small[3].wait()
     onehot_t[...] = hot_rows(owner, slot, rhs.shape[-1] // LANES).T[: onehot_t.shape[0]]
-    _, plane_a, plane_b, row = position()
     small[4].wait()
-    for s in range(4):
+    for s in (1, 2):
         slabs[s].wait()
 
         def body(lanes, s=s):
@@ -134,12 +157,12 @@
                 first[s, k, :, lanes] = swept[k]
 
         for_lanes(body, rhs.shape[-1])
+    for s in range(4):
         for k in range(5):
             raw[k, s, :] = first[s, k, row, :]
-    for k in range(5):
-        edge_a[k] = first[plane_a, k]
-        edge_b[k] = first[plane_b, k]
     wall_rows(splat, raw, edge_w)
+    slabs[0].wait()
+    slabs[3].wait()
 
 
 def local_apply(splat, planes, jac, lanes, s):
@@ -165,15 +188,20 @@
     ]
 
 
-def first_residual_kernel(splat, first, rhs, jac, rest):
-    def body(lanes):
-        planes = [[first[n, k, :, lanes] for k in range(5)] for n in range(4)]
-        for s in range(4):
+def first_residual_kernel(splat, first, rhs, jac_in, rest, jac, sems):
+    copies = [pltpu.make_async_copy(jac_in.at[s], jac.at[s], sems.at[s]) for s in range(4)]
+    for copy in copies:
+        copy.start()
+    for s in range(4):
+
+        def body(lanes, s=s):
+            planes = [[first[n, k, :, lanes] for k in range(5)] if abs(n - s) < 2 else None for n in range(4)]
             applied = local_apply(splat, planes, jac, lanes, s)
             for k in range(5):
                 rest[s, k, :, lanes] = rhs[s, k, :, lanes] - applied[k]
 
-    for_lanes(body, rhs.shape[-1])
+        copies[s].wait()
+        for_lanes(body, rhs.shape[-1])
 
 
 def second_local_kernel(first, rest, halo_w, jinv, inner):
@@ -321,7 +349,11 @@
     wall_rows(splat, raw, edge_w)
 
 
-def final_residual_kernel(splat, fix, jac, rest):
+def final_residual_kernel(splat, fix, jac, base_in, late_in, rest, base, late, sems):
+    loads = [pltpu.make_async_copy(base_in, base, sems.at[0]), pltpu.make_async_copy(late_in, late, sems.at[1])]
+    for load in loads:
+        load.start()
+
     def body(lanes):
         planes = [[fix[n, k, :, lanes] for k in range(5)] for n in range(4)]
         for s in range(4):
@@ -330,22 +362,15 @@
                 rest[s, k, :, lanes] = -applied[k]
 
     for_lanes(body, fix.shape[-1])
-
-
-def final_local_kernel(fix, rest, halo_w, jinv, base_in, late_in, out, inner, base, late, sems):
+    for load in loads:
+        load.wait()
+
+
+def final_local_kernel(fix, rest, halo_w, jinv, base, late, inner):
     row = position()[3]
-    loads = [
-        pltpu.make_async_copy(base_in.at[pl.ds(1, 2)], base.at[pl.ds(1, 2)], sems.at[0]),
-        pltpu.make_async_copy(late_in, late, sems.at[1]),
-        pltpu.make_async_copy(base_in.at[0], base.at[0], sems.at[2]),
-        pltpu.make_async_copy(base_in.at[3], base.at[3], sems.at[3]),
-    ]
-    for load in loads:
-        load.start()
-    stores = []
-    for s in (1, 2, 0, 3):
-
-        def body(lanes, s=s):
+
+    def body(lanes):
+        for s in range(4):
             known = with_wall(rest, halo_w, s, lanes, row)
             if s in (0, 3):
                 known = [known[k] + late[s // 3, k, :, lanes] for k in range(5)]
@@ -353,25 +378,15 @@
             for k in range(5):
                 inner[s, k, :, lanes] = (base[s, k, :, lanes] + fix[s, k, :, lanes]) + swept[k]
 
-        if s == 1:
-            loads[0].wait()
-        if s == 0:
-            for load in loads[1:]:
-                load.wait()
-        for_lanes(body, fix.shape[-1])
-        if s in (1, 2):
-            stores.append(pltpu.make_async_copy(inner.at[s], out.at[s], sems.at[3 + s]))
-            stores[-1].start()
-    for store in stores:
-        store.wait()
-
-
-def final_edge_kernel(splat, inner, halo_b, halo_a, jinv, out_in, out, edges, sems):
-    del out_in
+    for_lanes(body, fix.shape[-1])
+
+
+def final_edge_kernel(splat, inner, halo_b, halo_a, jinv, out, edges, sems):
     _, plane_a, plane_b, _ = position()
     real = inside()
-    stores = []
-    for n, (plane, halo, there) in enumerate(((plane_a, halo_a, None), (plane_b, halo_b, real))):
+    stores = [pltpu.make_async_copy(inner.at[pl.ds(1, 2)], out.at[pl.ds(1, 2)], sems.at[2])]
+    stores[0].start()
+    for n, (plane, halo, there) in enumerate(((plane_b, halo_b, real), (plane_a, halo_a, None))):
 
         def body(lanes, n=n, plane=plane, halo=halo, there=there):
             swept = sweep(jinv, plane, lanes, beyond_span(splat, halo, lanes, there))
@@ -409,14 +424,19 @@
     aggregates, columns = owners * slots, 5 * LANES
     chunks = shaped(owners, slots, columns)
 
-    rhs, jinv, splat, onehot_t, first, a, b, w = call(
-        first_kernel,
-        [
-            field, matrices, shaped(2, 5, 5, 8, LANES), shaped(aggregates, block_owner.size),
-            field, plane, plane, edge,
-        ],
-        [in_hbm(x) for x in (wall_coupling, span_coupling, block_owner, block_slot, rhs, jinv_in)],
-        places=[HBM] * 6,
+    rhs_in = rhs
+    a, b = call(
+        first_edge_kernel,
+        [plane, plane],
+        [rhs_in, in_hbm(jinv_in)],
+        places=[HBM] * 2,
+        scratch=[outer, pltpu.VMEM((2, *jinv_in.shape[1:]), F32), pltpu.SemaphoreType.DMA((2, 2))],
+    )
+    rhs, jinv, first, splat, onehot_t, w = call(
+        first_inner_kernel,
+        [field, matrices, field, shaped(2, 5, 5, 8, LANES), shaped(aggregates, block_owner.size), edge],
+        [*(in_hbm(x) for x in (wall_coupling, span_coupling, block_owner, block_slot, rhs_in, jinv_in)), b, a],
+        places=[HBM] * 6 + [VMEM] * 2,
         scratch=[
             pltpu.SMEM(wall_coupling.shape, F32),
             pltpu.SMEM(span_coupling.shape, F32),
@@ -427,9 +447,14 @@
             pltpu.SemaphoreType.DMA((4,)),
         ],
     )
-    jac, b = lax.optimization_barrier((jac_in, b))
     halo_a, halo_b, halo_w = exchange(a, b, w)
-    [rest] = call(first_residual_kernel, [field], [splat, first, rhs, jac])
+    rest, jac = call(
+        first_residual_kernel,
+        [field, matrices],
+        [splat, first, rhs, in_hbm(jac_in)],
+        places=[VMEM] * 3 + [HBM],
+        scratch=[pltpu.SemaphoreType.DMA((4,))],
+    )
     [inner] = call(second_local_kernel, [field], [first, rest, halo_w, jinv])
     a, b, w = call(
         second_edge_kernel, [plane, plane, edge], [splat, inner, halo_b, halo_a, jinv], scratch=[raw]
@@ -462,23 +487,20 @@
         scratch=[pltpu.VMEM((aggregates, columns), F32), raw],
     )
     halo_a, halo_b, halo_w = exchange(a, b, w)
-    [rest] = call(final_residual_kernel, [field], [splat, fix, jac])
-    out, inner = call(
-        final_local_kernel,
-        [field_out, field],
-        [fix, rest, halo_w, jinv_in, in_hbm(base), in_hbm(late)],
-        places=[VMEM] * 4 + [HBM] * 2,
-        out_places=[HBM, VMEM],
-        scratch=[pltpu.VMEM(rhs.shape, F32), outer, pltpu.SemaphoreType.DMA((6,))],
-    )
+    rest, base, late = call(
+        final_residual_kernel,
+        [field, field, shaped(2, *plane.shape)],
+        [splat, fix, jac_in, in_hbm(base), in_hbm(late)],
+        places=[VMEM] * 3 + [HBM] * 2,
+        scratch=[pltpu.SemaphoreType.DMA((2,))],
+    )
+    [inner] = call(final_local_kernel, [field], [fix, rest, halo_w, jinv_in, base, late])
     [out] = call(
         final_edge_kernel,
         [field_out],
-        [splat, inner, halo_b, halo_a, jinv_in, in_hbm(out)],
-        places=[VMEM] * 5 + [HBM],
+        [splat, inner, halo_b, halo_a, jinv_in],
         out_places=[HBM],
-        scratch=[outer, pltpu.SemaphoreType.DMA((2,))],
-        aliases={5: 0},
+        scratch=[outer, pltpu.SemaphoreType.DMA((3,))],
     )
     return out.transpose(0, 2, 1, 3)
 

time: 59 us -> 58.9 us (level)
  starting transfers between devices: 18.8 us -> 17.2 us
  Pallas kernels: 13.3 us -> 14.9 us
    pallas_call x13 -> x14, Pallas kernels: 13.3 us -> 14.9 us  [call(): pl.pallas_call(kernel, out_shape=outs, in_specs=places or [VMEM] * len(ar...]
    ppermute x1, starting transfers between devices: 4.25 us -> 2.61 us  [local(): theirs = lax.ppermute(mine, 'wall', [(0, 1), (1, 0)])]
    ppermute x3, starting transfers between devices: 0.01 us -> 1 us  [exchange(): halo_a = lax.ppermute(edge_a, 'span', even)]
    ppermute x3, starting transfers between devices: 4.83 us -> 3.95 us  [exchange(): halo_w = lax.ppermute(edge_w, 'wall', [(0, 1), (1, 0)])]
    ppermute x3, waiting for transfers between devices: 0.83 us -> 0.23 us  [exchange(): halo_a = lax.ppermute(edge_a, 'span', even)]
  transfers between devices with their start and end apart: 10 -> 10, of which waited for: 3 -> 3; matrix products, arithmetic and copies ran while one was open for 0% -> 0% of each run, Pallas kernels for 12% -> 17%
where the time goes in v6:
time: 58.9 us; the launch traced here: 58.4 us
  blocking collectives  23.6 us (40%)
  starting transfers between devices  17.2 us (29%)
  Pallas kernels  14.9 us (25%)
  waiting for transfers between devices  2.48 us (4%)
    pallas_call x14, Pallas kernels, call(): pl.pallas_call(kernel, out_shape=outs, in_specs=places or [VMEM] * len(ar...  14.9 us
    all_to_all x1, blocking collectives, local(): lax.all_to_all(partial, 'patch', split_axis=0, concat_axis=0, tiled=True)  13.9 us
    all_to_all x1, blocking collectives, local(): lax.all_to_all(reply, 'patch', split_axis=0, concat_axis=0, tiled=True)  9.77 us
    ppermute x3, starting transfers between devices, exchange(): halo_b = lax.ppermute(edge_b, 'span', odd)  9.6 us
    ppermute x3, starting transfers between devices, exchange(): halo_w = lax.ppermute(edge_w, 'wall', [(0, 1), (1, 0)])  3.95 us
    ppermute x1, starting transfers between devices, local(): theirs = lax.ppermute(mine, 'wall', [(0, 1), (1, 0)])  2.61 us
    ppermute x3, waiting for transfers between devices, exchange(): halo_b = lax.ppermute(edge_b, 'span', odd)  1.41 us
  transfers between devices with their start and end apart: 10, of which 3 were waited for; matrix products, arithmetic and copies ran while one was open for 0% of the time, Pallas kernels for 17%

profile of v6, /device:TPU:1, one launch (start us, length us, event | category | flops | bytes accessed | tf_op | source)
XLA Modules:
  0.0 58.4 jit_solution(16909254493679170628)
XLA Ops:
  0.0 1.7 %shard_map.82 = (f32[5,8,1024]{2,1,0:T(8,128)S(1)}, f32[5,8,1024]{2,1,0:T(8,128)S(1)}) custom-call(f32[4,5,8,1024]{3,2,1,0:T(8,128)} %bitcast.14, f32[4,5,5,8,1024]{4,3,2,1,0:T(8,128)} %bitcast.7), custom_call_target="tpu_custom_call" | custom-call | flops 2129920 | bytes 2129920 | tf_op jit(solution)/shard_map/pallas_call | solution.py:28
  1.7 6.5 %collective-permute-start.1 = (f32[5,8,1024]{2,1,0:T(8,128)S(1)}, f32[5,8,1024]{2,1,0:T(8,128)S(1)}, u32[]{:S(2)}, u32[]{:S(2)}) collective-permute-start(f32[5,8,1024]{2,1,0:T(8,128)S(1)} %get-tuple-element.29.edge_b), channel_id=1, source_target_pairs={{2,4},{4,2},{6,8},{8,6},{10,12},{12,10},{14,0},{0,14},{3,5},{5,3},... | collective-permute-start | bytes 491528 | tf_op jit(solution)/shard_map/ppermute | solution.py:407
  8.2 2.4 %shard_map.83 = (f32[4,5,8,1024]{3,2,1,0:T(8,128)S(1)}, f32[4,5,5,8,1024]{4,3,2,1,0:T(8,128)S(1)}, f32[4,5,8,1024]{3,2,1,0:T(8,128)S(1)}, f32[2,5,5,8,128]{4,3,2...) custom-call(f32[5,5]{1,0:T(8,128)} %wall_in.1, f32[5,5]{1,0:T(8,128)} %span_in.1, s32[4,8,8]{2,1,0:T(8,128)} %owner.1, ...), custom_call_target="tpu_custom_call" | custom-call | flops 4600932 | bytes 4600932 | tf_op jit(solution)/shard_map/pallas_call | solution.py:28
  10.6 1.0 %collective-permute-start = (f32[20,1024]{1,0:T(8,128)S(1)}, f32[20,1024]{1,0:T(8,128)S(1)}, u32[]{:S(2)}, u32[]{:S(2)}) collective-permute-start(f32[20,1024]{1,0:T(8,128)S(1)} %get-tuple-element.35), channel_id=1, source_target_pairs={{0,1},{1,0},{2,3},{3,2},{4,5},{5,4},{6,7},{7,6},{8,9},{9,8},{10,11... | collective-permute-start | bytes 245768 | tf_op jit(solution)/shard_map/ppermute | solution.py:408
  11.7 2.4 %shard_map.84 = (f32[4,5,8,1024]{3,2,1,0:T(8,128)S(1)}, f32[4,5,5,8,1024]{4,3,2,1,0:T(8,128)S(1)}) custom-call(f32[2,5,5,8,128]{4,3,2,1,0:T(8,128)S(1)} %get-tuple-element.31.splat, f32[4,5,8,1024]{3,2,1,0:T(8,128)S(1)} %get-tuple-element.32.first, f32[4,5,8,1024]{3,2,1,0:T(8,128)S(1)} %get-tuple-element.33.rhs, f32[4,5,5,8,1024]{4,3,2,1,0:T(8,128)} %bitcast.11), custom_call_target="tpu_custom_call" | custom-call | flops 4362240 | bytes 4362240 | tf_op jit(solution)/shard_map/pallas_call | solution.py:28
  14.1 0.7 %shard_map.85.inner = f32[4,5,8,1024]{3,2,1,0:T(8,128)S(1)} custom-call(f32[4,5,8,1024]{3,2,1,0:T(8,128)S(1)} %get-tuple-element.32.first, f32[4,5,8,1024]{3,2,1,0:T(8,128)S(1)} %get-tuple-element.34.rest, f32[20,1024]{1,0:T(8,128)S(1)} %collective-permute-done.halo_w, f32[4,5,5,8,1024]{4,3,2,1,0:T(8,128)S(1)} %get-tuple-element.36.jinv), custom_call_target="tpu_custom_call" | custom-call | flops 2662400 | bytes 2662400 | tf_op jit(solution)/shard_map/pallas_call | solution.py:28
  14.8 0.5 shard_map.86
  15.3 1.8 %collective-permute-start.4 = (f32[5,8,1024]{2,1,0:T(8,128)S(1)}, f32[5,8,1024]{2,1,0:T(8,128)S(1)}, u32[]{:S(2)}, u32[]{:S(2)}) collective-permute-start(f32[5,8,1024]{2,1,0:T(8,128)S(1)} %get-tuple-element.37.edge_b), channel_id=1, source_target_pairs={{2,4},{4,2},{6,8},{8,6},{10,12},{12,10},{14,0},{0,14},{3,5},{5,3},... | collective-permute-start | bytes 491528 | tf_op jit(solution)/shard_map/ppermute | solution.py:407
  17.1 0.7 %collective-permute-start.5 = (f32[5,8,1024]{2,1,0:T(8,128)S(1)}, f32[5,8,1024]{2,1,0:T(8,128)S(1)}, u32[]{:S(2)}, u32[]{:S(2)}) collective-permute-start(f32[5,8,1024]{2,1,0:T(8,128)S(1)} %get-tuple-element.38.edge_a), channel_id=1, source_target_pairs={{0,2},{2,0},{4,6},{6,4},{8,10},{10,8},{12,14},{14,12},{1,3},{3,1},... | collective-permute-start | bytes 491528 | tf_op jit(solution)/shard_map/ppermute | solution.py:409
  17.8 0.6 collective-permute-start.3
  18.4 0.9 %shard_map.87.rest = f32[4,5,8,1024]{3,2,1,0:T(8,128)S(1)} custom-call(f32[2,5,5,8,128]{4,3,2,1,0:T(8,128)S(1)} %get-tuple-element.31.splat, f32[4,5,8,1024]{3,2,1,0:T(8,128)S(1)} %shard_map.85.inner, f32[5,8,1024]{2,1,0:T(8,128)S(1)} %get-tuple-element.37.edge_b, f32[5,8,1024]{2,1,0:T(8,128)S(1)} %get-tuple-element.38.edge_a, ...), custom_call_target="tpu_custom_call" | custom-call | flops 2887680 | bytes 2887680 | tf_op jit(solution)/shard_map/pallas_call | solution.py:28
  19.4 1.6 %shard_map.88 = (f32[64,640]{1,0:T(8,128)S(1)}, f32[4,5,8,1024]{3,2,1,0:T(8,128)}) custom-call(f32[4,5,8,1024]{3,2,1,0:T(8,128)S(1)} %shard_map.85.inner, f32[5,8,1024]{2,1,0:T(8,128)S(1)} %get-tuple-element.37.edge_b, f32[5,8,1024]{2,1,0:T(8,128)S(1)} %get-tuple-element.38.edge_a, f32[4,5,8,1024]{3,2,1,0:T(8,128)S(1)} %shard_map.87.rest, ...), custom_call_target="tpu_custom_call" | custom-call | flops 2940928 | bytes 2940928 | tf_op jit(solution)/shard_map/pallas_call | solution.py:28
  20.9 1.4 %collective-permute-done.4.halo_b = f32[5,8,1024]{2,1,0:T(8,128)S(1)} collective-permute-done((f32[5,8,1024]{2,1,0:T(8,128)S(1)}, f32[5,8,1024]{2,1,0:T(8,128)S(1)}, u32[]{:S(2)}, u32[]{:S(2)}) %collective-permute-start.4) | collective-permute-done | bytes 163872 | tf_op jit(solution)/shard_map/ppermute | solution.py:407
  22.6 0.9 %shard_map.89 = (f32[16,4,640]{2,1,0:T(4,128)S(1)}, f32[2,5,8,1024]{3,2,1,0:T(8,128)}) custom-call(f32[2,5,5,8,128]{4,3,2,1,0:T(8,128)S(1)} %get-tuple-element.31.splat, f32[64,640]{1,0:T(8,128)S(1)} %get-tuple-element.42.inner, f32[5,8,1024]{2,1,0:T(8,128)S(1)} %collective-permute-done.4.halo_b, f32[5,8,1024]{2,1,0:T(8,128)S(1)} %collective-permute-done.5.halo_a, ...), custom_call_target="tpu_custom_call" | custom-call | flops 626688 | bytes 626688 | tf_op jit(solution)/shard_map/pallas_call | solution.py:28
  23.5 13.9 %all_to_all.10.received = f32[16,4,640]{2,1,0:T(4,128)S(1)} all-to-all(f32[16,4,640]{2,1,0:T(4,128)S(1)} %get-tuple-element.43), channel_id=1, replica_groups=mesh['patch'=16,'span'=8,'wall'=2] {'patch'}, dimensions={0} | all-to-all | bytes 327680 | tf_op jit(solution)/shard_map/all_to_all | solution.py:478
  37.4 2.6 %collective-permute-start.6 = (f32[4,640]{1,0:T(4,128)S(1)}, f32[4,640]{1,0:T(4,128)S(1)}, u32[]{:S(2)}, u32[]{:S(2)}) collective-permute-start(f32[4,640]{1,0:T(4,128)S(1)} %shard_map.90.own), channel_id=1, source_target_pairs={{0,1},{1,0},{2,3},{3,2},{4,5},{5,4},{6,7},{7,6},{8,9},{9,8},{10,11... | collective-permute-start | bytes 30728 | tf_op jit(solution)/shard_map/ppermute | solution.py:480
  40.0 0.8 %collective-permute-done.6.other = f32[4,640]{1,0:T(4,128)S(1)} collective-permute-done((f32[4,640]{1,0:T(4,128)S(1)}, f32[4,640]{1,0:T(4,128)S(1)}, u32[]{:S(2)}, u32[]{:S(2)}) %collective-permute-start.6) | collective-permute-done | bytes 10272 | tf_op jit(solution)/shard_map/ppermute | solution.py:480
  41.0 9.8 %all_to_all.11.fixes = f32[16,4,640]{2,1,0:T(4,128)S(1)} all-to-all(f32[16,4,640]{2,1,0:T(4,128)S(1)} %shard_map.91), channel_id=1, replica_groups=mesh['patch'=16,'span'=8,'wall'=2] {'patch'}, dimensions={0} | all-to-all | bytes 327680 | tf_op jit(solution)/shard_map/all_to_all | solution.py:482
  50.7 0.6 %shard_map.92 = (f32[4,5,8,1024]{3,2,1,0:T(8,128)S(1)}, f32[5,8,1024]{2,1,0:T(8,128)S(1)}, f32[5,8,1024]{2,1,0:T(8,128)S(1)}, f32[20,1024]{1,0:T(8,128)S(1)}) custom-call(f32[2,5,5,8,128]{4,3,2,1,0:T(8,128)S(1)} %get-tuple-element.31.splat, s32[4,8,8]{2,1,0:T(8,128)S(1)} %copy-done.2, s32[4,8,8]{2,1,0:T(8,128)S(1)} %copy-done.3, ...), custom_call_target="tpu_custom_call" | custom-call | flops 717824 | bytes 717824 | tf_op jit(solution)/shard_map/pallas_call | solution.py:28
  51.3 1.3 %collective-permute-start.8 = (f32[5,8,1024]{2,1,0:T(8,128)S(1)}, f32[5,8,1024]{2,1,0:T(8,128)S(1)}, u32[]{:S(2)}, u32[]{:S(2)}) collective-permute-start(f32[5,8,1024]{2,1,0:T(8,128)S(1)} %get-tuple-element.51), channel_id=1, source_target_pairs={{2,4},{4,2},{6,8},{8,6},{10,12},{12,10},{14,0},{0,14},{3,5},{5,3},... | collective-permute-start | bytes 491528 | tf_op jit(solution)/shard_map/ppermute | solution.py:407
  52.9 2.3 %collective-permute-start.7 = (f32[20,1024]{1,0:T(8,128)S(1)}, f32[20,1024]{1,0:T(8,128)S(1)}, u32[]{:S(2)}, u32[]{:S(2)}) collective-permute-start(f32[20,1024]{1,0:T(8,128)S(1)} %get-tuple-element.48), channel_id=1, source_target_pairs={{0,1},{1,0},{2,3},{3,2},{4,5},{5,4},{6,7},{7,6},{8,9},{9,8},{10,11... | collective-permute-start | bytes 245768 | tf_op jit(solution)/shard_map/ppermute | solution.py:408
  55.2 1.2 %shard_map.93 = (f32[4,5,8,1024]{3,2,1,0:T(8,128)S(1)}, f32[4,5,8,1024]{3,2,1,0:T(8,128)S(1)}, f32[2,5,8,1024]{3,2,1,0:T(8,128)S(1)}) custom-call(f32[2,5,5,8,128]{4,3,2,1,0:T(8,128)S(1)} %get-tuple-element.31.splat, f32[4,5,8,1024]{3,2,1,0:T(8,128)S(1)} %get-tuple-element.44.fix, f32[4,5,5,8,1024]{4,3,2,1,0:T(8,128)S(1)} %bitcast.12, ...), custom_call_target="tpu_custom_call" | custom-call | flops 3379200 | bytes 3379200 | tf_op jit(solution)/shard_map/pallas_call | solution.py:28
  56.5 0.8 %shard_map.94.inner = f32[4,5,8,1024]{3,2,1,0:T(8,128)S(1)} custom-call(f32[4,5,8,1024]{3,2,1,0:T(8,128)S(1)} %get-tuple-element.44.fix, f32[4,5,8,1024]{3,2,1,0:T(8,128)S(1)} %get-tuple-element.47.rest, f32[20,1024]{1,0:T(8,128)S(1)} %collective-permute-done.7.halo_w, f32[4,5,5,8,1024]{4,3,2,1,0:T(8,128)S(1)} %bitcast.9, ...), custom_call_target="tpu_custom_call" | custom-call | flops 3153920 | bytes 3153920 | tf_op jit(solution)/shard_map/pallas_call | solution.py:28
  57.3 1.1 %shard_map.95 = f32[4,5,8,1024]{3,2,1,0:T(8,128)} custom-call(f32[2,5,5,8,128]{4,3,2,1,0:T(8,128)S(1)} %get-tuple-element.31.splat, f32[4,5,8,1024]{3,2,1,0:T(8,128)S(1)} %shard_map.94.inner, f32[5,8,1024]{2,1,0:T(8,128)S(1)} %collective-permute-done.8.halo_b, f32[5,8,1024]{2,1,0:T(8,128)S(1)} %collective-permute-done.9.halo_a, ...), custom_call_target="tpu_custom_call" | custom-call | flops 2560000 | bytes 2560000 | tf_op jit(solution)/shard_map/pallas_call | solution.py:28
  (22 shorter events, 0.7 us)
Async XLA Ops:
  1.7 13.0 %collective-permute-start.1 = (f32[5,8,1024]{2,1,0:T(8,128)S(1)}, f32[5,8,1024]{2,1,0:T(8,128)S(1)}, u32[]{:S(2)}, u32[]{:S(2)}) collective-permute-start(f32[5,8,1024]{2,1,0:T(8,128)S(1)} %get-tuple-element.29.edge_b), channel_id=1, source_target_pairs={{2,4},{4,2},{6,8},{8,6},{10,12},{12,10},{14,0},{0,14},{3,5},{5,3},... | collective-permute-start | bytes 491528 | tf_op jit(solution)/shard_map/ppermute | solution.py:407
  8.2 6.6 %collective-permute-start.2 = (f32[5,8,1024]{2,1,0:T(8,128)S(1)}, f32[5,8,1024]{2,1,0:T(8,128)S(1)}, u32[]{:S(2)}, u32[]{:S(2)}) collective-permute-start(f32[5,8,1024]{2,1,0:T(8,128)S(1)} %get-tuple-element.30.edge_a), channel_id=1, source_target_pairs={{0,2},{2,0},{4,6},{6,4},{8,10},{10,8},{12,14},{14,12},{1,3},{3,1},... | collective-permute-start | bytes 491528 | tf_op jit(solution)/shard_map/ppermute | solution.py:409
  10.6 3.5 %collective-permute-start = (f32[20,1024]{1,0:T(8,128)S(1)}, f32[20,1024]{1,0:T(8,128)S(1)}, u32[]{:S(2)}, u32[]{:S(2)}) collective-permute-start(f32[20,1024]{1,0:T(8,128)S(1)} %get-tuple-element.35), channel_id=1, source_target_pairs={{0,1},{1,0},{2,3},{3,2},{4,5},{5,4},{6,7},{7,6},{8,9},{9,8},{10,11... | collective-permute-start | bytes 245768 | tf_op jit(solution)/shard_map/ppermute | solution.py:408
  15.3 7.1 %collective-permute-start.4 = (f32[5,8,1024]{2,1,0:T(8,128)S(1)}, f32[5,8,1024]{2,1,0:T(8,128)S(1)}, u32[]{:S(2)}, u32[]{:S(2)}) collective-permute-start(f32[5,8,1024]{2,1,0:T(8,128)S(1)} %get-tuple-element.37.edge_b), channel_id=1, source_target_pairs={{2,4},{4,2},{6,8},{8,6},{10,12},{12,10},{14,0},{0,14},{3,5},{5,3},... | collective-permute-start | bytes 491528 | tf_op jit(solution)/shard_map/ppermute | solution.py:407
  17.1 5.5 %collective-permute-start.5 = (f32[5,8,1024]{2,1,0:T(8,128)S(1)}, f32[5,8,1024]{2,1,0:T(8,128)S(1)}, u32[]{:S(2)}, u32[]{:S(2)}) collective-permute-start(f32[5,8,1024]{2,1,0:T(8,128)S(1)} %get-tuple-element.38.edge_a), channel_id=1, source_target_pairs={{0,2},{2,0},{4,6},{6,4},{8,10},{10,8},{12,14},{14,12},{1,3},{3,1},... | collective-permute-start | bytes 491528 | tf_op jit(solution)/shard_map/ppermute | solution.py:409
  17.8 1.5 %collective-permute-start.3 = (f32[20,1024]{1,0:T(8,128)S(1)}, f32[20,1024]{1,0:T(8,128)S(1)}, u32[]{:S(2)}, u32[]{:S(2)}) collective-permute-start(f32[20,1024]{1,0:T(8,128)S(1)} %get-tuple-element.40), channel_id=1, source_target_pairs={{0,1},{1,0},{2,3},{3,2},{4,5},{5,4},{6,7},{7,6},{8,9},{9,8},{10,11... | collective-permute-start | bytes 245768 | tf_op jit(solution)/shard_map/ppermute | solution.py:408
  19.3 21.5 %copy-start.4 = (f32[1,1,5,10,4]{3,4,2,1,0:T(4,128)S(1)}, f32[1,1,5,10,4]{3,4,2,1,0:T(4,128)}, u32[]{:S(2)}) copy-start(f32[1,1,5,10,4]{3,4,2,1,0:T(4,128)} %param.15) | copy-start | bytes 2404
  19.3 31.4 %copy-start.2 = (s32[4,8,8]{2,1,0:T(8,128)S(1)}, s32[4,8,8]{2,1,0:T(8,128)}, u32[]{:S(2)}) copy-start(s32[4,8,8]{2,1,0:T(8,128)} %owner.1) | copy-start | bytes 3076
  19.4 31.4 %copy-start.3 = (s32[4,8,8]{2,1,0:T(8,128)S(1)}, s32[4,8,8]{2,1,0:T(8,128)}, u32[]{:S(2)}) copy-start(s32[4,8,8]{2,1,0:T(8,128)} %slot.1) | copy-start | bytes 3076
  19.4 35.9 %copy-start.1 = (f32[4,8,5,5,1024]{4,1,3,2,0:T(8,128)S(1)}, f32[4,8,5,5,1024]{4,1,3,2,0:T(8,128)}, u32[]{:S(2)}) copy-start(f32[4,8,5,5,1024]{4,1,3,2,0:T(8,128)} %param.9) | copy-start | bytes 9830404
  23.5 33.0 %copy-start = (f32[4,8,5,5,1024]{4,1,3,2,0:T(8,128)S(1)}, f32[4,8,5,5,1024]{4,1,3,2,0:T(8,128)}, u32[]{:S(2)}) copy-start(f32[4,8,5,5,1024]{4,1,3,2,0:T(8,128)} %param.10) | copy-start | bytes 9830404
  37.4 3.4 %collective-permute-start.6 = (f32[4,640]{1,0:T(4,128)S(1)}, f32[4,640]{1,0:T(4,128)S(1)}, u32[]{:S(2)}, u32[]{:S(2)}) collective-permute-start(f32[4,640]{1,0:T(4,128)S(1)} %shard_map.90.own), channel_id=1, source_target_pairs={{0,1},{1,0},{2,3},{3,2},{4,5},{5,4},{6,7},{7,6},{8,9},{9,8},{10,11... | collective-permute-start | bytes 30728 | tf_op jit(solution)/shard_map/ppermute | solution.py:480
  51.3 5.9 %collective-permute-start.8 = (f32[5,8,1024]{2,1,0:T(8,128)S(1)}, f32[5,8,1024]{2,1,0:T(8,128)S(1)}, u32[]{:S(2)}, u32[]{:S(2)}) collective-permute-start(f32[5,8,1024]{2,1,0:T(8,128)S(1)} %get-tuple-element.51), channel_id=1, source_target_pairs={{2,4},{4,2},{6,8},{8,6},{10,12},{12,10},{14,0},{0,14},{3,5},{5,3},... | collective-permute-start | bytes 491528 | tf_op jit(solution)/shard_map/ppermute | solution.py:407
  52.6 4.7 %collective-permute-start.9 = (f32[5,8,1024]{2,1,0:T(8,128)S(1)}, f32[5,8,1024]{2,1,0:T(8,128)S(1)}, u32[]{:S(2)}, u32[]{:S(2)}) collective-permute-start(f32[5,8,1024]{2,1,0:T(8,128)S(1)} %get-tuple-element.52), channel_id=1, source_target_pairs={{0,2},{2,0},{4,6},{6,4},{8,10},{10,8},{12,14},{14,12},{1,3},{3,1},... | collective-permute-start | bytes 491528 | tf_op jit(solution)/shard_map/ppermute | solution.py:409
  52.9 3.5 %collective-permute-start.7 = (f32[20,1024]{1,0:T(8,128)S(1)}, f32[20,1024]{1,0:T(8,128)S(1)}, u32[]{:S(2)}, u32[]{:S(2)}) collective-permute-start(f32[20,1024]{1,0:T(8,128)S(1)} %get-tuple-element.48), channel_id=1, source_target_pairs={{0,1},{1,0},{2,3},{3,2},{4,5},{5,4},{6,7},{7,6},{8,9},{9,8},{10,11... | collective-permute-start | bytes 245768 | tf_op jit(solution)/shard_map/ppermute | solution.py:408

commit v7 on v6

--- a/solution.py
+++ b/solution.py
@@ -123,16 +123,16 @@
 
 def first_inner_kernel(
     wall_in, span_in, owner_in, slot_in, rhs_in, jinv_in, edge_b, edge_a,
-    rhs, jinv, first, splat, onehot_t, edge_w,
-    wall, span, owner, slot, raw, small_sems, sems,
+    rhs, first, splat, onehot_t, edge_w,
+    wall, span, owner, slot, raw, jinv, small_sems, sems,
 ):
     small = [
         pltpu.make_async_copy(source, here, small_sems.at[n])
         for n, (source, here) in enumerate(((wall_in, wall), (span_in, span), (owner_in, owner), (slot_in, slot)))
     ]
     small.append(pltpu.make_async_copy(rhs_in, rhs, small_sems.at[4]))
-    slabs = {s: pltpu.make_async_copy(jinv_in.at[s], jinv.at[s], sems.at[s]) for s in (1, 2, 0, 3)}
-    for copy in (*small, *slabs.values()):
+    slabs = [pltpu.make_async_copy(jinv_in.at[1 + m], jinv.at[m], sems.at[m]) for m in range(2)]
+    for copy in small + slabs:
         copy.start()
     even, _, _, row = position()
     for k in range(5):
@@ -149,10 +149,10 @@
     onehot_t[...] = hot_rows(owner, slot, rhs.shape[-1] // LANES).T[: onehot_t.shape[0]]
     small[4].wait()
     for s in (1, 2):
-        slabs[s].wait()
+        slabs[s - 1].wait()
 
         def body(lanes, s=s):
-            swept = sweep(jinv, s, lanes, [rhs[s, k, :, lanes] for k in range(5)])
+            swept = sweep(jinv, s - 1, lanes, [rhs[s, k, :, lanes] for k in range(5)])
             for k in range(5):
                 first[s, k, :, lanes] = swept[k]
 
@@ -161,8 +161,6 @@
         for k in range(5):
             raw[k, s, :] = first[s, k, row, :]
     wall_rows(splat, raw, edge_w)
-    slabs[0].wait()
-    slabs[3].wait()
 
 
 def local_apply(splat, planes, jac, lanes, s):
@@ -188,20 +186,15 @@
     ]
 
 
-def first_residual_kernel(splat, first, rhs, jac_in, rest, jac, sems):
-    copies = [pltpu.make_async_copy(jac_in.at[s], jac.at[s], sems.at[s]) for s in range(4)]
-    for copy in copies:
-        copy.start()
-    for s in range(4):
-
-        def body(lanes, s=s):
-            planes = [[first[n, k, :, lanes] for k in range(5)] if abs(n - s) < 2 else None for n in range(4)]
+def first_residual_kernel(splat, first, rhs, jac, rest):
+    def body(lanes):
+        planes = [[first[n, k, :, lanes] for k in range(5)] for n in range(4)]
+        for s in range(4):
             applied = local_apply(splat, planes, jac, lanes, s)
             for k in range(5):
                 rest[s, k, :, lanes] = rhs[s, k, :, lanes] - applied[k]
 
-        copies[s].wait()
-        for_lanes(body, rhs.shape[-1])
+    for_lanes(body, rhs.shape[-1])
 
 
 def second_local_kernel(first, rest, halo_w, jinv, inner):
@@ -417,7 +410,6 @@
     inv = coarse_inv[0, 0].transpose(0, 2, 1)
     field, plane, edge = shaped(*rhs.shape), shaped(*rhs.shape[1:]), shaped(20, rhs.shape[-1])
     field_out = pltpu.HBM(rhs.shape, F32)
-    matrices = shaped(*jac_in.shape)
     outer = pltpu.VMEM((2, *rhs.shape[1:]), F32)
     raw = pltpu.VMEM(rhs.shape[1:], F32)
     owners, slots = lax.axis_size("patch"), coarse_inv.shape[-1]
@@ -432,9 +424,9 @@
         places=[HBM] * 2,
         scratch=[outer, pltpu.VMEM((2, *jinv_in.shape[1:]), F32), pltpu.SemaphoreType.DMA((2, 2))],
     )
-    rhs, jinv, first, splat, onehot_t, w = call(
+    rhs, first, splat, onehot_t, w = call(
         first_inner_kernel,
-        [field, matrices, field, shaped(2, 5, 5, 8, LANES), shaped(aggregates, block_owner.size), edge],
+        [field, field, shaped(2, 5, 5, 8, LANES), shaped(aggregates, block_owner.size), edge],
         [*(in_hbm(x) for x in (wall_coupling, span_coupling, block_owner, block_slot, rhs_in, jinv_in)), b, a],
         places=[HBM] * 6 + [VMEM] * 2,
         scratch=[
@@ -443,28 +435,23 @@
             pltpu.VMEM(block_owner.shape, jnp.int32),
             pltpu.VMEM(block_owner.shape, jnp.int32),
             raw,
+            pltpu.VMEM((2, *jinv_in.shape[1:]), F32),
             pltpu.SemaphoreType.DMA((5,)),
-            pltpu.SemaphoreType.DMA((4,)),
+            pltpu.SemaphoreType.DMA((2,)),
         ],
     )
     halo_a, halo_b, halo_w = exchange(a, b, w)
-    rest, jac = call(
-        first_residual_kernel,
-        [field, matrices],
-        [splat, first, rhs, in_hbm(jac_in)],
-        places=[VMEM] * 3 + [HBM],
-        scratch=[pltpu.SemaphoreType.DMA((4,))],
-    )
-    [inner] = call(second_local_kernel, [field], [first, rest, halo_w, jinv])
+    [rest] = call(first_residual_kernel, [field], [splat, first, rhs, jac_in])
+    [inner] = call(second_local_kernel, [field], [first, rest, halo_w, jinv_in])
     a, b, w = call(
-        second_edge_kernel, [plane, plane, edge], [splat, inner, halo_b, halo_a, jinv], scratch=[raw]
+        second_edge_kernel, [plane, plane, edge], [splat, inner, halo_b, halo_a, jinv_in], scratch=[raw]
     )
     halo_a, halo_b, halo_w = exchange(a, b, w)
-    [rest] = call(second_residual_kernel, [field], [splat, inner, b, a, rhs, jac])
+    [rest] = call(second_residual_kernel, [field], [splat, inner, b, a, rhs, jac_in])
     partial, base = call(
         defect_local_kernel,
         [shaped(aggregates, columns), field_out],
-        [inner, b, a, rest, halo_w, jinv, onehot_t],
+        [inner, b, a, rest, halo_w, jinv_in, onehot_t],
         out_places=[VMEM, HBM],
         scratch=[pltpu.VMEM(rhs.shape, F32), pltpu.VMEM(rhs.shape, F32), pltpu.SemaphoreType.DMA((1,))],
     )

time: 58.9 us -> 57.5 us (0.976)
  Pallas kernels: 14.9 us -> 13.1 us
  starting transfers between devices: 17.2 us -> 18.8 us
  waiting for transfers between devices: 2.48 us -> 1.04 us
    pallas_call x14, Pallas kernels: 14.9 us -> 13.1 us  [call(): pl.pallas_call(kernel, out_shape=outs, in_specs=places or [VMEM] * len(ar...]
    ppermute x3, waiting for transfers between devices: 1.41 us -> 0.01 us  [exchange(): halo_b = lax.ppermute(edge_b, 'span', odd)]
    ppermute x1, starting transfers between devices: 2.61 us -> 3.78 us  [local(): theirs = lax.ppermute(mine, 'wall', [(0, 1), (1, 0)])]
  transfers between devices with their start and end apart: 10 -> 10, of which waited for: 3 -> 3; matrix products, arithmetic and copies ran while one was open for 0% -> 0% of each run, Pallas kernels for 17% -> 14%
where the time goes in v7:
time: 57.5 us; the launch traced here: 56.5 us
  blocking collectives  23.3 us (41%)
  starting transfers between devices  18.8 us (33%)
  Pallas kernels  13.1 us (23%)
  waiting for transfers between devices  1.04 us (2%)
    all_to_all x1, blocking collectives, local(): lax.all_to_all(partial, 'patch', split_axis=0, concat_axis=0, tiled=True)  13.6 us
    pallas_call x14, Pallas kernels, call(): pl.pallas_call(kernel, out_shape=outs, in_specs=places or [VMEM] * len(ar...  13.1 us
    ppermute x3, starting transfers between devices, exchange(): halo_b = lax.ppermute(edge_b, 'span', odd)  9.78 us
    all_to_all x1, blocking collectives, local(): lax.all_to_all(reply, 'patch', split_axis=0, concat_axis=0, tiled=True)  9.77 us
    ppermute x3, starting transfers between devices, exchange(): halo_w = lax.ppermute(edge_w, 'wall', [(0, 1), (1, 0)])  4.52 us
    ppermute x1, starting transfers between devices, local(): theirs = lax.ppermute(mine, 'wall', [(0, 1), (1, 0)])  3.78 us
  transfers between devices with their start and end apart: 10, of which 3 were waited for; matrix products, arithmetic and copies ran while one was open for 0% of the time, Pallas kernels for 14%

profile of v7, /device:TPU:1, one launch (start us, length us, event | category | flops | bytes accessed | tf_op | source)
XLA Modules:
  0.0 56.5 jit_solution(6195402688799298224)
XLA Ops:
  0.0 1.9 %shard_map.82 = (f32[5,8,1024]{2,1,0:T(8,128)S(1)}, f32[5,8,1024]{2,1,0:T(8,128)S(1)}) custom-call(f32[4,5,8,1024]{3,2,1,0:T(8,128)} %bitcast.18, f32[4,5,5,8,1024]{4,3,2,1,0:T(8,128)} %bitcast.7), custom_call_target="tpu_custom_call" | custom-call | flops 2129920 | bytes 2129920 | tf_op jit(solution)/shard_map/pallas_call | solution.py:28
  1.9 6.5 %collective-permute-start.1 = (f32[5,8,1024]{2,1,0:T(8,128)S(1)}, f32[5,8,1024]{2,1,0:T(8,128)S(1)}, u32[]{:S(2)}, u32[]{:S(2)}) collective-permute-start(f32[5,8,1024]{2,1,0:T(8,128)S(1)} %get-tuple-element.26.edge_b), channel_id=1, source_target_pairs={{2,4},{4,2},{6,8},{8,6},{10,12},{12,10},{14,0},{0,14},{3,5},{5,3},... | collective-permute-start | bytes 491528 | tf_op jit(solution)/shard_map/ppermute | solution.py:400
  8.4 1.9 %shard_map.83 = (f32[4,5,8,1024]{3,2,1,0:T(8,128)S(1)}, f32[4,5,8,1024]{3,2,1,0:T(8,128)S(1)}, f32[2,5,5,8,128]{4,3,2,1,0:T(8,128)S(1)}, f32[64,256]{1,0:T(8,128)S(1)}, f32[20,1024]{1,0:T(8,128)S(1)}) custom-call(f32[5,5]{1,0:T(8,128)} %wall_in.1, f32[5,5]{1,0:T(8,128)} %span_in.1, s32[4,8,8]{2,1,0:T(8,128)} %owner.1, s32[4,8,8]{2,1,0:T(8,128)} %slot.1, ...), custom_call_target="tpu_custom_call" | custom-call | flops 2962532 | bytes 2962532 | tf_op jit(solution)/shard_map/pallas_call | solution.py:28
  10.3 1.0 %collective-permute-start = (f32[20,1024]{1,0:T(8,128)S(1)}, f32[20,1024]{1,0:T(8,128)S(1)}, u32[]{:S(2)}, u32[]{:S(2)}) collective-permute-start(f32[20,1024]{1,0:T(8,128)S(1)} %get-tuple-element.31), channel_id=1, source_target_pairs={{0,1},{1,0},{2,3},{3,2},{4,5},{5,4},{6,7},{7,6},{8,9},{9,8},{10,11... | collective-permute-start | bytes 245768 | tf_op jit(solution)/shard_map/ppermute | solution.py:401
  11.4 0.9 %shard_map.84.rest = f32[4,5,8,1024]{3,2,1,0:T(8,128)S(1)} custom-call(f32[2,5,5,8,128]{4,3,2,1,0:T(8,128)S(1)} %get-tuple-element.28.splat, f32[4,5,8,1024]{3,2,1,0:T(8,128)S(1)} %get-tuple-element.29.first, f32[4,5,8,1024]{3,2,1,0:T(8,128)S(1)} %get-tuple-element.30.rhs, f32[4,5,5,8,1024]{4,3,2,1,0:T(8,128)S(1)} %bitcast.14), custom_call_target="tpu_custom_call" | custom-call | flops 2723840 | bytes 2723840 | tf_op jit(solution)/shard_map/pallas_call | solution.py:28
  12.3 0.7 %shard_map.85.inner = f32[4,5,8,1024]{3,2,1,0:T(8,128)S(1)} custom-call(f32[4,5,8,1024]{3,2,1,0:T(8,128)S(1)} %get-tuple-element.29.first, f32[4,5,8,1024]{3,2,1,0:T(8,128)S(1)} %shard_map.84.rest, f32[20,1024]{1,0:T(8,128)S(1)} %collective-permute-done.halo_w, f32[4,5,5,8,1024]{4,3,2,1,0:T(8,128)S(1)} %bitcast.9), custom_call_target="tpu_custom_call" | custom-call | flops 2662400 | bytes 2662400 | tf_op jit(solution)/shard_map/pallas_call | solution.py:28
  13.1 0.4 shard_map.86
  13.6 1.8 %collective-permute-start.4 = (f32[5,8,1024]{2,1,0:T(8,128)S(1)}, f32[5,8,1024]{2,1,0:T(8,128)S(1)}, u32[]{:S(2)}, u32[]{:S(2)}) collective-permute-start(f32[5,8,1024]{2,1,0:T(8,128)S(1)} %get-tuple-element.32.edge_b), channel_id=1, source_target_pairs={{2,4},{4,2},{6,8},{8,6},{10,12},{12,10},{14,0},{0,14},{3,5},{5,3},... | collective-permute-start | bytes 491528 | tf_op jit(solution)/shard_map/ppermute | solution.py:400
  15.3 0.7 %collective-permute-start.5 = (f32[5,8,1024]{2,1,0:T(8,128)S(1)}, f32[5,8,1024]{2,1,0:T(8,128)S(1)}, u32[]{:S(2)}, u32[]{:S(2)}) collective-permute-start(f32[5,8,1024]{2,1,0:T(8,128)S(1)} %get-tuple-element.33.edge_a), channel_id=1, source_target_pairs={{0,2},{2,0},{4,6},{6,4},{8,10},{10,8},{12,14},{14,12},{1,3},{3,1},... | collective-permute-start | bytes 491528 | tf_op jit(solution)/shard_map/ppermute | solution.py:402
  16.0 1.4 %collective-permute-start.3 = (f32[20,1024]{1,0:T(8,128)S(1)}, f32[20,1024]{1,0:T(8,128)S(1)}, u32[]{:S(2)}, u32[]{:S(2)}) collective-permute-start(f32[20,1024]{1,0:T(8,128)S(1)} %get-tuple-element.34), channel_id=1, source_target_pairs={{0,1},{1,0},{2,3},{3,2},{4,5},{5,4},{6,7},{7,6},{8,9},{9,8},{10,11... | collective-permute-start | bytes 245768 | tf_op jit(solution)/shard_map/ppermute | solution.py:401
  17.5 0.9 %shard_map.87.rest = f32[4,5,8,1024]{3,2,1,0:T(8,128)S(1)} custom-call(f32[2,5,5,8,128]{4,3,2,1,0:T(8,128)S(1)} %get-tuple-element.28.splat, f32[4,5,8,1024]{3,2,1,0:T(8,128)S(1)} %shard_map.85.inner, f32[5,8,1024]{2,1,0:T(8,128)S(1)} %get-tuple-element.32.edge_b, f32[5,8,1024]{2,1,0:T(8,128)S(1)} %get-tuple-element.33.edge_a, ...), custom_call_target="tpu_custom_call" | custom-call | flops 2887680 | bytes 2887680 | tf_op jit(solution)/shard_map/pallas_call | solution.py:28
  18.5 1.6 %shard_map.88 = (f32[64,640]{1,0:T(8,128)S(1)}, f32[4,5,8,1024]{3,2,1,0:T(8,128)}) custom-call(f32[4,5,8,1024]{3,2,1,0:T(8,128)S(1)} %shard_map.85.inner, f32[5,8,1024]{2,1,0:T(8,128)S(1)} %get-tuple-element.32.edge_b, f32[5,8,1024]{2,1,0:T(8,128)S(1)} %get-tuple-element.33.edge_a, f32[4,5,8,1024]{3,2,1,0:T(8,128)S(1)} %shard_map.87.rest, ...), custom_call_target="tpu_custom_call" | custom-call | flops 2940928 | bytes 2940928 | tf_op jit(solution)/shard_map/pallas_call | solution.py:28
  20.1 0.9 %shard_map.89 = (f32[16,4,640]{2,1,0:T(4,128)S(1)}, f32[2,5,8,1024]{3,2,1,0:T(8,128)}) custom-call(f32[2,5,5,8,128]{4,3,2,1,0:T(8,128)S(1)} %get-tuple-element.28.splat, f32[64,640]{1,0:T(8,128)S(1)} %get-tuple-element.36.inner, f32[5,8,1024]{2,1,0:T(8,128)S(1)} %collective-permute-done.4.halo_b, f32[5,8,1024]{2,1,0:T(8,128)S(1)} %collective-permute-done.5.halo_a, ...), custom_call_target="tpu_custom_call" | custom-call | flops 626688 | bytes 626688 | tf_op jit(solution)/shard_map/pallas_call | solution.py:28
  21.0 13.6 %all_to_all.10.received = f32[16,4,640]{2,1,0:T(4,128)S(1)} all-to-all(f32[16,4,640]{2,1,0:T(4,128)S(1)} %get-tuple-element.37), channel_id=1, replica_groups=mesh['patch'=16,'span'=8,'wall'=2] {'patch'}, dimensions={0} | all-to-all | bytes 327680 | tf_op jit(solution)/shard_map/all_to_all | solution.py:465
  34.6 3.8 %collective-permute-start.6 = (f32[4,640]{1,0:T(4,128)S(1)}, f32[4,640]{1,0:T(4,128)S(1)}, u32[]{:S(2)}, u32[]{:S(2)}) collective-permute-start(f32[4,640]{1,0:T(4,128)S(1)} %shard_map.90.own), channel_id=1, source_target_pairs={{0,1},{1,0},{2,3},{3,2},{4,5},{5,4},{6,7},{7,6},{8,9},{9,8},{10,11... | collective-permute-start | bytes 30728 | tf_op jit(solution)/shard_map/ppermute | solution.py:467
  38.3 0.8 %collective-permute-done.6.other = f32[4,640]{1,0:T(4,128)S(1)} collective-permute-done((f32[4,640]{1,0:T(4,128)S(1)}, f32[4,640]{1,0:T(4,128)S(1)}, u32[]{:S(2)}, u32[]{:S(2)}) %collective-permute-start.6) | collective-permute-done | bytes 10272 | tf_op jit(solution)/shard_map/ppermute | solution.py:467
  39.2 0.2 shard_map.91
  39.3 9.8 %all_to_all.11.fixes = f32[16,4,640]{2,1,0:T(4,128)S(1)} all-to-all(f32[16,4,640]{2,1,0:T(4,128)S(1)} %shard_map.91), channel_id=1, replica_groups=mesh['patch'=16,'span'=8,'wall'=2] {'patch'}, dimensions={0} | all-to-all | bytes 327680 | tf_op jit(solution)/shard_map/all_to_all | solution.py:469
  49.1 0.6 %shard_map.92 = (f32[4,5,8,1024]{3,2,1,0:T(8,128)S(1)}, f32[5,8,1024]{2,1,0:T(8,128)S(1)}, f32[5,8,1024]{2,1,0:T(8,128)S(1)}, f32[20,1024]{1,0:T(8,128)S(1)}) custom-call(f32[2,5,5,8,128]{4,3,2,1,0:T(8,128)S(1)} %get-tuple-element.28.splat, s32[4,8,8]{2,1,0:T(8,128)S(1)} %copy-done.2, s32[4,8,8]{2,1,0:T(8,128)S(1)} %copy-done.3, ...), custom_call_target="tpu_custom_call" | custom-call | flops 717824 | bytes 717824 | tf_op jit(solution)/shard_map/pallas_call | solution.py:28
  49.7 1.5 %collective-permute-start.8 = (f32[5,8,1024]{2,1,0:T(8,128)S(1)}, f32[5,8,1024]{2,1,0:T(8,128)S(1)}, u32[]{:S(2)}, u32[]{:S(2)}) collective-permute-start(f32[5,8,1024]{2,1,0:T(8,128)S(1)} %get-tuple-element.45), channel_id=1, source_target_pairs={{2,4},{4,2},{6,8},{8,6},{10,12},{12,10},{14,0},{0,14},{3,5},{5,3},... | collective-permute-start | bytes 491528 | tf_op jit(solution)/shard_map/ppermute | solution.py:400
  51.3 2.1 %collective-permute-start.7 = (f32[20,1024]{1,0:T(8,128)S(1)}, f32[20,1024]{1,0:T(8,128)S(1)}, u32[]{:S(2)}, u32[]{:S(2)}) collective-permute-start(f32[20,1024]{1,0:T(8,128)S(1)} %get-tuple-element.42), channel_id=1, source_target_pairs={{0,1},{1,0},{2,3},{3,2},{4,5},{5,4},{6,7},{7,6},{8,9},{9,8},{10,11... | collective-permute-start | bytes 245768 | tf_op jit(solution)/shard_map/ppermute | solution.py:401
  53.3 1.2 %shard_map.93 = (f32[4,5,8,1024]{3,2,1,0:T(8,128)S(1)}, f32[4,5,8,1024]{3,2,1,0:T(8,128)S(1)}, f32[2,5,8,1024]{3,2,1,0:T(8,128)S(1)}) custom-call(f32[2,5,5,8,128]{4,3,2,1,0:T(8,128)S(1)} %get-tuple-element.28.splat, f32[4,5,8,1024]{3,2,1,0:T(8,128)S(1)} %get-tuple-element.38.fix, f32[4,5,5,8,1024]{4,3,2,1,0:T(8,128)S(1)} %bitcast.16, ...), custom_call_target="tpu_custom_call" | custom-call | flops 3379200 | bytes 3379200 | tf_op jit(solution)/shard_map/pallas_call | solution.py:28
  54.5 0.8 %shard_map.94.inner = f32[4,5,8,1024]{3,2,1,0:T(8,128)S(1)} custom-call(f32[4,5,8,1024]{3,2,1,0:T(8,128)S(1)} %get-tuple-element.38.fix, f32[4,5,8,1024]{3,2,1,0:T(8,128)S(1)} %get-tuple-element.41.rest, f32[20,1024]{1,0:T(8,128)S(1)} %collective-permute-done.7.halo_w, f32[4,5,5,8,1024]{4,3,2,1,0:T(8,128)S(1)} %bitcast.12, ...), custom_call_target="tpu_custom_call" | custom-call | flops 3153920 | bytes 3153920 | tf_op jit(solution)/shard_map/pallas_call | solution.py:28
  55.4 1.1 %shard_map.95 = f32[4,5,8,1024]{3,2,1,0:T(8,128)} custom-call(f32[2,5,5,8,128]{4,3,2,1,0:T(8,128)S(1)} %get-tuple-element.28.splat, f32[4,5,8,1024]{3,2,1,0:T(8,128)S(1)} %shard_map.94.inner, f32[5,8,1024]{2,1,0:T(8,128)S(1)} %collective-permute-done.8.halo_b, f32[5,8,1024]{2,1,0:T(8,128)S(1)} %collective-permute-done.9.halo_a, ...), custom_call_target="tpu_custom_call" | custom-call | flops 2560000 | bytes 2560000 | tf_op jit(solution)/shard_map/pallas_call | solution.py:28
  (22 shorter events, 0.3 us)
Async XLA Ops:
  0.0 11.4 %copy-start.1 = (f32[4,8,5,5,1024]{4,1,3,2,0:T(8,128)S(1)}, f32[4,8,5,5,1024]{4,1,3,2,0:T(8,128)}, u32[]{:S(2)}) copy-start(f32[4,8,5,5,1024]{4,1,3,2,0:T(8,128)} %param.9) | copy-start | bytes 9830404
  1.9 11.1 %collective-permute-start.1 = (f32[5,8,1024]{2,1,0:T(8,128)S(1)}, f32[5,8,1024]{2,1,0:T(8,128)S(1)}, u32[]{:S(2)}, u32[]{:S(2)}) collective-permute-start(f32[5,8,1024]{2,1,0:T(8,128)S(1)} %get-tuple-element.26.edge_b), channel_id=1, source_target_pairs={{2,4},{4,2},{6,8},{8,6},{10,12},{12,10},{14,0},{0,14},{3,5},{5,3},... | collective-permute-start | bytes 491528 | tf_op jit(solution)/shard_map/ppermute | solution.py:400
  8.4 4.7 %collective-permute-start.2 = (f32[5,8,1024]{2,1,0:T(8,128)S(1)}, f32[5,8,1024]{2,1,0:T(8,128)S(1)}, u32[]{:S(2)}, u32[]{:S(2)}) collective-permute-start(f32[5,8,1024]{2,1,0:T(8,128)S(1)} %get-tuple-element.27.edge_a), channel_id=1, source_target_pairs={{0,2},{2,0},{4,6},{6,4},{8,10},{10,8},{12,14},{14,12},{1,3},{3,1},... | collective-permute-start | bytes 491528 | tf_op jit(solution)/shard_map/ppermute | solution.py:402
  10.3 2.0 %copy-start = (f32[4,8,5,5,1024]{4,1,3,2,0:T(8,128)S(1)}, f32[4,8,5,5,1024]{4,1,3,2,0:T(8,128)}, u32[]{:S(2)}) copy-start(f32[4,8,5,5,1024]{4,1,3,2,0:T(8,128)} %param.10) | copy-start | bytes 9830404
  10.3 2.0 %collective-permute-start = (f32[20,1024]{1,0:T(8,128)S(1)}, f32[20,1024]{1,0:T(8,128)S(1)}, u32[]{:S(2)}, u32[]{:S(2)}) collective-permute-start(f32[20,1024]{1,0:T(8,128)S(1)} %get-tuple-element.31), channel_id=1, source_target_pairs={{0,1},{1,0},{2,3},{3,2},{4,5},{5,4},{6,7},{7,6},{8,9},{9,8},{10,11... | collective-permute-start | bytes 245768 | tf_op jit(solution)/shard_map/ppermute | solution.py:401
  13.6 6.5 %collective-permute-start.4 = (f32[5,8,1024]{2,1,0:T(8,128)S(1)}, f32[5,8,1024]{2,1,0:T(8,128)S(1)}, u32[]{:S(2)}, u32[]{:S(2)}) collective-permute-start(f32[5,8,1024]{2,1,0:T(8,128)S(1)} %get-tuple-element.32.edge_b), channel_id=1, source_target_pairs={{2,4},{4,2},{6,8},{8,6},{10,12},{12,10},{14,0},{0,14},{3,5},{5,3},... | collective-permute-start | bytes 491528 | tf_op jit(solution)/shard_map/ppermute | solution.py:400
  15.3 4.7 %collective-permute-start.5 = (f32[5,8,1024]{2,1,0:T(8,128)S(1)}, f32[5,8,1024]{2,1,0:T(8,128)S(1)}, u32[]{:S(2)}, u32[]{:S(2)}) collective-permute-start(f32[5,8,1024]{2,1,0:T(8,128)S(1)} %get-tuple-element.33.edge_a), channel_id=1, source_target_pairs={{0,2},{2,0},{4,6},{6,4},{8,10},{10,8},{12,14},{14,12},{1,3},{3,1},... | collective-permute-start | bytes 491528 | tf_op jit(solution)/shard_map/ppermute | solution.py:402
  16.0 2.4 %collective-permute-start.3 = (f32[20,1024]{1,0:T(8,128)S(1)}, f32[20,1024]{1,0:T(8,128)S(1)}, u32[]{:S(2)}, u32[]{:S(2)}) collective-permute-start(f32[20,1024]{1,0:T(8,128)S(1)} %get-tuple-element.34), channel_id=1, source_target_pairs={{0,1},{1,0},{2,3},{3,2},{4,5},{5,4},{6,7},{7,6},{8,9},{9,8},{10,11... | collective-permute-start | bytes 245768 | tf_op jit(solution)/shard_map/ppermute | solution.py:401
  18.4 20.8 %copy-start.4 = (f32[1,1,5,10,4]{3,4,2,1,0:T(4,128)S(1)}, f32[1,1,5,10,4]{3,4,2,1,0:T(4,128)}, u32[]{:S(2)}) copy-start(f32[1,1,5,10,4]{3,4,2,1,0:T(4,128)} %param.15) | copy-start | bytes 2404
  18.4 30.7 %copy-start.2 = (s32[4,8,8]{2,1,0:T(8,128)S(1)}, s32[4,8,8]{2,1,0:T(8,128)}, u32[]{:S(2)}) copy-start(s32[4,8,8]{2,1,0:T(8,128)} %owner.1) | copy-start | bytes 3076
  18.4 30.7 %copy-start.3 = (s32[4,8,8]{2,1,0:T(8,128)S(1)}, s32[4,8,8]{2,1,0:T(8,128)}, u32[]{:S(2)}) copy-start(s32[4,8,8]{2,1,0:T(8,128)} %slot.1) | copy-start | bytes 3076
  34.6 4.6 %collective-permute-start.6 = (f32[4,640]{1,0:T(4,128)S(1)}, f32[4,640]{1,0:T(4,128)S(1)}, u32[]{:S(2)}, u32[]{:S(2)}) collective-permute-start(f32[4,640]{1,0:T(4,128)S(1)} %shard_map.90.own), channel_id=1, source_target_pairs={{0,1},{1,0},{2,3},{3,2},{4,5},{5,4},{6,7},{7,6},{8,9},{9,8},{10,11... | collective-permute-start | bytes 30728 | tf_op jit(solution)/shard_map/ppermute | solution.py:467
  49.7 5.6 %collective-permute-start.8 = (f32[5,8,1024]{2,1,0:T(8,128)S(1)}, f32[5,8,1024]{2,1,0:T(8,128)S(1)}, u32[]{:S(2)}, u32[]{:S(2)}) collective-permute-start(f32[5,8,1024]{2,1,0:T(8,128)S(1)} %get-tuple-element.45), channel_id=1, source_target_pairs={{2,4},{4,2},{6,8},{8,6},{10,12},{12,10},{14,0},{0,14},{3,5},{5,3},... | collective-permute-start | bytes 491528 | tf_op jit(solution)/shard_map/ppermute | solution.py:400
  51.2 4.2 %collective-permute-start.9 = (f32[5,8,1024]{2,1,0:T(8,128)S(1)}, f32[5,8,1024]{2,1,0:T(8,128)S(1)}, u32[]{:S(2)}, u32[]{:S(2)}) collective-permute-start(f32[5,8,1024]{2,1,0:T(8,128)S(1)} %get-tuple-element.46), channel_id=1, source_target_pairs={{0,2},{2,0},{4,6},{6,4},{8,10},{10,8},{12,14},{14,12},{1,3},{3,1},... | collective-permute-start | bytes 491528 | tf_op jit(solution)/shard_map/ppermute | solution.py:402
  51.3 3.2 %collective-permute-start.7 = (f32[20,1024]{1,0:T(8,128)S(1)}, f32[20,1024]{1,0:T(8,128)S(1)}, u32[]{:S(2)}, u32[]{:S(2)}) collective-permute-start(f32[20,1024]{1,0:T(8,128)S(1)} %get-tuple-element.42), channel_id=1, source_target_pairs={{0,1},{1,0},{2,3},{3,2},{4,5},{5,4},{6,7},{7,6},{8,9},{9,8},{10,11... | collective-permute-start | bytes 245768 | tf_op jit(solution)/shard_map/ppermute | solution.py:401

commit v8 on v7

--- a/solution.py
+++ b/solution.py
@@ -99,45 +99,24 @@
     return jnp.concatenate(hot, axis=0)
 
 
-def first_edge_kernel(rhs_in, jinv_in, edge_a, edge_b, rhs, jinv, sems):
+def first_edge_kernel(
+    wall_in, span_in, owner_in, slot_in, rhs_in, jinv_in,
+    edge_b, edge_a, splat, onehot_t,
+    wall, span, owner, slot, rhs, jinv, small_sems, sems,
+):
     _, plane_a, plane_b, _ = position()
     outer = ((plane_b, edge_b), (plane_a, edge_a))
+    small = [
+        pltpu.make_async_copy(source, here, small_sems.at[n])
+        for n, (source, here) in enumerate(((wall_in, wall), (span_in, span), (owner_in, owner), (slot_in, slot)))
+    ]
     copies = [
         pltpu.make_async_copy(source.at[plane], here.at[m], sems.at[n, m])
         for m, (plane, _) in enumerate(outer)
         for n, (source, here) in enumerate(((rhs_in, rhs), (jinv_in, jinv)))
     ]
-    for copy in copies:
+    for copy in small + copies:
         copy.start()
-    for m, (_, edge) in enumerate(outer):
-        copies[2 * m].wait()
-        copies[2 * m + 1].wait()
-
-        def body(lanes, m=m, edge=edge):
-            swept = sweep(jinv, m, lanes, [rhs[m, k, :, lanes] for k in range(5)])
-            for k in range(5):
-                edge[k, :, lanes] = swept[k]
-
-        for_lanes(body, rhs.shape[-1])
-
-
-def first_inner_kernel(
-    wall_in, span_in, owner_in, slot_in, rhs_in, jinv_in, edge_b, edge_a,
-    rhs, first, splat, onehot_t, edge_w,
-    wall, span, owner, slot, raw, jinv, small_sems, sems,
-):
-    small = [
-        pltpu.make_async_copy(source, here, small_sems.at[n])
-        for n, (source, here) in enumerate(((wall_in, wall), (span_in, span), (owner_in, owner), (slot_in, slot)))
-    ]
-    small.append(pltpu.make_async_copy(rhs_in, rhs, small_sems.at[4]))
-    slabs = [pltpu.make_async_copy(jinv_in.at[1 + m], jinv.at[m], sems.at[m]) for m in range(2)]
-    for copy in small + slabs:
-        copy.start()
-    even, _, _, row = position()
-    for k in range(5):
-        first[0, k] = jnp.where(even, edge_b[k], edge_a[k])
-        first[3, k] = jnp.where(even, edge_a[k], edge_b[k])
     small[0].wait()
     small[1].wait()
     for which, coupling in enumerate((wall, span)):
@@ -147,7 +126,28 @@
     small[2].wait()
     small[3].wait()
     onehot_t[...] = hot_rows(owner, slot, rhs.shape[-1] // LANES).T[: onehot_t.shape[0]]
-    small[4].wait()
+    for m, (_, edge) in enumerate(outer):
+        copies[2 * m].wait()
+        copies[2 * m + 1].wait()
+
+        def body(lanes, m=m, edge=edge):
+            swept = sweep(jinv, m, lanes, [rhs[m, k, :, lanes] for k in range(5)])
+            for k in range(5):
+                edge[k, :, lanes] = swept[k]
+
+        for_lanes(body, rhs.shape[-1])
+
+
+def first_inner_kernel(splat, edge_b, edge_a, rhs_in, jinv_in, rhs, first, edge_w, raw, jinv, sems):
+    whole = pltpu.make_async_copy(rhs_in, rhs, sems.at[2])
+    slabs = [pltpu.make_async_copy(jinv_in.at[1 + m], jinv.at[m], sems.at[m]) for m in range(2)]
+    for copy in (whole, *slabs):
+        copy.start()
+    even, _, _, row = position()
+    for k in range(5):
+        first[0, k] = jnp.where(even, edge_b[k], edge_a[k])
+        first[3, k] = jnp.where(even, edge_a[k], edge_b[k])
+    whole.wait()
     for s in (1, 2):
         slabs[s - 1].wait()
 
@@ -277,20 +277,20 @@
     store.wait()
 
 
-def restrict_kernel(splat, inner, halo_b, halo_a, onehot_t, partial, late_out, late, sems):
+def restrict_kernel(splat, inner, halo_b, halo_a, onehot_t, partial, late_out, sems):
     real = inside()
     at_a = 1 - lax.rem(lax.axis_index("span"), 2)
+    stores = [
+        pltpu.make_async_copy(halo_b, late_out.at[1 - at_a], sems.at[0]),
+        pltpu.make_async_copy(halo_a, late_out.at[at_a], sems.at[1]),
+    ]
+    for store in stores:
+        store.start()
     tiles = halo_a.shape[-1] // LANES
-    stores, parts = [], []
-    for n, (halo, there, at) in enumerate(((halo_b, real, 1 - at_a), (halo_a, None, at_a))):
+    parts = []
+    for halo, there in ((halo_b, real), (halo_a, None)):
         for q in range(tiles):
-            lanes = slice(q * LANES, (q + 1) * LANES)
-            beyond = beyond_span(splat, halo, lanes, there)
-            parts.append(beyond)
-            for k in range(5):
-                late[n, k, :, lanes] = beyond[k]
-        stores.append(pltpu.make_async_copy(late.at[n], late_out.at[at], sems.at[n]))
-        stores[-1].start()
+            parts.append(beyond_span(splat, halo, slice(q * LANES, (q + 1) * LANES), there))
     width = 8 * tiles
     even = at_a == 1
     low, high = onehot_t[:, :width], onehot_t[:, 3 * width :]
@@ -359,14 +359,17 @@
         load.wait()
 
 
-def final_local_kernel(fix, rest, halo_w, jinv, base, late, inner):
+def final_local_kernel(splat, fix, rest, halo_w, jinv, base, late, inner):
     row = position()[3]
+    at, size = lax.axis_index("span"), lax.axis_size("span")
+    there = {0: at > 0, 3: at < size - 1}
 
     def body(lanes):
         for s in range(4):
             known = with_wall(rest, halo_w, s, lanes, row)
             if s in (0, 3):
-                known = [known[k] + late[s // 3, k, :, lanes] for k in range(5)]
+                beyond = beyond_span(splat, late.at[s // 3], lanes, there[s])
+                known = [known[k] + beyond[k] for k in range(5)]
             swept = sweep(jinv, s, lanes, known)
             for k in range(5):
                 inner[s, k, :, lanes] = (base[s, k, :, lanes] + fix[s, k, :, lanes]) + swept[k]
@@ -417,28 +420,28 @@
     chunks = shaped(owners, slots, columns)
 
     rhs_in = rhs
-    a, b = call(
+    b, a, splat, onehot_t = call(
         first_edge_kernel,
-        [plane, plane],
-        [rhs_in, in_hbm(jinv_in)],
-        places=[HBM] * 2,
-        scratch=[outer, pltpu.VMEM((2, *jinv_in.shape[1:]), F32), pltpu.SemaphoreType.DMA((2, 2))],
-    )
-    rhs, first, splat, onehot_t, w = call(
-        first_inner_kernel,
-        [field, field, shaped(2, 5, 5, 8, LANES), shaped(aggregates, block_owner.size), edge],
-        [*(in_hbm(x) for x in (wall_coupling, span_coupling, block_owner, block_slot, rhs_in, jinv_in)), b, a],
-        places=[HBM] * 6 + [VMEM] * 2,
+        [plane, plane, shaped(2, 5, 5, 8, LANES), shaped(aggregates, block_owner.size)],
+        [in_hbm(x) for x in (wall_coupling, span_coupling, block_owner, block_slot, rhs_in, jinv_in)],
+        places=[HBM] * 6,
         scratch=[
             pltpu.SMEM(wall_coupling.shape, F32),
             pltpu.SMEM(span_coupling.shape, F32),
             pltpu.VMEM(block_owner.shape, jnp.int32),
             pltpu.VMEM(block_owner.shape, jnp.int32),
-            raw,
+            outer,
             pltpu.VMEM((2, *jinv_in.shape[1:]), F32),
-            pltpu.SemaphoreType.DMA((5,)),
-            pltpu.SemaphoreType.DMA((2,)),
+            pltpu.SemaphoreType.DMA((4,)),
+            pltpu.SemaphoreType.DMA((2, 2)),
         ],
+    )
+    rhs, first, w = call(
+        first_inner_kernel,
+        [field, field, edge],
+        [splat, b, a, rhs_in, in_hbm(jinv_in)],
+        places=[VMEM] * 3 + [HBM] * 2,
+        scratch=[raw, pltpu.VMEM((2, *jinv_in.shape[1:]), F32), pltpu.SemaphoreType.DMA((3,))],
     )
     halo_a, halo_b, halo_w = exchange(a, b, w)
     [rest] = call(first_residual_kernel, [field], [splat, first, rhs, jac_in])
@@ -460,7 +463,7 @@
         [chunks, pltpu.HBM((2, *plane.shape), F32)],
         [splat, partial, halo_b, halo_a, onehot_t],
         out_places=[VMEM, HBM],
-        scratch=[outer, pltpu.SemaphoreType.DMA((2,))],
+        scratch=[pltpu.SemaphoreType.DMA((2,))],
     )
     received = lax.all_to_all(partial, "patch", split_axis=0, concat_axis=0, tiled=True)
     [mine] = call(sum_kernel, [shaped(slots, columns)], [received])
@@ -481,7 +484,7 @@
         places=[VMEM] * 3 + [HBM] * 2,
         scratch=[pltpu.SemaphoreType.DMA((2,))],
     )
-    [inner] = call(final_local_kernel, [field], [fix, rest, halo_w, jinv_in, base, late])
+    [inner] = call(final_local_kernel, [field], [splat, fix, rest, halo_w, jinv_in, base, late])
     [out] = call(
         final_edge_kernel,
         [field_out],

time: 57.5 us -> 57.6 us (level)
  transfers between devices with their start and end apart: 10 -> 10, of which waited for: 3 -> 2; matrix products, arithmetic and copies ran while one was open for 0% -> 0% of each run, Pallas kernels for 14% -> 14%
where the time goes in v8:
time: 57.6 us; the launch traced here: 56.6 us
  blocking collectives  23.4 us (41%)
  starting transfers between devices  18.8 us (33%)
  Pallas kernels  13.1 us (23%)
  waiting for transfers between devices  1.06 us (2%)
    all_to_all x1, blocking collectives, local(): lax.all_to_all(partial, 'patch', split_axis=0, concat_axis=0, tiled=True)  13.6 us
    pallas_call x14, Pallas kernels, call(): pl.pallas_call(kernel, out_shape=outs, in_specs=places or [VMEM] * len(ar...  13.1 us
    all_to_all x1, blocking collectives, local(): lax.all_to_all(reply, 'patch', split_axis=0, concat_axis=0, tiled=True)  9.77 us
    ppermute x3, starting transfers between devices, exchange(): halo_b = lax.ppermute(edge_b, 'span', odd)  9.72 us
    ppermute x3, starting transfers between devices, exchange(): halo_w = lax.ppermute(edge_w, 'wall', [(0, 1), (1, 0)])  4.53 us
    ppermute x1, starting transfers between devices, local(): theirs = lax.ppermute(mine, 'wall', [(0, 1), (1, 0)])  3.84 us
  transfers between devices with their start and end apart: 10, of which 2 were waited for; matrix products, arithmetic and copies ran while one was open for 0% of the time, Pallas kernels for 14%

profile of v8, /device:TPU:1, one launch (start us, length us, event | category | flops | bytes accessed | tf_op | source)
XLA Modules:
  0.0 56.6 jit_solution(10086164384379417739)
XLA Ops:
  0.0 1.9 %shard_map.82 = (f32[5,8,1024]{2,1,0:T(8,128)S(1)}, f32[5,8,1024]{2,1,0:T(8,128)S(1)}, f32[2,5,5,8,128]{4,3,2,1,0:T(8,128)S(1)}, f32[64,256]{1,0:T(8,128)S(1)}) custom-call(f32[5,5]{1,0:T(8,128)} %wall_in.1, f32[5,5]{1,0:T(8,128)} %span_in.1, s32[4,8,8]{2,1,0:T(8,128)} %owner.1, s32[4,8,8]{2,1,0:T(8,128)} %slot.1, f32[4,5,8,1024]{3,2,1,0:T(8,128)} %bitcast.18, ...), custom_call_target="tpu_custom_call" | custom-call | flops 2266212 | bytes 2266212 | tf_op jit(solution)/shard_map/pallas_call | solution.py:28
  2.0 6.5 %collective-permute-start.1 = (f32[5,8,1024]{2,1,0:T(8,128)S(1)}, f32[5,8,1024]{2,1,0:T(8,128)S(1)}, u32[]{:S(2)}, u32[]{:S(2)}) collective-permute-start(f32[5,8,1024]{2,1,0:T(8,128)S(1)} %get-tuple-element.27.edge_b), channel_id=1, source_target_pairs={{2,4},{4,2},{6,8},{8,6},{10,12},{12,10},{14,0},{0,14},{3,5},{5,3},... | collective-permute-start | bytes 491528 | tf_op jit(solution)/shard_map/ppermute | solution.py:403
  8.4 1.9 %shard_map.83 = (f32[4,5,8,1024]{3,2,1,0:T(8,128)S(1)}, f32[4,5,8,1024]{3,2,1,0:T(8,128)S(1)}, f32[20,1024]{1,0:T(8,128)S(1)}) custom-call(f32[2,5,5,8,128]{4,3,2,1,0:T(8,128)S(1)} %get-tuple-element.26.splat, f32[5,8,1024]{2,1,0:T(8,128)S(1)} %get-tuple-element.27.edge_b, f32[5,8,1024]{2,1,0:T(8,128)S(1)} %get-tuple-element.28.edge_a, ...), custom_call_target="tpu_custom_call" | custom-call | flops 2928640 | bytes 2928640 | tf_op jit(solution)/shard_map/pallas_call | solution.py:28
  10.3 1.0 %collective-permute-start = (f32[20,1024]{1,0:T(8,128)S(1)}, f32[20,1024]{1,0:T(8,128)S(1)}, u32[]{:S(2)}, u32[]{:S(2)}) collective-permute-start(f32[20,1024]{1,0:T(8,128)S(1)} %get-tuple-element.31), channel_id=1, source_target_pairs={{0,1},{1,0},{2,3},{3,2},{4,5},{5,4},{6,7},{7,6},{8,9},{9,8},{10,11... | collective-permute-start | bytes 245768 | tf_op jit(solution)/shard_map/ppermute | solution.py:404
  11.4 0.9 %shard_map.84.rest = f32[4,5,8,1024]{3,2,1,0:T(8,128)S(1)} custom-call(f32[2,5,5,8,128]{4,3,2,1,0:T(8,128)S(1)} %get-tuple-element.26.splat, f32[4,5,8,1024]{3,2,1,0:T(8,128)S(1)} %get-tuple-element.29.first, f32[4,5,8,1024]{3,2,1,0:T(8,128)S(1)} %get-tuple-element.30.rhs, f32[4,5,5,8,1024]{4,3,2,1,0:T(8,128)S(1)} %bitcast.14), custom_call_target="tpu_custom_call" | custom-call | flops 2723840 | bytes 2723840 | tf_op jit(solution)/shard_map/pallas_call | solution.py:28
  12.3 0.7 %shard_map.85.inner = f32[4,5,8,1024]{3,2,1,0:T(8,128)S(1)} custom-call(f32[4,5,8,1024]{3,2,1,0:T(8,128)S(1)} %get-tuple-element.29.first, f32[4,5,8,1024]{3,2,1,0:T(8,128)S(1)} %shard_map.84.rest, f32[20,1024]{1,0:T(8,128)S(1)} %collective-permute-done.halo_w, f32[4,5,5,8,1024]{4,3,2,1,0:T(8,128)S(1)} %bitcast.9), custom_call_target="tpu_custom_call" | custom-call | flops 2662400 | bytes 2662400 | tf_op jit(solution)/shard_map/pallas_call | solution.py:28
  13.0 0.2 collective-permute-done.2.halo_a
  13.2 0.4 shard_map.86
  13.6 1.7 %collective-permute-start.4 = (f32[5,8,1024]{2,1,0:T(8,128)S(1)}, f32[5,8,1024]{2,1,0:T(8,128)S(1)}, u32[]{:S(2)}, u32[]{:S(2)}) collective-permute-start(f32[5,8,1024]{2,1,0:T(8,128)S(1)} %get-tuple-element.32.edge_b), channel_id=1, source_target_pairs={{2,4},{4,2},{6,8},{8,6},{10,12},{12,10},{14,0},{0,14},{3,5},{5,3},... | collective-permute-start | bytes 491528 | tf_op jit(solution)/shard_map/ppermute | solution.py:403
  15.3 0.7 %collective-permute-start.5 = (f32[5,8,1024]{2,1,0:T(8,128)S(1)}, f32[5,8,1024]{2,1,0:T(8,128)S(1)}, u32[]{:S(2)}, u32[]{:S(2)}) collective-permute-start(f32[5,8,1024]{2,1,0:T(8,128)S(1)} %get-tuple-element.33.edge_a), channel_id=1, source_target_pairs={{0,2},{2,0},{4,6},{6,4},{8,10},{10,8},{12,14},{14,12},{1,3},{3,1},... | collective-permute-start | bytes 491528 | tf_op jit(solution)/shard_map/ppermute | solution.py:405
  16.1 1.4 %collective-permute-start.3 = (f32[20,1024]{1,0:T(8,128)S(1)}, f32[20,1024]{1,0:T(8,128)S(1)}, u32[]{:S(2)}, u32[]{:S(2)}) collective-permute-start(f32[20,1024]{1,0:T(8,128)S(1)} %get-tuple-element.34), channel_id=1, source_target_pairs={{0,1},{1,0},{2,3},{3,2},{4,5},{5,4},{6,7},{7,6},{8,9},{9,8},{10,11... | collective-permute-start | bytes 245768 | tf_op jit(solution)/shard_map/ppermute | solution.py:404
  17.5 0.9 %shard_map.87.rest = f32[4,5,8,1024]{3,2,1,0:T(8,128)S(1)} custom-call(f32[2,5,5,8,128]{4,3,2,1,0:T(8,128)S(1)} %get-tuple-element.26.splat, f32[4,5,8,1024]{3,2,1,0:T(8,128)S(1)} %shard_map.85.inner, f32[5,8,1024]{2,1,0:T(8,128)S(1)} %get-tuple-element.32.edge_b, f32[5,8,1024]{2,1,0:T(8,128)S(1)} %get-tuple-element.33.edge_a, ...), custom_call_target="tpu_custom_call" | custom-call | flops 2887680 | bytes 2887680 | tf_op jit(solution)/shard_map/pallas_call | solution.py:28
  18.5 1.6 %shard_map.88 = (f32[64,640]{1,0:T(8,128)S(1)}, f32[4,5,8,1024]{3,2,1,0:T(8,128)}) custom-call(f32[4,5,8,1024]{3,2,1,0:T(8,128)S(1)} %shard_map.85.inner, f32[5,8,1024]{2,1,0:T(8,128)S(1)} %get-tuple-element.32.edge_b, f32[5,8,1024]{2,1,0:T(8,128)S(1)} %get-tuple-element.33.edge_a, f32[4,5,8,1024]{3,2,1,0:T(8,128)S(1)} %shard_map.87.rest, ...), custom_call_target="tpu_custom_call" | custom-call | flops 2940928 | bytes 2940928 | tf_op jit(solution)/shard_map/pallas_call | solution.py:28
  20.1 0.9 %shard_map.89 = (f32[16,4,640]{2,1,0:T(4,128)S(1)}, f32[2,5,8,1024]{3,2,1,0:T(8,128)}) custom-call(f32[2,5,5,8,128]{4,3,2,1,0:T(8,128)S(1)} %get-tuple-element.26.splat, f32[64,640]{1,0:T(8,128)S(1)} %get-tuple-element.36.inner, f32[5,8,1024]{2,1,0:T(8,128)S(1)} %collective-permute-done.4.halo_b, f32[5,8,1024]{2,1,0:T(8,128)S(1)} %collective-permute-done.5.halo_a, ...), custom_call_target="tpu_custom_call" | custom-call | flops 626688 | bytes 626688 | tf_op jit(solution)/shard_map/pallas_call | solution.py:28
  20.9 13.6 %all_to_all.10.received = f32[16,4,640]{2,1,0:T(4,128)S(1)} all-to-all(f32[16,4,640]{2,1,0:T(4,128)S(1)} %get-tuple-element.37), channel_id=1, replica_groups=mesh['patch'=16,'span'=8,'wall'=2] {'patch'}, dimensions={0} | all-to-all | bytes 327680 | tf_op jit(solution)/shard_map/all_to_all | solution.py:468
  34.5 3.8 %collective-permute-start.6 = (f32[4,640]{1,0:T(4,128)S(1)}, f32[4,640]{1,0:T(4,128)S(1)}, u32[]{:S(2)}, u32[]{:S(2)}) collective-permute-start(f32[4,640]{1,0:T(4,128)S(1)} %shard_map.90.own), channel_id=1, source_target_pairs={{0,1},{1,0},{2,3},{3,2},{4,5},{5,4},{6,7},{7,6},{8,9},{9,8},{10,11... | collective-permute-start | bytes 30728 | tf_op jit(solution)/shard_map/ppermute | solution.py:470
  38.4 0.8 %collective-permute-done.6.other = f32[4,640]{1,0:T(4,128)S(1)} collective-permute-done((f32[4,640]{1,0:T(4,128)S(1)}, f32[4,640]{1,0:T(4,128)S(1)}, u32[]{:S(2)}, u32[]{:S(2)}) %collective-permute-start.6) | collective-permute-done | bytes 10272 | tf_op jit(solution)/shard_map/ppermute | solution.py:470
  39.4 9.8 %all_to_all.11.fixes = f32[16,4,640]{2,1,0:T(4,128)S(1)} all-to-all(f32[16,4,640]{2,1,0:T(4,128)S(1)} %shard_map.91), channel_id=1, replica_groups=mesh['patch'=16,'span'=8,'wall'=2] {'patch'}, dimensions={0} | all-to-all | bytes 327680 | tf_op jit(solution)/shard_map/all_to_all | solution.py:472
  49.1 0.6 %shard_map.92 = (f32[4,5,8,1024]{3,2,1,0:T(8,128)S(1)}, f32[5,8,1024]{2,1,0:T(8,128)S(1)}, f32[5,8,1024]{2,1,0:T(8,128)S(1)}, f32[20,1024]{1,0:T(8,128)S(1)}) custom-call(f32[2,5,5,8,128]{4,3,2,1,0:T(8,128)S(1)} %get-tuple-element.26.splat, s32[4,8,8]{2,1,0:T(8,128)S(1)} %copy-done.2, s32[4,8,8]{2,1,0:T(8,128)S(1)} %copy-done.3, ...), custom_call_target="tpu_custom_call" | custom-call | flops 717824 | bytes 717824 | tf_op jit(solution)/shard_map/pallas_call | solution.py:28
  49.7 1.5 %collective-permute-start.8 = (f32[5,8,1024]{2,1,0:T(8,128)S(1)}, f32[5,8,1024]{2,1,0:T(8,128)S(1)}, u32[]{:S(2)}, u32[]{:S(2)}) collective-permute-start(f32[5,8,1024]{2,1,0:T(8,128)S(1)} %get-tuple-element.45), channel_id=1, source_target_pairs={{2,4},{4,2},{6,8},{8,6},{10,12},{12,10},{14,0},{0,14},{3,5},{5,3},... | collective-permute-start | bytes 491528 | tf_op jit(solution)/shard_map/ppermute | solution.py:403
  51.3 2.1 %collective-permute-start.7 = (f32[20,1024]{1,0:T(8,128)S(1)}, f32[20,1024]{1,0:T(8,128)S(1)}, u32[]{:S(2)}, u32[]{:S(2)}) collective-permute-start(f32[20,1024]{1,0:T(8,128)S(1)} %get-tuple-element.42), channel_id=1, source_target_pairs={{0,1},{1,0},{2,3},{3,2},{4,5},{5,4},{6,7},{7,6},{8,9},{9,8},{10,11... | collective-permute-start | bytes 245768 | tf_op jit(solution)/shard_map/ppermute | solution.py:404
  53.3 1.2 %shard_map.93 = (f32[4,5,8,1024]{3,2,1,0:T(8,128)S(1)}, f32[4,5,8,1024]{3,2,1,0:T(8,128)S(1)}, f32[2,5,8,1024]{3,2,1,0:T(8,128)S(1)}) custom-call(f32[2,5,5,8,128]{4,3,2,1,0:T(8,128)S(1)} %get-tuple-element.26.splat, f32[4,5,8,1024]{3,2,1,0:T(8,128)S(1)} %get-tuple-element.38.fix, f32[4,5,5,8,1024]{4,3,2,1,0:T(8,128)S(1)} %bitcast.16, ...), custom_call_target="tpu_custom_call" | custom-call | flops 3379200 | bytes 3379200 | tf_op jit(solution)/shard_map/pallas_call | solution.py:28
  54.5 0.9 %shard_map.94.inner = f32[4,5,8,1024]{3,2,1,0:T(8,128)S(1)} custom-call(f32[2,5,5,8,128]{4,3,2,1,0:T(8,128)S(1)} %get-tuple-element.26.splat, f32[4,5,8,1024]{3,2,1,0:T(8,128)S(1)} %get-tuple-element.38.fix, f32[4,5,8,1024]{3,2,1,0:T(8,128)S(1)} %get-tuple-element.41.rest, f32[20,1024]{1,0:T(8,128)S(1)} %collective-permute-done.7.halo_w, ...), custom_call_target="tpu_custom_call" | custom-call | flops 3256320 | bytes 3256320 | tf_op jit(solution)/shard_map/pallas_call | solution.py:28
  55.5 1.1 %shard_map.95 = f32[4,5,8,1024]{3,2,1,0:T(8,128)} custom-call(f32[2,5,5,8,128]{4,3,2,1,0:T(8,128)S(1)} %get-tuple-element.26.splat, f32[4,5,8,1024]{3,2,1,0:T(8,128)S(1)} %shard_map.94.inner, f32[5,8,1024]{2,1,0:T(8,128)S(1)} %collective-permute-done.8.halo_b, f32[5,8,1024]{2,1,0:T(8,128)S(1)} %collective-permute-done.9.halo_a, ...), custom_call_target="tpu_custom_call" | custom-call | flops 2560000 | bytes 2560000 | tf_op jit(solution)/shard_map/pallas_call | solution.py:28
  (22 shorter events, 0.3 us)
Async XLA Ops:
  0.0 11.4 %copy-start.1 = (f32[4,8,5,5,1024]{4,1,3,2,0:T(8,128)S(1)}, f32[4,8,5,5,1024]{4,1,3,2,0:T(8,128)}, u32[]{:S(2)}) copy-start(f32[4,8,5,5,1024]{4,1,3,2,0:T(8,128)} %param.9) | copy-start | bytes 9830404
  2.0 11.1 %collective-permute-start.1 = (f32[5,8,1024]{2,1,0:T(8,128)S(1)}, f32[5,8,1024]{2,1,0:T(8,128)S(1)}, u32[]{:S(2)}, u32[]{:S(2)}) collective-permute-start(f32[5,8,1024]{2,1,0:T(8,128)S(1)} %get-tuple-element.27.edge_b), channel_id=1, source_target_pairs={{2,4},{4,2},{6,8},{8,6},{10,12},{12,10},{14,0},{0,14},{3,5},{5,3},... | collective-permute-start | bytes 491528 | tf_op jit(solution)/shard_map/ppermute | solution.py:403
  8.4 4.7 %collective-permute-start.2 = (f32[5,8,1024]{2,1,0:T(8,128)S(1)}, f32[5,8,1024]{2,1,0:T(8,128)S(1)}, u32[]{:S(2)}, u32[]{:S(2)}) collective-permute-start(f32[5,8,1024]{2,1,0:T(8,128)S(1)} %get-tuple-element.28.edge_a), channel_id=1, source_target_pairs={{0,2},{2,0},{4,6},{6,4},{8,10},{10,8},{12,14},{14,12},{1,3},{3,1},... | collective-permute-start | bytes 491528 | tf_op jit(solution)/shard_map/ppermute | solution.py:405
  10.3 2.0 %copy-start = (f32[4,8,5,5,1024]{4,1,3,2,0:T(8,128)S(1)}, f32[4,8,5,5,1024]{4,1,3,2,0:T(8,128)}, u32[]{:S(2)}) copy-start(f32[4,8,5,5,1024]{4,1,3,2,0:T(8,128)} %param.10) | copy-start | bytes 9830404
  10.3 2.0 %collective-permute-start = (f32[20,1024]{1,0:T(8,128)S(1)}, f32[20,1024]{1,0:T(8,128)S(1)}, u32[]{:S(2)}, u32[]{:S(2)}) collective-permute-start(f32[20,1024]{1,0:T(8,128)S(1)} %get-tuple-element.31), channel_id=1, source_target_pairs={{0,1},{1,0},{2,3},{3,2},{4,5},{5,4},{6,7},{7,6},{8,9},{9,8},{10,11... | collective-permute-start | bytes 245768 | tf_op jit(solution)/shard_map/ppermute | solution.py:404
  13.6 6.4 %collective-permute-start.4 = (f32[5,8,1024]{2,1,0:T(8,128)S(1)}, f32[5,8,1024]{2,1,0:T(8,128)S(1)}, u32[]{:S(2)}, u32[]{:S(2)}) collective-permute-start(f32[5,8,1024]{2,1,0:T(8,128)S(1)} %get-tuple-element.32.edge_b), channel_id=1, source_target_pairs={{2,4},{4,2},{6,8},{8,6},{10,12},{12,10},{14,0},{0,14},{3,5},{5,3},... | collective-permute-start | bytes 491528 | tf_op jit(solution)/shard_map/ppermute | solution.py:403
  15.3 4.7 %collective-permute-start.5 = (f32[5,8,1024]{2,1,0:T(8,128)S(1)}, f32[5,8,1024]{2,1,0:T(8,128)S(1)}, u32[]{:S(2)}, u32[]{:S(2)}) collective-permute-start(f32[5,8,1024]{2,1,0:T(8,128)S(1)} %get-tuple-element.33.edge_a), channel_id=1, source_target_pairs={{0,2},{2,0},{4,6},{6,4},{8,10},{10,8},{12,14},{14,12},{1,3},{3,1},... | collective-permute-start | bytes 491528 | tf_op jit(solution)/shard_map/ppermute | solution.py:405
  16.1 2.4 %collective-permute-start.3 = (f32[20,1024]{1,0:T(8,128)S(1)}, f32[20,1024]{1,0:T(8,128)S(1)}, u32[]{:S(2)}, u32[]{:S(2)}) collective-permute-start(f32[20,1024]{1,0:T(8,128)S(1)} %get-tuple-element.34), channel_id=1, source_target_pairs={{0,1},{1,0},{2,3},{3,2},{4,5},{5,4},{6,7},{7,6},{8,9},{9,8},{10,11... | collective-permute-start | bytes 245768 | tf_op jit(solution)/shard_map/ppermute | solution.py:404
  18.4 20.8 %copy-start.4 = (f32[1,1,5,10,4]{3,4,2,1,0:T(4,128)S(1)}, f32[1,1,5,10,4]{3,4,2,1,0:T(4,128)}, u32[]{:S(2)}) copy-start(f32[1,1,5,10,4]{3,4,2,1,0:T(4,128)} %param.15) | copy-start | bytes 2404
  18.4 30.7 %copy-start.2 = (s32[4,8,8]{2,1,0:T(8,128)S(1)}, s32[4,8,8]{2,1,0:T(8,128)}, u32[]{:S(2)}) copy-start(s32[4,8,8]{2,1,0:T(8,128)} %owner.1) | copy-start | bytes 3076
  18.5 30.7 %copy-start.3 = (s32[4,8,8]{2,1,0:T(8,128)S(1)}, s32[4,8,8]{2,1,0:T(8,128)}, u32[]{:S(2)}) copy-start(s32[4,8,8]{2,1,0:T(8,128)} %slot.1) | copy-start | bytes 3076
  34.5 4.7 %collective-permute-start.6 = (f32[4,640]{1,0:T(4,128)S(1)}, f32[4,640]{1,0:T(4,128)S(1)}, u32[]{:S(2)}, u32[]{:S(2)}) collective-permute-start(f32[4,640]{1,0:T(4,128)S(1)} %shard_map.90.own), channel_id=1, source_target_pairs={{0,1},{1,0},{2,3},{3,2},{4,5},{5,4},{6,7},{7,6},{8,9},{9,8},{10,11... | collective-permute-start | bytes 30728 | tf_op jit(solution)/shard_map/ppermute | solution.py:470
  49.7 5.7 %collective-permute-start.8 = (f32[5,8,1024]{2,1,0:T(8,128)S(1)}, f32[5,8,1024]{2,1,0:T(8,128)S(1)}, u32[]{:S(2)}, u32[]{:S(2)}) collective-permute-start(f32[5,8,1024]{2,1,0:T(8,128)S(1)} %get-tuple-element.45), channel_id=1, source_target_pairs={{2,4},{4,2},{6,8},{8,6},{10,12},{12,10},{14,0},{0,14},{3,5},{5,3},... | collective-permute-start | bytes 491528 | tf_op jit(solution)/shard_map/ppermute | solution.py:403
  51.3 4.2 %collective-permute-start.9 = (f32[5,8,1024]{2,1,0:T(8,128)S(1)}, f32[5,8,1024]{2,1,0:T(8,128)S(1)}, u32[]{:S(2)}, u32[]{:S(2)}) collective-permute-start(f32[5,8,1024]{2,1,0:T(8,128)S(1)} %get-tuple-element.46), channel_id=1, source_target_pairs={{0,2},{2,0},{4,6},{6,4},{8,10},{10,8},{12,14},{14,12},{1,3},{3,1},... | collective-permute-start | bytes 491528 | tf_op jit(solution)/shard_map/ppermute | solution.py:405
  51.3 3.2 %collective-permute-start.7 = (f32[20,1024]{1,0:T(8,128)S(1)}, f32[20,1024]{1,0:T(8,128)S(1)}, u32[]{:S(2)}, u32[]{:S(2)}) collective-permute-start(f32[20,1024]{1,0:T(8,128)S(1)} %get-tuple-element.42), channel_id=1, source_target_pairs={{0,1},{1,0},{2,3},{3,2},{4,5},{5,4},{6,7},{7,6},{8,9},{9,8},{10,11... | collective-permute-start | bytes 245768 | tf_op jit(solution)/shard_map/ppermute | solution.py:404

commit v9 on v8

--- a/solution.py
+++ b/solution.py
@@ -90,10 +90,10 @@
     return total([jnp.dot(hot, part, preferred_element_type=F32) for part in (low, middle, high)])
 
 
-def hot_rows(owner, slot, tiles):
+def hot_rows(owner, slot, tiles, cells=range(4)):
     ids = lax.broadcasted_iota(jnp.int32, (8, LANES), 1)
     hot = []
-    for s in range(4):
+    for s in cells:
         named = owner[s] * 4 + slot[s]
         hot += [jnp.where(named[:, q : q + 1] == ids, 1.0, 0.0) for q in range(tiles)]
     return jnp.concatenate(hot, axis=0)
@@ -209,17 +209,21 @@
     for_lanes(body, rest.shape[-1])
 
 
-def second_edge_kernel(splat, inner, halo_b, halo_a, jinv, edge_a, edge_b, edge_w, raw):
-    even, plane_a, plane_b, row = position()
+def second_edge_kernel(splat, inner, halo_b, halo_a, jinv, edge_b, edge_a):
+    _, plane_a, plane_b, _ = position()
     real = inside()
 
     def body(lanes):
-        for plane, halo, edge, there in ((plane_a, halo_a, edge_a, None), (plane_b, halo_b, edge_b, real)):
+        for plane, halo, edge, there in ((plane_b, halo_b, edge_b, real), (plane_a, halo_a, edge_a, None)):
             swept = sweep(jinv, plane, lanes, beyond_span(splat, halo, lanes, there))
             for k in range(5):
                 edge[k, :, lanes] = inner[plane, k, :, lanes] + swept[k]
 
     for_lanes(body, inner.shape[-1])
+
+
+def second_wall_kernel(splat, inner, edge_b, edge_a, edge_w, raw):
+    even, _, _, row = position()
     for k in range(5):
         for s in (1, 2):
             raw[k, s, :] = inner[s, k, row, :]
@@ -321,22 +325,38 @@
             out[p, :, i * LANES : (i + 1) * LANES] = fix
 
 
-def prolong_kernel(splat, owner, slot, fixes, out, edge_a, edge_b, edge_w, fix, raw):
-    _, plane_a, plane_b, row = position()
-    tiles = out.shape[-1] // LANES
+def prolonged(owner, slot, fixes, fix, tiles, cells):
     owners, slots, _ = fixes.shape
     for p in range(owners):
         fix[p * slots : (p + 1) * slots, :] = fixes[p]
-    hot = hot_rows(owner, slot, tiles)[:, : owners * slots]
-    for k in range(5):
-        rows = picked_sums(hot, fix[:, k * LANES : (k + 1) * LANES])
-        for s in range(4):
+    hot = hot_rows(owner, slot, tiles, cells)[:, : owners * slots]
+    rows = [picked_sums(hot, fix[:, k * LANES : (k + 1) * LANES]) for k in range(5)]
+    return lambda k, n, q: rows[k][(n * tiles + q) * 8 : (n * tiles + q) * 8 + 8]
+
+
+def prolong_edge_kernel(owner, slot, fixes, edge_b, edge_a, fix):
+    even = position()[0]
+    tiles = edge_a.shape[-1] // LANES
+    tile = prolonged(owner, slot, fixes, fix, tiles, (0, 3))
+    for k in range(5):
+        for q in range(tiles):
+            lanes = slice(q * LANES, (q + 1) * LANES)
+            low, high = tile(k, 0, q), tile(k, 1, q)
+            edge_b[k, :, lanes] = jnp.where(even, low, high)
+            edge_a[k, :, lanes] = jnp.where(even, high, low)
+
+
+def prolong_inner_kernel(splat, owner, slot, fixes, edge_b, edge_a, out, edge_w, fix, raw):
+    even, _, _, row = position()
+    tiles = out.shape[-1] // LANES
+    tile = prolonged(owner, slot, fixes, fix, tiles, (1, 2))
+    for k in range(5):
+        out[0, k] = jnp.where(even, edge_b[k], edge_a[k])
+        out[3, k] = jnp.where(even, edge_a[k], edge_b[k])
+        for n in range(2):
             for q in range(tiles):
-                at = (s * tiles + q) * 8
-                out[s, k, :, q * LANES : (q + 1) * LANES] = rows[at : at + 8]
-    for k in range(5):
-        edge_a[k] = out[plane_a, k]
-        edge_b[k] = out[plane_b, k]
+                out[1 + n, k, :, q * LANES : (q + 1) * LANES] = tile(k, n, q)
+    for k in range(5):
         for s in range(4):
             raw[k, s, :] = out[s, k, row, :]
     wall_rows(splat, raw, edge_w)
@@ -446,9 +466,8 @@
     halo_a, halo_b, halo_w = exchange(a, b, w)
     [rest] = call(first_residual_kernel, [field], [splat, first, rhs, jac_in])
     [inner] = call(second_local_kernel, [field], [first, rest, halo_w, jinv_in])
-    a, b, w = call(
-        second_edge_kernel, [plane, plane, edge], [splat, inner, halo_b, halo_a, jinv_in], scratch=[raw]
-    )
+    b, a = call(second_edge_kernel, [plane, plane], [splat, inner, halo_b, halo_a, jinv_in])
+    [w] = call(second_wall_kernel, [edge], [splat, inner, b, a], scratch=[raw])
     halo_a, halo_b, halo_w = exchange(a, b, w)
     [rest] = call(second_residual_kernel, [field], [splat, inner, b, a, rhs, jac_in])
     partial, base = call(
@@ -470,11 +489,10 @@
     theirs = lax.ppermute(mine, "wall", [(0, 1), (1, 0)])
     [reply] = call(coarse_kernel, [chunks], [inv, mine, theirs])
     fixes = lax.all_to_all(reply, "patch", split_axis=0, concat_axis=0, tiled=True)
-    fix, a, b, w = call(
-        prolong_kernel,
-        [field, plane, plane, edge],
-        [splat, block_owner, block_slot, fixes],
-        scratch=[pltpu.VMEM((aggregates, columns), F32), raw],
+    held = pltpu.VMEM((aggregates, columns), F32)
+    b, a = call(prolong_edge_kernel, [plane, plane], [block_owner, block_slot, fixes], scratch=[held])
+    fix, w = call(
+        prolong_inner_kernel, [field, edge], [splat, block_owner, block_slot, fixes, b, a], scratch=[held, raw]
     )
     halo_a, halo_b, halo_w = exchange(a, b, w)
     rest, base, late = call(

time: 57.6 us -> 57.2 us (level)
    pallas_call x14 -> x16, Pallas kernels: 13.1 us -> 13.3 us  [call(): pl.pallas_call(kernel, out_shape=outs, in_specs=places or [VMEM] * len(ar...]
  transfers between devices with their start and end apart: 10 -> 10, of which waited for: 2 -> 2; matrix products, arithmetic and copies ran while one was open for 0% -> 0% of each run, Pallas kernels for 14% -> 15%
where the time goes in v9:
time: 57.2 us; the launch traced here: 56.7 us
  blocking collectives  23.3 us (41%)
  starting transfers between devices  18.8 us (33%)
  Pallas kernels  13.3 us (23%)
  waiting for transfers between devices  1.03 us (2%)
    all_to_all x1, blocking collectives, local(): lax.all_to_all(partial, 'patch', split_axis=0, concat_axis=0, tiled=True)  13.6 us
    pallas_call x16, Pallas kernels, call(): pl.pallas_call(kernel, out_shape=outs, in_specs=places or [VMEM] * len(ar...  13.3 us
    all_to_all x1, blocking collectives, local(): lax.all_to_all(reply, 'patch', split_axis=0, concat_axis=0, tiled=True)  9.77 us
    ppermute x3, starting transfers between devices, exchange(): halo_b = lax.ppermute(edge_b, 'span', odd)  9.72 us
    ppermute x3, starting transfers between devices, exchange(): halo_w = lax.ppermute(edge_w, 'wall', [(0, 1), (1, 0)])  4.7 us
    ppermute x1, starting transfers between devices, local(): theirs = lax.ppermute(mine, 'wall', [(0, 1), (1, 0)])  3.68 us
  transfers between devices with their start and end apart: 10, of which 2 were waited for; matrix products, arithmetic and copies ran while one was open for 0% of the time, Pallas kernels for 15%

profile of v9, /device:TPU:1, one launch (start us, length us, event | category | flops | bytes accessed | tf_op | source)
XLA Modules:
  0.0 56.7 jit_solution(8372627723369874600)
XLA Ops:
  0.0 1.9 %shard_map.82 = (f32[5,8,1024]{2,1,0:T(8,128)S(1)}, f32[5,8,1024]{2,1,0:T(8,128)S(1)}, f32[2,5,5,8,128]{4,3,2,1,0:T(8,128)S(1)}, f32[64,256]{1,0:T(8,128)S(1)}) custom-call(f32[5,5]{1,0:T(8,128)} %wall_in.1, f32[5,5]{1,0:T(8,128)} %span_in.1, s32[4,8,8]{2,1,0:T(8,128)} %owner.3, s32[4,8,8]{2,1,0:T(8,128)} %slot.3, f32[4,5,8,1024]{3,2,1,0:T(8,128)} %bitcast.18, ...), custom_call_target="tpu_custom_call" | custom-call | flops 2266212 | bytes 2266212 | tf_op jit(solution)/shard_map/pallas_call | solution.py:28
  2.0 6.5 %collective-permute-start.1 = (f32[5,8,1024]{2,1,0:T(8,128)S(1)}, f32[5,8,1024]{2,1,0:T(8,128)S(1)}, u32[]{:S(2)}, u32[]{:S(2)}) collective-permute-start(f32[5,8,1024]{2,1,0:T(8,128)S(1)} %get-tuple-element.26.edge_b), channel_id=1, source_target_pairs={{2,4},{4,2},{6,8},{8,6},{10,12},{12,10},{14,0},{0,14},{3,5},{5,3},... | collective-permute-start | bytes 491528 | tf_op jit(solution)/shard_map/ppermute | solution.py:423
  8.4 1.9 %shard_map.83 = (f32[4,5,8,1024]{3,2,1,0:T(8,128)S(1)}, f32[4,5,8,1024]{3,2,1,0:T(8,128)S(1)}, f32[20,1024]{1,0:T(8,128)S(1)}) custom-call(f32[2,5,5,8,128]{4,3,2,1,0:T(8,128)S(1)} %get-tuple-element.25.splat, f32[5,8,1024]{2,1,0:T(8,128)S(1)} %get-tuple-element.26.edge_b, f32[5,8,1024]{2,1,0:T(8,128)S(1)} %get-tuple-element.27.edge_a, ...), custom_call_target="tpu_custom_call" | custom-call | flops 2928640 | bytes 2928640 | tf_op jit(solution)/shard_map/pallas_call | solution.py:28
  10.3 1.0 %collective-permute-start = (f32[20,1024]{1,0:T(8,128)S(1)}, f32[20,1024]{1,0:T(8,128)S(1)}, u32[]{:S(2)}, u32[]{:S(2)}) collective-permute-start(f32[20,1024]{1,0:T(8,128)S(1)} %get-tuple-element.30), channel_id=1, source_target_pairs={{0,1},{1,0},{2,3},{3,2},{4,5},{5,4},{6,7},{7,6},{8,9},{9,8},{10,11... | collective-permute-start | bytes 245768 | tf_op jit(solution)/shard_map/ppermute | solution.py:424
  11.4 0.9 %shard_map.84.rest = f32[4,5,8,1024]{3,2,1,0:T(8,128)S(1)} custom-call(f32[2,5,5,8,128]{4,3,2,1,0:T(8,128)S(1)} %get-tuple-element.25.splat, f32[4,5,8,1024]{3,2,1,0:T(8,128)S(1)} %get-tuple-element.28.first, f32[4,5,8,1024]{3,2,1,0:T(8,128)S(1)} %get-tuple-element.29.rhs, f32[4,5,5,8,1024]{4,3,2,1,0:T(8,128)S(1)} %bitcast.14), custom_call_target="tpu_custom_call" | custom-call | flops 2723840 | bytes 2723840 | tf_op jit(solution)/shard_map/pallas_call | solution.py:28
  12.3 0.7 %shard_map.85.inner = f32[4,5,8,1024]{3,2,1,0:T(8,128)S(1)} custom-call(f32[4,5,8,1024]{3,2,1,0:T(8,128)S(1)} %get-tuple-element.28.first, f32[4,5,8,1024]{3,2,1,0:T(8,128)S(1)} %shard_map.84.rest, f32[20,1024]{1,0:T(8,128)S(1)} %collective-permute-done.halo_w, f32[4,5,5,8,1024]{4,3,2,1,0:T(8,128)S(1)} %bitcast.9), custom_call_target="tpu_custom_call" | custom-call | flops 2662400 | bytes 2662400 | tf_op jit(solution)/shard_map/pallas_call | solution.py:28
  13.2 0.4 shard_map.86
  13.6 1.7 %collective-permute-start.4 = (f32[5,8,1024]{2,1,0:T(8,128)S(1)}, f32[5,8,1024]{2,1,0:T(8,128)S(1)}, u32[]{:S(2)}, u32[]{:S(2)}) collective-permute-start(f32[5,8,1024]{2,1,0:T(8,128)S(1)} %get-tuple-element.31.edge_b), channel_id=1, source_target_pairs={{2,4},{4,2},{6,8},{8,6},{10,12},{12,10},{14,0},{0,14},{3,5},{5,3},... | collective-permute-start | bytes 491528 | tf_op jit(solution)/shard_map/ppermute | solution.py:423
  15.2 0.7 %collective-permute-start.5 = (f32[5,8,1024]{2,1,0:T(8,128)S(1)}, f32[5,8,1024]{2,1,0:T(8,128)S(1)}, u32[]{:S(2)}, u32[]{:S(2)}) collective-permute-start(f32[5,8,1024]{2,1,0:T(8,128)S(1)} %get-tuple-element.32.edge_a), channel_id=1, source_target_pairs={{0,2},{2,0},{4,6},{6,4},{8,10},{10,8},{12,14},{14,12},{1,3},{3,1},... | collective-permute-start | bytes 491528 | tf_op jit(solution)/shard_map/ppermute | solution.py:425
  16.1 1.5 %collective-permute-start.3 = (f32[20,1024]{1,0:T(8,128)S(1)}, f32[20,1024]{1,0:T(8,128)S(1)}, u32[]{:S(2)}, u32[]{:S(2)}) collective-permute-start(f32[20,1024]{1,0:T(8,128)S(1)} %shard_map.88), channel_id=1, source_target_pairs={{0,1},{1,0},{2,3},{3,2},{4,5},{5,4},{6,7},{7,6},{8,9},{9,8},{10,11... | collective-permute-start | bytes 245768 | tf_op jit(solution)/shard_map/ppermute | solution.py:424
  17.6 0.9 %shard_map.87.rest = f32[4,5,8,1024]{3,2,1,0:T(8,128)S(1)} custom-call(f32[2,5,5,8,128]{4,3,2,1,0:T(8,128)S(1)} %get-tuple-element.25.splat, f32[4,5,8,1024]{3,2,1,0:T(8,128)S(1)} %shard_map.85.inner, f32[5,8,1024]{2,1,0:T(8,128)S(1)} %get-tuple-element.31.edge_b, f32[5,8,1024]{2,1,0:T(8,128)S(1)} %get-tuple-element.32.edge_a, ...), custom_call_target="tpu_custom_call" | custom-call | flops 2887680 | bytes 2887680 | tf_op jit(solution)/shard_map/pallas_call | solution.py:28
  18.6 1.6 %shard_map.89 = (f32[64,640]{1,0:T(8,128)S(1)}, f32[4,5,8,1024]{3,2,1,0:T(8,128)}) custom-call(f32[4,5,8,1024]{3,2,1,0:T(8,128)S(1)} %shard_map.85.inner, f32[5,8,1024]{2,1,0:T(8,128)S(1)} %get-tuple-element.31.edge_b, f32[5,8,1024]{2,1,0:T(8,128)S(1)} %get-tuple-element.32.edge_a, f32[4,5,8,1024]{3,2,1,0:T(8,128)S(1)} %shard_map.87.rest, ...), custom_call_target="tpu_custom_call" | custom-call | flops 2940928 | bytes 2940928 | tf_op jit(solution)/shard_map/pallas_call | solution.py:28
  20.2 0.9 %shard_map.90 = (f32[16,4,640]{2,1,0:T(4,128)S(1)}, f32[2,5,8,1024]{3,2,1,0:T(8,128)}) custom-call(f32[2,5,5,8,128]{4,3,2,1,0:T(8,128)S(1)} %get-tuple-element.25.splat, f32[64,640]{1,0:T(8,128)S(1)} %get-tuple-element.34.inner, f32[5,8,1024]{2,1,0:T(8,128)S(1)} %collective-permute-done.4.halo_b, f32[5,8,1024]{2,1,0:T(8,128)S(1)} %collective-permute-done.5.halo_a, ...), custom_call_target="tpu_custom_call" | custom-call | flops 626688 | bytes 626688 | tf_op jit(solution)/shard_map/pallas_call | solution.py:28
  21.0 13.6 %all_to_all.10.received = f32[16,4,640]{2,1,0:T(4,128)S(1)} all-to-all(f32[16,4,640]{2,1,0:T(4,128)S(1)} %get-tuple-element.35), channel_id=1, replica_groups=mesh['patch'=16,'span'=8,'wall'=2] {'patch'}, dimensions={0} | all-to-all | bytes 327680 | tf_op jit(solution)/shard_map/all_to_all | solution.py:487
  34.6 3.7 %collective-permute-start.6 = (f32[4,640]{1,0:T(4,128)S(1)}, f32[4,640]{1,0:T(4,128)S(1)}, u32[]{:S(2)}, u32[]{:S(2)}) collective-permute-start(f32[4,640]{1,0:T(4,128)S(1)} %shard_map.91.own), channel_id=1, source_target_pairs={{0,1},{1,0},{2,3},{3,2},{4,5},{5,4},{6,7},{7,6},{8,9},{9,8},{10,11... | collective-permute-start | bytes 30728 | tf_op jit(solution)/shard_map/ppermute | solution.py:489
  38.3 0.8 %collective-permute-done.6.other = f32[4,640]{1,0:T(4,128)S(1)} collective-permute-done((f32[4,640]{1,0:T(4,128)S(1)}, f32[4,640]{1,0:T(4,128)S(1)}, u32[]{:S(2)}, u32[]{:S(2)}) %collective-permute-start.6) | collective-permute-done | bytes 10272 | tf_op jit(solution)/shard_map/ppermute | solution.py:489
  39.3 9.8 %all_to_all.11.fixes = f32[16,4,640]{2,1,0:T(4,128)S(1)} all-to-all(f32[16,4,640]{2,1,0:T(4,128)S(1)} %shard_map.92), channel_id=1, replica_groups=mesh['patch'=16,'span'=8,'wall'=2] {'patch'}, dimensions={0} | all-to-all | bytes 327680 | tf_op jit(solution)/shard_map/all_to_all | solution.py:491
  49.1 0.3 shard_map.93
  49.4 1.5 %collective-permute-start.8 = (f32[5,8,1024]{2,1,0:T(8,128)S(1)}, f32[5,8,1024]{2,1,0:T(8,128)S(1)}, u32[]{:S(2)}, u32[]{:S(2)}) collective-permute-start(f32[5,8,1024]{2,1,0:T(8,128)S(1)} %get-tuple-element.36.edge_b), channel_id=1, source_target_pairs={{2,4},{4,2},{6,8},{8,6},{10,12},{12,10},{14,0},{0,14},{3,5},{5,3},... | collective-permute-start | bytes 491528 | tf_op jit(solution)/shard_map/ppermute | solution.py:423
  51.0 0.4 shard_map.94
  51.4 2.1 %collective-permute-start.7 = (f32[20,1024]{1,0:T(8,128)S(1)}, f32[20,1024]{1,0:T(8,128)S(1)}, u32[]{:S(2)}, u32[]{:S(2)}) collective-permute-start(f32[20,1024]{1,0:T(8,128)S(1)} %get-tuple-element.42), channel_id=1, source_target_pairs={{0,1},{1,0},{2,3},{3,2},{4,5},{5,4},{6,7},{7,6},{8,9},{9,8},{10,11... | collective-permute-start | bytes 245768 | tf_op jit(solution)/shard_map/ppermute | solution.py:424
  53.5 1.2 %shard_map.95 = (f32[4,5,8,1024]{3,2,1,0:T(8,128)S(1)}, f32[4,5,8,1024]{3,2,1,0:T(8,128)S(1)}, f32[2,5,8,1024]{3,2,1,0:T(8,128)S(1)}) custom-call(f32[2,5,5,8,128]{4,3,2,1,0:T(8,128)S(1)} %get-tuple-element.25.splat, f32[4,5,8,1024]{3,2,1,0:T(8,128)S(1)} %get-tuple-element.38.fix, f32[4,5,5,8,1024]{4,3,2,1,0:T(8,128)S(1)} %bitcast.16, ...), custom_call_target="tpu_custom_call" | custom-call | flops 3379200 | bytes 3379200 | tf_op jit(solution)/shard_map/pallas_call | solution.py:28
  54.7 0.9 %shard_map.96.inner = f32[4,5,8,1024]{3,2,1,0:T(8,128)S(1)} custom-call(f32[2,5,5,8,128]{4,3,2,1,0:T(8,128)S(1)} %get-tuple-element.25.splat, f32[4,5,8,1024]{3,2,1,0:T(8,128)S(1)} %get-tuple-element.38.fix, f32[4,5,8,1024]{3,2,1,0:T(8,128)S(1)} %get-tuple-element.41.rest, f32[20,1024]{1,0:T(8,128)S(1)} %collective-permute-done.7.halo_w, ...), custom_call_target="tpu_custom_call" | custom-call | flops 3256320 | bytes 3256320 | tf_op jit(solution)/shard_map/pallas_call | solution.py:28
  55.6 1.1 %shard_map.97 = f32[4,5,8,1024]{3,2,1,0:T(8,128)} custom-call(f32[2,5,5,8,128]{4,3,2,1,0:T(8,128)S(1)} %get-tuple-element.25.splat, f32[4,5,8,1024]{3,2,1,0:T(8,128)S(1)} %shard_map.96.inner, f32[5,8,1024]{2,1,0:T(8,128)S(1)} %collective-permute-done.8.halo_b, f32[5,8,1024]{2,1,0:T(8,128)S(1)} %collective-permute-done.9.halo_a, ...), custom_call_target="tpu_custom_call" | custom-call | flops 2560000 | bytes 2560000 | tf_op jit(solution)/shard_map/pallas_call | solution.py:28
  (24 shorter events, 0.5 us)
Async XLA Ops:
  0.0 11.4 %copy-start.1 = (f32[4,8,5,5,1024]{4,1,3,2,0:T(8,128)S(1)}, f32[4,8,5,5,1024]{4,1,3,2,0:T(8,128)}, u32[]{:S(2)}) copy-start(f32[4,8,5,5,1024]{4,1,3,2,0:T(8,128)} %param.9) | copy-start | bytes 9830404
  2.0 11.1 %collective-permute-start.1 = (f32[5,8,1024]{2,1,0:T(8,128)S(1)}, f32[5,8,1024]{2,1,0:T(8,128)S(1)}, u32[]{:S(2)}, u32[]{:S(2)}) collective-permute-start(f32[5,8,1024]{2,1,0:T(8,128)S(1)} %get-tuple-element.26.edge_b), channel_id=1, source_target_pairs={{2,4},{4,2},{6,8},{8,6},{10,12},{12,10},{14,0},{0,14},{3,5},{5,3},... | collective-permute-start | bytes 491528 | tf_op jit(solution)/shard_map/ppermute | solution.py:423
  8.4 4.7 %collective-permute-start.2 = (f32[5,8,1024]{2,1,0:T(8,128)S(1)}, f32[5,8,1024]{2,1,0:T(8,128)S(1)}, u32[]{:S(2)}, u32[]{:S(2)}) collective-permute-start(f32[5,8,1024]{2,1,0:T(8,128)S(1)} %get-tuple-element.27.edge_a), channel_id=1, source_target_pairs={{0,2},{2,0},{4,6},{6,4},{8,10},{10,8},{12,14},{14,12},{1,3},{3,1},... | collective-permute-start | bytes 491528 | tf_op jit(solution)/shard_map/ppermute | solution.py:425
  10.3 2.0 %copy-start = (f32[4,8,5,5,1024]{4,1,3,2,0:T(8,128)S(1)}, f32[4,8,5,5,1024]{4,1,3,2,0:T(8,128)}, u32[]{:S(2)}) copy-start(f32[4,8,5,5,1024]{4,1,3,2,0:T(8,128)} %param.10) | copy-start | bytes 9830404
  10.3 2.0 %collective-permute-start = (f32[20,1024]{1,0:T(8,128)S(1)}, f32[20,1024]{1,0:T(8,128)S(1)}, u32[]{:S(2)}, u32[]{:S(2)}) collective-permute-start(f32[20,1024]{1,0:T(8,128)S(1)} %get-tuple-element.30), channel_id=1, source_target_pairs={{0,1},{1,0},{2,3},{3,2},{4,5},{5,4},{6,7},{7,6},{8,9},{9,8},{10,11... | collective-permute-start | bytes 245768 | tf_op jit(solution)/shard_map/ppermute | solution.py:424
  13.6 6.6 %collective-permute-start.4 = (f32[5,8,1024]{2,1,0:T(8,128)S(1)}, f32[5,8,1024]{2,1,0:T(8,128)S(1)}, u32[]{:S(2)}, u32[]{:S(2)}) collective-permute-start(f32[5,8,1024]{2,1,0:T(8,128)S(1)} %get-tuple-element.31.edge_b), channel_id=1, source_target_pairs={{2,4},{4,2},{6,8},{8,6},{10,12},{12,10},{14,0},{0,14},{3,5},{5,3},... | collective-permute-start | bytes 491528 | tf_op jit(solution)/shard_map/ppermute | solution.py:423
  15.2 4.9 %collective-permute-start.5 = (f32[5,8,1024]{2,1,0:T(8,128)S(1)}, f32[5,8,1024]{2,1,0:T(8,128)S(1)}, u32[]{:S(2)}, u32[]{:S(2)}) collective-permute-start(f32[5,8,1024]{2,1,0:T(8,128)S(1)} %get-tuple-element.32.edge_a), channel_id=1, source_target_pairs={{0,2},{2,0},{4,6},{6,4},{8,10},{10,8},{12,14},{14,12},{1,3},{3,1},... | collective-permute-start | bytes 491528 | tf_op jit(solution)/shard_map/ppermute | solution.py:425
  16.1 2.5 %collective-permute-start.3 = (f32[20,1024]{1,0:T(8,128)S(1)}, f32[20,1024]{1,0:T(8,128)S(1)}, u32[]{:S(2)}, u32[]{:S(2)}) collective-permute-start(f32[20,1024]{1,0:T(8,128)S(1)} %shard_map.88), channel_id=1, source_target_pairs={{0,1},{1,0},{2,3},{3,2},{4,5},{5,4},{6,7},{7,6},{8,9},{9,8},{10,11... | collective-permute-start | bytes 245768 | tf_op jit(solution)/shard_map/ppermute | solution.py:424
  18.5 20.6 %copy-start.4 = (f32[1,1,5,10,4]{3,4,2,1,0:T(4,128)S(1)}, f32[1,1,5,10,4]{3,4,2,1,0:T(4,128)}, u32[]{:S(2)}) copy-start(f32[1,1,5,10,4]{3,4,2,1,0:T(4,128)} %param.15) | copy-start | bytes 2404
  18.5 30.5 %copy-start.2 = (s32[4,8,8]{2,1,0:T(8,128)S(1)}, s32[4,8,8]{2,1,0:T(8,128)}, u32[]{:S(2)}) copy-start(s32[4,8,8]{2,1,0:T(8,128)} %owner.3) | copy-start | bytes 3076
  18.6 30.5 %copy-start.3 = (s32[4,8,8]{2,1,0:T(8,128)S(1)}, s32[4,8,8]{2,1,0:T(8,128)}, u32[]{:S(2)}) copy-start(s32[4,8,8]{2,1,0:T(8,128)} %slot.3) | copy-start | bytes 3076
  34.6 4.5 %collective-permute-start.6 = (f32[4,640]{1,0:T(4,128)S(1)}, f32[4,640]{1,0:T(4,128)S(1)}, u32[]{:S(2)}, u32[]{:S(2)}) collective-permute-start(f32[4,640]{1,0:T(4,128)S(1)} %shard_map.91.own), channel_id=1, source_target_pairs={{0,1},{1,0},{2,3},{3,2},{4,5},{5,4},{6,7},{7,6},{8,9},{9,8},{10,11... | collective-permute-start | bytes 30728 | tf_op jit(solution)/shard_map/ppermute | solution.py:489
  49.4 6.2 %collective-permute-start.8 = (f32[5,8,1024]{2,1,0:T(8,128)S(1)}, f32[5,8,1024]{2,1,0:T(8,128)S(1)}, u32[]{:S(2)}, u32[]{:S(2)}) collective-permute-start(f32[5,8,1024]{2,1,0:T(8,128)S(1)} %get-tuple-element.36.edge_b), channel_id=1, source_target_pairs={{2,4},{4,2},{6,8},{8,6},{10,12},{12,10},{14,0},{0,14},{3,5},{5,3},... | collective-permute-start | bytes 491528 | tf_op jit(solution)/shard_map/ppermute | solution.py:423
  50.9 4.6 %collective-permute-start.9 = (f32[5,8,1024]{2,1,0:T(8,128)S(1)}, f32[5,8,1024]{2,1,0:T(8,128)S(1)}, u32[]{:S(2)}, u32[]{:S(2)}) collective-permute-start(f32[5,8,1024]{2,1,0:T(8,128)S(1)} %get-tuple-element.37.edge_a), channel_id=1, source_target_pairs={{0,2},{2,0},{4,6},{6,4},{8,10},{10,8},{12,14},{14,12},{1,3},{3,1},... | collective-permute-start | bytes 491528 | tf_op jit(solution)/shard_map/ppermute | solution.py:425
  51.4 3.3 %collective-permute-start.7 = (f32[20,1024]{1,0:T(8,128)S(1)}, f32[20,1024]{1,0:T(8,128)S(1)}, u32[]{:S(2)}, u32[]{:S(2)}) collective-permute-start(f32[20,1024]{1,0:T(8,128)S(1)} %get-tuple-element.42), channel_id=1, source_target_pairs={{0,1},{1,0},{2,3},{3,2},{4,5},{5,4},{6,7},{7,6},{8,9},{9,8},{10,11... | collective-permute-start | bytes 245768 | tf_op jit(solution)/shard_map/ppermute | solution.py:424

commit v10 on v9

--- a/solution.py
+++ b/solution.py
@@ -23,7 +23,7 @@
     return pltpu.with_memory_space_constraint(array, pltpu.HBM)
 
 
-def call(kernel, outs, args, places=None, out_places=None, scratch=()):
+def call(kernel, outs, args, places=None, out_places=None, scratch=(), aliases=None):
     size = 2 * sum(math.prod(a.shape) for a in (*args, *outs))
     return pl.pallas_call(
         kernel,
@@ -31,6 +31,7 @@
         in_specs=places or [VMEM] * len(args),
         out_specs=out_places or [VMEM] * len(outs),
         scratch_shapes=scratch,
+        input_output_aliases=aliases or {},
         cost_estimate=pl.CostEstimate(flops=size, bytes_accessed=size, transcendentals=0),
         compiler_params=pltpu.CompilerParams(vmem_limit_bytes=8 * 2**20),
     )(*args)
@@ -379,29 +380,34 @@
         load.wait()
 
 
-def final_local_kernel(splat, fix, rest, halo_w, jinv, base, late, inner):
+def final_local_kernel(splat, fix, rest, halo_w, jinv, base, late, inner, out, sems):
     row = position()[3]
     at, size = lax.axis_index("span"), lax.axis_size("span")
     there = {0: at > 0, 3: at < size - 1}
-
-    def body(lanes):
-        for s in range(4):
-            known = with_wall(rest, halo_w, s, lanes, row)
-            if s in (0, 3):
-                beyond = beyond_span(splat, late.at[s // 3], lanes, there[s])
-                known = [known[k] + beyond[k] for k in range(5)]
-            swept = sweep(jinv, s, lanes, known)
-            for k in range(5):
-                inner[s, k, :, lanes] = (base[s, k, :, lanes] + fix[s, k, :, lanes]) + swept[k]
-
-    for_lanes(body, fix.shape[-1])
-
-
-def final_edge_kernel(splat, inner, halo_b, halo_a, jinv, out, edges, sems):
+    store = pltpu.make_async_copy(inner.at[pl.ds(1, 2)], out.at[pl.ds(1, 2)], sems.at[0])
+    for cells in ((1, 2), (0, 3)):
+
+        def body(lanes, cells=cells):
+            for s in cells:
+                known = with_wall(rest, halo_w, s, lanes, row)
+                if s in there:
+                    beyond = beyond_span(splat, late.at[s // 3], lanes, there[s])
+                    known = [known[k] + beyond[k] for k in range(5)]
+                swept = sweep(jinv, s, lanes, known)
+                for k in range(5):
+                    inner[s, k, :, lanes] = (base[s, k, :, lanes] + fix[s, k, :, lanes]) + swept[k]
+
+        for_lanes(body, fix.shape[-1])
+        if cells == (1, 2):
+            store.start()
+    store.wait()
+
+
+def final_edge_kernel(splat, inner, halo_b, halo_a, jinv, out_had, out, edges, sems):
+    del out_had
     _, plane_a, plane_b, _ = position()
     real = inside()
-    stores = [pltpu.make_async_copy(inner.at[pl.ds(1, 2)], out.at[pl.ds(1, 2)], sems.at[2])]
-    stores[0].start()
+    stores = []
     for n, (plane, halo, there) in enumerate(((plane_b, halo_b, real), (plane_a, halo_a, None))):
 
         def body(lanes, n=n, plane=plane, halo=halo, there=there):
@@ -502,13 +508,21 @@
         places=[VMEM] * 3 + [HBM] * 2,
         scratch=[pltpu.SemaphoreType.DMA((2,))],
     )
-    [inner] = call(final_local_kernel, [field], [splat, fix, rest, halo_w, jinv_in, base, late])
+    inner, out = call(
+        final_local_kernel,
+        [field, field_out],
+        [splat, fix, rest, halo_w, jinv_in, base, late],
+        out_places=[VMEM, HBM],
+        scratch=[pltpu.SemaphoreType.DMA((1,))],
+    )
     [out] = call(
         final_edge_kernel,
         [field_out],
-        [splat, inner, halo_b, halo_a, jinv_in],
+        [splat, inner, halo_b, halo_a, jinv_in, in_hbm(out)],
+        places=[VMEM] * 5 + [HBM],
         out_places=[HBM],
-        scratch=[outer, pltpu.SemaphoreType.DMA((3,))],
+        scratch=[outer, pltpu.SemaphoreType.DMA((2,))],
+        aliases={5: 0},
     )
     return out.transpose(0, 2, 1, 3)
 

time: 57.2 us -> 57.2 us (level)
  no operation moved by 1% of the time
where the time goes in v10:
time: 57.2 us; the launch traced here: 57 us
  blocking collectives  23.3 us (41%)
  starting transfers between devices  18.8 us (33%)
  Pallas kernels  13.6 us (24%)
  waiting for transfers between devices  1.03 us (2%)
    pallas_call x16, Pallas kernels, call(): pl.pallas_call(kernel, out_shape=outs, in_specs=places or [VMEM] * len(ar...  13.6 us
    all_to_all x1, blocking collectives, local(): lax.all_to_all(partial, 'patch', split_axis=0, concat_axis=0, tiled=True)  13.6 us
    all_to_all x1, blocking collectives, local(): lax.all_to_all(reply, 'patch', split_axis=0, concat_axis=0, tiled=True)  9.77 us
    ppermute x3, starting transfers between devices, exchange(): halo_b = lax.ppermute(edge_b, 'span', odd)  9.72 us
    ppermute x3, starting transfers between devices, exchange(): halo_w = lax.ppermute(edge_w, 'wall', [(0, 1), (1, 0)])  4.69 us
    ppermute x1, starting transfers between devices, local(): theirs = lax.ppermute(mine, 'wall', [(0, 1), (1, 0)])  3.68 us
  transfers between devices with their start and end apart: 10, of which 2 were waited for; matrix products, arithmetic and copies ran while one was open for 0% of the time, Pallas kernels for 15%

profile of v10, /device:TPU:1, one launch (start us, length us, event | category | flops | bytes accessed | tf_op | source)
XLA Modules:
  0.0 57.0 jit_solution(17838499610571066252)
XLA Ops:
  0.0 1.9 %shard_map.82 = (f32[5,8,1024]{2,1,0:T(8,128)S(1)}, f32[5,8,1024]{2,1,0:T(8,128)S(1)}, f32[2,5,5,8,128]{4,3,2,1,0:T(8,128)S(1)}, f32[64,256]{1,0:T(8,128)S(1)}) custom-call(f32[5,5]{1,0:T(8,128)} %wall_in.1, f32[5,5]{1,0:T(8,128)} %span_in.1, s32[4,8,8]{2,1,0:T(8,128)} %owner.3, s32[4,8,8]{2,1,0:T(8,128)} %slot.3, f32[4,5,8,1024]{3,2,1,0:T(8,128)} %bitcast.18, ...), custom_call_target="tpu_custom_call" | custom-call | flops 2266212 | bytes 2266212 | tf_op jit(solution)/shard_map/pallas_call | solution.py:28
  2.0 6.5 %collective-permute-start.1 = (f32[5,8,1024]{2,1,0:T(8,128)S(1)}, f32[5,8,1024]{2,1,0:T(8,128)S(1)}, u32[]{:S(2)}, u32[]{:S(2)}) collective-permute-start(f32[5,8,1024]{2,1,0:T(8,128)S(1)} %get-tuple-element.28.edge_b), channel_id=1, source_target_pairs={{2,4},{4,2},{6,8},{8,6},{10,12},{12,10},{14,0},{0,14},{3,5},{5,3},... | collective-permute-start | bytes 491528 | tf_op jit(solution)/shard_map/ppermute | solution.py:429
  8.4 1.9 %shard_map.83 = (f32[4,5,8,1024]{3,2,1,0:T(8,128)S(1)}, f32[4,5,8,1024]{3,2,1,0:T(8,128)S(1)}, f32[20,1024]{1,0:T(8,128)S(1)}) custom-call(f32[2,5,5,8,128]{4,3,2,1,0:T(8,128)S(1)} %get-tuple-element.27.splat, f32[5,8,1024]{2,1,0:T(8,128)S(1)} %get-tuple-element.28.edge_b, f32[5,8,1024]{2,1,0:T(8,128)S(1)} %get-tuple-element.29.edge_a, ...), custom_call_target="tpu_custom_call" | custom-call | flops 2928640 | bytes 2928640 | tf_op jit(solution)/shard_map/pallas_call | solution.py:28
  10.3 1.0 %collective-permute-start = (f32[20,1024]{1,0:T(8,128)S(1)}, f32[20,1024]{1,0:T(8,128)S(1)}, u32[]{:S(2)}, u32[]{:S(2)}) collective-permute-start(f32[20,1024]{1,0:T(8,128)S(1)} %get-tuple-element.32), channel_id=1, source_target_pairs={{0,1},{1,0},{2,3},{3,2},{4,5},{5,4},{6,7},{7,6},{8,9},{9,8},{10,11... | collective-permute-start | bytes 245768 | tf_op jit(solution)/shard_map/ppermute | solution.py:430
  11.4 0.9 %shard_map.84.rest = f32[4,5,8,1024]{3,2,1,0:T(8,128)S(1)} custom-call(f32[2,5,5,8,128]{4,3,2,1,0:T(8,128)S(1)} %get-tuple-element.27.splat, f32[4,5,8,1024]{3,2,1,0:T(8,128)S(1)} %get-tuple-element.30.first, f32[4,5,8,1024]{3,2,1,0:T(8,128)S(1)} %get-tuple-element.31.rhs, f32[4,5,5,8,1024]{4,3,2,1,0:T(8,128)S(1)} %bitcast.14), custom_call_target="tpu_custom_call" | custom-call | flops 2723840 | bytes 2723840 | tf_op jit(solution)/shard_map/pallas_call | solution.py:28
  12.3 0.7 %shard_map.85.inner = f32[4,5,8,1024]{3,2,1,0:T(8,128)S(1)} custom-call(f32[4,5,8,1024]{3,2,1,0:T(8,128)S(1)} %get-tuple-element.30.first, f32[4,5,8,1024]{3,2,1,0:T(8,128)S(1)} %shard_map.84.rest, f32[20,1024]{1,0:T(8,128)S(1)} %collective-permute-done.halo_w, f32[4,5,5,8,1024]{4,3,2,1,0:T(8,128)S(1)} %bitcast.9), custom_call_target="tpu_custom_call" | custom-call | flops 2662400 | bytes 2662400 | tf_op jit(solution)/shard_map/pallas_call | solution.py:28
  13.2 0.4 shard_map.86
  13.6 1.7 %collective-permute-start.4 = (f32[5,8,1024]{2,1,0:T(8,128)S(1)}, f32[5,8,1024]{2,1,0:T(8,128)S(1)}, u32[]{:S(2)}, u32[]{:S(2)}) collective-permute-start(f32[5,8,1024]{2,1,0:T(8,128)S(1)} %get-tuple-element.33.edge_b), channel_id=1, source_target_pairs={{2,4},{4,2},{6,8},{8,6},{10,12},{12,10},{14,0},{0,14},{3,5},{5,3},... | collective-permute-start | bytes 491528 | tf_op jit(solution)/shard_map/ppermute | solution.py:429
  15.2 0.7 %collective-permute-start.5 = (f32[5,8,1024]{2,1,0:T(8,128)S(1)}, f32[5,8,1024]{2,1,0:T(8,128)S(1)}, u32[]{:S(2)}, u32[]{:S(2)}) collective-permute-start(f32[5,8,1024]{2,1,0:T(8,128)S(1)} %get-tuple-element.34.edge_a), channel_id=1, source_target_pairs={{0,2},{2,0},{4,6},{6,4},{8,10},{10,8},{12,14},{14,12},{1,3},{3,1},... | collective-permute-start | bytes 491528 | tf_op jit(solution)/shard_map/ppermute | solution.py:431
  16.1 1.5 %collective-permute-start.3 = (f32[20,1024]{1,0:T(8,128)S(1)}, f32[20,1024]{1,0:T(8,128)S(1)}, u32[]{:S(2)}, u32[]{:S(2)}) collective-permute-start(f32[20,1024]{1,0:T(8,128)S(1)} %shard_map.88), channel_id=1, source_target_pairs={{0,1},{1,0},{2,3},{3,2},{4,5},{5,4},{6,7},{7,6},{8,9},{9,8},{10,11... | collective-permute-start | bytes 245768 | tf_op jit(solution)/shard_map/ppermute | solution.py:430
  17.6 0.9 %shard_map.87.rest = f32[4,5,8,1024]{3,2,1,0:T(8,128)S(1)} custom-call(f32[2,5,5,8,128]{4,3,2,1,0:T(8,128)S(1)} %get-tuple-element.27.splat, f32[4,5,8,1024]{3,2,1,0:T(8,128)S(1)} %shard_map.85.inner, f32[5,8,1024]{2,1,0:T(8,128)S(1)} %get-tuple-element.33.edge_b, f32[5,8,1024]{2,1,0:T(8,128)S(1)} %get-tuple-element.34.edge_a, ...), custom_call_target="tpu_custom_call" | custom-call | flops 2887680 | bytes 2887680 | tf_op jit(solution)/shard_map/pallas_call | solution.py:28
  18.6 1.6 %shard_map.89 = (f32[64,640]{1,0:T(8,128)S(1)}, f32[4,5,8,1024]{3,2,1,0:T(8,128)}) custom-call(f32[4,5,8,1024]{3,2,1,0:T(8,128)S(1)} %shard_map.85.inner, f32[5,8,1024]{2,1,0:T(8,128)S(1)} %get-tuple-element.33.edge_b, f32[5,8,1024]{2,1,0:T(8,128)S(1)} %get-tuple-element.34.edge_a, f32[4,5,8,1024]{3,2,1,0:T(8,128)S(1)} %shard_map.87.rest, ...), custom_call_target="tpu_custom_call" | custom-call | flops 2940928 | bytes 2940928 | tf_op jit(solution)/shard_map/pallas_call | solution.py:28
  20.2 0.8 %shard_map.90 = (f32[16,4,640]{2,1,0:T(4,128)S(1)}, f32[2,5,8,1024]{3,2,1,0:T(8,128)}) custom-call(f32[2,5,5,8,128]{4,3,2,1,0:T(8,128)S(1)} %get-tuple-element.27.splat, f32[64,640]{1,0:T(8,128)S(1)} %get-tuple-element.36.inner, f32[5,8,1024]{2,1,0:T(8,128)S(1)} %collective-permute-done.4.halo_b, f32[5,8,1024]{2,1,0:T(8,128)S(1)} %collective-permute-done.5.halo_a, ...), custom_call_target="tpu_custom_call" | custom-call | flops 626688 | bytes 626688 | tf_op jit(solution)/shard_map/pallas_call | solution.py:28
  21.0 13.6 %all_to_all.10.received = f32[16,4,640]{2,1,0:T(4,128)S(1)} all-to-all(f32[16,4,640]{2,1,0:T(4,128)S(1)} %get-tuple-element.37), channel_id=1, replica_groups=mesh['patch'=16,'span'=8,'wall'=2] {'patch'}, dimensions={0} | all-to-all | bytes 327680 | tf_op jit(solution)/shard_map/all_to_all | solution.py:493
  34.6 3.7 %collective-permute-start.6 = (f32[4,640]{1,0:T(4,128)S(1)}, f32[4,640]{1,0:T(4,128)S(1)}, u32[]{:S(2)}, u32[]{:S(2)}) collective-permute-start(f32[4,640]{1,0:T(4,128)S(1)} %shard_map.91.own), channel_id=1, source_target_pairs={{0,1},{1,0},{2,3},{3,2},{4,5},{5,4},{6,7},{7,6},{8,9},{9,8},{10,11... | collective-permute-start | bytes 30728 | tf_op jit(solution)/shard_map/ppermute | solution.py:495
  38.3 0.8 %collective-permute-done.6.other = f32[4,640]{1,0:T(4,128)S(1)} collective-permute-done((f32[4,640]{1,0:T(4,128)S(1)}, f32[4,640]{1,0:T(4,128)S(1)}, u32[]{:S(2)}, u32[]{:S(2)}) %collective-permute-start.6) | collective-permute-done | bytes 10272 | tf_op jit(solution)/shard_map/ppermute | solution.py:495
  39.3 9.8 %all_to_all.11.fixes = f32[16,4,640]{2,1,0:T(4,128)S(1)} all-to-all(f32[16,4,640]{2,1,0:T(4,128)S(1)} %shard_map.92), channel_id=1, replica_groups=mesh['patch'=16,'span'=8,'wall'=2] {'patch'}, dimensions={0} | all-to-all | bytes 327680 | tf_op jit(solution)/shard_map/all_to_all | solution.py:497
  49.0 0.3 shard_map.93
  49.4 1.5 %collective-permute-start.8 = (f32[5,8,1024]{2,1,0:T(8,128)S(1)}, f32[5,8,1024]{2,1,0:T(8,128)S(1)}, u32[]{:S(2)}, u32[]{:S(2)}) collective-permute-start(f32[5,8,1024]{2,1,0:T(8,128)S(1)} %get-tuple-element.38.edge_b), channel_id=1, source_target_pairs={{2,4},{4,2},{6,8},{8,6},{10,12},{12,10},{14,0},{0,14},{3,5},{5,3},... | collective-permute-start | bytes 491528 | tf_op jit(solution)/shard_map/ppermute | solution.py:429
  51.0 0.4 shard_map.94
  51.4 2.1 %collective-permute-start.7 = (f32[20,1024]{1,0:T(8,128)S(1)}, f32[20,1024]{1,0:T(8,128)S(1)}, u32[]{:S(2)}, u32[]{:S(2)}) collective-permute-start(f32[20,1024]{1,0:T(8,128)S(1)} %get-tuple-element.44), channel_id=1, source_target_pairs={{0,1},{1,0},{2,3},{3,2},{4,5},{5,4},{6,7},{7,6},{8,9},{9,8},{10,11... | collective-permute-start | bytes 245768 | tf_op jit(solution)/shard_map/ppermute | solution.py:430
  53.5 1.2 %shard_map.95 = (f32[4,5,8,1024]{3,2,1,0:T(8,128)S(1)}, f32[4,5,8,1024]{3,2,1,0:T(8,128)S(1)}, f32[2,5,8,1024]{3,2,1,0:T(8,128)S(1)}) custom-call(f32[2,5,5,8,128]{4,3,2,1,0:T(8,128)S(1)} %get-tuple-element.27.splat, f32[4,5,8,1024]{3,2,1,0:T(8,128)S(1)} %get-tuple-element.40.fix, f32[4,5,5,8,1024]{4,3,2,1,0:T(8,128)S(1)} %bitcast.16, ...), custom_call_target="tpu_custom_call" | custom-call | flops 3379200 | bytes 3379200 | tf_op jit(solution)/shard_map/pallas_call | solution.py:28
  54.7 1.1 %shard_map.96 = (f32[4,5,8,1024]{3,2,1,0:T(8,128)S(1)}, f32[4,5,8,1024]{3,2,1,0:T(8,128)}) custom-call(f32[2,5,5,8,128]{4,3,2,1,0:T(8,128)S(1)} %get-tuple-element.27.splat, f32[4,5,8,1024]{3,2,1,0:T(8,128)S(1)} %get-tuple-element.40.fix, f32[4,5,8,1024]{3,2,1,0:T(8,128)S(1)} %get-tuple-element.43.rest, f32[20,1024]{1,0:T(8,128)S(1)} %collective-permute-done.7.halo_w, ...), custom_call_target="tpu_custom_call" | custom-call | flops 3584000 | bytes 3584000 | tf_op jit(solution)/shard_map/pallas_call | solution.py:28
  55.9 1.1 %shard_map.97 = f32[4,5,8,1024]{3,2,1,0:T(8,128)} custom-call(f32[2,5,5,8,128]{4,3,2,1,0:T(8,128)S(1)} %get-tuple-element.27.splat, f32[4,5,8,1024]{3,2,1,0:T(8,128)S(1)} %get-tuple-element.47.inner, f32[5,8,1024]{2,1,0:T(8,128)S(1)} %collective-permute-done.8.halo_b, ...), custom_call_target="tpu_custom_call", output_to_operand_aliasing={{}: (5, {})} | custom-call | flops 2887680 | bytes 2887680 | tf_op jit(solution)/shard_map/pallas_call | solution.py:28
  (24 shorter events, 0.5 us)
Async XLA Ops:
  0.0 11.4 %copy-start.1 = (f32[4,8,5,5,1024]{4,1,3,2,0:T(8,128)S(1)}, f32[4,8,5,5,1024]{4,1,3,2,0:T(8,128)}, u32[]{:S(2)}) copy-start(f32[4,8,5,5,1024]{4,1,3,2,0:T(8,128)} %param.9) | copy-start | bytes 9830404
  2.0 11.1 %collective-permute-start.1 = (f32[5,8,1024]{2,1,0:T(8,128)S(1)}, f32[5,8,1024]{2,1,0:T(8,128)S(1)}, u32[]{:S(2)}, u32[]{:S(2)}) collective-permute-start(f32[5,8,1024]{2,1,0:T(8,128)S(1)} %get-tuple-element.28.edge_b), channel_id=1, source_target_pairs={{2,4},{4,2},{6,8},{8,6},{10,12},{12,10},{14,0},{0,14},{3,5},{5,3},... | collective-permute-start | bytes 491528 | tf_op jit(solution)/shard_map/ppermute | solution.py:429
  8.4 4.7 %collective-permute-start.2 = (f32[5,8,1024]{2,1,0:T(8,128)S(1)}, f32[5,8,1024]{2,1,0:T(8,128)S(1)}, u32[]{:S(2)}, u32[]{:S(2)}) collective-permute-start(f32[5,8,1024]{2,1,0:T(8,128)S(1)} %get-tuple-element.29.edge_a), channel_id=1, source_target_pairs={{0,2},{2,0},{4,6},{6,4},{8,10},{10,8},{12,14},{14,12},{1,3},{3,1},... | collective-permute-start | bytes 491528 | tf_op jit(solution)/shard_map/ppermute | solution.py:431
  10.3 2.0 %copy-start = (f32[4,8,5,5,1024]{4,1,3,2,0:T(8,128)S(1)}, f32[4,8,5,5,1024]{4,1,3,2,0:T(8,128)}, u32[]{:S(2)}) copy-start(f32[4,8,5,5,1024]{4,1,3,2,0:T(8,128)} %param.10) | copy-start | bytes 9830404
  10.3 2.0 %collective-permute-start = (f32[20,1024]{1,0:T(8,128)S(1)}, f32[20,1024]{1,0:T(8,128)S(1)}, u32[]{:S(2)}, u32[]{:S(2)}) collective-permute-start(f32[20,1024]{1,0:T(8,128)S(1)} %get-tuple-element.32), channel_id=1, source_target_pairs={{0,1},{1,0},{2,3},{3,2},{4,5},{5,4},{6,7},{7,6},{8,9},{9,8},{10,11... | collective-permute-start | bytes 245768 | tf_op jit(solution)/shard_map/ppermute | solution.py:430
  13.6 6.6 %collective-permute-start.4 = (f32[5,8,1024]{2,1,0:T(8,128)S(1)}, f32[5,8,1024]{2,1,0:T(8,128)S(1)}, u32[]{:S(2)}, u32[]{:S(2)}) collective-permute-start(f32[5,8,1024]{2,1,0:T(8,128)S(1)} %get-tuple-element.33.edge_b), channel_id=1, source_target_pairs={{2,4},{4,2},{6,8},{8,6},{10,12},{12,10},{14,0},{0,14},{3,5},{5,3},... | collective-permute-start | bytes 491528 | tf_op jit(solution)/shard_map/ppermute | solution.py:429
  15.2 4.9 %collective-permute-start.5 = (f32[5,8,1024]{2,1,0:T(8,128)S(1)}, f32[5,8,1024]{2,1,0:T(8,128)S(1)}, u32[]{:S(2)}, u32[]{:S(2)}) collective-permute-start(f32[5,8,1024]{2,1,0:T(8,128)S(1)} %get-tuple-element.34.edge_a), channel_id=1, source_target_pairs={{0,2},{2,0},{4,6},{6,4},{8,10},{10,8},{12,14},{14,12},{1,3},{3,1},... | collective-permute-start | bytes 491528 | tf_op jit(solution)/shard_map/ppermute | solution.py:431
  16.1 2.5 %collective-permute-start.3 = (f32[20,1024]{1,0:T(8,128)S(1)}, f32[20,1024]{1,0:T(8,128)S(1)}, u32[]{:S(2)}, u32[]{:S(2)}) collective-permute-start(f32[20,1024]{1,0:T(8,128)S(1)} %shard_map.88), channel_id=1, source_target_pairs={{0,1},{1,0},{2,3},{3,2},{4,5},{5,4},{6,7},{7,6},{8,9},{9,8},{10,11... | collective-permute-start | bytes 245768 | tf_op jit(solution)/shard_map/ppermute | solution.py:430
  18.5 20.6 %copy-start.4 = (f32[1,1,5,10,4]{3,4,2,1,0:T(4,128)S(1)}, f32[1,1,5,10,4]{3,4,2,1,0:T(4,128)}, u32[]{:S(2)}) copy-start(f32[1,1,5,10,4]{3,4,2,1,0:T(4,128)} %param.15) | copy-start | bytes 2404
  18.5 30.5 %copy-start.2 = (s32[4,8,8]{2,1,0:T(8,128)S(1)}, s32[4,8,8]{2,1,0:T(8,128)}, u32[]{:S(2)}) copy-start(s32[4,8,8]{2,1,0:T(8,128)} %owner.3) | copy-start | bytes 3076
  18.6 30.5 %copy-start.3 = (s32[4,8,8]{2,1,0:T(8,128)S(1)}, s32[4,8,8]{2,1,0:T(8,128)}, u32[]{:S(2)}) copy-start(s32[4,8,8]{2,1,0:T(8,128)} %slot.3) | copy-start | bytes 3076
  34.6 4.5 %collective-permute-start.6 = (f32[4,640]{1,0:T(4,128)S(1)}, f32[4,640]{1,0:T(4,128)S(1)}, u32[]{:S(2)}, u32[]{:S(2)}) collective-permute-start(f32[4,640]{1,0:T(4,128)S(1)} %shard_map.91.own), channel_id=1, source_target_pairs={{0,1},{1,0},{2,3},{3,2},{4,5},{5,4},{6,7},{7,6},{8,9},{9,8},{10,11... | collective-permute-start | bytes 30728 | tf_op jit(solution)/shard_map/ppermute | solution.py:495
  49.4 6.5 %collective-permute-start.8 = (f32[5,8,1024]{2,1,0:T(8,128)S(1)}, f32[5,8,1024]{2,1,0:T(8,128)S(1)}, u32[]{:S(2)}, u32[]{:S(2)}) collective-permute-start(f32[5,8,1024]{2,1,0:T(8,128)S(1)} %get-tuple-element.38.edge_b), channel_id=1, source_target_pairs={{2,4},{4,2},{6,8},{8,6},{10,12},{12,10},{14,0},{0,14},{3,5},{5,3},... | collective-permute-start | bytes 491528 | tf_op jit(solution)/shard_map/ppermute | solution.py:429
  50.9 4.9 %collective-permute-start.9 = (f32[5,8,1024]{2,1,0:T(8,128)S(1)}, f32[5,8,1024]{2,1,0:T(8,128)S(1)}, u32[]{:S(2)}, u32[]{:S(2)}) collective-permute-start(f32[5,8,1024]{2,1,0:T(8,128)S(1)} %get-tuple-element.39.edge_a), channel_id=1, source_target_pairs={{0,2},{2,0},{4,6},{6,4},{8,10},{10,8},{12,14},{14,12},{1,3},{3,1},... | collective-permute-start | bytes 491528 | tf_op jit(solution)/shard_map/ppermute | solution.py:431
  51.4 3.3 %collective-permute-start.7 = (f32[20,1024]{1,0:T(8,128)S(1)}, f32[20,1024]{1,0:T(8,128)S(1)}, u32[]{:S(2)}, u32[]{:S(2)}) collective-permute-start(f32[20,1024]{1,0:T(8,128)S(1)} %get-tuple-element.44), channel_id=1, source_target_pairs={{0,1},{1,0},{2,3},{3,2},{4,5},{5,4},{6,7},{7,6},{8,9},{9,8},{10,11... | collective-permute-start | bytes 245768 | tf_op jit(solution)/shard_map/ppermute | solution.py:430

commit v11 on v10

--- a/solution.py
+++ b/solution.py
@@ -140,16 +140,16 @@
 
 
 def first_inner_kernel(splat, edge_b, edge_a, rhs_in, jinv_in, rhs, first, edge_w, raw, jinv, sems):
-    whole = pltpu.make_async_copy(rhs_in, rhs, sems.at[2])
     slabs = [pltpu.make_async_copy(jinv_in.at[1 + m], jinv.at[m], sems.at[m]) for m in range(2)]
-    for copy in (whole, *slabs):
+    sides = [pltpu.make_async_copy(rhs_in.at[s], rhs.at[s], sems.at[2 + s]) for s in range(4)]
+    for copy in (sides[1], slabs[0], sides[2], slabs[1], sides[0], sides[3]):
         copy.start()
     even, _, _, row = position()
     for k in range(5):
         first[0, k] = jnp.where(even, edge_b[k], edge_a[k])
         first[3, k] = jnp.where(even, edge_a[k], edge_b[k])
-    whole.wait()
     for s in (1, 2):
+        sides[s].wait()
         slabs[s - 1].wait()
 
         def body(lanes, s=s):
@@ -162,6 +162,8 @@
         for k in range(5):
             raw[k, s, :] = first[s, k, row, :]
     wall_rows(splat, raw, edge_w)
+    sides[0].wait()
+    sides[3].wait()
 
 
 def local_apply(splat, planes, jac, lanes, s):
@@ -467,7 +469,7 @@
         [field, field, edge],
         [splat, b, a, rhs_in, in_hbm(jinv_in)],
         places=[VMEM] * 3 + [HBM] * 2,
-        scratch=[raw, pltpu.VMEM((2, *jinv_in.shape[1:]), F32), pltpu.SemaphoreType.DMA((3,))],
+        scratch=[raw, pltpu.VMEM((2, *jinv_in.shape[1:]), F32), pltpu.SemaphoreType.DMA((6,))],
     )
     halo_a, halo_b, halo_w = exchange(a, b, w)
     [rest] = call(first_residual_kernel, [field], [splat, first, rhs, jac_in])

time: 57.2 us -> 57.2 us (level)
  no operation moved by 1% of the time
where the time goes in v11:
time: 57.2 us; the launch traced here: 57 us
  blocking collectives  23.3 us (41%)
  starting transfers between devices  18.8 us (33%)
  Pallas kernels  13.6 us (24%)
  waiting for transfers between devices  1.05 us (2%)
    all_to_all x1, blocking collectives, local(): lax.all_to_all(partial, 'patch', split_axis=0, concat_axis=0, tiled=True)  13.6 us
    pallas_call x16, Pallas kernels, call(): pl.pallas_call(kernel, out_shape=outs, in_specs=places or [VMEM] * len(ar...  13.6 us
    all_to_all x1, blocking collectives, local(): lax.all_to_all(reply, 'patch', split_axis=0, concat_axis=0, tiled=True)  9.77 us
    ppermute x3, starting transfers between devices, exchange(): halo_b = lax.ppermute(edge_b, 'span', odd)  9.7 us
    ppermute x3, starting transfers between devices, exchange(): halo_w = lax.ppermute(edge_w, 'wall', [(0, 1), (1, 0)])  4.69 us
    ppermute x1, starting transfers between devices, local(): theirs = lax.ppermute(mine, 'wall', [(0, 1), (1, 0)])  3.71 us
  transfers between devices with their start and end apart: 10, of which 2 were waited for; matrix products, arithmetic and copies ran while one was open for 0% of the time, Pallas kernels for 15%

profile of v11, /device:TPU:1, one launch (start us, length us, event | category | flops | bytes accessed | tf_op | source)
XLA Modules:
  0.0 57.0 jit_solution(10669899189691645802)
XLA Ops:
  0.0 1.9 %shard_map.82 = (f32[5,8,1024]{2,1,0:T(8,128)S(1)}, f32[5,8,1024]{2,1,0:T(8,128)S(1)}, f32[2,5,5,8,128]{4,3,2,1,0:T(8,128)S(1)}, f32[64,256]{1,0:T(8,128)S(1)}) custom-call(f32[5,5]{1,0:T(8,128)} %wall_in.1, f32[5,5]{1,0:T(8,128)} %span_in.1, s32[4,8,8]{2,1,0:T(8,128)} %owner.3, s32[4,8,8]{2,1,0:T(8,128)} %slot.3, f32[4,5,8,1024]{3,2,1,0:T(8,128)} %bitcast.18, ...), custom_call_target="tpu_custom_call" | custom-call | flops 2266212 | bytes 2266212 | tf_op jit(solution)/shard_map/pallas_call | solution.py:28
  2.0 6.5 %collective-permute-start.1 = (f32[5,8,1024]{2,1,0:T(8,128)S(1)}, f32[5,8,1024]{2,1,0:T(8,128)S(1)}, u32[]{:S(2)}, u32[]{:S(2)}) collective-permute-start(f32[5,8,1024]{2,1,0:T(8,128)S(1)} %get-tuple-element.28.edge_b), channel_id=1, source_target_pairs={{2,4},{4,2},{6,8},{8,6},{10,12},{12,10},{14,0},{0,14},{3,5},{5,3},... | collective-permute-start | bytes 491528 | tf_op jit(solution)/shard_map/ppermute | solution.py:431
  8.4 1.8 %shard_map.83 = (f32[4,5,8,1024]{3,2,1,0:T(8,128)S(1)}, f32[4,5,8,1024]{3,2,1,0:T(8,128)S(1)}, f32[20,1024]{1,0:T(8,128)S(1)}) custom-call(f32[2,5,5,8,128]{4,3,2,1,0:T(8,128)S(1)} %get-tuple-element.27.splat, f32[5,8,1024]{2,1,0:T(8,128)S(1)} %get-tuple-element.28.edge_b, f32[5,8,1024]{2,1,0:T(8,128)S(1)} %get-tuple-element.29.edge_a, ...), custom_call_target="tpu_custom_call" | custom-call | flops 2928640 | bytes 2928640 | tf_op jit(solution)/shard_map/pallas_call | solution.py:28
  10.3 1.0 %collective-permute-start = (f32[20,1024]{1,0:T(8,128)S(1)}, f32[20,1024]{1,0:T(8,128)S(1)}, u32[]{:S(2)}, u32[]{:S(2)}) collective-permute-start(f32[20,1024]{1,0:T(8,128)S(1)} %get-tuple-element.32), channel_id=1, source_target_pairs={{0,1},{1,0},{2,3},{3,2},{4,5},{5,4},{6,7},{7,6},{8,9},{9,8},{10,11... | collective-permute-start | bytes 245768 | tf_op jit(solution)/shard_map/ppermute | solution.py:432
  11.4 0.9 %shard_map.84.rest = f32[4,5,8,1024]{3,2,1,0:T(8,128)S(1)} custom-call(f32[2,5,5,8,128]{4,3,2,1,0:T(8,128)S(1)} %get-tuple-element.27.splat, f32[4,5,8,1024]{3,2,1,0:T(8,128)S(1)} %get-tuple-element.30.first, f32[4,5,8,1024]{3,2,1,0:T(8,128)S(1)} %get-tuple-element.31.rhs, f32[4,5,5,8,1024]{4,3,2,1,0:T(8,128)S(1)} %bitcast.14), custom_call_target="tpu_custom_call" | custom-call | flops 2723840 | bytes 2723840 | tf_op jit(solution)/shard_map/pallas_call | solution.py:28
  12.3 0.7 %shard_map.85.inner = f32[4,5,8,1024]{3,2,1,0:T(8,128)S(1)} custom-call(f32[4,5,8,1024]{3,2,1,0:T(8,128)S(1)} %get-tuple-element.30.first, f32[4,5,8,1024]{3,2,1,0:T(8,128)S(1)} %shard_map.84.rest, f32[20,1024]{1,0:T(8,128)S(1)} %collective-permute-done.halo_w, f32[4,5,5,8,1024]{4,3,2,1,0:T(8,128)S(1)} %bitcast.9), custom_call_target="tpu_custom_call" | custom-call | flops 2662400 | bytes 2662400 | tf_op jit(solution)/shard_map/pallas_call | solution.py:28
  13.2 0.4 shard_map.86
  13.6 1.7 %collective-permute-start.4 = (f32[5,8,1024]{2,1,0:T(8,128)S(1)}, f32[5,8,1024]{2,1,0:T(8,128)S(1)}, u32[]{:S(2)}, u32[]{:S(2)}) collective-permute-start(f32[5,8,1024]{2,1,0:T(8,128)S(1)} %get-tuple-element.33.edge_b), channel_id=1, source_target_pairs={{2,4},{4,2},{6,8},{8,6},{10,12},{12,10},{14,0},{0,14},{3,5},{5,3},... | collective-permute-start | bytes 491528 | tf_op jit(solution)/shard_map/ppermute | solution.py:431
  15.2 0.7 %collective-permute-start.5 = (f32[5,8,1024]{2,1,0:T(8,128)S(1)}, f32[5,8,1024]{2,1,0:T(8,128)S(1)}, u32[]{:S(2)}, u32[]{:S(2)}) collective-permute-start(f32[5,8,1024]{2,1,0:T(8,128)S(1)} %get-tuple-element.34.edge_a), channel_id=1, source_target_pairs={{0,2},{2,0},{4,6},{6,4},{8,10},{10,8},{12,14},{14,12},{1,3},{3,1},... | collective-permute-start | bytes 491528 | tf_op jit(solution)/shard_map/ppermute | solution.py:433
  16.0 1.5 %collective-permute-start.3 = (f32[20,1024]{1,0:T(8,128)S(1)}, f32[20,1024]{1,0:T(8,128)S(1)}, u32[]{:S(2)}, u32[]{:S(2)}) collective-permute-start(f32[20,1024]{1,0:T(8,128)S(1)} %shard_map.88), channel_id=1, source_target_pairs={{0,1},{1,0},{2,3},{3,2},{4,5},{5,4},{6,7},{7,6},{8,9},{9,8},{10,11... | collective-permute-start | bytes 245768 | tf_op jit(solution)/shard_map/ppermute | solution.py:432
  17.6 0.9 %shard_map.87.rest = f32[4,5,8,1024]{3,2,1,0:T(8,128)S(1)} custom-call(f32[2,5,5,8,128]{4,3,2,1,0:T(8,128)S(1)} %get-tuple-element.27.splat, f32[4,5,8,1024]{3,2,1,0:T(8,128)S(1)} %shard_map.85.inner, f32[5,8,1024]{2,1,0:T(8,128)S(1)} %get-tuple-element.33.edge_b, f32[5,8,1024]{2,1,0:T(8,128)S(1)} %get-tuple-element.34.edge_a, ...), custom_call_target="tpu_custom_call" | custom-call | flops 2887680 | bytes 2887680 | tf_op jit(solution)/shard_map/pallas_call | solution.py:28
  18.5 1.6 %shard_map.89 = (f32[64,640]{1,0:T(8,128)S(1)}, f32[4,5,8,1024]{3,2,1,0:T(8,128)}) custom-call(f32[4,5,8,1024]{3,2,1,0:T(8,128)S(1)} %shard_map.85.inner, f32[5,8,1024]{2,1,0:T(8,128)S(1)} %get-tuple-element.33.edge_b, f32[5,8,1024]{2,1,0:T(8,128)S(1)} %get-tuple-element.34.edge_a, f32[4,5,8,1024]{3,2,1,0:T(8,128)S(1)} %shard_map.87.rest, ...), custom_call_target="tpu_custom_call" | custom-call | flops 2940928 | bytes 2940928 | tf_op jit(solution)/shard_map/pallas_call | solution.py:28
  20.1 0.8 %shard_map.90 = (f32[16,4,640]{2,1,0:T(4,128)S(1)}, f32[2,5,8,1024]{3,2,1,0:T(8,128)}) custom-call(f32[2,5,5,8,128]{4,3,2,1,0:T(8,128)S(1)} %get-tuple-element.27.splat, f32[64,640]{1,0:T(8,128)S(1)} %get-tuple-element.36.inner, f32[5,8,1024]{2,1,0:T(8,128)S(1)} %collective-permute-done.4.halo_b, f32[5,8,1024]{2,1,0:T(8,128)S(1)} %collective-permute-done.5.halo_a, ...), custom_call_target="tpu_custom_call" | custom-call | flops 626688 | bytes 626688 | tf_op jit(solution)/shard_map/pallas_call | solution.py:28
  21.0 13.6 %all_to_all.10.received = f32[16,4,640]{2,1,0:T(4,128)S(1)} all-to-all(f32[16,4,640]{2,1,0:T(4,128)S(1)} %get-tuple-element.37), channel_id=1, replica_groups=mesh['patch'=16,'span'=8,'wall'=2] {'patch'}, dimensions={0} | all-to-all | bytes 327680 | tf_op jit(solution)/shard_map/all_to_all | solution.py:495
  34.6 3.7 %collective-permute-start.6 = (f32[4,640]{1,0:T(4,128)S(1)}, f32[4,640]{1,0:T(4,128)S(1)}, u32[]{:S(2)}, u32[]{:S(2)}) collective-permute-start(f32[4,640]{1,0:T(4,128)S(1)} %shard_map.91.own), channel_id=1, source_target_pairs={{0,1},{1,0},{2,3},{3,2},{4,5},{5,4},{6,7},{7,6},{8,9},{9,8},{10,11... | collective-permute-start | bytes 30728 | tf_op jit(solution)/shard_map/ppermute | solution.py:497
  38.3 0.8 %collective-permute-done.6.other = f32[4,640]{1,0:T(4,128)S(1)} collective-permute-done((f32[4,640]{1,0:T(4,128)S(1)}, f32[4,640]{1,0:T(4,128)S(1)}, u32[]{:S(2)}, u32[]{:S(2)}) %collective-permute-start.6) | collective-permute-done | bytes 10272 | tf_op jit(solution)/shard_map/ppermute | solution.py:497
  39.3 9.8 %all_to_all.11.fixes = f32[16,4,640]{2,1,0:T(4,128)S(1)} all-to-all(f32[16,4,640]{2,1,0:T(4,128)S(1)} %shard_map.92), channel_id=1, replica_groups=mesh['patch'=16,'span'=8,'wall'=2] {'patch'}, dimensions={0} | all-to-all | bytes 327680 | tf_op jit(solution)/shard_map/all_to_all | solution.py:499
  49.0 0.3 shard_map.93
  49.4 1.5 %collective-permute-start.8 = (f32[5,8,1024]{2,1,0:T(8,128)S(1)}, f32[5,8,1024]{2,1,0:T(8,128)S(1)}, u32[]{:S(2)}, u32[]{:S(2)}) collective-permute-start(f32[5,8,1024]{2,1,0:T(8,128)S(1)} %get-tuple-element.38.edge_b), channel_id=1, source_target_pairs={{2,4},{4,2},{6,8},{8,6},{10,12},{12,10},{14,0},{0,14},{3,5},{5,3},... | collective-permute-start | bytes 491528 | tf_op jit(solution)/shard_map/ppermute | solution.py:431
  51.0 0.4 shard_map.94
  51.4 2.1 %collective-permute-start.7 = (f32[20,1024]{1,0:T(8,128)S(1)}, f32[20,1024]{1,0:T(8,128)S(1)}, u32[]{:S(2)}, u32[]{:S(2)}) collective-permute-start(f32[20,1024]{1,0:T(8,128)S(1)} %get-tuple-element.44), channel_id=1, source_target_pairs={{0,1},{1,0},{2,3},{3,2},{4,5},{5,4},{6,7},{7,6},{8,9},{9,8},{10,11... | collective-permute-start | bytes 245768 | tf_op jit(solution)/shard_map/ppermute | solution.py:432
  53.5 1.2 %shard_map.95 = (f32[4,5,8,1024]{3,2,1,0:T(8,128)S(1)}, f32[4,5,8,1024]{3,2,1,0:T(8,128)S(1)}, f32[2,5,8,1024]{3,2,1,0:T(8,128)S(1)}) custom-call(f32[2,5,5,8,128]{4,3,2,1,0:T(8,128)S(1)} %get-tuple-element.27.splat, f32[4,5,8,1024]{3,2,1,0:T(8,128)S(1)} %get-tuple-element.40.fix, f32[4,5,5,8,1024]{4,3,2,1,0:T(8,128)S(1)} %bitcast.16, ...), custom_call_target="tpu_custom_call" | custom-call | flops 3379200 | bytes 3379200 | tf_op jit(solution)/shard_map/pallas_call | solution.py:28
  54.7 1.1 %shard_map.96 = (f32[4,5,8,1024]{3,2,1,0:T(8,128)S(1)}, f32[4,5,8,1024]{3,2,1,0:T(8,128)}) custom-call(f32[2,5,5,8,128]{4,3,2,1,0:T(8,128)S(1)} %get-tuple-element.27.splat, f32[4,5,8,1024]{3,2,1,0:T(8,128)S(1)} %get-tuple-element.40.fix, f32[4,5,8,1024]{3,2,1,0:T(8,128)S(1)} %get-tuple-element.43.rest, f32[20,1024]{1,0:T(8,128)S(1)} %collective-permute-done.7.halo_w, ...), custom_call_target="tpu_custom_call" | custom-call | flops 3584000 | bytes 3584000 | tf_op jit(solution)/shard_map/pallas_call | solution.py:28
  55.9 1.1 %shard_map.97 = f32[4,5,8,1024]{3,2,1,0:T(8,128)} custom-call(f32[2,5,5,8,128]{4,3,2,1,0:T(8,128)S(1)} %get-tuple-element.27.splat, f32[4,5,8,1024]{3,2,1,0:T(8,128)S(1)} %get-tuple-element.47.inner, f32[5,8,1024]{2,1,0:T(8,128)S(1)} %collective-permute-done.8.halo_b, ...), custom_call_target="tpu_custom_call", output_to_operand_aliasing={{}: (5, {})} | custom-call | flops 2887680 | bytes 2887680 | tf_op jit(solution)/shard_map/pallas_call | solution.py:28
  (24 shorter events, 0.5 us)
Async XLA Ops:
  0.0 11.4 %copy-start.1 = (f32[4,8,5,5,1024]{4,1,3,2,0:T(8,128)S(1)}, f32[4,8,5,5,1024]{4,1,3,2,0:T(8,128)}, u32[]{:S(2)}) copy-start(f32[4,8,5,5,1024]{4,1,3,2,0:T(8,128)} %param.9) | copy-start | bytes 9830404
  2.0 11.1 %collective-permute-start.1 = (f32[5,8,1024]{2,1,0:T(8,128)S(1)}, f32[5,8,1024]{2,1,0:T(8,128)S(1)}, u32[]{:S(2)}, u32[]{:S(2)}) collective-permute-start(f32[5,8,1024]{2,1,0:T(8,128)S(1)} %get-tuple-element.28.edge_b), channel_id=1, source_target_pairs={{2,4},{4,2},{6,8},{8,6},{10,12},{12,10},{14,0},{0,14},{3,5},{5,3},... | collective-permute-start | bytes 491528 | tf_op jit(solution)/shard_map/ppermute | solution.py:431
  8.4 4.7 %collective-permute-start.2 = (f32[5,8,1024]{2,1,0:T(8,128)S(1)}, f32[5,8,1024]{2,1,0:T(8,128)S(1)}, u32[]{:S(2)}, u32[]{:S(2)}) collective-permute-start(f32[5,8,1024]{2,1,0:T(8,128)S(1)} %get-tuple-element.29.edge_a), channel_id=1, source_target_pairs={{0,2},{2,0},{4,6},{6,4},{8,10},{10,8},{12,14},{14,12},{1,3},{3,1},... | collective-permute-start | bytes 491528 | tf_op jit(solution)/shard_map/ppermute | solution.py:433
  10.3 2.0 %copy-start = (f32[4,8,5,5,1024]{4,1,3,2,0:T(8,128)S(1)}, f32[4,8,5,5,1024]{4,1,3,2,0:T(8,128)}, u32[]{:S(2)}) copy-start(f32[4,8,5,5,1024]{4,1,3,2,0:T(8,128)} %param.10) | copy-start | bytes 9830404
  10.3 2.0 %collective-permute-start = (f32[20,1024]{1,0:T(8,128)S(1)}, f32[20,1024]{1,0:T(8,128)S(1)}, u32[]{:S(2)}, u32[]{:S(2)}) collective-permute-start(f32[20,1024]{1,0:T(8,128)S(1)} %get-tuple-element.32), channel_id=1, source_target_pairs={{0,1},{1,0},{2,3},{3,2},{4,5},{5,4},{6,7},{7,6},{8,9},{9,8},{10,11... | collective-permute-start | bytes 245768 | tf_op jit(solution)/shard_map/ppermute | solution.py:432
  13.6 6.6 %collective-permute-start.4 = (f32[5,8,1024]{2,1,0:T(8,128)S(1)}, f32[5,8,1024]{2,1,0:T(8,128)S(1)}, u32[]{:S(2)}, u32[]{:S(2)}) collective-permute-start(f32[5,8,1024]{2,1,0:T(8,128)S(1)} %get-tuple-element.33.edge_b), channel_id=1, source_target_pairs={{2,4},{4,2},{6,8},{8,6},{10,12},{12,10},{14,0},{0,14},{3,5},{5,3},... | collective-permute-start | bytes 491528 | tf_op jit(solution)/shard_map/ppermute | solution.py:431
  15.2 4.9 %collective-permute-start.5 = (f32[5,8,1024]{2,1,0:T(8,128)S(1)}, f32[5,8,1024]{2,1,0:T(8,128)S(1)}, u32[]{:S(2)}, u32[]{:S(2)}) collective-permute-start(f32[5,8,1024]{2,1,0:T(8,128)S(1)} %get-tuple-element.34.edge_a), channel_id=1, source_target_pairs={{0,2},{2,0},{4,6},{6,4},{8,10},{10,8},{12,14},{14,12},{1,3},{3,1},... | collective-permute-start | bytes 491528 | tf_op jit(solution)/shard_map/ppermute | solution.py:433
  16.0 2.5 %collective-permute-start.3 = (f32[20,1024]{1,0:T(8,128)S(1)}, f32[20,1024]{1,0:T(8,128)S(1)}, u32[]{:S(2)}, u32[]{:S(2)}) collective-permute-start(f32[20,1024]{1,0:T(8,128)S(1)} %shard_map.88), channel_id=1, source_target_pairs={{0,1},{1,0},{2,3},{3,2},{4,5},{5,4},{6,7},{7,6},{8,9},{9,8},{10,11... | collective-permute-start | bytes 245768 | tf_op jit(solution)/shard_map/ppermute | solution.py:432
  18.5 20.6 %copy-start.4 = (f32[1,1,5,10,4]{3,4,2,1,0:T(4,128)S(1)}, f32[1,1,5,10,4]{3,4,2,1,0:T(4,128)}, u32[]{:S(2)}) copy-start(f32[1,1,5,10,4]{3,4,2,1,0:T(4,128)} %param.15) | copy-start | bytes 2404
  18.5 30.5 %copy-start.2 = (s32[4,8,8]{2,1,0:T(8,128)S(1)}, s32[4,8,8]{2,1,0:T(8,128)}, u32[]{:S(2)}) copy-start(s32[4,8,8]{2,1,0:T(8,128)} %owner.3) | copy-start | bytes 3076
  18.5 30.5 %copy-start.3 = (s32[4,8,8]{2,1,0:T(8,128)S(1)}, s32[4,8,8]{2,1,0:T(8,128)}, u32[]{:S(2)}) copy-start(s32[4,8,8]{2,1,0:T(8,128)} %slot.3) | copy-start | bytes 3076
  34.6 4.5 %collective-permute-start.6 = (f32[4,640]{1,0:T(4,128)S(1)}, f32[4,640]{1,0:T(4,128)S(1)}, u32[]{:S(2)}, u32[]{:S(2)}) collective-permute-start(f32[4,640]{1,0:T(4,128)S(1)} %shard_map.91.own), channel_id=1, source_target_pairs={{0,1},{1,0},{2,3},{3,2},{4,5},{5,4},{6,7},{7,6},{8,9},{9,8},{10,11... | collective-permute-start | bytes 30728 | tf_op jit(solution)/shard_map/ppermute | solution.py:497
  49.4 6.5 %collective-permute-start.8 = (f32[5,8,1024]{2,1,0:T(8,128)S(1)}, f32[5,8,1024]{2,1,0:T(8,128)S(1)}, u32[]{:S(2)}, u32[]{:S(2)}) collective-permute-start(f32[5,8,1024]{2,1,0:T(8,128)S(1)} %get-tuple-element.38.edge_b), channel_id=1, source_target_pairs={{2,4},{4,2},{6,8},{8,6},{10,12},{12,10},{14,0},{0,14},{3,5},{5,3},... | collective-permute-start | bytes 491528 | tf_op jit(solution)/shard_map/ppermute | solution.py:431
  50.9 4.9 %collective-permute-start.9 = (f32[5,8,1024]{2,1,0:T(8,128)S(1)}, f32[5,8,1024]{2,1,0:T(8,128)S(1)}, u32[]{:S(2)}, u32[]{:S(2)}) collective-permute-start(f32[5,8,1024]{2,1,0:T(8,128)S(1)} %get-tuple-element.39.edge_a), channel_id=1, source_target_pairs={{0,2},{2,0},{4,6},{6,4},{8,10},{10,8},{12,14},{14,12},{1,3},{3,1},... | collective-permute-start | bytes 491528 | tf_op jit(solution)/shard_map/ppermute | solution.py:433
  51.4 3.3 %collective-permute-start.7 = (f32[20,1024]{1,0:T(8,128)S(1)}, f32[20,1024]{1,0:T(8,128)S(1)}, u32[]{:S(2)}, u32[]{:S(2)}) collective-permute-start(f32[20,1024]{1,0:T(8,128)S(1)} %get-tuple-element.44), channel_id=1, source_target_pairs={{0,1},{1,0},{2,3},{3,2},{4,5},{5,4},{6,7},{7,6},{8,9},{9,8},{10,11... | collective-permute-start | bytes 245768 | tf_op jit(solution)/shard_map/ppermute | solution.py:432
